TPU v7x, 32 devices: a whole 2x2x4 slice. The times are simulated.
32 devices in a mesh: layer: 2 (over x), row: 16 (over z, y, core).
Axes of the slice: x: 2, y: 2, z: 4, core: 2. Of those that a mesh axis runs over, the one named last changes fastest.
Arguments:
- left_factors: bfloat16 [2, 16384, 128], P('layer', 'row'), may hold values from -0.375 to 0.375
- right_factors: bfloat16 [2, 16384, 128], P('layer', 'row'), may hold values from -0.1875 to 0.1875
- sketch: bfloat16 [16384, 128], P('row'), may hold values from -0.1875 to 0.1875
- row_basis: bfloat16 [16384, 128], P('row'), may hold values from -0.4375 to 0.4375
- inverse_diag: bfloat16 [16384, 1024], P('row'), may hold values from -0.0625 to 1.44125, as said below
- right_side: bfloat16 [16384, 1024], P('row', 'layer'), may hold values from -6 to 6
- incoming: float32 [128, 1024], P(None, 'layer'), may hold values from -6 to 6
Outputs:
- solution: bfloat16 [16384, 1024], P('row', 'layer')
Inputs may be any that keep to these rules, and one draw needn't show every extreme that they name: `inverse_diag`: each block of 1024 rows is the inverse of that row group's diagonal tile.
All inputs are finite; a program needn't handle non-finite values.
Results may differ from a plain program's by a relative error of at most 0.0095.
Values may be sent and summed in bfloat16 or wider, within the bound.
No kernel may reach another device: no remote copies, remote signals or barrier semaphores. Data moves between devices by JAX's collectives and lax.ppermute only.
A program may use at most 128 MiB of HBM per device.

v0:
```python
import jax
import jax.numpy as jnp
from jax import lax
from jax.sharding import PartitionSpec as P


def shifted(value, axis, steps):
    count = lax.axis_size(axis)
    leading, last = (max(0, -steps), min(count, count - steps))
    return lax.ppermute(value, axis, [(source, source + steps) for source in range(leading, last)])


def entering(value, axis, combine, identity):
    count, here = (lax.axis_size(axis), lax.axis_index(axis))
    everything = jax.tree.map(lambda part: lax.all_gather(part, axis), value)
    start = jax.tree.map(
        lambda part, zero: jnp.broadcast_to(jnp.asarray(zero, part.dtype), part.shape),
        value,
        identity,
    )

    def lap(k, before):
        reached = k < here
        new = combine(before, jax.tree.map(lambda part: part[k], everything))
        return jax.tree.map(lambda a, b: jnp.where(reached, a, b), new, before)

    return lax.fori_loop(0, count, lap, start)


def project(basis, vectors):
    return lax.dot_general(
        basis, vectors, (((0,), (0,)), ((), ())), preferred_element_type=jnp.float32
    )


def body(left_factors, right_factors, sketch, row_basis, inverse_diag, right_side, incoming):
    full = lax.Precision.HIGHEST
    rank = sketch.shape[1]
    width = right_side.shape[1]
    core = project(right_factors[0], sketch).astype(jnp.bfloat16)
    partial_range = -jnp.dot(left_factors[0], core, preferred_element_type=jnp.float32)
    tile_range = lax.psum(partial_range, "layer").astype(jnp.bfloat16)
    applied = jnp.dot(inverse_diag, right_side, preferred_element_type=jnp.float32).astype(
        jnp.bfloat16
    )
    gain = jnp.dot(inverse_diag, tile_range, preferred_element_type=jnp.float32).astype(
        jnp.bfloat16
    )

    def combine(earlier, later):
        return (
            jnp.dot(later[0], earlier[0], precision=full),
            jnp.dot(later[0], earlier[1], precision=full) + later[1],
        )

    identity = (jnp.eye(rank, dtype=jnp.float32), jnp.zeros((rank, width), jnp.float32))
    next_rows = shifted(row_basis, "row", -1)
    step_map = -project(next_rows, gain)
    step_shift = project(next_rows, applied)
    prefix = entering((step_map, step_shift), "row", combine, identity)
    coupled = jnp.dot(prefix[0], incoming, precision=full) + prefix[1]
    result = applied.astype(jnp.float32) - jnp.dot(
        gain.astype(jnp.float32), coupled, precision=full
    )
    return result.astype(jnp.bfloat16)


def solution(mesh):
    return jax.shard_map(
        body,
        mesh=mesh,
        in_specs=(
            P("layer", "row", None),
            P("layer", "row", None),
            P("row", None),
            P("row", None),
            P("row", None),
            P("row", "layer"),
            P(None, "layer"),
        ),
        out_specs=P("row", "layer"),
        check_vma=False,
    )
```

profile of v0, /device:TPU:0, one launch (start us, length us, event | category | flops | bytes accessed | tf_op | source)
XLA Modules:
  0.0 181.3 jit_solution(14721510377165093769)
XLA Ops:
  6.5 1.4 collective-permute-start
  8.0 1.6 fusion.11
  9.6 20.7 %all-reduce.1 = bf16[1024,128]{0,1:T(8,128)(2,1)S(1)} all-reduce(f32[1024,128]{0,1:T(8,128)S(1)} %fusion.11), channel_id=1, replica_groups=mesh['layer'=2,'row'=16] {'layer'}, use_global_device_ids=true, to_apply=%region_0.0 | all-reduce | flops 131072 | bytes 786432 | tf_op jit(solution)/shard_map/psum | solution.py:42
  32.8 2.5 %convolution_convert_fusion = bf16[1024,512]{1,0:T(8,128)(2,1)S(1)} fusion(bf16[1024,1024]{1,0:T(8,128)(2,1)S(1)} %copy-done, bf16[1024,512]{1,0:T(8,128)(2,1)} %param.14), kind=kOutput, calls=%fused_computation.14 | convolution fusion | flops 1074266112 | bytes 4194304 | tf_op jit(solution)/shard_map/dot_general | solution.py:43
  36.5 33.5 %all-gather.5.cloned.1.call-done = f32[2048,128]{0,1:T(8,128)} async-done(((f32[128,128]{0,1:T(8,128)}), f32[2048,128]{0,1:T(8,128)}) %all-gather.5.cloned.1.call-update) | async-done | bytes 1048592 | tf_op jit(solution)/shard_map/all_gather | solution.py:15
  70.0 2.5 %copy.10 = f32[2048,128]{1,0:T(8,128)} copy(f32[2048,128]{0,1:T(8,128)} %all-gather.5.cloned.1.call-done) | data formatting | bytes 2097152
  72.5 52.4 %all-gather.7.cloned.1.call-done = f32[2048,512]{0,1:T(8,128)} async-done(((f32[128,512]{0,1:T(8,128)}), f32[2048,512]{0,1:T(8,128)}) %all-gather.7.cloned.1.call-update) | async-done | bytes 4194320 | tf_op jit(solution)/shard_map/all_gather | solution.py:15
  124.9 5.4 %copy.11 = f32[2048,512]{1,0:T(8,128)} copy(f32[2048,512]{0,1:T(8,128)} %all-gather.7.cloned.1.call-done) | data formatting | bytes 8388608
  130.2 39.9 %while.16 = (s32[]{:T(128)}, f32[128,128]{1,0:T(8,128)S(1)}, f32[128,512]{1,0:T(8,128)S(1)}, s32[]{:T(128)}, f32[16,128,128]{2,1,0:T(8,128)}, /*index=5*/f32[16,128,512]{2,1,0:T(8,128)}, s32[]{:T(128)}, s32[]{:T(128)}) while((s32[]{:T(128)}, f32[128,128]{1,0:T(8,128)S(1)}, f32[128,512]{1,0:T(8,128)S(1)}, s32[]{:T(128)}, ...), condition=%wide.region_2.3_spmd.clone, body=%wide.region_1.2_spmd.clone.sunk | while | flops 126107648 | bytes 2034792 | solution.py:27
  130.2 1.4 fusion.41
  132.7 1.4 fusion.41
  135.2 1.4 fusion.41
  137.7 1.4 fusion.41
  140.2 1.4 fusion.41
  142.7 1.4 fusion.41
  145.2 1.4 fusion.41
  147.7 1.4 fusion.41
  150.2 1.4 fusion.41
  152.7 1.4 fusion.41
  155.2 1.4 fusion.41
  157.7 1.4 fusion.41
  160.2 1.4 fusion.41
  165.2 1.4 fusion.41
  171.5 3.0 %subtract_convert_fusion = bf16[1024,512]{1,0:T(8,128)(2,1)} fusion(bf16[1024,512]{1,0:T(8,128)(2,1)S(1)} %convolution_convert_fusion, bf16[128,1024]{1,0:T(8,128)(2,1)} %copy-done.1, f32[128,512]{1,0:T(8,128)S(1)} %convolution_add_fusion.1), kind=kOutput, calls=%fused_computation.13 | convolution fusion | flops 806879232 | bytes 2621440 | tf_op jit(solution)/shard_map/dot_general | solution.py:62
  (65 shorter events, 24.9 us)
Async XLA Ops:
  6.5 23.8 %copy-start = (bf16[1024,1024]{1,0:T(8,128)(2,1)S(1)}, bf16[1024,1024]{1,0:T(8,128)(2,1)}, u32[]{:S(2)}) copy-start(bf16[1024,1024]{1,0:T(8,128)(2,1)} %param.13) | copy-start | bytes 6291460
  6.5 63.4 %all-gather.5.cloned.1.call-start = ((), (), s32[]{:S(2)}) async-start(), calls=%async_computation | async-start | bytes 1114112 | tf_op jit(solution)/shard_map/all_gather | solution.py:15
  6.5 24.6 %collective-permute-start = (bf16[1024,128]{1,0:T(8,128)(2,1)}, bf16[1024,128]{1,0:T(8,128)(2,1)S(1)}, u32[]{:S(2)}, u32[]{:S(2)}) collective-permute-start(bf16[1024,128]{1,0:T(8,128)(2,1)} %param.12), channel_id=1, source_target_pairs={{1,0},{2,1},{3,2},{4,3},{5,4},{6,5},{7,6},{8,7},{9,8},{10,9},{11,1... | collective-permute-start | bytes 786440 | tf_op jit(solution)/shard_map/ppermute | solution.py:10
  31.1 0.7 copy-start.1
  32.7 92.1 %all-gather.7.cloned.1.call-start = ((), (), s32[]{:S(2)}) async-start(), calls=%async_computation.1 | async-start | bytes 4456448 | tf_op jit(solution)/shard_map/all_gather | solution.py:15
Sparse Core Ops, SparseCore 0:
  32.9 37.0 all-gather.4
  72.1 52.6 all-gather.6
where the time goes:
time: 183 us; the launch traced here: 181 us
  waiting for transfers between devices  85.9 us (47%)
  matrix products  50 us (27%)
  blocking collectives  20.7 us (11%)
  between operations  13.5 us (7%)
  local copies, waits for them, and re-layouts  9 us (5%)
    all_gather x2, waiting for transfers between devices, entering(): everything = jax.tree.map(lambda part: lax.all_gather(part, axis), value)  85.8 us
    dot_general x16, matrix products, combine(): jnp.dot(later[0], earlier[1], precision=full) + later[1]  21.9 us
    psum x1, blocking collectives, body(): tile_range = lax.psum(partial_range, 'layer').astype(jnp.bfloat16)  20.7 us
    dot_general x16, matrix products, combine(): jnp.dot(later[0], earlier[0], precision=full)  16.8 us
    unnamed x6, local copies, waits for them, and re-layouts  8.6 us
  transfers between devices with their start and end apart: 3, of which 2 were waited for; matrix products, arithmetic and copies ran while one was open for 5% of the time, Pallas kernels for 0%

commit v1 on v0

v1 whole, which is shorter than its diff:
```python
import jax
import jax.numpy as jnp
from jax import lax
from jax.sharding import PartitionSpec as P


def shifted(value, axis, steps):
    count = lax.axis_size(axis)
    leading, last = (max(0, -steps), min(count, count - steps))
    return lax.ppermute(value, axis, [(source, source + steps) for source in range(leading, last)])


def rotated(value, axis, steps):
    count = lax.axis_size(axis)
    return lax.ppermute(value, axis, [(source, (source + steps) % count) for source in range(count)])


def project(basis, vectors):
    return lax.dot_general(
        basis, vectors, (((0,), (0,)), ((), ())), preferred_element_type=jnp.float32
    )


def product(a, b):
    return jnp.dot(a, b, preferred_element_type=jnp.float32)


def body(left_factors, right_factors, sketch, row_basis, inverse_diag, right_side, incoming):
    half = jnp.bfloat16
    rank = sketch.shape[1]
    layers, groups = lax.axis_size("layer"), lax.axis_size("row")
    here = lax.axis_index("row")

    lefts = [left_factors[0]] + [rotated(left_factors[0], "layer", k) for k in range(1, layers)]
    next_rows = shifted(row_basis, "row", -1)
    core = project(right_factors[0], sketch).astype(half)
    cores = [core] + [rotated(core, "layer", k) for k in range(1, layers)]
    applied = product(inverse_diag, right_side).astype(half)
    tile_range = -sum(product(left, core) for left, core in zip(lefts, cores))
    gain = product(inverse_diag, tile_range.astype(half)).astype(half)
    step_map = -project(next_rows, gain)
    step_shift = project(next_rows, applied)

    step = jnp.concatenate([step_map, step_shift], axis=1).astype(half)
    begin = jnp.concatenate([jnp.zeros_like(step_map), incoming], axis=1).astype(half)

    def combine(later, earlier):
        moved = product(later[:, :rank], earlier)
        return moved + jnp.pad(later[:, rank:].astype(jnp.float32), ((0, 0), (rank, 0)))

    first = jnp.where(here == 0, begin, shifted(step, "row", 1))
    second = jnp.where(here == 1, begin, shifted(step, "row", 2))
    prefix = combine(first, second)
    span = 2
    while span < groups:
        sent = prefix.astype(half)
        if span * 2 >= groups:
            arrived = shifted(sent[:, rank:], "row", span)
            coupled = product(sent[:, :rank], arrived) + prefix[:, rank:]
        else:
            arrived = shifted(sent, "row", span)
            prefix = product(sent[:, :rank], arrived) + jnp.pad(prefix[:, rank:], ((0, 0), (rank, 0)))
        span *= 2
    result = applied.astype(jnp.float32) - product(gain, coupled.astype(half))
    return result.astype(half)


def solution(mesh):
    return jax.shard_map(
        body,
        mesh=mesh,
        in_specs=(
            P("layer", "row", None),
            P("layer", "row", None),
            P("row", None),
            P("row", None),
            P("row", None),
            P("row", "layer"),
            P(None, "layer"),
        ),
        out_specs=P("row", "layer"),
        check_vma=False,
    )
```

time: 183 us -> 63.4 us (0.35)
  the two profiles are of different devices: /device:TPU:0 before, /device:TPU:24 now
where the time goes in v1:
time: 63.4 us; the launch traced here: 63 us
  waiting for transfers between devices  29.7 us (47%)
  starting transfers between devices  16.2 us (26%)
  matrix products  13.5 us (21%)
  local copies, waits for them, and re-layouts  1.79 us (3%)
  other arithmetic  1.64 us (3%)
    ppermute x6, waiting for transfers between devices, shifted(): lax.ppermute(value, axis, [(source, source + steps) for source in range(l...  25.3 us
    ppermute x6, starting transfers between devices, shifted(): lax.ppermute(value, axis, [(source, source + steps) for source in range(l...  14.1 us
    dot_general x7, matrix products, product(): return jnp.dot(a, b, preferred_element_type=jnp.float32)  9.41 us
    ppermute x2, waiting for transfers between devices, rotated(): lax.ppermute(value, axis, [(source, (source + steps) % count) for source...  4.4 us
    dot_general x3, matrix products, project(): lax.dot_general(basis, vectors, (((0,), (0,)), ((), ())), preferred_eleme...  4.04 us
    ppermute x2, starting transfers between devices, rotated(): lax.ppermute(value, axis, [(source, (source + steps) % count) for source...  2.15 us
    unnamed x7, local copies, waits for them, and re-layouts  1.74 us
  transfers between devices with their start and end apart: 8, of which 6 were waited for; matrix products, arithmetic and copies ran while one was open for 12% of the time, Pallas kernels for 0%

profile of v1, /device:TPU:24, one launch (start us, length us, event | category | flops | bytes accessed | tf_op | source)
XLA Modules:
  0.0 63.0 jit_solution(15095431035079877022)
XLA Ops:
  0.0 1.4 %convolution_convert_fusion.3 = bf16[128,128]{1,0:T(8,128)(2,1)S(1)} fusion(bf16[1024,128]{1,0:T(8,128)(2,1)} %param.9, bf16[1,1024,128]{2,1,0:T(8,128)(2,1)} %param.8), kind=kOutput, calls=%fused_computation.15 | convolution fusion | flops 33570816 | bytes 557056 | tf_op jit(solution)/shard_map/dot_general | solution.py:19
  1.5 1.6 %collective-permute-start = (bf16[128,128]{1,0:T(8,128)(2,1)S(1)}, bf16[128,128]{1,0:T(8,128)(2,1)S(1)}, u32[]{:S(2)}, u32[]{:S(2)}) collective-permute-start(bf16[128,128]{1,0:T(8,128)(2,1)S(1)} %convolution_convert_fusion.3), channel_id=1, source_target_pairs={{0,16},{16,0},{1,17},{17,1},{2,18},{18,2},{3,19},{19,3},{4,20},{20... | collective-permute-start | bytes 98312 | tf_op jit(solution)/shard_map/ppermute | solution.py:15
  3.0 2.5 %collective-permute-start.2 = (bf16[1024,128]{1,0:T(8,128)(2,1)}, bf16[1024,128]{1,0:T(8,128)(2,1)}, u32[]{:S(2)}, u32[]{:S(2)}) collective-permute-start(bf16[1024,128]{1,0:T(8,128)(2,1)} %param.10), channel_id=1, source_target_pairs={{1,0},{2,1},{3,2},{4,3},{5,4},{6,5},{7,6},{8,7},{9,8},{10,9},{11,1... | collective-permute-start | bytes 786440 | tf_op jit(solution)/shard_map/ppermute | solution.py:10
  6.1 2.5 %convolution_convert_fusion = bf16[1024,512]{1,0:T(8,128)(2,1)S(1)} fusion(bf16[1024,1024]{1,0:T(8,128)(2,1)S(1)} %copy-done, bf16[1024,512]{1,0:T(8,128)(2,1)} %param.12), kind=kOutput, calls=%fused_computation.1 | convolution fusion | flops 1074266112 | bytes 4194304 | tf_op jit(solution)/shard_map/dot_general | solution.py:25
  8.6 1.0 %fusion.16 = f32[128,1024]{1,0:T(8,128)} fusion(bf16[128,128]{1,0:T(8,128)(2,1)S(1)} %convolution_convert_fusion.3, bf16[1,1024,128]{2,1,0:T(8,128)(2,1)S(1)} %copy-done.2), kind=kOutput, calls=%fused_computation.28 | convolution fusion | flops 33554432 | bytes 819200 | tf_op jit(solution)/shard_map/dot_general | solution.py:25
  9.6 4.4 %collective-permute-done.1 = bf16[1024,128]{1,0:T(8,128)(2,1)} collective-permute-done((bf16[1024,128]{1,0:T(8,128)(2,1)}, bf16[1024,128]{1,0:T(8,128)(2,1)}, u32[]{:S(2)}, u32[]{:S(2)}) %collective-permute-start.1) | collective-permute-done | bytes 262176 | tf_op jit(solution)/shard_map/ppermute | solution.py:15
  14.0 2.1 %convolution_convert_fusion.1 = bf16[128,1024]{1,0:T(8,128)(2,1)S(1)} fusion(bf16[1024,1024]{1,0:T(8,128)(2,1)S(1)} %copy-done, f32[128,1024]{1,0:T(8,128)} %fusion.16, bf16[128,128]{1,0:T(8,128)(2,1)S(1)} %collective-permute-done, bf16[1024,128]{1,0:T(8,128)(2,1)} %collective-permute-done.1), kind=kOutput, calls=%fused_computation.5 | convolution fusion | flops 302514176 | bytes 3178496 | tf_op jit(solution)/shard_map/dot_general | solution.py:25
  16.1 1.2 %fusion.5 = bf16[128,128]{0,1:T(8,128)(2,1)S(1)} fusion(bf16[128,1024]{1,0:T(8,128)(2,1)S(1)} %convolution_convert_fusion.1, bf16[1024,128]{1,0:T(8,128)(2,1)} %collective-permute-done.2), kind=kOutput, calls=%fused_computation.16 | convolution fusion | flops 33587200 | bytes 557056 | tf_op jit(solution)/shard_map/dot_general | solution.py:19
  17.3 1.4 %fusion.3 = bf16[128,512]{0,1:T(8,128)(2,1)S(1)} fusion(bf16[1024,512]{1,0:T(8,128)(2,1)S(1)} %convolution_convert_fusion, bf16[1024,128]{1,0:T(8,128)(2,1)} %collective-permute-done.2), kind=kOutput, calls=%fused_computation.12 | convolution fusion | flops 134283264 | bytes 1441792 | tf_op jit(solution)/shard_map/dot_general | solution.py:19
  18.7 0.7 %pad_maximum_fusion = bf16[128,640]{0,1:T(8,128)(2,1)} fusion(bf16[128,512]{0,1:T(8,128)(2,1)S(1)} %fusion.3, bf16[128,128]{0,1:T(8,128)(2,1)S(1)} %fusion.5), kind=kLoop, calls=%fused_computation.19 | loop fusion | flops 327680 | bytes 327680 | tf_op jit(solution)/shard_map/concatenate | solution.py:44
  19.4 1.9 %collective-permute-start.3 = (bf16[128,640]{0,1:T(8,128)(2,1)}, bf16[128,640]{0,1:T(8,128)(2,1)}, u32[]{:S(2)}, u32[]{:S(2)}) collective-permute-start(bf16[128,640]{0,1:T(8,128)(2,1)} %pad_maximum_fusion), channel_id=1, source_target_pairs={{0,1},{1,2},{2,3},{3,4},{4,5},{5,6},{6,7},{7,8},{8,9},{9,10},{10,1... | collective-permute-start | bytes 491528 | tf_op jit(solution)/shard_map/ppermute | solution.py:10
  21.3 1.1 %copy.8 = bf16[128,512]{0,1:T(8,128)(2,1)S(1)} copy(f32[128,512]{1,0:T(8,128)} %param.13) | data formatting | bytes 393216 | tf_op args[6]
  22.4 3.9 %collective-permute-start.4 = (bf16[128,640]{0,1:T(8,128)(2,1)}, bf16[128,640]{0,1:T(8,128)(2,1)S(1)}, u32[]{:S(2)}, u32[]{:S(2)}) collective-permute-start(bf16[128,640]{0,1:T(8,128)(2,1)} %pad_maximum_fusion), channel_id=1, source_target_pairs={{0,2},{1,3},{2,4},{3,5},{4,6},{5,7},{6,8},{7,9},{8,10},{9,11},{10,... | collective-permute-start | bytes 491528 | tf_op jit(solution)/shard_map/ppermute | solution.py:10
  26.3 1.0 %collective-permute-done.3 = bf16[128,640]{0,1:T(8,128)(2,1)} collective-permute-done((bf16[128,640]{0,1:T(8,128)(2,1)}, bf16[128,640]{0,1:T(8,128)(2,1)}, u32[]{:S(2)}, u32[]{:S(2)}) %collective-permute-start.3) | collective-permute-done | bytes 163872 | tf_op jit(solution)/shard_map/ppermute | solution.py:10
  27.3 1.0 %broadcast_select_fusion = bf16[128,640]{0,1:T(8,128)(2,1)S(1)} fusion(bf16[128,640]{0,1:T(8,128)(2,1)} %collective-permute-done.3, pred[]{:T(512)S(6)} %eq.6, bf16[128,512]{0,1:T(8,128)(2,1)S(1)} %copy.8), kind=kLoop, calls=%fused_computation.22 | loop fusion | flops 81920 | bytes 458753 | tf_op jit(solution)/shard_map/jit(_where)/select_n | solution.py:51
  28.2 3.3 %collective-permute-done.4 = bf16[128,640]{0,1:T(8,128)(2,1)S(1)} collective-permute-done((bf16[128,640]{0,1:T(8,128)(2,1)}, bf16[128,640]{0,1:T(8,128)(2,1)S(1)}, u32[]{:S(2)}, u32[]{:S(2)}) %collective-permute-start.4) | collective-permute-done | bytes 163872 | tf_op jit(solution)/shard_map/ppermute | solution.py:10
  31.7 3.2 %collective-permute-start.5 = (bf16[128,640]{0,1:T(8,128)(2,1)S(1)}, bf16[128,640]{0,1:T(8,128)(2,1)S(1)}, u32[]{:S(2)}, u32[]{:S(2)}) collective-permute-start(bf16[128,640]{0,1:T(8,128)(2,1)S(1)} %get-tuple-element.5), channel_id=1, source_target_pairs={{0,2},{1,3},{2,4},{3,5},{4,6},{5,7},{6,8},{7,9},{8,10},{9,11},{10,... | collective-permute-start | bytes 491528 | tf_op jit(solution)/shard_map/ppermute | solution.py:10
  35.0 6.4 %collective-permute-done.5 = bf16[128,640]{0,1:T(8,128)(2,1)S(1)} collective-permute-done((bf16[128,640]{0,1:T(8,128)(2,1)S(1)}, bf16[128,640]{0,1:T(8,128)(2,1)S(1)}, u32[]{:S(2)}, u32[]{:S(2)}) %collective-permute-start.5) | collective-permute-done | bytes 163872 | tf_op jit(solution)/shard_map/ppermute | solution.py:10
  41.6 1.3 %collective-permute-start.6 = (bf16[128,640]{0,1:T(8,128)(2,1)S(1)}, bf16[128,640]{0,1:T(8,128)(2,1)S(1)}, u32[]{:S(2)}, u32[]{:S(2)}) collective-permute-start(bf16[128,640]{0,1:T(8,128)(2,1)S(1)} %get-tuple-element.7), channel_id=1, source_target_pairs={{0,4},{1,5},{2,6},{3,7},{4,8},{5,9},{6,10},{7,11},{8,12},{9,13},{1... | collective-permute-start | bytes 491528 | tf_op jit(solution)/shard_map/ppermute | solution.py:10
  42.9 6.6 %collective-permute-done.6 = bf16[128,640]{0,1:T(8,128)(2,1)S(1)} collective-permute-done((bf16[128,640]{0,1:T(8,128)(2,1)S(1)}, bf16[128,640]{0,1:T(8,128)(2,1)S(1)}, u32[]{:S(2)}, u32[]{:S(2)}) %collective-permute-start.6) | collective-permute-done | bytes 163872 | tf_op jit(solution)/shard_map/ppermute | solution.py:10
  49.5 0.9 %fusion.21 = (bf16[128,640]{0,1:T(8,128)(2,1)S(1)}, f32[128,640]{0,1:T(8,128)}) fusion(f32[128,512]{0,1:T(8,128)S(1)} %slice.41, bf16[128,640]{0,1:T(8,128)(2,1)S(1)} %collective-permute-done.6, bf16[128,640]{0,1:T(8,128)(2,1)S(1)} %get-tuple-element.7), kind=kOutput, calls=%fused_computation.33 | convolution fusion | flops 21135360 | bytes 950272 | tf_op jit(solution)/shard_map/dot_general | solution.py:25
  51.1 1.3 %collective-permute-start.7 = (bf16[128,512]{0,1:T(8,128)(2,1)S(1)}, bf16[128,512]{0,1:T(8,128)(2,1)S(1)}, u32[]{:S(2)}, u32[]{:S(2)}) collective-permute-start(bf16[128,512]{0,1:T(8,128)(2,1)S(1)} %slice.42), channel_id=1, source_target_pairs={{0,8},{1,9},{2,10},{3,11},{4,12},{5,13},{6,14},{7,15},{16,24},{17,... | collective-permute-start | bytes 393224 | tf_op jit(solution)/shard_map/ppermute | solution.py:10
  52.4 8.1 %collective-permute-done.7 = bf16[128,512]{0,1:T(8,128)(2,1)S(1)} collective-permute-done((bf16[128,512]{0,1:T(8,128)(2,1)S(1)}, bf16[128,512]{0,1:T(8,128)(2,1)S(1)}, u32[]{:S(2)}, u32[]{:S(2)}) %collective-permute-start.7) | collective-permute-done | bytes 131104 | tf_op jit(solution)/shard_map/ppermute | solution.py:10
  60.5 2.5 %subtract_convert_fusion = bf16[1024,512]{1,0:T(8,128)(2,1)} fusion(bf16[1024,512]{1,0:T(8,128)(2,1)S(1)} %convolution_convert_fusion, bf16[128,1024]{1,0:T(8,128)(2,1)S(1)} %convolution_convert_fusion.1, bf16[128,512]{0,1:T(8,128)(2,1)S(1)} %collective-permute-done.7, f32[128,640]{0,1:T(8,128)} %get-tuple-element.10, bf16[128,640]{0,1:T(8,128)(2,1)} %copy-done.1), kind=kOutput, calls=%fused_computation | convolution fusion | flops 152698880 | bytes 2785280 | tf_op jit(solution)/shard_map/dot_general | solution.py:25
  (15 shorter events, 1.7 us)
Async XLA Ops:
  0.0 6.1 %copy-start = (bf16[1024,1024]{1,0:T(8,128)(2,1)S(1)}, bf16[1024,1024]{1,0:T(8,128)(2,1)}, u32[]{:S(2)}) copy-start(bf16[1024,1024]{1,0:T(8,128)(2,1)} %param.11) | copy-start | bytes 6291460
  1.5 8.2 %collective-permute-start = (bf16[128,128]{1,0:T(8,128)(2,1)S(1)}, bf16[128,128]{1,0:T(8,128)(2,1)S(1)}, u32[]{:S(2)}, u32[]{:S(2)}) collective-permute-start(bf16[128,128]{1,0:T(8,128)(2,1)S(1)} %convolution_convert_fusion.3), channel_id=1, source_target_pairs={{0,16},{16,0},{1,17},{17,1},{2,18},{18,2},{3,19},{19,3},{4,20},{20... | collective-permute-start | bytes 98312 | tf_op jit(solution)/shard_map/ppermute | solution.py:15
  3.0 13.1 %collective-permute-start.2 = (bf16[1024,128]{1,0:T(8,128)(2,1)}, bf16[1024,128]{1,0:T(8,128)(2,1)}, u32[]{:S(2)}, u32[]{:S(2)}) collective-permute-start(bf16[1024,128]{1,0:T(8,128)(2,1)} %param.10), channel_id=1, source_target_pairs={{1,0},{2,1},{3,2},{4,3},{5,4},{6,5},{7,6},{8,7},{9,8},{10,9},{11,1... | collective-permute-start | bytes 786440 | tf_op jit(solution)/shard_map/ppermute | solution.py:10
  5.5 3.1 %copy-start.2 = (bf16[1,1024,128]{2,1,0:T(8,128)(2,1)S(1)}, bf16[1,1024,128]{2,1,0:T(8,128)(2,1)}, u32[]{:S(2)}) copy-start(bf16[1,1024,128]{2,1,0:T(8,128)(2,1)} %param.7) | copy-start | bytes 786436
  5.5 8.5 %collective-permute-start.1 = (bf16[1024,128]{1,0:T(8,128)(2,1)}, bf16[1024,128]{1,0:T(8,128)(2,1)}, u32[]{:S(2)}, u32[]{:S(2)}) collective-permute-start(bf16[1024,128]{1,0:T(8,128)(2,1)} %bitcast.25), channel_id=1, source_target_pairs={{0,16},{16,0},{1,17},{17,1},{2,18},{18,2},{3,19},{19,3},{4,20},{20... | collective-permute-start | bytes 786440 | tf_op jit(solution)/shard_map/ppermute | solution.py:15
  19.4 7.8 %collective-permute-start.3 = (bf16[128,640]{0,1:T(8,128)(2,1)}, bf16[128,640]{0,1:T(8,128)(2,1)}, u32[]{:S(2)}, u32[]{:S(2)}) collective-permute-start(bf16[128,640]{0,1:T(8,128)(2,1)} %pad_maximum_fusion), channel_id=1, source_target_pairs={{0,1},{1,2},{2,3},{3,4},{4,5},{5,6},{6,7},{7,8},{8,9},{9,10},{10,1... | collective-permute-start | bytes 491528 | tf_op jit(solution)/shard_map/ppermute | solution.py:10
  22.4 9.1 %collective-permute-start.4 = (bf16[128,640]{0,1:T(8,128)(2,1)}, bf16[128,640]{0,1:T(8,128)(2,1)S(1)}, u32[]{:S(2)}, u32[]{:S(2)}) collective-permute-start(bf16[128,640]{0,1:T(8,128)(2,1)} %pad_maximum_fusion), channel_id=1, source_target_pairs={{0,2},{1,3},{2,4},{3,5},{4,6},{5,7},{6,8},{7,9},{8,10},{9,11},{10,... | collective-permute-start | bytes 491528 | tf_op jit(solution)/shard_map/ppermute | solution.py:10
  31.7 9.7 %collective-permute-start.5 = (bf16[128,640]{0,1:T(8,128)(2,1)S(1)}, bf16[128,640]{0,1:T(8,128)(2,1)S(1)}, u32[]{:S(2)}, u32[]{:S(2)}) collective-permute-start(bf16[128,640]{0,1:T(8,128)(2,1)S(1)} %get-tuple-element.5), channel_id=1, source_target_pairs={{0,2},{1,3},{2,4},{3,5},{4,6},{5,7},{6,8},{7,9},{8,10},{9,11},{10,... | collective-permute-start | bytes 491528 | tf_op jit(solution)/shard_map/ppermute | solution.py:10
  41.6 7.9 %collective-permute-start.6 = (bf16[128,640]{0,1:T(8,128)(2,1)S(1)}, bf16[128,640]{0,1:T(8,128)(2,1)S(1)}, u32[]{:S(2)}, u32[]{:S(2)}) collective-permute-start(bf16[128,640]{0,1:T(8,128)(2,1)S(1)} %get-tuple-element.7), channel_id=1, source_target_pairs={{0,4},{1,5},{2,6},{3,7},{4,8},{5,9},{6,10},{7,11},{8,12},{9,13},{1... | collective-permute-start | bytes 491528 | tf_op jit(solution)/shard_map/ppermute | solution.py:10
  50.4 0.7 %copy-start.1 = (bf16[128,640]{0,1:T(8,128)(2,1)}, bf16[128,640]{0,1:T(8,128)(2,1)S(1)}, u32[]{:S(2)}) copy-start(bf16[128,640]{0,1:T(8,128)(2,1)S(1)} %get-tuple-element.9) | copy-start | bytes 491524
  51.1 9.4 %collective-permute-start.7 = (bf16[128,512]{0,1:T(8,128)(2,1)S(1)}, bf16[128,512]{0,1:T(8,128)(2,1)S(1)}, u32[]{:S(2)}, u32[]{:S(2)}) collective-permute-start(bf16[128,512]{0,1:T(8,128)(2,1)S(1)} %slice.42), channel_id=1, source_target_pairs={{0,8},{1,9},{2,10},{3,11},{4,12},{5,13},{6,14},{7,15},{16,24},{17,... | collective-permute-start | bytes 393224 | tf_op jit(solution)/shard_map/ppermute | solution.py:10

commit v2 on v1

v2 whole, which is shorter than its diff:
```python
import jax
import jax.numpy as jnp
from jax import lax
from jax.experimental import pallas as pl
from jax.experimental.pallas import tpu as pltpu
from jax.sharding import PartitionSpec as P


def shifted(value, axis, steps):
    count = lax.axis_size(axis)
    leading, last = (max(0, -steps), min(count, count - steps))
    return lax.ppermute(value, axis, [(source, source + steps) for source in range(leading, last)])


def rotated(value, axis, steps):
    count = lax.axis_size(axis)
    return lax.ppermute(value, axis, [(source, (source + steps) % count) for source in range(count)])


def project(basis, vectors):
    return lax.dot_general(
        basis, vectors, (((0,), (0,)), ((), ())), preferred_element_type=jnp.float32
    )


def product(a, b):
    return jnp.dot(a, b, preferred_element_type=jnp.float32)


def recurrence(maps_ref, shifts_ref, incoming_ref, coupled_ref):
    groups, width, _ = shifts_ref.shape
    state = incoming_ref[...]
    for group in range(groups):
        high = state.astype(jnp.bfloat16)
        coupled_ref[group] = high
        if group + 1 < groups:
            low = (state - high.astype(jnp.float32)).astype(jnp.bfloat16)
            both = product(jnp.concatenate([high, low], axis=0), maps_ref[group])
            state = both[:width] + both[width:] + shifts_ref[group].astype(jnp.float32)


def exchanged(blocks):
    return lax.all_to_all(blocks, "row", 0, 0, tiled=True)


def body(left_factors, right_factors, sketch, row_basis, inverse_diag, right_side, incoming):
    half = jnp.bfloat16
    rank = sketch.shape[1]
    width = right_side.shape[1]
    layers, groups = lax.axis_size("layer"), lax.axis_size("row")
    here = lax.axis_index("row")
    share = width // groups

    lefts = [left_factors[0]] + [rotated(left_factors[0], "layer", k) for k in range(1, layers)]
    next_rows = shifted(row_basis, "row", -1)
    core = project(right_factors[0], sketch).astype(half)
    cores = [core] + [rotated(core, "layer", k) for k in range(1, layers)]
    applied = product(inverse_diag, right_side).astype(half)

    shift_t = project(applied, next_rows).astype(half)
    shifts = exchanged(shift_t.reshape(groups, share, rank))
    begin = lax.dynamic_slice_in_dim(incoming, here * share, share, 1).T

    tile_range = -sum(product(left, core) for left, core in zip(lefts, cores))
    gain = product(inverse_diag, tile_range.astype(half)).astype(half)
    map_t = (-project(gain, next_rows)).astype(half)
    maps = exchanged(jnp.broadcast_to(map_t[None], (groups, rank, rank)))
    coupled = pl.pallas_call(
        recurrence,
        out_shape=jax.ShapeDtypeStruct((groups, share, rank), half),
        name="recurrence",
    )(maps, shifts, begin)
    coupled_t = exchanged(coupled).reshape(width, rank)
    moved = lax.dot_general(
        gain, coupled_t, (((1,), (1,)), ((), ())), preferred_element_type=jnp.float32
    )
    return (applied.astype(jnp.float32) - moved).astype(half)


def solution(mesh):
    return jax.shard_map(
        body,
        mesh=mesh,
        in_specs=(
            P("layer", "row", None),
            P("layer", "row", None),
            P("row", None),
            P("row", None),
            P("row", None),
            P("row", "layer"),
            P(None, "layer"),
        ),
        out_specs=P("row", "layer"),
        check_vma=False,
    )
```

time: 63.4 us -> 65.8 us (1.038)
  the two profiles are of different devices: /device:TPU:24 before, /device:TPU:0 now
where the time goes in v2:
time: 65.8 us; the launch traced here: 65.1 us
  starting transfers between devices  15.7 us (24%)
  waiting for transfers between devices  15.4 us (23%)
  matrix products  12.8 us (19%)
  blocking collectives  12 us (18%)
  local copies, waits for them, and re-layouts  5.46 us (8%)
  Pallas kernels  3.64 us (6%)
    all_to_all x2, waiting for transfers between devices, exchanged(): return lax.all_to_all(blocks, 'row', 0, 0, tiled=True)  15.4 us
    all_to_all x1, blocking collectives, exchanged(): return lax.all_to_all(blocks, 'row', 0, 0, tiled=True)  12 us
    all_to_all x2, starting transfers between devices, exchanged(): return lax.all_to_all(blocks, 'row', 0, 0, tiled=True)  11.4 us
    dot_general x3, matrix products, product(): return jnp.dot(a, b, preferred_element_type=jnp.float32)  6.38 us
    dot_general x3, matrix products, project(): lax.dot_general(basis, vectors, (((0,), (0,)), ((), ())), preferred_eleme...  4.97 us
    pallas_call x1, Pallas kernels, body(): pl.pallas_call(recurrence, out_shape=jax.ShapeDtypeStruct((groups, share,...  3.64 us
    ppermute x2, starting transfers between devices, rotated(): lax.ppermute(value, axis, [(source, (source + steps) % count) for source...  3.01 us
    unnamed x9, local copies, waits for them, and re-layouts  2.24 us
  transfers between devices with their start and end apart: 5, of which 2 were waited for; matrix products, arithmetic and copies ran while one was open for 19% of the time, Pallas kernels for 0%

profile of v2, /device:TPU:0, one launch (start us, length us, event | category | flops | bytes accessed | tf_op | source)
XLA Modules:
  0.0 65.1 jit_solution(17378028158703698378)
XLA Ops:
  0.0 2.1 %convolution_convert_fusion.3 = bf16[128,128]{1,0:T(8,128)(2,1)} fusion(bf16[1024,128]{1,0:T(8,128)(2,1)} %param.9, bf16[1,1024,128]{2,1,0:T(8,128)(2,1)} %param.8), kind=kOutput, calls=%fused_computation.9 | convolution fusion | flops 33570816 | bytes 557056 | tf_op jit(solution)/shard_map/dot_general | solution.py:21
  2.1 2.9 %collective-permute-start = (bf16[128,128]{1,0:T(8,128)(2,1)}, bf16[128,128]{1,0:T(8,128)(2,1)}, u32[]{:S(2)}, u32[]{:S(2)}) collective-permute-start(bf16[128,128]{1,0:T(8,128)(2,1)} %convolution_convert_fusion.3), channel_id=1, source_target_pairs={{0,16},{16,0},{1,17},{17,1},{2,18},{18,2},{3,19},{19,3},{4,20},{20... | collective-permute-start | bytes 98312 | tf_op jit(solution)/shard_map/ppermute | solution.py:17
  5.0 1.3 %collective-permute-start.2 = (bf16[1024,128]{1,0:T(8,128)(2,1)}, bf16[1024,128]{1,0:T(8,128)(2,1)S(1)}, u32[]{:S(2)}, u32[]{:S(2)}) collective-permute-start(bf16[1024,128]{1,0:T(8,128)(2,1)} %param.10), channel_id=1, source_target_pairs={{1,0},{2,1},{3,2},{4,3},{5,4},{6,5},{7,6},{8,7},{9,8},{10,9},{11,1... | collective-permute-start | bytes 786440 | tf_op jit(solution)/shard_map/ppermute | solution.py:12
  6.3 0.0 copy-start.3
  6.3 0.1 collective-permute-start.1
  6.4 2.5 %convolution_convert_fusion = bf16[1024,512]{1,0:T(8,128)(2,1)S(1)} fusion(bf16[1024,1024]{1,0:T(8,128)(2,1)S(1)} %copy-done, bf16[1024,512]{1,0:T(8,128)(2,1)} %param.12), kind=kOutput, calls=%fused_computation.1 | convolution fusion | flops 1074266112 | bytes 4194304 | tf_op jit(solution)/shard_map/dot_general | solution.py:27
  8.9 1.8 %fusion.4 = f32[128,1024]{1,0:T(8,128)} fusion(bf16[128,128]{1,0:T(8,128)(2,1)} %convolution_convert_fusion.3, bf16[1,1024,128]{2,1,0:T(8,128)(2,1)S(1)} %copy-done.3), kind=kOutput, calls=%fused_computation.12 | convolution fusion | flops 33554432 | bytes 819200 | tf_op jit(solution)/shard_map/dot_general | solution.py:27
  10.7 0.0 collective-permute-done.2
  10.7 0.7 %copy-done.1 = bf16[1024,128]{1,0:T(8,128)(2,1)} copy-done((bf16[1024,128]{1,0:T(8,128)(2,1)}, bf16[1024,128]{1,0:T(8,128)(2,1)S(1)}, u32[]{:S(2)}) %copy-start.1) | copy-done | bytes 262168
  11.4 1.1 %convolution_convert_fusion.2 = bf16[512,128]{1,0:T(8,128)(2,1)} fusion(bf16[1024,512]{1,0:T(8,128)(2,1)S(1)} %convolution_convert_fusion, bf16[1024,128]{1,0:T(8,128)(2,1)S(1)} %collective-permute-done.2), kind=kOutput, calls=%fused_computation.6 | convolution fusion | flops 134283264 | bytes 1441792 | tf_op jit(solution)/shard_map/dot_general | solution.py:21
  12.5 7.2 %all-to-all-start.1 = ((bf16[16,32,128]{2,1,0:T(8,128)(2,1)}), bf16[16,32,128]{2,1,0:T(8,128)(2,1)S(1)}, u32[]{:S(2)}, u32[]{:S(2)}) async-start(bf16[16,32,128]{2,1,0:T(8,128)(2,1)} %bitcast.2), calls=%async_computation.1 | async-start | bytes 262144 | tf_op jit(solution)/shard_map/all_to_all | solution.py:43
  19.7 0.0 collective-permute-done
  19.7 0.0 collective-permute-done.1
  19.8 2.1 %convolution_convert_fusion.1 = bf16[128,1024]{1,0:T(8,128)(2,1)S(1)} fusion(bf16[1024,1024]{1,0:T(8,128)(2,1)S(1)} %copy-done, f32[128,1024]{1,0:T(8,128)} %fusion.4, bf16[128,128]{1,0:T(8,128)(2,1)} %collective-permute-done, bf16[1024,128]{1,0:T(8,128)(2,1)} %collective-permute-done.1), kind=kOutput, calls=%fused_computation.5 | convolution fusion | flops 302514176 | bytes 3178496 | tf_op jit(solution)/shard_map/dot_general | solution.py:27
  21.8 1.8 %fusion.2 = bf16[128,128]{1,0:T(8,128)(2,1)} fusion(bf16[128,1024]{1,0:T(8,128)(2,1)S(1)} %convolution_convert_fusion.1, bf16[1024,128]{1,0:T(8,128)(2,1)} %copy-done.1), kind=kOutput, calls=%fused_computation.8 | convolution fusion | flops 33587200 | bytes 557056 | tf_op jit(solution)/shard_map/dot_general | solution.py:21
  23.6 4.0 %all-to-all-done.1.shifts_ref = bf16[16,32,128]{2,1,0:T(8,128)(2,1)S(1)} async-done(((bf16[16,32,128]{2,1,0:T(8,128)(2,1)}), bf16[16,32,128]{2,1,0:T(8,128)(2,1)S(1)}, u32[]{:S(2)}, u32[]{:S(2)}) %all-to-all-start.1) | async-done | bytes 131104 | tf_op jit(solution)/shard_map/all_to_all | solution.py:43
  27.7 1.7 %broadcast_in_dim.2 = bf16[16,128,128]{2,1,0:T(8,128)(2,1)} broadcast(bf16[128,128]{1,0:T(8,128)(2,1)} %fusion.2), dimensions={1,2} | broadcast | bytes 557056 | tf_op jit(solution)/shard_map/broadcast_in_dim | solution.py:67
  29.3 4.3 %all-to-all-start = ((bf16[16,128,128]{2,1,0:T(8,128)(2,1)}), bf16[16,128,128]{2,1,0:T(8,128)(2,1)}, u32[]{:S(2)}, u32[]{:S(2)}) async-start(bf16[16,128,128]{2,1,0:T(8,128)(2,1)} %broadcast_in_dim.2), calls=%async_computation | async-start | bytes 1048576 | tf_op jit(solution)/shard_map/all_to_all | solution.py:43
  33.6 1.6 %constant_dynamic-slice_fusion = f32[128,32]{1,0:T(8,128)} fusion(f32[128,512]{1,0:T(8,128)} %param.13, s32[]{:T(128)S(6)} %select_n.3), kind=kLoop, calls=%fused_computation.11 | loop fusion | bytes 32772 | tf_op jit(solution)/shard_map/dynamic_slice | solution.py:62
  35.1 1.5 %copy.9 = f32[128,32]{0,1:T(8,128)} copy(f32[128,32]{1,0:T(8,128)} %constant_dynamic-slice_fusion) | data formatting | bytes 32768
  36.7 11.4 %all-to-all-done.maps_ref = bf16[16,128,128]{2,1,0:T(8,128)(2,1)} async-done(((bf16[16,128,128]{2,1,0:T(8,128)(2,1)}), bf16[16,128,128]{2,1,0:T(8,128)(2,1)}, u32[]{:S(2)}, u32[]{:S(2)}) %all-to-all-start) | async-done | bytes 524320 | tf_op jit(solution)/shard_map/all_to_all | solution.py:43
  48.1 3.6 %recurrence.1 = bf16[16,32,128]{2,1,0:T(8,128)(2,1)} custom-call(bf16[16,128,128]{2,1,0:T(8,128)(2,1)} %all-to-all-done.maps_ref, bf16[16,32,128]{2,1,0:T(8,128)(2,1)} %copy-done.2, f32[32,128]{1,0:T(8,128)} %bitcast.24), custom_call_target="tpu_custom_call" | custom-call | tf_op jit(solution)/shard_map/recurrence/pallas_call | solution.py:68
  51.7 12.0 %all_to_all.15 = bf16[16,32,128]{2,1,0:T(8,128)(2,1)S(1)} all-to-all(bf16[16,32,128]{2,1,0:T(8,128)(2,1)} %recurrence.1), channel_id=1, replica_groups=mesh['layer'=2,'row'=16] {'row'}, dimensions={0} | all-to-all | bytes 262144 | tf_op jit(solution)/shard_map/all_to_all | solution.py:43
  63.6 1.4 %subtract_convert_fusion = bf16[1024,512]{1,0:T(8,128)(2,1)} fusion(bf16[1024,512]{1,0:T(8,128)(2,1)S(1)} %convolution_convert_fusion, bf16[128,1024]{1,0:T(8,128)(2,1)S(1)} %convolution_convert_fusion.1, bf16[512,128]{1,0:T(8,128)(2,1)S(1)} %bitcast.22), kind=kOutput, calls=%fused_computation | convolution fusion | flops 135790592 | bytes 2490368 | tf_op jit(solution)/shard_map/dot_general | solution.py:74
  (6 shorter events, 0.0 us)
Async XLA Ops:
  0.0 6.4 %copy-start = (bf16[1024,1024]{1,0:T(8,128)(2,1)S(1)}, bf16[1024,1024]{1,0:T(8,128)(2,1)}, u32[]{:S(2)}) copy-start(bf16[1024,1024]{1,0:T(8,128)(2,1)} %param.11) | copy-start | bytes 6291460
  2.1 17.7 %collective-permute-start = (bf16[128,128]{1,0:T(8,128)(2,1)}, bf16[128,128]{1,0:T(8,128)(2,1)}, u32[]{:S(2)}, u32[]{:S(2)}) collective-permute-start(bf16[128,128]{1,0:T(8,128)(2,1)} %convolution_convert_fusion.3), channel_id=1, source_target_pairs={{0,16},{16,0},{1,17},{17,1},{2,18},{18,2},{3,19},{19,3},{4,20},{20... | collective-permute-start | bytes 98312 | tf_op jit(solution)/shard_map/ppermute | solution.py:17
  5.0 5.7 %collective-permute-start.2 = (bf16[1024,128]{1,0:T(8,128)(2,1)}, bf16[1024,128]{1,0:T(8,128)(2,1)S(1)}, u32[]{:S(2)}, u32[]{:S(2)}) collective-permute-start(bf16[1024,128]{1,0:T(8,128)(2,1)} %param.10), channel_id=1, source_target_pairs={{1,0},{2,1},{3,2},{4,3},{5,4},{6,5},{7,6},{8,7},{9,8},{10,9},{11,1... | collective-permute-start | bytes 786440 | tf_op jit(solution)/shard_map/ppermute | solution.py:12
  6.3 2.6 %copy-start.3 = (bf16[1,1024,128]{2,1,0:T(8,128)(2,1)S(1)}, bf16[1,1024,128]{2,1,0:T(8,128)(2,1)}, u32[]{:S(2)}) copy-start(bf16[1,1024,128]{2,1,0:T(8,128)(2,1)} %param.7) | copy-start | bytes 786436
  6.3 13.4 %collective-permute-start.1 = (bf16[1024,128]{1,0:T(8,128)(2,1)}, bf16[1024,128]{1,0:T(8,128)(2,1)}, u32[]{:S(2)}, u32[]{:S(2)}) collective-permute-start(bf16[1024,128]{1,0:T(8,128)(2,1)} %bitcast.23), channel_id=1, source_target_pairs={{0,16},{16,0},{1,17},{17,1},{2,18},{18,2},{3,19},{19,3},{4,20},{20... | collective-permute-start | bytes 786440 | tf_op jit(solution)/shard_map/ppermute | solution.py:17
  10.7 0.7 %copy-start.1 = (bf16[1024,128]{1,0:T(8,128)(2,1)}, bf16[1024,128]{1,0:T(8,128)(2,1)S(1)}, u32[]{:S(2)}) copy-start(bf16[1024,128]{1,0:T(8,128)(2,1)S(1)} %collective-permute-done.2) | copy-start | bytes 786436
  12.5 15.1 %all-to-all-start.1 = ((bf16[16,32,128]{2,1,0:T(8,128)(2,1)}), bf16[16,32,128]{2,1,0:T(8,128)(2,1)S(1)}, u32[]{:S(2)}, u32[]{:S(2)}) async-start(bf16[16,32,128]{2,1,0:T(8,128)(2,1)} %bitcast.2), calls=%async_computation.1 | async-start | bytes 262144 | tf_op jit(solution)/shard_map/all_to_all | solution.py:43
  27.7 20.4 %copy-start.2 = (bf16[16,32,128]{2,1,0:T(8,128)(2,1)}, bf16[16,32,128]{2,1,0:T(8,128)(2,1)S(1)}, u32[]{:S(2)}) copy-start(bf16[16,32,128]{2,1,0:T(8,128)(2,1)S(1)} %all-to-all-done.1.shifts_ref) | copy-start | bytes 393220
  29.3 18.7 %all-to-all-start = ((bf16[16,128,128]{2,1,0:T(8,128)(2,1)}), bf16[16,128,128]{2,1,0:T(8,128)(2,1)}, u32[]{:S(2)}, u32[]{:S(2)}) async-start(bf16[16,128,128]{2,1,0:T(8,128)(2,1)} %broadcast_in_dim.2), calls=%async_computation | async-start | bytes 1048576 | tf_op jit(solution)/shard_map/all_to_all | solution.py:43

commit v3 on v2

--- a/solution.py
+++ b/solution.py
@@ -27,20 +27,37 @@
     return jnp.dot(a, b, preferred_element_type=jnp.float32)
 
 
-def recurrence(maps_ref, shifts_ref, incoming_ref, coupled_ref):
-    groups, width, _ = shifts_ref.shape
-    state = incoming_ref[...]
-    for group in range(groups):
-        high = state.astype(jnp.bfloat16)
-        coupled_ref[group] = high
-        if group + 1 < groups:
-            low = (state - high.astype(jnp.float32)).astype(jnp.bfloat16)
-            both = product(jnp.concatenate([high, low], axis=0), maps_ref[group])
-            state = both[:width] + both[width:] + shifts_ref[group].astype(jnp.float32)
+def compose(maps_ref, shifts_ref, begin_ref, total_ref, prefixes_ref):
+    count = maps_ref.shape[0]
+    rank = maps_ref.shape[1]
+    state = begin_ref[...]
+    for member in range(count):
+        prefixes_ref[member] = state
+        moved = product(state.astype(jnp.bfloat16), maps_ref[member])
+        state = jnp.concatenate(
+            [moved[:rank], moved[rank:] + shifts_ref[member].astype(jnp.float32)], axis=0
+        )
+    total = state.astype(jnp.bfloat16)
+    for target in range(total_ref.shape[0]):
+        total_ref[target] = total
 
 
-def exchanged(blocks):
-    return lax.all_to_all(blocks, "row", 0, 0, tiled=True)
+def enter(upper_ref, totals_ref, prefixes_ref, coupled_ref):
+    rank = totals_ref.shape[2]
+    upper = upper_ref[0]
+    state = jnp.zeros(coupled_ref.shape[1:], jnp.float32)
+    for source in range(totals_ref.shape[0] - 1):
+        moved = product(state.astype(jnp.bfloat16), totals_ref[source, :rank])
+        moved = moved + totals_ref[source, rank:].astype(jnp.float32)
+        state = jnp.where(source < upper, moved, state)
+    state = state.astype(jnp.bfloat16)
+    for member in range(coupled_ref.shape[0]):
+        moved = product(state, prefixes_ref[member, :rank].astype(jnp.bfloat16))
+        coupled_ref[member] = (moved + prefixes_ref[member, rank:]).astype(jnp.bfloat16)
+
+
+def exchanged(blocks, members):
+    return lax.all_to_all(blocks, "row", 0, 0, axis_index_groups=members, tiled=True)
 
 
 def body(left_factors, right_factors, sketch, row_basis, inverse_diag, right_side, incoming):
@@ -48,8 +65,15 @@
     rank = sketch.shape[1]
     width = right_side.shape[1]
     layers, groups = lax.axis_size("layer"), lax.axis_size("row")
+    lowers = 1
+    while lowers * lowers < groups:
+        lowers *= 2
+    uppers = groups // lowers
     here = lax.axis_index("row")
-    share = width // groups
+    upper, lower = here // lowers, here % lowers
+    share = width // lowers
+    near = [[u * lowers + l for l in range(lowers)] for u in range(uppers)]
+    far = [[u * lowers + l for u in range(uppers)] for l in range(lowers)]
 
     lefts = [left_factors[0]] + [rotated(left_factors[0], "layer", k) for k in range(1, layers)]
     next_rows = shifted(row_basis, "row", -1)
@@ -58,19 +82,35 @@
     applied = product(inverse_diag, right_side).astype(half)
 
     shift_t = project(applied, next_rows).astype(half)
-    shifts = exchanged(shift_t.reshape(groups, share, rank))
-    begin = lax.dynamic_slice_in_dim(incoming, here * share, share, 1).T
+    shifts = exchanged(shift_t.reshape(lowers, share, rank), near)
+    entry = lax.dynamic_slice_in_dim(incoming, lower * share, share, 1).T
+    begin = jnp.concatenate(
+        [
+            jnp.where(upper == 0, 0.0, jnp.eye(rank, dtype=jnp.float32)),
+            jnp.where(upper == 0, entry, 0.0),
+        ]
+    )
 
     tile_range = -sum(product(left, core) for left, core in zip(lefts, cores))
     gain = product(inverse_diag, tile_range.astype(half)).astype(half)
     map_t = (-project(gain, next_rows)).astype(half)
-    maps = exchanged(jnp.broadcast_to(map_t[None], (groups, rank, rank)))
+    maps = exchanged(jnp.broadcast_to(map_t[None], (lowers, rank, rank)), near)
+    total, prefixes = pl.pallas_call(
+        compose,
+        out_shape=(
+            jax.ShapeDtypeStruct((uppers, rank + share, rank), half),
+            jax.ShapeDtypeStruct((lowers, rank + share, rank), jnp.float32),
+        ),
+        name="compose",
+    )(maps, shifts, begin)
+    totals = exchanged(total, far)
     coupled = pl.pallas_call(
-        recurrence,
-        out_shape=jax.ShapeDtypeStruct((groups, share, rank), half),
-        name="recurrence",
-    )(maps, shifts, begin)
-    coupled_t = exchanged(coupled).reshape(width, rank)
+        enter,
+        in_specs=[pl.BlockSpec(memory_space=pltpu.SMEM)] + [pl.BlockSpec(memory_space=pltpu.VMEM)] * 2,
+        out_shape=jax.ShapeDtypeStruct((lowers, share, rank), half),
+        name="enter",
+    )(upper.reshape(1), totals, prefixes)
+    coupled_t = exchanged(coupled, near).reshape(width, rank)
     moved = lax.dot_general(
         gain, coupled_t, (((1,), (1,)), ((), ())), preferred_element_type=jnp.float32
     )

time: 65.8 us -> 64.3 us (0.977)
  blocking collectives: 12 us -> 21.7 us
  waiting for transfers between devices: 15.4 us -> 8.16 us
  starting transfers between devices: 15.7 us -> 11.6 us
  local copies, waits for them, and re-layouts: 5.46 us -> 2.33 us
  other arithmetic: 0 us -> 2.19 us
  Pallas kernels: 3.64 us -> 4.62 us
    all_to_all x1 -> x2, blocking collectives: 12 us -> 21.7 us  [exchanged(): lax.all_to_all(blocks, 'row', 0, 0, axis_index_groups=members, tiled=True)]
    all_to_all x2, waiting for transfers between devices: 15.4 us -> 5.67 us  [exchanged(): lax.all_to_all(blocks, 'row', 0, 0, axis_index_groups=members, tiled=True)]
    all_to_all x2, starting transfers between devices: 11.4 us -> 7.26 us  [exchanged(): lax.all_to_all(blocks, 'row', 0, 0, axis_index_groups=members, tiled=True)]
    ppermute x2, waiting for transfers between devices: 0.01 us -> 2.48 us  [rotated(): lax.ppermute(value, axis, [(source, (source + steps) % count) for source...]
    unnamed x9 -> x5, local copies, waits for them, and re-layouts: 2.24 us -> 0.1 us
    concatenate x0 -> x1, other arithmetic: none -> 1.53 us  [body(): jnp.concatenate([jnp.where(upper == 0, 0.0, jnp.eye(rank, dtype=jnp.float...]
    broadcast_in_dim x1, local copies, waits for them, and re-layouts: 1.65 us -> 0.67 us  [body(): maps = exchanged(jnp.broadcast_to(map_t[None], (lowers, rank, rank)), near)]
    pallas_call x1 -> x2, Pallas kernels: 3.64 us -> 4.62 us  [the longest x1 2.31 us: body(): pl.pallas_call(enter, in_specs=[pl.BlockSpec(memory_space=pltpu.SMEM)] +...]
  transfers between devices with their start and end apart: 5 -> 5, of which waited for: 2 -> 3; matrix products, arithmetic and copies ran while one was open for 19% -> 20% of each run, Pallas kernels for 0% -> 0%
where the time goes in v3:
time: 64.3 us; the launch traced here: 63.4 us
  blocking collectives  21.7 us (34%)
  matrix products  12.7 us (20%)
  starting transfers between devices  11.6 us (18%)
  waiting for transfers between devices  8.16 us (13%)
  Pallas kernels  4.62 us (7%)
  local copies, waits for them, and re-layouts  2.33 us (4%)
  other arithmetic  2.19 us (3%)
    all_to_all x2, blocking collectives, exchanged(): lax.all_to_all(blocks, 'row', 0, 0, axis_index_groups=members, tiled=True)  21.7 us
    all_to_all x2, starting transfers between devices, exchanged(): lax.all_to_all(blocks, 'row', 0, 0, axis_index_groups=members, tiled=True)  7.26 us
    dot_general x3, matrix products, product(): return jnp.dot(a, b, preferred_element_type=jnp.float32)  6.56 us
    all_to_all x2, waiting for transfers between devices, exchanged(): lax.all_to_all(blocks, 'row', 0, 0, axis_index_groups=members, tiled=True)  5.67 us
    dot_general x3, matrix products, project(): lax.dot_general(basis, vectors, (((0,), (0,)), ((), ())), preferred_eleme...  4.69 us
    ppermute x2, starting transfers between devices, rotated(): lax.ppermute(value, axis, [(source, (source + steps) % count) for source...  3.09 us
    ppermute x2, waiting for transfers between devices, rotated(): lax.ppermute(value, axis, [(source, (source + steps) % count) for source...  2.48 us
    pallas_call x1, Pallas kernels, body(): pl.pallas_call(enter, in_specs=[pl.BlockSpec(memory_space=pltpu.SMEM)] +...  2.31 us
  transfers between devices with their start and end apart: 5, of which 3 were waited for; matrix products, arithmetic and copies ran while one was open for 20% of the time, Pallas kernels for 0%

profile of v3, /device:TPU:0, one launch (start us, length us, event | category | flops | bytes accessed | tf_op | source)
XLA Modules:
  0.0 63.4 jit_solution(6916449227295430913)
XLA Ops:
  0.0 1.4 %convolution_convert_fusion.3 = bf16[128,128]{1,0:T(8,128)(2,1)S(1)} fusion(bf16[1024,128]{1,0:T(8,128)(2,1)} %param.9, bf16[1,1024,128]{2,1,0:T(8,128)(2,1)} %param.8), kind=kOutput, calls=%fused_computation.9 | convolution fusion | flops 33570816 | bytes 557056 | tf_op jit(solution)/shard_map/dot_general | solution.py:21
  1.5 3.0 %collective-permute-start = (bf16[128,128]{1,0:T(8,128)(2,1)S(1)}, bf16[128,128]{1,0:T(8,128)(2,1)S(1)}, u32[]{:S(2)}, u32[]{:S(2)}) collective-permute-start(bf16[128,128]{1,0:T(8,128)(2,1)S(1)} %convolution_convert_fusion.3), channel_id=1, source_target_pairs={{0,16},{16,0},{1,17},{17,1},{2,18},{18,2},{3,19},{19,3},{4,20},{20... | collective-permute-start | bytes 98312 | tf_op jit(solution)/shard_map/ppermute | solution.py:17
  4.5 1.3 %collective-permute-start.2 = (bf16[1024,128]{1,0:T(8,128)(2,1)}, bf16[1024,128]{1,0:T(8,128)(2,1)}, u32[]{:S(2)}, u32[]{:S(2)}) collective-permute-start(bf16[1024,128]{1,0:T(8,128)(2,1)} %param.10), channel_id=1, source_target_pairs={{1,0},{2,1},{3,2},{4,3},{5,4},{6,5},{7,6},{8,7},{9,8},{10,9},{11,1... | collective-permute-start | bytes 786440 | tf_op jit(solution)/shard_map/ppermute | solution.py:12
  5.7 0.1 collective-permute-start.1
  5.8 2.0 %fusion.4 = f32[128,1024]{1,0:T(8,128)} fusion(bf16[128,128]{1,0:T(8,128)(2,1)S(1)} %convolution_convert_fusion.3, bf16[1,1024,128]{2,1,0:T(8,128)(2,1)} %param.7), kind=kOutput, calls=%fused_computation.16 | convolution fusion | flops 33554432 | bytes 819200 | tf_op jit(solution)/shard_map/dot_general | solution.py:27
  7.9 0.8 %constant_dynamic-slice_fusion = f32[128,128]{1,0:T(8,128)S(1)} fusion(f32[128,512]{1,0:T(8,128)} %param.13, s32[]{:T(128)S(6)} %select_n.35), kind=kLoop, calls=%fused_computation.15 | loop fusion | bytes 131076 | tf_op jit(solution)/shard_map/dynamic_slice | solution.py:86
  8.8 2.5 %convolution_convert_fusion = bf16[1024,512]{1,0:T(8,128)(2,1)S(1)} fusion(bf16[1024,1024]{1,0:T(8,128)(2,1)S(1)} %copy-done, bf16[1024,512]{1,0:T(8,128)(2,1)} %param.12), kind=kOutput, calls=%fused_computation.1 | convolution fusion | flops 1074266112 | bytes 4194304 | tf_op jit(solution)/shard_map/dot_general | solution.py:27
  11.3 0.6 %select_bitcast_fusion = f32[128,128]{1,0:T(8,128)} fusion(f32[128,128]{0,1:T(8,128)S(1)} %copy.10, pred[]{:T(512)S(6)} %eq.9), kind=kLoop, calls=%fused_computation.12 | loop fusion | flops 16384 | bytes 131073 | tf_op jit(solution)/shard_map/jit(_where)/select_n | solution.py:90
  11.9 0.7 %copy.9 = f32[128,128]{1,0:T(8,128)} copy(f32[128,128]{0,1:T(8,128)S(1)} %convert_select_fusion) | data formatting | bytes 131072 | tf_op jit(solution)/shard_map/jit(_where)/select_n | solution.py:89
  12.7 2.5 %collective-permute-done.1 = bf16[1024,128]{1,0:T(8,128)(2,1)} collective-permute-done((bf16[1024,128]{1,0:T(8,128)(2,1)}, bf16[1024,128]{1,0:T(8,128)(2,1)}, u32[]{:S(2)}, u32[]{:S(2)}) %collective-permute-start.1) | collective-permute-done | bytes 262176 | tf_op jit(solution)/shard_map/ppermute | solution.py:17
  15.1 2.1 %convolution_convert_fusion.1 = bf16[128,1024]{1,0:T(8,128)(2,1)S(1)} fusion(bf16[1024,1024]{1,0:T(8,128)(2,1)S(1)} %copy-done, f32[128,1024]{1,0:T(8,128)} %fusion.4, bf16[128,128]{1,0:T(8,128)(2,1)S(1)} %collective-permute-done, bf16[1024,128]{1,0:T(8,128)(2,1)} %collective-permute-done.1), kind=kOutput, calls=%fused_computation.5 | convolution fusion | flops 302514176 | bytes 3178496 | tf_op jit(solution)/shard_map/dot_general | solution.py:27
  17.2 1.2 %fusion.2 = bf16[128,128]{1,0:T(8,128)(2,1)S(1)} fusion(bf16[128,1024]{1,0:T(8,128)(2,1)S(1)} %convolution_convert_fusion.1, bf16[1024,128]{1,0:T(8,128)(2,1)} %collective-permute-done.2), kind=kOutput, calls=%fused_computation.8 | convolution fusion | flops 33587200 | bytes 557056 | tf_op jit(solution)/shard_map/dot_general | solution.py:21
  18.4 0.7 %broadcast_in_dim.12 = bf16[4,128,128]{2,1,0:T(8,128)(2,1)} broadcast(bf16[128,128]{1,0:T(8,128)(2,1)S(1)} %fusion.2), dimensions={1,2} | broadcast | bytes 163840 | tf_op jit(solution)/shard_map/broadcast_in_dim | solution.py:97
  19.1 3.3 %all-to-all-start = ((bf16[4,128,128]{2,1,0:T(8,128)(2,1)}), bf16[4,128,128]{2,1,0:T(8,128)(2,1)S(1)}, u32[]{:S(2)}, u32[]{:S(2)}) async-start(bf16[4,128,128]{2,1,0:T(8,128)(2,1)} %broadcast_in_dim.12), calls=%async_computation | async-start | bytes 262144 | tf_op jit(solution)/shard_map/all_to_all | solution.py:60
  22.4 2.1 %convolution_convert_fusion.2 = bf16[512,128]{1,0:T(8,128)(2,1)} fusion(bf16[1024,512]{1,0:T(8,128)(2,1)S(1)} %convolution_convert_fusion, bf16[1024,128]{1,0:T(8,128)(2,1)} %collective-permute-done.2), kind=kOutput, calls=%fused_computation.6 | convolution fusion | flops 134283264 | bytes 1441792 | tf_op jit(solution)/shard_map/dot_general | solution.py:21
  24.5 2.5 %all-to-all-done.maps_ref = bf16[4,128,128]{2,1,0:T(8,128)(2,1)S(1)} async-done(((bf16[4,128,128]{2,1,0:T(8,128)(2,1)}), bf16[4,128,128]{2,1,0:T(8,128)(2,1)S(1)}, u32[]{:S(2)}, u32[]{:S(2)}) %all-to-all-start) | async-done | bytes 131104 | tf_op jit(solution)/shard_map/all_to_all | solution.py:60
  27.0 3.9 %all-to-all-start.1 = ((bf16[4,128,128]{2,1,0:T(8,128)(2,1)}), bf16[4,128,128]{2,1,0:T(8,128)(2,1)}, u32[]{:S(2)}, u32[]{:S(2)}) async-start(bf16[4,128,128]{2,1,0:T(8,128)(2,1)} %bitcast.25), calls=%async_computation.1 | async-start | bytes 262144 | tf_op jit(solution)/shard_map/all_to_all | solution.py:60
  31.0 1.5 %pad_maximum_fusion.begin_ref = f32[256,128]{1,0:T(8,128)} fusion(f32[128,128]{1,0:T(8,128)} %select_bitcast_fusion, f32[128,128]{1,0:T(8,128)} %copy.9), kind=kLoop, calls=%fused_computation.11 | loop fusion | flops 32768 | bytes 262144 | tf_op jit(solution)/shard_map/concatenate | solution.py:87
  32.5 3.2 %all-to-all-done.1.shifts_ref = bf16[4,128,128]{2,1,0:T(8,128)(2,1)} async-done(((bf16[4,128,128]{2,1,0:T(8,128)(2,1)}), bf16[4,128,128]{2,1,0:T(8,128)(2,1)}, u32[]{:S(2)}, u32[]{:S(2)}) %all-to-all-start.1) | async-done | bytes 131104 | tf_op jit(solution)/shard_map/all_to_all | solution.py:60
  35.6 2.3 %compose.1 = (bf16[4,256,128]{2,1,0:T(8,128)(2,1)}, f32[4,256,128]{2,1,0:T(8,128)}) custom-call(bf16[4,128,128]{2,1,0:T(8,128)(2,1)} %copy-done.1, bf16[4,128,128]{2,1,0:T(8,128)(2,1)} %all-to-all-done.1.shifts_ref, f32[256,128]{1,0:T(8,128)} %pad_maximum_fusion.begin_ref), custom_call_target="tpu_custom_call" | custom-call | tf_op jit(solution)/shard_map/compose/pallas_call | solution.py:98
  38.0 13.8 %all_to_all.20.totals_ref = bf16[4,256,128]{2,1,0:T(8,128)(2,1)} all-to-all(bf16[4,256,128]{2,1,0:T(8,128)(2,1)} %get-tuple-element.7), channel_id=1, replica_groups={{0,4,8,12},{1,5,9,13},{2,6,10,14},{3,7,11,15},{16,20,24,28},{17,21,25,2..., dimensions={0} | all-to-all | bytes 524288 | tf_op jit(solution)/shard_map/all_to_all | solution.py:60
  51.8 2.3 %enter.1 = bf16[4,128,128]{2,1,0:T(8,128)(2,1)} custom-call(s32[1]{0:T(128)} %bitcast.2.upper_ref, bf16[4,256,128]{2,1,0:T(8,128)(2,1)} %all_to_all.20.totals_ref, f32[4,256,128]{2,1,0:T(8,128)} %get-tuple-element.8.prefixes_ref), custom_call_target="tpu_custom_call" | custom-call | tf_op jit(solution)/shard_map/enter/pallas_call | solution.py:107
  54.1 7.9 %all_to_all.21 = bf16[4,128,128]{2,1,0:T(8,128)(2,1)S(1)} all-to-all(bf16[4,128,128]{2,1,0:T(8,128)(2,1)} %enter.1), channel_id=1, replica_groups={{0,1,2,3},{4,5,6,7},{8,9,10,11},{12,13,14,15},{16,17,18,19},{20,21,22,2..., dimensions={0} | all-to-all | bytes 262144 | tf_op jit(solution)/shard_map/all_to_all | solution.py:60
  62.0 1.4 %subtract_convert_fusion = bf16[1024,512]{1,0:T(8,128)(2,1)} fusion(bf16[1024,512]{1,0:T(8,128)(2,1)S(1)} %convolution_convert_fusion, bf16[128,1024]{1,0:T(8,128)(2,1)S(1)} %convolution_convert_fusion.1, bf16[512,128]{1,0:T(8,128)(2,1)S(1)} %bitcast.24), kind=kOutput, calls=%fused_computation | convolution fusion | flops 135790592 | bytes 2490368 | tf_op jit(solution)/shard_map/dot_general | solution.py:114
  (8 shorter events, 0.1 us)
Async XLA Ops:
  0.0 8.8 %copy-start = (bf16[1024,1024]{1,0:T(8,128)(2,1)S(1)}, bf16[1024,1024]{1,0:T(8,128)(2,1)}, u32[]{:S(2)}) copy-start(bf16[1024,1024]{1,0:T(8,128)(2,1)} %param.11) | copy-start | bytes 6291460
  1.5 11.2 %collective-permute-start = (bf16[128,128]{1,0:T(8,128)(2,1)S(1)}, bf16[128,128]{1,0:T(8,128)(2,1)S(1)}, u32[]{:S(2)}, u32[]{:S(2)}) collective-permute-start(bf16[128,128]{1,0:T(8,128)(2,1)S(1)} %convolution_convert_fusion.3), channel_id=1, source_target_pairs={{0,16},{16,0},{1,17},{17,1},{2,18},{18,2},{3,19},{19,3},{4,20},{20... | collective-permute-start | bytes 98312 | tf_op jit(solution)/shard_map/ppermute | solution.py:17
  4.5 12.8 %collective-permute-start.2 = (bf16[1024,128]{1,0:T(8,128)(2,1)}, bf16[1024,128]{1,0:T(8,128)(2,1)}, u32[]{:S(2)}, u32[]{:S(2)}) collective-permute-start(bf16[1024,128]{1,0:T(8,128)(2,1)} %param.10), channel_id=1, source_target_pairs={{1,0},{2,1},{3,2},{4,3},{5,4},{6,5},{7,6},{8,7},{9,8},{10,9},{11,1... | collective-permute-start | bytes 786440 | tf_op jit(solution)/shard_map/ppermute | solution.py:12
  5.7 9.4 %collective-permute-start.1 = (bf16[1024,128]{1,0:T(8,128)(2,1)}, bf16[1024,128]{1,0:T(8,128)(2,1)}, u32[]{:S(2)}, u32[]{:S(2)}) collective-permute-start(bf16[1024,128]{1,0:T(8,128)(2,1)} %bitcast.26), channel_id=1, source_target_pairs={{0,16},{16,0},{1,17},{17,1},{2,18},{18,2},{3,19},{19,3},{4,20},{20... | collective-permute-start | bytes 786440 | tf_op jit(solution)/shard_map/ppermute | solution.py:17
  19.1 7.9 %all-to-all-start = ((bf16[4,128,128]{2,1,0:T(8,128)(2,1)}), bf16[4,128,128]{2,1,0:T(8,128)(2,1)S(1)}, u32[]{:S(2)}, u32[]{:S(2)}) async-start(bf16[4,128,128]{2,1,0:T(8,128)(2,1)} %broadcast_in_dim.12), calls=%async_computation | async-start | bytes 262144 | tf_op jit(solution)/shard_map/all_to_all | solution.py:60
  27.0 8.6 %copy-start.1 = (bf16[4,128,128]{2,1,0:T(8,128)(2,1)}, bf16[4,128,128]{2,1,0:T(8,128)(2,1)S(1)}, u32[]{:S(2)}) copy-start(bf16[4,128,128]{2,1,0:T(8,128)(2,1)S(1)} %all-to-all-done.maps_ref) | copy-start | bytes 393220
  27.0 8.6 %all-to-all-start.1 = ((bf16[4,128,128]{2,1,0:T(8,128)(2,1)}), bf16[4,128,128]{2,1,0:T(8,128)(2,1)}, u32[]{:S(2)}, u32[]{:S(2)}) async-start(bf16[4,128,128]{2,1,0:T(8,128)(2,1)} %bitcast.25), calls=%async_computation.1 | async-start | bytes 262144 | tf_op jit(solution)/shard_map/all_to_all | solution.py:60

commit v4 on v1

v4 whole, which is shorter than its diff:
```python
import jax
import jax.numpy as jnp
from jax import lax
from jax.experimental import pallas as pl
from jax.experimental.pallas import tpu as pltpu
from jax.sharding import PartitionSpec as P


def shifted(value, axis, steps):
    count = lax.axis_size(axis)
    leading, last = (max(0, -steps), min(count, count - steps))
    return lax.ppermute(value, axis, [(source, source + steps) for source in range(leading, last)])


def rotated(value, axis, steps):
    count = lax.axis_size(axis)
    return lax.ppermute(value, axis, [(source, (source + steps) % count) for source in range(count)])


def project(basis, vectors):
    return lax.dot_general(
        basis, vectors, (((0,), (0,)), ((), ())), preferred_element_type=jnp.float32
    )


def product(a, b):
    return jnp.dot(a, b, preferred_element_type=jnp.float32)


VMEM = pl.BlockSpec(memory_space=pltpu.VMEM)
SMEM = pl.BlockSpec(memory_space=pltpu.SMEM)
FLIPPED = (((1,), (1,)), ((), ()))


def make_maps(layers, *refs):
    lefts, cores = refs[:layers], refs[layers : 2 * layers]
    inverse_ref, next_ref, gain_ref, maps_ref = refs[2 * layers :]
    tile_range = product(lefts[0][...], cores[0][...])
    for left, core in zip(lefts[1:], cores[1:]):
        tile_range += product(left[...], core[...])
    gain = product(inverse_ref[...], (-tile_range).astype(jnp.bfloat16)).astype(jnp.bfloat16)
    gain_ref[...] = gain
    map_t = (-project(gain, next_ref[...])).astype(jnp.bfloat16)
    for target in range(maps_ref.shape[0]):
        maps_ref[target] = map_t


def compose(place_ref, maps_ref, shifts_ref, entry_ref, own_ref, sent_ref):
    count, rank, _ = maps_ref.shape
    share = entry_ref.shape[0]
    upper, lower = place_ref[0], place_ref[1]
    rows = lax.broadcasted_iota(jnp.int32, (rank, rank), 0)
    cols = lax.broadcasted_iota(jnp.int32, (rank, rank), 1)
    identity = jnp.where(rows == cols, 1.0, 0.0).astype(jnp.float32)
    before = jnp.where(upper == 0, entry_ref[...], 0.0)
    state = jnp.concatenate([identity, before], axis=0)
    own = identity
    for member in range(count):
        reached = (upper > 0) & (lower == member)
        own = jnp.where(reached, state[:rank], own)
        value = state[rank:].astype(jnp.bfloat16)
        sent_ref[member] = value
        sent_ref[count + member] = value
        moved = product(state.astype(jnp.bfloat16), maps_ref[member])
        state = jnp.concatenate(
            [moved[:rank], moved[rank:] + shifts_ref[member].astype(jnp.float32)], axis=0
        )
    own_ref[...] = own.astype(jnp.bfloat16)

    @pl.when(upper == 0)
    def _():
        value = state[rank:].astype(jnp.bfloat16)
        for member in range(count):
            sent_ref[count + member] = value


def solve(place_ref, parts_ref, own_ref, gain_ref, applied_ref, result_ref, coupled_ref):
    @pl.when(pl.program_id(0) == 0)
    def _():
        count = parts_ref.shape[0] // 2
        shape = coupled_ref.shape
        moved = product(parts_ref[:count].reshape(shape), own_ref[...])
        rest = parts_ref[count:].reshape(shape).astype(jnp.float32)
        coupled = moved + jnp.where(place_ref[0] == 0, 0.0, rest)
        coupled_ref[...] = coupled.astype(jnp.bfloat16)

    moved = lax.dot_general(
        gain_ref[...], coupled_ref[...], FLIPPED, preferred_element_type=jnp.float32
    )
    result_ref[...] = (applied_ref[...].astype(jnp.float32) - moved).astype(jnp.bfloat16)


def exchanged(blocks, members=None):
    return lax.all_to_all(blocks, "row", 0, 0, axis_index_groups=members, tiled=True)


def body(left_factors, right_factors, sketch, row_basis, inverse_diag, right_side, incoming):
    half = jnp.bfloat16
    order, rank = sketch.shape
    width = right_side.shape[1]
    layers, groups = lax.axis_size("layer"), lax.axis_size("row")
    lowers = groups // 2
    here = lax.axis_index("row")
    place = jnp.stack([here // lowers, here % lowers])
    share = width // lowers
    near = [list(range(lowers)), list(range(lowers, groups))]

    lefts = [left_factors[0]] + [rotated(left_factors[0], "layer", k) for k in range(1, layers)]
    next_rows = shifted(row_basis, "row", -1)
    applied = product(inverse_diag, right_side).astype(half)
    sketch, applied = lax.optimization_barrier((sketch, applied))
    core = project(right_factors[0], sketch).astype(half)
    cores = [core] + [rotated(core, "layer", k) for k in range(1, layers)]

    shift_t = project(applied, next_rows).astype(half)
    shifts = exchanged(shift_t.reshape(lowers, share, rank), near)
    entry = lax.dynamic_slice_in_dim(incoming, place[1] * share, share, 1).T
    lefts[-1], shifts, entry = lax.optimization_barrier((lefts[-1], shifts, entry))

    gain, maps = pl.pallas_call(
        lambda *refs: make_maps(layers, *refs),
        in_specs=[VMEM] * (2 * layers + 2),
        out_specs=[VMEM] * 2,
        out_shape=(
            jax.ShapeDtypeStruct((order, rank), half),
            jax.ShapeDtypeStruct((lowers, rank, rank), half),
        ),
        name="make_maps",
    )(*lefts, *cores, inverse_diag, next_rows)
    maps = exchanged(maps, near)
    own, sent = pl.pallas_call(
        compose,
        in_specs=[SMEM] + [VMEM] * 3,
        out_specs=[VMEM] * 2,
        out_shape=(
            jax.ShapeDtypeStruct((rank, rank), half),
            jax.ShapeDtypeStruct((groups, share, rank), half),
        ),
        name="compose",
    )(place, maps, shifts, entry)

    parts = exchanged(sent)
    tile = order // 4
    return pl.pallas_call(
        solve,
        grid=(4,),
        in_specs=[
            SMEM,
            pl.BlockSpec((groups, share, rank), lambda i: (0, 0, 0)),
            pl.BlockSpec((rank, rank), lambda i: (0, 0)),
            pl.BlockSpec((tile, rank), lambda i: (i, 0)),
            pl.BlockSpec((tile, width), lambda i: (i, 0)),
        ],
        out_specs=pl.BlockSpec((tile, width), lambda i: (i, 0)),
        out_shape=jax.ShapeDtypeStruct((order, width), half),
        scratch_shapes=[pltpu.VMEM((width, rank), half)],
        name="solve",
    )(place, parts, own, gain, applied)


def solution(mesh):
    return jax.shard_map(
        body,
        mesh=mesh,
        in_specs=(
            P("layer", "row", None),
            P("layer", "row", None),
            P("row", None),
            P("row", None),
            P("row", None),
            P("row", "layer"),
            P(None, "layer"),
        ),
        out_specs=P("row", "layer"),
        check_vma=False,
    )
```

time: 63.4 us -> 57.5 us (0.907)
  the two profiles are of different devices: /device:TPU:24 before, /device:TPU:0 now
where the time goes in v4:
time: 57.5 us; the launch traced here: 56.9 us
  starting transfers between devices  16 us (28%)
  blocking collectives  14.2 us (25%)
  Pallas kernels  10.8 us (19%)
  waiting for transfers between devices  7.87 us (14%)
  matrix products  4.27 us (7%)
  local copies, waits for them, and re-layouts  3.02 us (5%)
  other arithmetic  0.61 us (1%)
    all_to_all x1, blocking collectives, exchanged(): lax.all_to_all(blocks, 'row', 0, 0, axis_index_groups=members, tiled=True)  14.2 us
    all_to_all x2, starting transfers between devices, exchanged(): lax.all_to_all(blocks, 'row', 0, 0, axis_index_groups=members, tiled=True)  11 us
    all_to_all x2, waiting for transfers between devices, exchanged(): lax.all_to_all(blocks, 'row', 0, 0, axis_index_groups=members, tiled=True)  7.86 us
    pallas_call x1, Pallas kernels, body(): pl.pallas_call(solve, grid=(4,), in_specs=[SMEM, pl.BlockSpec((groups, sh...  4.15 us
    pallas_call x1, Pallas kernels, body(): pl.pallas_call(lambda *refs: make_maps(layers, *refs), in_specs=[VMEM] *...  3.89 us
    ppermute x2, starting transfers between devices, rotated(): lax.ppermute(value, axis, [(source, (source + steps) % count) for source...  3.73 us
    dot_general x1, matrix products, product(): return jnp.dot(a, b, preferred_element_type=jnp.float32)  2.83 us
    pallas_call x1, Pallas kernels, body(): pl.pallas_call(compose, in_specs=[SMEM] + [VMEM] * 3, out_specs=[VMEM] *...  2.74 us
  transfers between devices with their start and end apart: 5, of which 2 were waited for; matrix products, arithmetic and copies ran while one was open for 11% of the time, Pallas kernels for 0%

profile of v4, /device:TPU:0, one launch (start us, length us, event | category | flops | bytes accessed | tf_op | source)
XLA Modules:
  0.0 56.9 jit_solution(7686212777521153939)
XLA Ops:
  0.0 3.0 %collective-permute-start = (bf16[1024,128]{1,0:T(8,128)(2,1)}, bf16[1024,128]{1,0:T(8,128)(2,1)S(1)}, u32[]{:S(2)}, u32[]{:S(2)}) collective-permute-start(bf16[1024,128]{1,0:T(8,128)(2,1)} %bitcast.15), channel_id=1, source_target_pairs={{0,16},{16,0},{1,17},{17,1},{2,18},{18,2},{3,19},{19,3},{4,20},{20... | collective-permute-start | bytes 786440 | tf_op jit(solution)/shard_map/ppermute | solution.py:17
  3.0 1.3 %collective-permute-start.1 = (bf16[1024,128]{1,0:T(8,128)(2,1)}, bf16[1024,128]{1,0:T(8,128)(2,1)S(1)}, u32[]{:S(2)}, u32[]{:S(2)}) collective-permute-start(bf16[1024,128]{1,0:T(8,128)(2,1)} %param.10), channel_id=1, source_target_pairs={{1,0},{2,1},{3,2},{4,3},{5,4},{6,5},{7,6},{8,7},{9,8},{10,9},{11,1... | collective-permute-start | bytes 786440 | tf_op jit(solution)/shard_map/ppermute | solution.py:12
  4.3 2.8 %convolution_convert_fusion.applied_ref = bf16[1024,512]{1,0:T(8,128)(2,1)S(1)} fusion(bf16[1024,1024]{1,0:T(8,128)(2,1)} %refs_4_.1, bf16[1024,512]{1,0:T(8,128)(2,1)S(1)} %copy-done), kind=kOutput, calls=%fused_computation | convolution fusion | flops 1074266112 | bytes 4194304 | tf_op jit(solution)/shard_map/dot_general | solution.py:27
  7.2 0.0 collective-permute-done.1.refs_5_
  7.2 1.2 %convolution_convert_fusion.1 = bf16[512,128]{1,0:T(8,128)(2,1)} fusion(bf16[1024,512]{1,0:T(8,128)(2,1)S(1)} %convolution_convert_fusion.applied_ref, bf16[1024,128]{1,0:T(8,128)(2,1)S(1)} %collective-permute-done.1.refs_5_), kind=kOutput, calls=%fused_computation.1 | convolution fusion | flops 134283264 | bytes 1441792 | tf_op jit(solution)/shard_map/dot_general | solution.py:21
  8.3 7.6 %all-to-all-start = ((bf16[8,64,128]{2,1,0:T(8,128)(2,1)}), bf16[8,64,128]{2,1,0:T(8,128)(2,1)S(1)}, u32[]{:S(2)}, u32[]{:S(2)}) async-start(bf16[8,64,128]{2,1,0:T(8,128)(2,1)} %bitcast.3), calls=%async_computation | async-start | bytes 262144 | tf_op jit(solution)/shard_map/all_to_all | solution.py:94
  15.9 0.3 fusion.refs_2_
  16.2 0.7 %collective-permute-start.2 = (bf16[128,128]{1,0:T(8,128)(2,1)S(1)}, bf16[128,128]{1,0:T(8,128)(2,1)S(1)}, u32[]{:S(2)}, u32[]{:S(2)}) collective-permute-start(bf16[128,128]{1,0:T(8,128)(2,1)S(1)} %fusion.refs_2_), channel_id=1, source_target_pairs={{0,16},{16,0},{1,17},{17,1},{2,18},{18,2},{3,19},{19,3},{4,20},{20... | collective-permute-start | bytes 98312 | tf_op jit(solution)/shard_map/ppermute | solution.py:17
  17.0 0.9 %constant_dynamic-slice_fusion = f32[128,64]{1,0:T(8,128)S(1)} fusion(f32[128,512]{1,0:T(8,128)} %param.13, s32[]{:T(128)S(6)} %select_n.16), kind=kLoop, calls=%fused_computation.6 | loop fusion | bytes 65540 | tf_op jit(solution)/shard_map/dynamic_slice | solution.py:117
  17.9 0.7 %copy.11 = f32[128,64]{0,1:T(8,128)} copy(f32[128,64]{1,0:T(8,128)S(1)} %constant_dynamic-slice_fusion) | data formatting | bytes 65536
  18.6 0.0 collective-permute-done.refs_1_
  18.6 2.5 %all-to-all-done.shifts_ref = bf16[8,64,128]{2,1,0:T(8,128)(2,1)S(1)} async-done(((bf16[8,64,128]{2,1,0:T(8,128)(2,1)}), bf16[8,64,128]{2,1,0:T(8,128)(2,1)S(1)}, u32[]{:S(2)}, u32[]{:S(2)}) %all-to-all-start) | async-done | bytes 131104 | tf_op jit(solution)/shard_map/all_to_all | solution.py:94
  21.1 0.0 collective-permute-done.2.refs_3_
  21.1 0.0 copy-done.8
  21.1 0.0 copy-done.5
  21.1 0.7 %copy-done.9 = bf16[128,128]{1,0:T(8,128)(2,1)} copy-done((bf16[128,128]{1,0:T(8,128)(2,1)}, bf16[128,128]{1,0:T(8,128)(2,1)S(1)}, u32[]{:S(2)}) %copy-start.9) | copy-done | bytes 32792
  21.8 3.9 %make_maps.1 = (bf16[1024,128]{1,0:T(8,128)(2,1)}, bf16[8,128,128]{2,1,0:T(8,128)(2,1)}) custom-call(bf16[1024,128]{1,0:T(8,128)(2,1)} %bitcast.16, bf16[1024,128]{1,0:T(8,128)(2,1)} %copy-done.5, bf16[128,128]{1,0:T(8,128)(2,1)} %copy-done.8, bf16[128,128]{1,0:T(8,128)(2,1)} %copy-done.9, bf16[1024,1024]{1,0:T(8,128)(2,1)} %refs_4_.1, ...), custom_call_target="tpu_custom_call" | custom-call | tf_op jit(solution)/shard_map/make_maps/pallas_call | solution.py:120
  25.7 3.4 %all-to-all-start.1 = ((bf16[8,128,128]{2,1,0:T(8,128)(2,1)}), bf16[8,128,128]{2,1,0:T(8,128)(2,1)S(1)}, u32[]{:S(2)}, u32[]{:S(2)}) async-start(bf16[8,128,128]{2,1,0:T(8,128)(2,1)} %get-tuple-element.17), calls=%async_computation.1 | async-start | bytes 524288 | tf_op jit(solution)/shard_map/all_to_all | solution.py:94
  29.1 0.6 %pad_add_fusion.place_ref = s32[2]{0:T(128)} fusion(s32[1]{0:T(128)} %bitcast.1, s32[1]{0:T(128)} %bitcast), kind=kLoop, calls=%fused_computation.5 | loop fusion | flops 2 | bytes 16 | tf_op jit(solution)/shard_map/stack | solution.py:104
  29.8 5.3 %all-to-all-done.1.maps_ref = bf16[8,128,128]{2,1,0:T(8,128)(2,1)S(1)} async-done(((bf16[8,128,128]{2,1,0:T(8,128)(2,1)}), bf16[8,128,128]{2,1,0:T(8,128)(2,1)S(1)}, u32[]{:S(2)}, u32[]{:S(2)}) %all-to-all-start.1) | async-done | bytes 262176 | tf_op jit(solution)/shard_map/all_to_all | solution.py:94
  35.1 0.7 %copy-done.3 = bf16[8,128,128]{2,1,0:T(8,128)(2,1)} copy-done((bf16[8,128,128]{2,1,0:T(8,128)(2,1)}, bf16[8,128,128]{2,1,0:T(8,128)(2,1)S(1)}, u32[]{:S(2)}) %copy-start.3) | copy-done | bytes 262168
  35.8 2.7 %compose.1 = (bf16[128,128]{1,0:T(8,128)(2,1)}, bf16[16,64,128]{2,1,0:T(8,128)(2,1)}) custom-call(s32[2]{0:T(128)} %pad_add_fusion.place_ref, bf16[8,128,128]{2,1,0:T(8,128)(2,1)} %copy-done.3, bf16[8,64,128]{2,1,0:T(8,128)(2,1)} %copy-done.4, f32[64,128]{1,0:T(8,128)} %bitcast.17), custom_call_target="tpu_custom_call" | custom-call | tf_op jit(solution)/shard_map/compose/pallas_call | solution.py:131
  38.5 14.2 %all_to_all.15.parts_ref = bf16[16,64,128]{2,1,0:T(8,128)(2,1)} all-to-all(bf16[16,64,128]{2,1,0:T(8,128)(2,1)} %get-tuple-element.20), channel_id=1, replica_groups=mesh['layer'=2,'row'=16] {'row'}, dimensions={0} | all-to-all | bytes 524288 | tf_op jit(solution)/shard_map/all_to_all | solution.py:94
  52.8 4.1 %solve.1 = bf16[1024,512]{1,0:T(8,128)(2,1)} custom-call(s32[2]{0:T(128)} %pad_add_fusion.place_ref, bf16[16,64,128]{2,1,0:T(8,128)(2,1)} %all_to_all.15.parts_ref, bf16[128,128]{1,0:T(8,128)(2,1)} %get-tuple-element.21.own_ref, bf16[1024,128]{1,0:T(8,128)(2,1)} %get-tuple-element.22.gain_ref, bf16[1024,512]{1,0:T(8,128)(2,1)} %copy-done.1), custom_call_target="tpu_custom_call" | custom-call | tf_op jit(solution)/shard_map/solve/pallas_call | solution.py:144
  (16 shorter events, 0.0 us)
Async XLA Ops:
  0.0 4.3 %copy-start = (bf16[1024,512]{1,0:T(8,128)(2,1)S(1)}, bf16[1024,512]{1,0:T(8,128)(2,1)}, u32[]{:S(2)}) copy-start(bf16[1024,512]{1,0:T(8,128)(2,1)} %param.12) | copy-start | bytes 3145732
  0.0 15.9 %copy-start.6 = (bf16[1024,128]{1,0:T(8,128)(2,1)S(1)}, bf16[1024,128]{1,0:T(8,128)(2,1)}, u32[]{:S(2)}) copy-start(bf16[1024,128]{1,0:T(8,128)(2,1)} %param.9) | copy-start | bytes 786436
  0.0 15.9 %copy-start.7 = (bf16[1,1024,128]{2,1,0:T(8,128)(2,1)S(1)}, bf16[1,1024,128]{2,1,0:T(8,128)(2,1)}, u32[]{:S(2)}) copy-start(bf16[1,1024,128]{2,1,0:T(8,128)(2,1)} %param.8) | copy-start | bytes 786436
  0.0 18.6 %collective-permute-start = (bf16[1024,128]{1,0:T(8,128)(2,1)}, bf16[1024,128]{1,0:T(8,128)(2,1)S(1)}, u32[]{:S(2)}, u32[]{:S(2)}) collective-permute-start(bf16[1024,128]{1,0:T(8,128)(2,1)} %bitcast.15), channel_id=1, source_target_pairs={{0,16},{16,0},{1,17},{17,1},{2,18},{18,2},{3,19},{19,3},{4,20},{20... | collective-permute-start | bytes 786440 | tf_op jit(solution)/shard_map/ppermute | solution.py:17
  3.0 4.1 %collective-permute-start.1 = (bf16[1024,128]{1,0:T(8,128)(2,1)}, bf16[1024,128]{1,0:T(8,128)(2,1)S(1)}, u32[]{:S(2)}, u32[]{:S(2)}) collective-permute-start(bf16[1024,128]{1,0:T(8,128)(2,1)} %param.10), channel_id=1, source_target_pairs={{1,0},{2,1},{3,2},{4,3},{5,4},{6,5},{7,6},{8,7},{9,8},{10,9},{11,1... | collective-permute-start | bytes 786440 | tf_op jit(solution)/shard_map/ppermute | solution.py:12
  7.2 18.6 %copy-start.1 = (bf16[1024,512]{1,0:T(8,128)(2,1)}, bf16[1024,512]{1,0:T(8,128)(2,1)S(1)}, u32[]{:S(2)}) copy-start(bf16[1024,512]{1,0:T(8,128)(2,1)S(1)} %convolution_convert_fusion.applied_ref) | copy-start | bytes 3145732
  7.2 13.9 %copy-start.2 = (bf16[1024,128]{1,0:T(8,128)(2,1)}, bf16[1024,128]{1,0:T(8,128)(2,1)S(1)}, u32[]{:S(2)}) copy-start(bf16[1024,128]{1,0:T(8,128)(2,1)S(1)} %collective-permute-done.1.refs_5_) | copy-start | bytes 786436
  8.3 12.8 %all-to-all-start = ((bf16[8,64,128]{2,1,0:T(8,128)(2,1)}), bf16[8,64,128]{2,1,0:T(8,128)(2,1)S(1)}, u32[]{:S(2)}, u32[]{:S(2)}) async-start(bf16[8,64,128]{2,1,0:T(8,128)(2,1)} %bitcast.3), calls=%async_computation | async-start | bytes 262144 | tf_op jit(solution)/shard_map/all_to_all | solution.py:94
  16.2 4.9 %copy-start.8 = (bf16[128,128]{1,0:T(8,128)(2,1)}, bf16[128,128]{1,0:T(8,128)(2,1)S(1)}, u32[]{:S(2)}) copy-start(bf16[128,128]{1,0:T(8,128)(2,1)S(1)} %fusion.refs_2_) | copy-start | bytes 98308
  16.2 4.9 %collective-permute-start.2 = (bf16[128,128]{1,0:T(8,128)(2,1)S(1)}, bf16[128,128]{1,0:T(8,128)(2,1)S(1)}, u32[]{:S(2)}, u32[]{:S(2)}) collective-permute-start(bf16[128,128]{1,0:T(8,128)(2,1)S(1)} %fusion.refs_2_), channel_id=1, source_target_pairs={{0,16},{16,0},{1,17},{17,1},{2,18},{18,2},{3,19},{19,3},{4,20},{20... | collective-permute-start | bytes 98312 | tf_op jit(solution)/shard_map/ppermute | solution.py:17
  18.6 2.5 %copy-start.5 = (bf16[1024,128]{1,0:T(8,128)(2,1)}, bf16[1024,128]{1,0:T(8,128)(2,1)S(1)}, u32[]{:S(2)}) copy-start(bf16[1024,128]{1,0:T(8,128)(2,1)S(1)} %collective-permute-done.refs_1_) | copy-start | bytes 786436
  21.1 14.0 %copy-start.4 = (bf16[8,64,128]{2,1,0:T(8,128)(2,1)}, bf16[8,64,128]{2,1,0:T(8,128)(2,1)S(1)}, u32[]{:S(2)}) copy-start(bf16[8,64,128]{2,1,0:T(8,128)(2,1)S(1)} %all-to-all-done.shifts_ref) | copy-start | bytes 393220
  21.1 0.7 %copy-start.9 = (bf16[128,128]{1,0:T(8,128)(2,1)}, bf16[128,128]{1,0:T(8,128)(2,1)S(1)}, u32[]{:S(2)}) copy-start(bf16[128,128]{1,0:T(8,128)(2,1)S(1)} %collective-permute-done.2.refs_3_) | copy-start | bytes 98308
  25.7 9.4 %all-to-all-start.1 = ((bf16[8,128,128]{2,1,0:T(8,128)(2,1)}), bf16[8,128,128]{2,1,0:T(8,128)(2,1)S(1)}, u32[]{:S(2)}, u32[]{:S(2)}) async-start(bf16[8,128,128]{2,1,0:T(8,128)(2,1)} %get-tuple-element.17), calls=%async_computation.1 | async-start | bytes 524288 | tf_op jit(solution)/shard_map/all_to_all | solution.py:94
  35.1 0.7 %copy-start.3 = (bf16[8,128,128]{2,1,0:T(8,128)(2,1)}, bf16[8,128,128]{2,1,0:T(8,128)(2,1)S(1)}, u32[]{:S(2)}) copy-start(bf16[8,128,128]{2,1,0:T(8,128)(2,1)S(1)} %all-to-all-done.1.maps_ref) | copy-start | bytes 786436

commit v5 on v4

v5 whole, which is shorter than its diff:
```python
import jax
import jax.numpy as jnp
from jax import lax
from jax.experimental import pallas as pl
from jax.experimental.pallas import tpu as pltpu
from jax.sharding import PartitionSpec as P


def shifted(value, axis, steps):
    count = lax.axis_size(axis)
    leading, last = (max(0, -steps), min(count, count - steps))
    return lax.ppermute(value, axis, [(source, source + steps) for source in range(leading, last)])


def rotated(value, axis, steps):
    count = lax.axis_size(axis)
    return lax.ppermute(value, axis, [(source, (source + steps) % count) for source in range(count)])


def project(basis, vectors):
    return lax.dot_general(
        basis, vectors, (((0,), (0,)), ((), ())), preferred_element_type=jnp.float32
    )


def product(a, b):
    return jnp.dot(a, b, preferred_element_type=jnp.float32)


VMEM = pl.BlockSpec(memory_space=pltpu.VMEM)
SMEM = pl.BlockSpec(memory_space=pltpu.SMEM)
FLIPPED = (((1,), (1,)), ((), ()))


def make_maps(layers, *refs):
    lefts, cores = refs[:layers], refs[layers : 2 * layers]
    weights_ref, shift_ref, tile_range_ref, sent_ref = refs[2 * layers :]
    total = product(lefts[0][...], cores[0][...])
    for left, core in zip(lefts[1:], cores[1:]):
        total += product(left[...], core[...])
    tile_range = (-total).astype(jnp.bfloat16)
    tile_range_ref[...] = tile_range
    rank = tile_range.shape[1]
    parts = product(weights_ref[...], tile_range)
    map_t = (-(parts[:rank] + parts[rank:])).T.astype(jnp.bfloat16)
    for target in range(sent_ref.shape[0]):
        sent_ref[target, :rank] = map_t
        sent_ref[target, rank:] = shift_ref[target]


def compose(place_ref, steps_ref, entry_ref, own_ref, sent_ref):
    count, _, rank = steps_ref.shape
    share = entry_ref.shape[0]
    upper, lower = place_ref[0], place_ref[1]
    rows = lax.broadcasted_iota(jnp.int32, (rank, rank), 0)
    cols = lax.broadcasted_iota(jnp.int32, (rank, rank), 1)
    identity = jnp.where(rows == cols, 1.0, 0.0).astype(jnp.float32)
    before = jnp.where(upper == 0, entry_ref[...], 0.0)
    state = jnp.concatenate([identity, before], axis=0)
    own = identity
    for member in range(count):
        reached = (upper > 0) & (lower == member)
        own = jnp.where(reached, state[:rank], own)
        value = state[rank:].astype(jnp.bfloat16)
        sent_ref[member] = value
        sent_ref[count + member] = value
        moved = product(state.astype(jnp.bfloat16), steps_ref[member, :rank])
        state = jnp.concatenate(
            [moved[:rank], moved[rank:] + steps_ref[member, rank:].astype(jnp.float32)], axis=0
        )
    own_ref[...] = own.astype(jnp.bfloat16)

    @pl.when(upper == 0)
    def _():
        value = state[rank:].astype(jnp.bfloat16)
        for member in range(count):
            sent_ref[count + member] = value


def exchanged(blocks, members=None):
    return lax.all_to_all(blocks, "row", 0, 0, axis_index_groups=members, tiled=True)


def body(left_factors, right_factors, sketch, row_basis, inverse_diag, right_side, incoming):
    half = jnp.bfloat16
    order, rank = sketch.shape
    width = right_side.shape[1]
    layers, groups = lax.axis_size("layer"), lax.axis_size("row")
    lowers = groups // 2
    here = lax.axis_index("row")
    place = jnp.stack([lax.div(here, lowers), lax.rem(here, lowers)])
    share = width // lowers
    near = [list(range(lowers)), list(range(lowers, groups))]

    lefts = [left_factors[0]] + [rotated(left_factors[0], "layer", k) for k in range(1, layers)]
    next_rows = shifted(row_basis, "row", -1)
    applied = product(inverse_diag, right_side).astype(half)
    sketch, applied = lax.optimization_barrier((sketch, applied))
    core = project(right_factors[0], sketch).astype(half)
    cores = [core] + [rotated(core, "layer", k) for k in range(1, layers)]

    shift_t = project(applied, next_rows).astype(half).reshape(lowers, share, rank)
    entry = lax.dynamic_slice_in_dim(incoming, place[1] * share, share, 1).T
    weights = project(next_rows, inverse_diag)
    high = weights.astype(half)
    low = (weights - high.astype(jnp.float32)).astype(half)
    weights = jnp.concatenate([high, low])
    lefts[-1], shift_t, weights, entry, place = lax.optimization_barrier(
        (lefts[-1], shift_t, weights, entry, place)
    )

    tile_range, sent = pl.pallas_call(
        lambda *refs: make_maps(layers, *refs),
        in_specs=[VMEM] * (2 * layers + 2),
        out_specs=[VMEM] * 2,
        out_shape=(
            jax.ShapeDtypeStruct((order, rank), half),
            jax.ShapeDtypeStruct((lowers, rank + share, rank), half),
        ),
        name="make_maps",
    )(*lefts, *cores, weights, shift_t)
    steps = exchanged(sent, near)
    gain = product(inverse_diag, tile_range).astype(half)
    gain, steps = lax.optimization_barrier((gain, steps))
    own, sent = pl.pallas_call(
        compose,
        in_specs=[SMEM] + [VMEM] * 2,
        out_specs=[VMEM] * 2,
        out_shape=(
            jax.ShapeDtypeStruct((rank, rank), half),
            jax.ShapeDtypeStruct((groups, share, rank), half),
        ),
        name="compose",
    )(place, steps, entry)

    parts = exchanged(sent)
    rest = parts[lowers:].reshape(width, rank).astype(jnp.float32)
    coupled = product(parts[:lowers].reshape(width, rank), own)
    coupled = (coupled + jnp.where(place[0] == 0, 0.0, rest)).astype(half)
    moved = lax.dot_general(gain, coupled, FLIPPED, preferred_element_type=jnp.float32)
    return (applied.astype(jnp.float32) - moved).astype(half)


def solution(mesh):
    return jax.shard_map(
        body,
        mesh=mesh,
        in_specs=(
            P("layer", "row", None),
            P("layer", "row", None),
            P("row", None),
            P("row", None),
            P("row", None),
            P("row", "layer"),
            P(None, "layer"),
        ),
        out_specs=P("row", "layer"),
        check_vma=False,
    )
```

time: 57.5 us -> 50.4 us (0.88)
  blocking collectives: 14.2 us -> 0 us
  waiting for transfers between devices: 7.87 us -> 15 us
  Pallas kernels: 10.8 us -> 5.49 us
  matrix products: 4.27 us -> 9.47 us
  other arithmetic: 0.61 us -> 2.19 us
  starting transfers between devices: 16 us -> 14.6 us
    all_to_all x1 -> x0, blocking collectives: 14.2 us -> none  [exchanged(): lax.all_to_all(blocks, 'row', 0, 0, axis_index_groups=members, tiled=True)]
    all_to_all x2, waiting for transfers between devices: 7.86 us -> 15 us  [exchanged(): lax.all_to_all(blocks, 'row', 0, 0, axis_index_groups=members, tiled=True)]
    pallas_call x2 -> x1, Pallas kernels: 6.89 us -> 2.71 us  [body(): pl.pallas_call(compose, in_specs=[SMEM] + [VMEM] * 2, out_specs=[VMEM] *...]
    dot_general x0 -> x1, matrix products: none -> 2.62 us  [body(): lax.dot_general(gain, coupled, FLIPPED, preferred_element_type=jnp.float32)]
    dot_general x1 -> x2, matrix products: 2.83 us -> 4.96 us  [product(): return jnp.dot(a, b, preferred_element_type=jnp.float32)]
    pallas_call x1, Pallas kernels: 3.89 us -> 2.78 us  [body(): pl.pallas_call(lambda *refs: make_maps(layers, *refs), in_specs=[VMEM] *...]
    all_to_all x2, starting transfers between devices: 11 us -> 10 us  [exchanged(): lax.all_to_all(blocks, 'row', 0, 0, axis_index_groups=members, tiled=True)]
    concatenate x0 -> x1, other arithmetic: none -> 0.83 us  [body(): weights = jnp.concatenate([high, low])]
  transfers between devices with their start and end apart: 5 -> 5, of which waited for: 2 -> 2; matrix products, arithmetic and copies ran while one was open for 11% -> 20% of each run, Pallas kernels for 0% -> 0%
where the time goes in v5:
time: 50.4 us; the launch traced here: 49.9 us
  waiting for transfers between devices  15 us (30%)
  starting transfers between devices  14.6 us (29%)
  matrix products  9.47 us (19%)
  Pallas kernels  5.49 us (11%)
  local copies, waits for them, and re-layouts  3 us (6%)
  other arithmetic  2.19 us (4%)
    all_to_all x2, waiting for transfers between devices, exchanged(): lax.all_to_all(blocks, 'row', 0, 0, axis_index_groups=members, tiled=True)  15 us
    all_to_all x2, starting transfers between devices, exchanged(): lax.all_to_all(blocks, 'row', 0, 0, axis_index_groups=members, tiled=True)  10 us
    dot_general x2, matrix products, product(): return jnp.dot(a, b, preferred_element_type=jnp.float32)  4.96 us
    ppermute x2, starting transfers between devices, rotated(): lax.ppermute(value, axis, [(source, (source + steps) % count) for source...  3.28 us
    pallas_call x1, Pallas kernels, body(): pl.pallas_call(lambda *refs: make_maps(layers, *refs), in_specs=[VMEM] *...  2.78 us
    pallas_call x1, Pallas kernels, body(): pl.pallas_call(compose, in_specs=[SMEM] + [VMEM] * 2, out_specs=[VMEM] *...  2.71 us
    dot_general x1, matrix products, body(): lax.dot_general(gain, coupled, FLIPPED, preferred_element_type=jnp.float32)  2.62 us
    unnamed x15, local copies, waits for them, and re-layouts  2.07 us
  transfers between devices with their start and end apart: 5, of which 2 were waited for; matrix products, arithmetic and copies ran while one was open for 20% of the time, Pallas kernels for 0%

profile of v5, /device:TPU:0, one launch (start us, length us, event | category | flops | bytes accessed | tf_op | source)
XLA Modules:
  0.0 49.9 jit_solution(4558137237680822983)
XLA Ops:
  0.0 3.0 %collective-permute-start = (bf16[1024,128]{1,0:T(8,128)(2,1)}, bf16[1024,128]{1,0:T(8,128)(2,1)}, u32[]{:S(2)}, u32[]{:S(2)}) collective-permute-start(bf16[1024,128]{1,0:T(8,128)(2,1)} %bitcast.31), channel_id=1, source_target_pairs={{0,16},{16,0},{1,17},{17,1},{2,18},{18,2},{3,19},{19,3},{4,20},{20... | collective-permute-start | bytes 786440 | tf_op jit(solution)/shard_map/ppermute | solution.py:17
  3.0 1.3 %collective-permute-start.1 = (bf16[1024,128]{1,0:T(8,128)(2,1)}, bf16[1024,128]{1,0:T(8,128)(2,1)S(1)}, u32[]{:S(2)}, u32[]{:S(2)}) collective-permute-start(bf16[1024,128]{1,0:T(8,128)(2,1)} %param.10), channel_id=1, source_target_pairs={{1,0},{2,1},{3,2},{4,3},{5,4},{6,5},{7,6},{8,7},{9,8},{10,9},{11,1... | collective-permute-start | bytes 786440 | tf_op jit(solution)/shard_map/ppermute | solution.py:12
  4.3 2.5 %convolution_convert_fusion = bf16[1024,512]{1,0:T(8,128)(2,1)S(1)} fusion(bf16[1024,1024]{1,0:T(8,128)(2,1)S(1)} %copy-done, bf16[1024,512]{1,0:T(8,128)(2,1)} %param.12), kind=kOutput, calls=%fused_computation.1 | convolution fusion | flops 1074266112 | bytes 4194304 | tf_op jit(solution)/shard_map/dot_general | solution.py:27
  6.8 0.3 fusion.2.refs_2_
  7.1 0.3 collective-permute-start.2
  7.4 0.9 %constant_dynamic-slice_fusion = f32[128,64]{1,0:T(8,128)S(1)} fusion(f32[128,512]{1,0:T(8,128)} %param.13, s32[]{:T(128)S(6)} %select_n.14), kind=kLoop, calls=%fused_computation.14 | loop fusion | bytes 65540 | tf_op jit(solution)/shard_map/dynamic_slice | solution.py:103
  8.3 0.7 %copy.11 = f32[128,64]{0,1:T(8,128)} copy(f32[128,64]{1,0:T(8,128)S(1)} %constant_dynamic-slice_fusion) | data formatting | bytes 65536
  9.0 0.6 %pad_add_fusion.place_ref = s32[2]{0:T(128)} fusion(s32[1]{0:T(128)} %bitcast.4, s32[1]{0:T(128)} %bitcast.3), kind=kLoop, calls=%fused_computation.13 | loop fusion | flops 2 | bytes 16 | tf_op jit(solution)/shard_map/stack | solution.py:91
  9.6 0.0 collective-permute-done.1
  9.6 0.5 subtract_convert_fusion.1
  10.1 1.1 %convolution_convert_fusion.2 = bf16[512,128]{1,0:T(8,128)(2,1)} fusion(bf16[1024,512]{1,0:T(8,128)(2,1)S(1)} %convolution_convert_fusion, bf16[1024,128]{1,0:T(8,128)(2,1)S(1)} %collective-permute-done.1), kind=kOutput, calls=%fused_computation.6 | convolution fusion | flops 134283264 | bytes 1441792 | tf_op jit(solution)/shard_map/dot_general | solution.py:21
  11.3 0.8 %pad_maximum_fusion.refs_4_ = bf16[256,1024]{1,0:T(8,128)(2,1)} fusion(bf16[128,1024]{1,0:T(8,128)(2,1)S(1)} %get-tuple-element.31, bf16[128,1024]{1,0:T(8,128)(2,1)S(1)} %get-tuple-element.32), kind=kLoop, calls=%fused_computation.9 | loop fusion | flops 1048576 | bytes 1048576 | tf_op jit(solution)/shard_map/concatenate | solution.py:107
  12.1 0.0 collective-permute-done.refs_1_
  12.1 0.6 %copy-done.5 = bf16[128,128]{1,0:T(8,128)(2,1)} copy-done((bf16[128,128]{1,0:T(8,128)(2,1)}, bf16[128,128]{1,0:T(8,128)(2,1)S(1)}, u32[]{:S(2)}) %copy-start.5) | copy-done | bytes 32792
  12.7 2.8 %make_maps.1 = (bf16[1024,128]{1,0:T(8,128)(2,1)}, bf16[8,192,128]{2,1,0:T(8,128)(2,1)}) custom-call(bf16[1024,128]{1,0:T(8,128)(2,1)} %bitcast.32, bf16[1024,128]{1,0:T(8,128)(2,1)} %collective-permute-done.refs_1_, bf16[128,128]{1,0:T(8,128)(2,1)} %copy-done.4, bf16[128,128]{1,0:T(8,128)(2,1)} %copy-done.5, bf16[256,1024]{1,0:T(8,128)(2,1)} %pad_maximum_fusion.refs_4_, ...), custom_call_target="tpu_custom_call" | custom-call | tf_op jit(solution)/shard_map/make_maps/pallas_call | solution.py:112
  15.5 5.3 %all-to-all-start = ((bf16[8,192,128]{2,1,0:T(8,128)(2,1)}), bf16[8,192,128]{2,1,0:T(8,128)(2,1)S(1)}, u32[]{:S(2)}, u32[]{:S(2)}) async-start(bf16[8,192,128]{2,1,0:T(8,128)(2,1)} %get-tuple-element.24), calls=%async_computation | async-start | bytes 786432 | tf_op jit(solution)/shard_map/all_to_all | solution.py:81
  20.8 2.5 %fusion = bf16[1024,128]{0,1:T(8,128)(2,1)} fusion(bf16[1024,128]{1,0:T(8,128)(2,1)} %get-tuple-element.23, bf16[1024,1024]{1,0:T(8,128)(2,1)S(1)} %copy-done), kind=kOutput, calls=%fused_computation.3 | convolution fusion | flops 268566528 | bytes 2621440 | tf_op jit(solution)/shard_map/dot_general | solution.py:27
  23.3 5.0 %all-to-all-done.steps_ref = bf16[8,192,128]{2,1,0:T(8,128)(2,1)S(1)} async-done(((bf16[8,192,128]{2,1,0:T(8,128)(2,1)}), bf16[8,192,128]{2,1,0:T(8,128)(2,1)S(1)}, u32[]{:S(2)}, u32[]{:S(2)}) %all-to-all-start) | async-done | bytes 393248 | tf_op jit(solution)/shard_map/all_to_all | solution.py:81
  28.3 0.7 %copy-done.1 = bf16[8,192,128]{2,1,0:T(8,128)(2,1)} copy-done((bf16[8,192,128]{2,1,0:T(8,128)(2,1)}, bf16[8,192,128]{2,1,0:T(8,128)(2,1)S(1)}, u32[]{:S(2)}) %copy-start.1) | copy-done | bytes 393240
  29.0 2.7 %compose.1 = (bf16[128,128]{1,0:T(8,128)(2,1)}, bf16[16,64,128]{2,1,0:T(8,128)(2,1)}) custom-call(s32[2]{0:T(128)} %pad_add_fusion.place_ref, bf16[8,192,128]{2,1,0:T(8,128)(2,1)} %copy-done.1, f32[64,128]{1,0:T(8,128)} %bitcast.33), custom_call_target="tpu_custom_call" | custom-call | tf_op jit(solution)/shard_map/compose/pallas_call | solution.py:125
  31.7 4.8 %all-to-all-start.1 = ((bf16[16,64,128]{2,1,0:T(8,128)(2,1)}), bf16[16,64,128]{2,1,0:T(8,128)(2,1)S(1)}, u32[]{:S(2)}, u32[]{:S(2)}) async-start(bf16[16,64,128]{2,1,0:T(8,128)(2,1)} %get-tuple-element.29), calls=%async_computation.1 | async-start | bytes 524288 | tf_op jit(solution)/shard_map/all_to_all | solution.py:81
  36.5 10.0 %all-to-all-done.1 = bf16[16,64,128]{2,1,0:T(8,128)(2,1)S(1)} async-done(((bf16[16,64,128]{2,1,0:T(8,128)(2,1)}), bf16[16,64,128]{2,1,0:T(8,128)(2,1)S(1)}, u32[]{:S(2)}, u32[]{:S(2)}) %all-to-all-start.1) | async-done | bytes 262176 | tf_op jit(solution)/shard_map/all_to_all | solution.py:81
  46.6 0.7 %convert_select_fusion = f32[8,64,128]{2,1,0:T(8,128)} fusion(bf16[16,64,128]{2,1,0:T(8,128)(2,1)S(1)} %all-to-all-done.1, pred[]{:T(512)} %bitcast.9), kind=kLoop, calls=%fused_computation.12 | loop fusion | flops 131072 | bytes 393217 | tf_op jit(solution)/shard_map/jit(_where)/select_n | solution.py:139
  47.3 2.6 %subtract_convert_fusion = bf16[1024,512]{1,0:T(8,128)(2,1)} fusion(bf16[1024,512]{1,0:T(8,128)(2,1)S(1)} %convolution_convert_fusion, bf16[1024,128]{0,1:T(8,128)(2,1)} %fusion, f32[512,128]{1,0:T(8,128)} %bitcast.28, bf16[512,128]{1,0:T(8,128)(2,1)S(1)} %bitcast.29, bf16[128,128]{1,0:T(8,128)(2,1)} %get-tuple-element.30), kind=kOutput, calls=%fused_computation | convolution fusion | flops 152698880 | bytes 2785280 | tf_op jit(solution)/shard_map/dot_general | solution.py:140
  (14 shorter events, 0.0 us)
Async XLA Ops:
  0.0 4.3 %copy-start = (bf16[1024,1024]{1,0:T(8,128)(2,1)S(1)}, bf16[1024,1024]{1,0:T(8,128)(2,1)}, u32[]{:S(2)}) copy-start(bf16[1024,1024]{1,0:T(8,128)(2,1)} %param.11) | copy-start | bytes 6291460
  0.0 6.8 %copy-start.2 = (bf16[1024,128]{1,0:T(8,128)(2,1)S(1)}, bf16[1024,128]{1,0:T(8,128)(2,1)}, u32[]{:S(2)}) copy-start(bf16[1024,128]{1,0:T(8,128)(2,1)} %param.9) | copy-start | bytes 786436
  0.0 6.8 %copy-start.3 = (bf16[1,1024,128]{2,1,0:T(8,128)(2,1)S(1)}, bf16[1,1024,128]{2,1,0:T(8,128)(2,1)}, u32[]{:S(2)}) copy-start(bf16[1,1024,128]{2,1,0:T(8,128)(2,1)} %param.8) | copy-start | bytes 786436
  0.0 12.1 %collective-permute-start = (bf16[1024,128]{1,0:T(8,128)(2,1)}, bf16[1024,128]{1,0:T(8,128)(2,1)}, u32[]{:S(2)}, u32[]{:S(2)}) collective-permute-start(bf16[1024,128]{1,0:T(8,128)(2,1)} %bitcast.31), channel_id=1, source_target_pairs={{0,16},{16,0},{1,17},{17,1},{2,18},{18,2},{3,19},{19,3},{4,20},{20... | collective-permute-start | bytes 786440 | tf_op jit(solution)/shard_map/ppermute | solution.py:17
  3.0 6.6 %collective-permute-start.1 = (bf16[1024,128]{1,0:T(8,128)(2,1)}, bf16[1024,128]{1,0:T(8,128)(2,1)S(1)}, u32[]{:S(2)}, u32[]{:S(2)}) collective-permute-start(bf16[1024,128]{1,0:T(8,128)(2,1)} %param.10), channel_id=1, source_target_pairs={{1,0},{2,1},{3,2},{4,3},{5,4},{6,5},{7,6},{8,7},{9,8},{10,9},{11,1... | collective-permute-start | bytes 786440 | tf_op jit(solution)/shard_map/ppermute | solution.py:12
  7.1 4.2 %copy-start.4 = (bf16[128,128]{1,0:T(8,128)(2,1)}, bf16[128,128]{1,0:T(8,128)(2,1)S(1)}, u32[]{:S(2)}) copy-start(bf16[128,128]{1,0:T(8,128)(2,1)S(1)} %fusion.2.refs_2_) | copy-start | bytes 98308
  7.1 5.0 %collective-permute-start.2 = (bf16[128,128]{1,0:T(8,128)(2,1)S(1)}, bf16[128,128]{1,0:T(8,128)(2,1)S(1)}, u32[]{:S(2)}, u32[]{:S(2)}) collective-permute-start(bf16[128,128]{1,0:T(8,128)(2,1)S(1)} %fusion.2.refs_2_), channel_id=1, source_target_pairs={{0,16},{16,0},{1,17},{17,1},{2,18},{18,2},{3,19},{19,3},{4,20},{20... | collective-permute-start | bytes 98312 | tf_op jit(solution)/shard_map/ppermute | solution.py:17
  12.1 0.6 %copy-start.5 = (bf16[128,128]{1,0:T(8,128)(2,1)}, bf16[128,128]{1,0:T(8,128)(2,1)S(1)}, u32[]{:S(2)}) copy-start(bf16[128,128]{1,0:T(8,128)(2,1)S(1)} %collective-permute-done.2.refs_3_) | copy-start | bytes 98308
  15.5 21.0 %copy-start.6 = (s32[2]{0:T(128)S(1)}, s32[2]{0:T(128)}, u32[]{:S(2)}) copy-start(s32[2]{0:T(128)} %pad_add_fusion.place_ref) | copy-start | bytes 28
  15.5 12.7 %all-to-all-start = ((bf16[8,192,128]{2,1,0:T(8,128)(2,1)}), bf16[8,192,128]{2,1,0:T(8,128)(2,1)S(1)}, u32[]{:S(2)}, u32[]{:S(2)}) async-start(bf16[8,192,128]{2,1,0:T(8,128)(2,1)} %get-tuple-element.24), calls=%async_computation | async-start | bytes 786432 | tf_op jit(solution)/shard_map/all_to_all | solution.py:81
  28.3 0.7 %copy-start.1 = (bf16[8,192,128]{2,1,0:T(8,128)(2,1)}, bf16[8,192,128]{2,1,0:T(8,128)(2,1)S(1)}, u32[]{:S(2)}) copy-start(bf16[8,192,128]{2,1,0:T(8,128)(2,1)S(1)} %all-to-all-done.steps_ref) | copy-start | bytes 1179652
  31.7 14.8 %all-to-all-start.1 = ((bf16[16,64,128]{2,1,0:T(8,128)(2,1)}), bf16[16,64,128]{2,1,0:T(8,128)(2,1)S(1)}, u32[]{:S(2)}, u32[]{:S(2)}) async-start(bf16[16,64,128]{2,1,0:T(8,128)(2,1)} %get-tuple-element.29), calls=%async_computation.1 | async-start | bytes 524288 | tf_op jit(solution)/shard_map/all_to_all | solution.py:81

commit v6 on v1

v6 whole, which is shorter than its diff:
```python
import jax
import jax.numpy as jnp
from jax import lax
from jax.sharding import PartitionSpec as P


def shifted(value, axis, steps):
    count = lax.axis_size(axis)
    leading, last = (max(0, -steps), min(count, count - steps))
    return lax.ppermute(value, axis, [(source, source + steps) for source in range(leading, last)])


def rotated(value, axis, steps):
    count = lax.axis_size(axis)
    return lax.ppermute(value, axis, [(source, (source + steps) % count) for source in range(count)])


def project(basis, vectors):
    return lax.dot_general(
        basis, vectors, (((0,), (0,)), ((), ())), preferred_element_type=jnp.float32
    )


def product(a, b):
    return jnp.dot(a, b, preferred_element_type=jnp.float32)


FLIPPED = (((1,), (1,)), ((), ()))


def exchanged(blocks, members):
    return lax.all_to_all(blocks, "row", 0, 0, axis_index_groups=members, tiled=True)


def body(left_factors, right_factors, sketch, row_basis, inverse_diag, right_side, incoming):
    half = jnp.bfloat16
    rank = sketch.shape[1]
    width = right_side.shape[1]
    layers, groups = lax.axis_size("layer"), lax.axis_size("row")
    lowers = groups // 2
    here = lax.axis_index("row")
    upper, lower = lax.div(here, lowers), lax.rem(here, lowers)
    share = width // lowers
    near = [list(range(lowers)), list(range(lowers, groups))]

    lefts = [left_factors[0]] + [rotated(left_factors[0], "layer", k) for k in range(1, layers)]
    next_rows = shifted(row_basis, "row", -1)
    applied = product(inverse_diag, right_side).astype(half)
    sketch, applied = lax.optimization_barrier((sketch, applied))
    core = project(right_factors[0], sketch).astype(half)
    cores = [core] + [rotated(core, "layer", k) for k in range(1, layers)]

    shift_t = project(applied, next_rows).astype(half).reshape(lowers, share, rank)
    weights = project(next_rows, inverse_diag)
    high = weights.astype(half)
    low = (weights - high.astype(jnp.float32)).astype(half)
    partial_range = product(lefts[0], cores[0])
    lefts[-1], shift_t, high, low, partial_range = lax.optimization_barrier(
        (lefts[-1], shift_t, high, low, partial_range)
    )
    for left, core in zip(lefts[1:], cores[1:]):
        partial_range += product(left, core)
    tile_range = (-partial_range).astype(half)
    flip = (((0,), (1,)), ((), ()))
    map_t = lax.dot_general(tile_range, high, flip, preferred_element_type=jnp.float32)
    map_t += lax.dot_general(tile_range, low, flip, preferred_element_type=jnp.float32)
    map_t = (-map_t).astype(half)
    sent = jnp.concatenate([jnp.broadcast_to(map_t, (lowers, rank, rank)), shift_t], axis=1)
    steps = exchanged(sent, near)
    gain = product(inverse_diag, tile_range).astype(half)
    gain, steps = lax.optimization_barrier((gain, steps))

    entry = lax.dynamic_slice_in_dim(incoming, lower * share, share, 1).T
    entry = jnp.where(upper == 0, entry, 0.0).astype(half)
    state = jnp.concatenate([jnp.eye(rank, dtype=half), entry])
    is_shift = lax.broadcasted_iota(jnp.int32, state.shape, 0) >= rank
    states = []
    for member in range(lowers):
        states.append(state)
        moved = product(state, steps[member, :rank])
        state = (moved + jnp.where(is_shift, steps[member], 0).astype(jnp.float32)).astype(half)
    entered = shifted(state[rank:], "row", lowers)
    states = jnp.stack(states)
    coupled = lax.dot_general(
        jnp.broadcast_to(entered, (lowers, share, rank)),
        states[:, :rank],
        (((2,), (1,)), ((0,), (0,))),
        preferred_element_type=jnp.float32,
    )
    coupled = (coupled + states[:, rank:].astype(jnp.float32)).astype(half)
    coupled = exchanged(coupled, near).reshape(width, rank)
    moved = lax.dot_general(gain, coupled, FLIPPED, preferred_element_type=jnp.float32)
    return (applied.astype(jnp.float32) - moved).astype(half)


def solution(mesh):
    return jax.shard_map(
        body,
        mesh=mesh,
        in_specs=(
            P("layer", "row", None),
            P("layer", "row", None),
            P("row", None),
            P("row", None),
            P("row", None),
            P("row", "layer"),
            P(None, "layer"),
        ),
        out_specs=P("row", "layer"),
        check_vma=False,
    )
```

time: 63.4 us -> 57.9 us (0.913)
  the two profiles are of different devices: /device:TPU:24 before, /device:TPU:0 now
where the time goes in v6:
time: 57.9 us; the launch traced here: 56.9 us
  matrix products  23 us (40%)
  starting transfers between devices  14.1 us (24%)
  waiting for transfers between devices  8.41 us (15%)
  blocking collectives  7.73 us (13%)
  local copies, waits for them, and re-layouts  1.86 us (3%)
  other arithmetic  1.6 us (3%)
    dot_general x12, matrix products, product(): return jnp.dot(a, b, preferred_element_type=jnp.float32)  18.7 us
    all_to_all x1, blocking collectives, exchanged(): lax.all_to_all(blocks, 'row', 0, 0, axis_index_groups=members, tiled=True)  7.73 us
    ppermute x2, starting transfers between devices, shifted(): lax.ppermute(value, axis, [(source, source + steps) for source in range(l...  6.09 us
    all_to_all x1, waiting for transfers between devices, exchanged(): lax.all_to_all(blocks, 'row', 0, 0, axis_index_groups=members, tiled=True)  5.38 us
    all_to_all x1, starting transfers between devices, exchanged(): lax.all_to_all(blocks, 'row', 0, 0, axis_index_groups=members, tiled=True)  4.85 us
    ppermute x2, starting transfers between devices, rotated(): lax.ppermute(value, axis, [(source, (source + steps) % count) for source...  3.14 us
    ppermute x2, waiting for transfers between devices, rotated(): lax.ppermute(value, axis, [(source, (source + steps) % count) for source...  1.61 us
    dot_general x1, matrix products, body(): lax.dot_general(gain, coupled, FLIPPED, preferred_element_type=jnp.float32)  1.43 us
  transfers between devices with their start and end apart: 5, of which 4 were waited for; matrix products, arithmetic and copies ran while one was open for 14% of the time, Pallas kernels for 0%

profile of v6, /device:TPU:0, one launch (start us, length us, event | category | flops | bytes accessed | tf_op | source)
XLA Modules:
  0.0 56.9 jit_solution(5698227136467189729)
XLA Ops:
  0.0 1.4 %collective-permute-start.1 = (bf16[1024,128]{1,0:T(8,128)(2,1)}, bf16[1024,128]{1,0:T(8,128)(2,1)S(1)}, u32[]{:S(2)}, u32[]{:S(2)}) collective-permute-start(bf16[1024,128]{1,0:T(8,128)(2,1)} %param.10), channel_id=1, source_target_pairs={{1,0},{2,1},{3,2},{4,3},{5,4},{6,5},{7,6},{8,7},{9,8},{10,9},{11,1... | collective-permute-start | bytes 786440 | tf_op jit(solution)/shard_map/ppermute | solution.py:10
  1.4 3.0 %collective-permute-start = (bf16[1024,128]{1,0:T(8,128)(2,1)}, bf16[1024,128]{1,0:T(8,128)(2,1)}, u32[]{:S(2)}, u32[]{:S(2)}) collective-permute-start(bf16[1024,128]{1,0:T(8,128)(2,1)} %bitcast.126), channel_id=1, source_target_pairs={{0,16},{16,0},{1,17},{17,1},{2,18},{18,2},{3,19},{19,3},{4,20},{20... | collective-permute-start | bytes 786440 | tf_op jit(solution)/shard_map/ppermute | solution.py:15
  4.4 2.5 %convolution_convert_fusion = bf16[1024,512]{1,0:T(8,128)(2,1)S(1)} fusion(bf16[1024,1024]{1,0:T(8,128)(2,1)S(1)} %copy-done, bf16[1024,512]{1,0:T(8,128)(2,1)} %param.12), kind=kOutput, calls=%fused_computation.1 | convolution fusion | flops 1074266112 | bytes 4194304 | tf_op jit(solution)/shard_map/dot_general | solution.py:25
  7.4 0.9 %constant_dynamic-slice_fusion = bf16[128,64]{1,0:T(8,128)(2,1)S(1)} fusion(f32[128,512]{1,0:T(8,128)} %param.13, s32[]{:T(128)S(6)} %select_n.38), kind=kLoop, calls=%fused_computation.74 | loop fusion | bytes 32772 | tf_op jit(solution)/shard_map/dynamic_slice | solution.py:73
  8.4 1.2 %convolution_bitcast_fusion = f32[1024,128]{0,1:T(8,128)S(1)} fusion(bf16[128,128]{1,0:T(8,128)(2,1)S(1)} %convolution_convert_fusion.3, bf16[1,1024,128]{2,1,0:T(8,128)(2,1)} %param.7), kind=kOutput, calls=%fused_computation.2 | convolution fusion | flops 33554432 | bytes 819200 | tf_op jit(solution)/shard_map/dot_general | solution.py:25
  10.6 1.0 %collective-permute-done = bf16[1024,128]{1,0:T(8,128)(2,1)} collective-permute-done((bf16[1024,128]{1,0:T(8,128)(2,1)}, bf16[1024,128]{1,0:T(8,128)(2,1)}, u32[]{:S(2)}, u32[]{:S(2)}) %collective-permute-start) | collective-permute-done | bytes 262176 | tf_op jit(solution)/shard_map/ppermute | solution.py:15
  12.2 1.2 %fusion.36 = f32[1024,128]{0,1:T(8,128)S(1)} fusion(bf16[1024,128]{1,0:T(8,128)(2,1)} %collective-permute-done, bf16[128,128]{0,1:T(8,128)(2,1)S(1)} %collective-permute-done.2), kind=kOutput, calls=%fused_computation.77 | convolution fusion | flops 33554432 | bytes 819200 | tf_op jit(solution)/shard_map/dot_general | solution.py:25
  14.7 4.9 %all-to-all-start = ((bf16[8,192,128]{2,1,0:T(8,128)(2,1)}), bf16[8,192,128]{2,1,0:T(8,128)(2,1)}, u32[]{:S(2)}, u32[]{:S(2)}) async-start(bf16[8,192,128]{2,1,0:T(8,128)(2,1)} %pad_maximum_fusion), calls=%async_computation | async-start | bytes 786432 | tf_op jit(solution)/shard_map/all_to_all | solution.py:32
  20.2 1.6 %fusion = bf16[1024,128]{0,1:T(8,128)(2,1)} fusion(bf16[1024,128]{0,1:T(8,128)(2,1)S(1)} %negate_convert_fusion, bf16[1024,1024]{1,0:T(8,128)(2,1)S(1)} %copy-done), kind=kOutput, calls=%fused_computation.4 | convolution fusion | flops 268566528 | bytes 2621440 | tf_op jit(solution)/shard_map/dot_general | solution.py:25
  21.8 5.4 %all-to-all-done = bf16[8,192,128]{2,1,0:T(8,128)(2,1)} async-done(((bf16[8,192,128]{2,1,0:T(8,128)(2,1)}), bf16[8,192,128]{2,1,0:T(8,128)(2,1)}, u32[]{:S(2)}, u32[]{:S(2)}) %all-to-all-start) | async-done | bytes 393248 | tf_op jit(solution)/shard_map/all_to_all | solution.py:32
  27.2 0.8 %slice_bitcast_fusion = bf16[192,128]{1,0:T(8,128)(2,1)S(1)} fusion(bf16[8,192,128]{2,1,0:T(8,128)(2,1)} %all-to-all-done), kind=kLoop, calls=%fused_computation.50 | loop fusion | bytes 98304 | tf_op jit(solution)/shard_map/squeeze | solution.py:81
  28.0 1.6 %bitcast_dynamic-update-slice_fusion.6 = (bf16[8,192,128]{2,1,0:T(8,128)(2,1)}, bf16[192,128]{1,0:T(8,128)(2,1)S(1)}) fusion(bf16[8,192,128]{2,1,0:T(8,128)(2,1)} %bitcast_dynamic-update-slice_fusion.7, bf16[8,192,128]{2,1,0:T(8,128)(2,1)} %all-to-all-done, pred[192]{0:T(512)(128)(4,1)S(1)} %iota_compare_fusion.1, bf16[64,128]{1,0:T(8,128)(2,1)S(1)} %fusion.33, ...), kind=kOutput, calls=%fused_computation.41 | convolution fusion | flops 6488064 | bytes 229568 | tf_op jit(solution)/shard_map/dot_general | solution.py:25
  29.6 1.6 %bitcast_dynamic-update-slice_fusion.5 = (bf16[8,192,128]{2,1,0:T(8,128)(2,1)}, bf16[192,128]{1,0:T(8,128)(2,1)S(1)}) fusion(bf16[8,192,128]{2,1,0:T(8,128)(2,1)} %get-tuple-element.25, bf16[8,192,128]{2,1,0:T(8,128)(2,1)} %all-to-all-done, pred[192]{0:T(512)(128)(4,1)S(1)} %iota_compare_fusion.1, bf16[192,128]{1,0:T(8,128)(2,1)S(1)} %get-tuple-element.26), kind=kOutput, calls=%fused_computation.40 | convolution fusion | flops 6389760 | bytes 229568 | tf_op jit(solution)/shard_map/dot_general | solution.py:25
  31.3 1.6 %bitcast_dynamic-update-slice_fusion.4 = (bf16[8,192,128]{2,1,0:T(8,128)(2,1)}, bf16[192,128]{1,0:T(8,128)(2,1)S(1)}) fusion(bf16[8,192,128]{2,1,0:T(8,128)(2,1)} %get-tuple-element.27, bf16[8,192,128]{2,1,0:T(8,128)(2,1)} %all-to-all-done, pred[192]{0:T(512)(128)(4,1)S(1)} %iota_compare_fusion.1, bf16[192,128]{1,0:T(8,128)(2,1)S(1)} %get-tuple-element.28), kind=kOutput, calls=%fused_computation.39 | convolution fusion | flops 6389760 | bytes 229568 | tf_op jit(solution)/shard_map/dot_general | solution.py:25
  32.9 1.6 %bitcast_dynamic-update-slice_fusion.3 = (bf16[8,192,128]{2,1,0:T(8,128)(2,1)}, bf16[192,128]{1,0:T(8,128)(2,1)S(1)}) fusion(bf16[8,192,128]{2,1,0:T(8,128)(2,1)} %get-tuple-element.29, bf16[8,192,128]{2,1,0:T(8,128)(2,1)} %all-to-all-done, pred[192]{0:T(512)(128)(4,1)S(1)} %iota_compare_fusion.1, bf16[192,128]{1,0:T(8,128)(2,1)S(1)} %get-tuple-element.30), kind=kOutput, calls=%fused_computation.38 | convolution fusion | flops 6389760 | bytes 229568 | tf_op jit(solution)/shard_map/dot_general | solution.py:25
  34.5 1.6 %bitcast_dynamic-update-slice_fusion.2 = (bf16[8,192,128]{2,1,0:T(8,128)(2,1)}, bf16[192,128]{1,0:T(8,128)(2,1)S(1)}) fusion(bf16[8,192,128]{2,1,0:T(8,128)(2,1)} %get-tuple-element.31, bf16[8,192,128]{2,1,0:T(8,128)(2,1)} %all-to-all-done, pred[192]{0:T(512)(128)(4,1)S(1)} %iota_compare_fusion.1, bf16[192,128]{1,0:T(8,128)(2,1)S(1)} %get-tuple-element.32), kind=kOutput, calls=%fused_computation.37 | convolution fusion | flops 6389760 | bytes 229568 | tf_op jit(solution)/shard_map/dot_general | solution.py:25
  36.2 1.6 %bitcast_dynamic-update-slice_fusion.1 = (bf16[8,192,128]{2,1,0:T(8,128)(2,1)}, bf16[192,128]{1,0:T(8,128)(2,1)S(1)}) fusion(bf16[8,192,128]{2,1,0:T(8,128)(2,1)} %get-tuple-element.33, bf16[8,192,128]{2,1,0:T(8,128)(2,1)} %all-to-all-done, pred[192]{0:T(512)(128)(4,1)S(1)} %iota_compare_fusion.1, bf16[192,128]{1,0:T(8,128)(2,1)S(1)} %get-tuple-element.34), kind=kOutput, calls=%fused_computation.36 | convolution fusion | flops 6389760 | bytes 229568 | tf_op jit(solution)/shard_map/dot_general | solution.py:25
  37.8 1.6 %bitcast_dynamic-update-slice_fusion = (bf16[8,192,128]{2,1,0:T(8,128)(2,1)}, bf16[192,128]{1,0:T(8,128)(2,1)S(1)}) fusion(bf16[8,192,128]{2,1,0:T(8,128)(2,1)} %get-tuple-element.35, bf16[8,192,128]{2,1,0:T(8,128)(2,1)} %all-to-all-done, pred[192]{0:T(512)(128)(4,1)S(1)} %iota_compare_fusion.1, bf16[192,128]{1,0:T(8,128)(2,1)S(1)} %get-tuple-element.36), kind=kOutput, calls=%fused_computation.35 | convolution fusion | flops 6389760 | bytes 229568 | tf_op jit(solution)/shard_map/dot_general | solution.py:25
  39.5 0.9 %fusion.16 = f32[192,128]{1,0:T(8,128)S(1)} fusion(bf16[192,128]{1,0:T(8,128)(2,1)S(1)} %get-tuple-element.38, bf16[8,192,128]{2,1,0:T(8,128)(2,1)} %all-to-all-done), kind=kOutput, calls=%fused_computation.53 | convolution fusion | flops 6291456 | bytes 180224 | tf_op jit(solution)/shard_map/dot_general | solution.py:25
  40.4 4.7 %collective-permute-start.3 = (bf16[64,128]{1,0:T(8,128)(2,1)S(1)}, bf16[64,128]{1,0:T(8,128)(2,1)S(1)}, u32[]{:S(2)}, u32[]{:S(2)}) collective-permute-start(bf16[64,128]{1,0:T(8,128)(2,1)S(1)} %fusion.15), channel_id=1, source_target_pairs={{0,8},{1,9},{2,10},{3,11},{4,12},{5,13},{6,14},{7,15},{16,24},{17,... | collective-permute-start | bytes 49160 | tf_op jit(solution)/shard_map/ppermute | solution.py:10
  45.1 1.4 %collective-permute-done.3 = bf16[64,128]{1,0:T(8,128)(2,1)S(1)} collective-permute-done((bf16[64,128]{1,0:T(8,128)(2,1)S(1)}, bf16[64,128]{1,0:T(8,128)(2,1)S(1)}, u32[]{:S(2)}, u32[]{:S(2)}) %collective-permute-start.3) | collective-permute-done | bytes 16416 | tf_op jit(solution)/shard_map/ppermute | solution.py:10
  46.6 1.2 %fusion.1 = bf16[8,64,128]{2,1,0:T(8,128)(2,1)S(1)} fusion(bf16[8,192,128]{2,1,0:T(8,128)(2,1)} %get-tuple-element.37, bf16[64,128]{1,0:T(8,128)(2,1)S(1)} %collective-permute-done.3), kind=kOutput, calls=%fused_computation.6 | convolution fusion | flops 16973824 | bytes 540672 | tf_op jit(solution)/shard_map/dot_general | solution.py:84
  47.7 7.7 %all_to_all.10 = bf16[8,64,128]{2,1,0:T(8,128)(2,1)S(1)} all-to-all(bf16[8,64,128]{2,1,0:T(8,128)(2,1)S(1)} %fusion.1), channel_id=1, replica_groups={{0,1,2,3,4,5,6,7},{8,9,10,11,12,13,14,15},{16,17,18,19,20,21,22,23},{24..., dimensions={0} | all-to-all | bytes 262144 | tf_op jit(solution)/shard_map/all_to_all | solution.py:32
  55.5 1.4 %subtract_convert_fusion = bf16[1024,512]{1,0:T(8,128)(2,1)} fusion(bf16[1024,512]{1,0:T(8,128)(2,1)S(1)} %convolution_convert_fusion, bf16[1024,128]{0,1:T(8,128)(2,1)S(1)} %copy-done.1, bf16[512,128]{1,0:T(8,128)(2,1)S(1)} %bitcast.124), kind=kOutput, calls=%fused_computation | convolution fusion | flops 135790592 | bytes 2490368 | tf_op jit(solution)/shard_map/dot_general | solution.py:92
  (26 shorter events, 4.2 us)
Async XLA Ops:
  0.0 4.4 %copy-start = (bf16[1024,1024]{1,0:T(8,128)(2,1)S(1)}, bf16[1024,1024]{1,0:T(8,128)(2,1)}, u32[]{:S(2)}) copy-start(bf16[1024,1024]{1,0:T(8,128)(2,1)} %param.11) | copy-start | bytes 6291460
  0.0 9.6 %collective-permute-start.1 = (bf16[1024,128]{1,0:T(8,128)(2,1)}, bf16[1024,128]{1,0:T(8,128)(2,1)S(1)}, u32[]{:S(2)}, u32[]{:S(2)}) collective-permute-start(bf16[1024,128]{1,0:T(8,128)(2,1)} %param.10), channel_id=1, source_target_pairs={{1,0},{2,1},{3,2},{4,3},{5,4},{6,5},{7,6},{8,7},{9,8},{10,9},{11,1... | collective-permute-start | bytes 786440 | tf_op jit(solution)/shard_map/ppermute | solution.py:10
  1.4 5.5 %copy-start.2 = (bf16[1024,128]{1,0:T(8,128)(2,1)S(1)}, bf16[1024,128]{1,0:T(8,128)(2,1)}, u32[]{:S(2)}) copy-start(bf16[1024,128]{1,0:T(8,128)(2,1)} %param.9) | copy-start | bytes 786436
  1.4 5.5 %copy-start.3 = (bf16[1,1024,128]{2,1,0:T(8,128)(2,1)S(1)}, bf16[1,1024,128]{2,1,0:T(8,128)(2,1)}, u32[]{:S(2)}) copy-start(bf16[1,1024,128]{2,1,0:T(8,128)(2,1)} %param.8) | copy-start | bytes 786436
  1.4 10.1 %collective-permute-start = (bf16[1024,128]{1,0:T(8,128)(2,1)}, bf16[1024,128]{1,0:T(8,128)(2,1)}, u32[]{:S(2)}, u32[]{:S(2)}) collective-permute-start(bf16[1024,128]{1,0:T(8,128)(2,1)} %bitcast.126), channel_id=1, source_target_pairs={{0,16},{16,0},{1,17},{17,1},{2,18},{18,2},{3,19},{19,3},{4,20},{20... | collective-permute-start | bytes 786440 | tf_op jit(solution)/shard_map/ppermute | solution.py:15
  7.2 4.9 %collective-permute-start.2 = (bf16[128,128]{0,1:T(8,128)(2,1)S(1)}, bf16[128,128]{0,1:T(8,128)(2,1)S(1)}, u32[]{:S(2)}, u32[]{:S(2)}) collective-permute-start(bf16[128,128]{0,1:T(8,128)(2,1)S(1)} %bitcast.127), channel_id=1, source_target_pairs={{0,16},{16,0},{1,17},{17,1},{2,18},{18,2},{3,19},{19,3},{4,20},{20... | collective-permute-start | bytes 98312 | tf_op jit(solution)/shard_map/ppermute | solution.py:15
  14.7 12.4 %all-to-all-start = ((bf16[8,192,128]{2,1,0:T(8,128)(2,1)}), bf16[8,192,128]{2,1,0:T(8,128)(2,1)}, u32[]{:S(2)}, u32[]{:S(2)}) async-start(bf16[8,192,128]{2,1,0:T(8,128)(2,1)} %pad_maximum_fusion), calls=%async_computation | async-start | bytes 786432 | tf_op jit(solution)/shard_map/all_to_all | solution.py:32
  21.8 33.7 %copy-start.1 = (bf16[1024,128]{0,1:T(8,128)(2,1)S(1)}, bf16[1024,128]{0,1:T(8,128)(2,1)}, u32[]{:S(2)}) copy-start(bf16[1024,128]{0,1:T(8,128)(2,1)} %fusion) | copy-start | bytes 786436
  40.4 6.1 %collective-permute-start.3 = (bf16[64,128]{1,0:T(8,128)(2,1)S(1)}, bf16[64,128]{1,0:T(8,128)(2,1)S(1)}, u32[]{:S(2)}, u32[]{:S(2)}) collective-permute-start(bf16[64,128]{1,0:T(8,128)(2,1)S(1)} %fusion.15), channel_id=1, source_target_pairs={{0,8},{1,9},{2,10},{3,11},{4,12},{5,13},{6,14},{7,15},{16,24},{17,... | collective-permute-start | bytes 49160 | tf_op jit(solution)/shard_map/ppermute | solution.py:10

commit v7 on v6

v7 whole, which is shorter than its diff:
```python
import jax
import jax.numpy as jnp
from jax import lax
from jax.experimental import pallas as pl
from jax.experimental.pallas import tpu as pltpu
from jax.sharding import PartitionSpec as P


def shifted(value, axis, steps):
    count = lax.axis_size(axis)
    leading, last = (max(0, -steps), min(count, count - steps))
    return lax.ppermute(value, axis, [(source, source + steps) for source in range(leading, last)])


def rotated(value, axis, steps):
    count = lax.axis_size(axis)
    return lax.ppermute(value, axis, [(source, (source + steps) % count) for source in range(count)])


def project(basis, vectors):
    return lax.dot_general(
        basis, vectors, (((0,), (0,)), ((), ())), preferred_element_type=jnp.float32
    )


def product(a, b):
    return jnp.dot(a, b, preferred_element_type=jnp.float32)


VMEM = pl.BlockSpec(memory_space=pltpu.VMEM)
FLIPPED = (((1,), (1,)), ((), ()))


def split(value):
    high = value.astype(jnp.bfloat16)
    return high, (value - high.astype(jnp.float32)).astype(jnp.bfloat16)


def wide(value, matrix):
    both = product(jnp.concatenate(split(value)), matrix)
    return both[: value.shape[0]] + both[value.shape[0] :]


def make_maps(layers, *refs):
    lefts = jnp.concatenate([ref[...] for ref in refs[:layers]], axis=1)
    cores = jnp.concatenate([ref[...] for ref in refs[layers : 2 * layers]], axis=0)
    weights_ref, shift_ref, sent_ref = refs[2 * layers :]
    map_t = wide(wide(weights_ref[...], lefts), cores).T.astype(jnp.bfloat16)
    rank = map_t.shape[0]
    for target in range(sent_ref.shape[0]):
        sent_ref[target, :rank] = map_t
        sent_ref[target, rank:] = shift_ref[target]


def compose_values(steps_ref, entry_ref, values_ref, last_ref):
    count, _, rank = steps_ref.shape
    state = entry_ref[...]
    for member in range(count):
        values_ref[member] = state
        state = wide(state, steps_ref[member, :rank])
        state = state + steps_ref[member, rank:].astype(jnp.float32)
    last_ref[...] = state.astype(jnp.bfloat16)


def compose_maps(steps_ref, maps_ref):
    count, rank, _ = maps_ref.shape
    state = steps_ref[0, :rank]
    for member in range(1, count):
        maps_ref[member] = state
        if member + 1 < count:
            state = product(state, steps_ref[member, :rank]).astype(jnp.bfloat16)


def enter(entered_ref, maps_ref, values_ref, coupled_ref):
    entered = entered_ref[...]
    coupled_ref[0] = (entered.astype(jnp.float32) + values_ref[0]).astype(jnp.bfloat16)
    for member in range(1, coupled_ref.shape[0]):
        moved = product(entered, maps_ref[member])
        coupled_ref[member] = (moved + values_ref[member]).astype(jnp.bfloat16)


def local(kernel, inputs, *outputs):
    return pl.pallas_call(
        kernel,
        in_specs=[VMEM] * len(inputs),
        out_specs=[VMEM] * len(outputs),
        out_shape=[jax.ShapeDtypeStruct(*output) for output in outputs],
    )(*inputs)


def exchanged(blocks, members):
    return lax.all_to_all(blocks, "row", 0, 0, axis_index_groups=members, tiled=True)


def body(left_factors, right_factors, sketch, row_basis, inverse_diag, right_side, incoming):
    half = jnp.bfloat16
    rank = sketch.shape[1]
    width = right_side.shape[1]
    layers, groups = lax.axis_size("layer"), lax.axis_size("row")
    lowers = groups // 2
    here = lax.axis_index("row")
    upper, lower = lax.div(here, lowers), lax.rem(here, lowers)
    share = width // lowers
    near = [list(range(lowers)), list(range(lowers, groups))]

    lefts = [left_factors[0]] + [rotated(left_factors[0], "layer", k) for k in range(1, layers)]
    next_rows = shifted(row_basis, "row", -1)
    applied = product(inverse_diag, right_side).astype(half)
    sketch, applied = lax.optimization_barrier((sketch, applied))
    core = project(right_factors[0], sketch).astype(half)
    cores = [core] + [rotated(core, "layer", k) for k in range(1, layers)]

    shift_t = project(applied, next_rows).astype(half).reshape(lowers, share, rank)
    weights = project(next_rows, inverse_diag)
    lefts[-1], shift_t, weights = lax.optimization_barrier((lefts[-1], shift_t, weights))
    (sent,) = local(
        lambda *refs: make_maps(layers, *refs),
        (*lefts, *cores, weights, shift_t),
        ((lowers, rank + share, rank), half),
    )
    lefts, incoming, sent = lax.optimization_barrier((lefts, incoming, sent))
    steps = exchanged(sent, near)
    entry = lax.dynamic_slice_in_dim(incoming, lower * share, share, 1).T
    entry = jnp.where(upper == 0, entry, 0.0)
    tile_range = -sum(product(left, core) for left, core in zip(lefts, cores))
    gain = product(inverse_diag, tile_range.astype(half)).astype(half)
    gain, entry, steps = lax.optimization_barrier((gain, entry, steps))

    values, last = local(
        compose_values,
        (steps, entry),
        ((lowers, share, rank), jnp.float32),
        ((share, rank), half),
    )
    entered = shifted(last, "row", lowers)
    steps, _ = lax.optimization_barrier((steps, last))
    (maps,) = local(compose_maps, (steps,), ((lowers, rank, rank), half))
    (coupled,) = local(enter, (entered, maps, values), ((lowers, share, rank), half))
    coupled = exchanged(coupled, near).reshape(width, rank)
    moved = lax.dot_general(gain, coupled, FLIPPED, preferred_element_type=jnp.float32)
    return (applied.astype(jnp.float32) - moved).astype(half)


def solution(mesh):
    return jax.shard_map(
        body,
        mesh=mesh,
        in_specs=(
            P("layer", "row", None),
            P("layer", "row", None),
            P("row", None),
            P("row", None),
            P("row", None),
            P("row", "layer"),
            P(None, "layer"),
        ),
        out_specs=P("row", "layer"),
        check_vma=False,
    )
```

time: 57.9 us -> 53.2 us (0.919)
  matrix products: 23 us -> 12.3 us
  Pallas kernels: 0 us -> 9.52 us
  waiting for transfers between devices: 8.41 us -> 1.47 us
  local copies, waits for them, and re-layouts: 1.86 us -> 3.76 us
  blocking collectives: 7.73 us -> 9.37 us
  starting transfers between devices: 14.1 us -> 14.7 us
    dot_general x12 -> x3, matrix products: 18.7 us -> 7.26 us  [product(): return jnp.dot(a, b, preferred_element_type=jnp.float32)]
    pallas_call x0 -> x4, Pallas kernels: none -> 9.52 us  [local(): pl.pallas_call(kernel, in_specs=[VMEM] * len(inputs), out_specs=[VMEM] *...]
    all_to_all x1, waiting for transfers between devices: 5.38 us -> 0.01 us  [exchanged(): lax.all_to_all(blocks, 'row', 0, 0, axis_index_groups=members, tiled=True)]
    unnamed x9 -> x16, local copies, waits for them, and re-layouts: 0.1 us -> 1.97 us
    optimization_barrier x0 -> x1, local copies, waits for them, and re-layouts: none -> 1.78 us  [body(): lefts, incoming, sent = lax.optimization_barrier((lefts, incoming, sent))]
    all_to_all x1, starting transfers between devices: 4.85 us -> 6.63 us  [exchanged(): lax.all_to_all(blocks, 'row', 0, 0, axis_index_groups=members, tiled=True)]
    dot_general x3 -> x0, matrix products: 1.65 us -> none  [the longest x1 1.19 us: body(): lax.dot_general(jnp.broadcast_to(entered, (lowers, share, rank)), states[...]
    all_to_all x1, blocking collectives: 7.73 us -> 9.37 us  [exchanged(): lax.all_to_all(blocks, 'row', 0, 0, axis_index_groups=members, tiled=True)]
  transfers between devices with their start and end apart: 5 -> 5, of which waited for: 4 -> 1; matrix products, arithmetic and copies ran while one was open for 14% -> 25% of each run, Pallas kernels for 0% -> 5%
where the time goes in v7:
time: 53.2 us; the launch traced here: 52.6 us
  starting transfers between devices  14.7 us (28%)
  matrix products  12.3 us (23%)
  Pallas kernels  9.52 us (18%)
  blocking collectives  9.37 us (18%)
  local copies, waits for them, and re-layouts  3.76 us (7%)
  waiting for transfers between devices  1.47 us (3%)
  other arithmetic  1.37 us (3%)
    pallas_call x4, Pallas kernels, local(): pl.pallas_call(kernel, in_specs=[VMEM] * len(inputs), out_specs=[VMEM] *...  9.52 us
    all_to_all x1, blocking collectives, exchanged(): lax.all_to_all(blocks, 'row', 0, 0, axis_index_groups=members, tiled=True)  9.37 us
    dot_general x3, matrix products, product(): return jnp.dot(a, b, preferred_element_type=jnp.float32)  7.26 us
    all_to_all x1, starting transfers between devices, exchanged(): lax.all_to_all(blocks, 'row', 0, 0, axis_index_groups=members, tiled=True)  6.63 us
    ppermute x2, starting transfers between devices, shifted(): lax.ppermute(value, axis, [(source, source + steps) for source in range(l...  4.77 us
    ppermute x2, starting transfers between devices, rotated(): lax.ppermute(value, axis, [(source, (source + steps) % count) for source...  3.28 us
    dot_general x3, matrix products, project(): lax.dot_general(basis, vectors, (((0,), (0,)), ((), ())), preferred_eleme...  2.69 us
    dot_general x1, matrix products, body(): lax.dot_general(gain, coupled, FLIPPED, preferred_element_type=jnp.float32)  2.38 us
  transfers between devices with their start and end apart: 5, of which 1 were waited for; matrix products, arithmetic and copies ran while one was open for 25% of the time, Pallas kernels for 5%

profile of v7, /device:TPU:0, one launch (start us, length us, event | category | flops | bytes accessed | tf_op | source)
XLA Modules:
  0.0 52.6 jit_solution(9019545338519392331)
XLA Ops:
  0.0 3.0 %collective-permute-start = (bf16[1024,128]{1,0:T(8,128)(2,1)}, bf16[1024,128]{1,0:T(8,128)(2,1)S(1)}, u32[]{:S(2)}, u32[]{:S(2)}) collective-permute-start(bf16[1024,128]{1,0:T(8,128)(2,1)} %bitcast.25), channel_id=1, source_target_pairs={{0,16},{16,0},{1,17},{17,1},{2,18},{18,2},{3,19},{19,3},{4,20},{20... | collective-permute-start | bytes 786440 | tf_op jit(solution)/shard_map/ppermute | solution.py:17
  3.0 1.3 %collective-permute-start.1 = (bf16[1024,128]{1,0:T(8,128)(2,1)}, bf16[1024,128]{1,0:T(8,128)(2,1)S(1)}, u32[]{:S(2)}, u32[]{:S(2)}) collective-permute-start(bf16[1024,128]{1,0:T(8,128)(2,1)} %param.10), channel_id=1, source_target_pairs={{1,0},{2,1},{3,2},{4,3},{5,4},{6,5},{7,6},{8,7},{9,8},{10,9},{11,1... | collective-permute-start | bytes 786440 | tf_op jit(solution)/shard_map/ppermute | solution.py:12
  4.3 2.5 %convolution_convert_fusion = bf16[1024,512]{1,0:T(8,128)(2,1)S(1)} fusion(bf16[1024,1024]{1,0:T(8,128)(2,1)S(1)} %copy-done, bf16[1024,512]{1,0:T(8,128)(2,1)} %param.12), kind=kOutput, calls=%fused_computation.1 | convolution fusion | flops 1074266112 | bytes 4194304 | tf_op jit(solution)/shard_map/dot_general | solution.py:27
  6.8 0.3 convolution_convert_fusion.3
  7.1 0.3 collective-permute-start.2
  7.4 0.0 collective-permute-done.1
  7.4 1.3 %fusion.4.refs_4_ = f32[128,1024]{1,0:T(8,128)} fusion(bf16[1024,128]{1,0:T(8,128)(2,1)S(1)} %collective-permute-done.1, bf16[1024,1024]{1,0:T(8,128)(2,1)S(1)} %copy-done), kind=kOutput, calls=%fused_computation.11 | convolution fusion | flops 268435456 | bytes 2883584 | tf_op jit(solution)/shard_map/dot_general | solution.py:21
  8.6 1.1 %convolution_convert_fusion.2 = bf16[512,128]{1,0:T(8,128)(2,1)} fusion(bf16[1024,512]{1,0:T(8,128)(2,1)S(1)} %convolution_convert_fusion, bf16[1024,128]{1,0:T(8,128)(2,1)S(1)} %collective-permute-done.1), kind=kOutput, calls=%fused_computation.7 | convolution fusion | flops 134283264 | bytes 1441792 | tf_op jit(solution)/shard_map/dot_general | solution.py:21
  9.8 1.5 %collective-permute-done.2.refs_3_ = bf16[128,128]{1,0:T(8,128)(2,1)S(1)} collective-permute-done((bf16[128,128]{1,0:T(8,128)(2,1)S(1)}, bf16[128,128]{1,0:T(8,128)(2,1)S(1)}, u32[]{:S(2)}, u32[]{:S(2)}) %collective-permute-start.2) | collective-permute-done | bytes 32800 | tf_op jit(solution)/shard_map/ppermute | solution.py:17
  11.3 0.6 %copy-done.6 = bf16[128,128]{1,0:T(8,128)(2,1)} copy-done((bf16[128,128]{1,0:T(8,128)(2,1)}, bf16[128,128]{1,0:T(8,128)(2,1)S(1)}, u32[]{:S(2)}) %copy-start.6) | copy-done | bytes 32792
  11.9 2.6 %shard_map.73 = bf16[8,192,128]{2,1,0:T(8,128)(2,1)} custom-call(bf16[1024,128]{1,0:T(8,128)(2,1)} %bitcast.26, bf16[1024,128]{1,0:T(8,128)(2,1)} %copy-done.2, bf16[128,128]{1,0:T(8,128)(2,1)} %bitcast.31, bf16[128,128]{1,0:T(8,128)(2,1)} %copy-done.6, f32[128,1024]{1,0:T(8,128)} %fusion.4.refs_4_, bf16[8,64,128]{2,1,0:T(8,128)(2,1)} %bitcast.29), custom_call_target="tpu_custom_call" | custom-call | tf_op jit(solution)/shard_map/pallas_call | solution.py:83
  14.4 6.6 %all-to-all-start = ((bf16[8,192,128]{2,1,0:T(8,128)(2,1)}), bf16[8,192,128]{2,1,0:T(8,128)(2,1)S(1)}, u32[]{:S(2)}, u32[]{:S(2)}) async-start(bf16[8,192,128]{2,1,0:T(8,128)(2,1)} %shard_map.73), calls=%async_computation | async-start | bytes 786432 | tf_op jit(solution)/shard_map/all_to_all | solution.py:92
  21.1 1.8 %copy.9 = f32[128,512]{0,1:T(8,128)} copy(f32[128,512]{1,0:T(8,128)} %param.13) | data formatting | bytes 524288 | tf_op jit(solution)/shard_map/optimization_barrier | solution.py:121
  22.9 1.4 %select_bitcast_fusion.entry_ref = f32[64,128]{1,0:T(8,128)} fusion(f32[128,512]{0,1:T(8,128)} %copy.9, s32[]{:T(128)S(6)} %select_n.15, pred[]{:T(512)S(6)} %eq.3), kind=kLoop, calls=%fused_computation.10 | loop fusion | flops 8192 | bytes 65541 | tf_op jit(solution)/shard_map/jit(_where)/select_n | solution.py:124
  24.2 1.9 %fusion.5 = f32[1024,128]{1,0:T(8,128)} fusion(bf16[1024,128]{1,0:T(8,128)(2,1)} %copy-done.2, bf16[128,128]{1,0:T(8,128)(2,1)} %copy-done.6), kind=kOutput, calls=%fused_computation.12 | convolution fusion | flops 33554432 | bytes 819200 | tf_op jit(solution)/shard_map/dot_general | solution.py:27
  26.2 2.8 %fusion.2 = bf16[1024,128]{0,1:T(8,128)(2,1)} fusion(bf16[1024,1024]{1,0:T(8,128)(2,1)S(1)} %copy-done, f32[1024,128]{1,0:T(8,128)} %fusion.5, bf16[1024,128]{1,0:T(8,128)(2,1)} %bitcast.27, bf16[128,128]{0,1:T(8,128)(2,1)} %copy-done.3), kind=kOutput, calls=%fused_computation.6 | convolution fusion | flops 302514176 | bytes 3178496 | tf_op jit(solution)/shard_map/dot_general | solution.py:27
  29.0 0.7 %copy-done.1 = bf16[8,192,128]{2,1,0:T(8,128)(2,1)} copy-done((bf16[8,192,128]{2,1,0:T(8,128)(2,1)}, bf16[8,192,128]{2,1,0:T(8,128)(2,1)S(1)}, u32[]{:S(2)}) %copy-start.1) | copy-done | bytes 393240
  29.8 2.6 %shard_map.74 = (f32[8,64,128]{2,1,0:T(8,128)}, bf16[64,128]{1,0:T(8,128)(2,1)}) custom-call(bf16[8,192,128]{2,1,0:T(8,128)(2,1)} %copy-done.1, f32[64,128]{1,0:T(8,128)} %select_bitcast_fusion.entry_ref), custom_call_target="tpu_custom_call" | custom-call | tf_op jit(solution)/shard_map/pallas_call | solution.py:83
  32.4 3.5 %collective-permute-start.3 = (bf16[64,128]{1,0:T(8,128)(2,1)}, bf16[64,128]{1,0:T(8,128)(2,1)S(1)}, u32[]{:S(2)}, u32[]{:S(2)}) collective-permute-start(bf16[64,128]{1,0:T(8,128)(2,1)} %get-tuple-element.32), channel_id=1, source_target_pairs={{0,8},{1,9},{2,10},{3,11},{4,12},{5,13},{6,14},{7,15},{16,24},{17,... | collective-permute-start | bytes 49160 | tf_op jit(solution)/shard_map/ppermute | solution.py:12
  35.9 2.4 %shard_map.75.maps_ref = bf16[8,128,128]{2,1,0:T(8,128)(2,1)} custom-call(bf16[8,192,128]{2,1,0:T(8,128)(2,1)} %copy-done.1), custom_call_target="tpu_custom_call" | custom-call | tf_op jit(solution)/shard_map/pallas_call | solution.py:83
  38.3 0.6 %copy-done.7 = bf16[64,128]{1,0:T(8,128)(2,1)} copy-done((bf16[64,128]{1,0:T(8,128)(2,1)}, bf16[64,128]{1,0:T(8,128)(2,1)S(1)}, u32[]{:S(2)}) %copy-start.7) | copy-done | bytes 16408
  38.9 1.9 %shard_map.76 = bf16[8,64,128]{2,1,0:T(8,128)(2,1)} custom-call(bf16[64,128]{1,0:T(8,128)(2,1)} %copy-done.7, bf16[8,128,128]{2,1,0:T(8,128)(2,1)} %shard_map.75.maps_ref, f32[8,64,128]{2,1,0:T(8,128)} %get-tuple-element.34.values_ref), custom_call_target="tpu_custom_call" | custom-call | tf_op jit(solution)/shard_map/pallas_call | solution.py:83
  40.8 9.4 %all_to_all.10 = bf16[8,64,128]{2,1,0:T(8,128)(2,1)S(1)} all-to-all(bf16[8,64,128]{2,1,0:T(8,128)(2,1)} %shard_map.76), channel_id=1, replica_groups={{0,1,2,3,4,5,6,7},{8,9,10,11,12,13,14,15},{16,17,18,19,20,21,22,23},{24..., dimensions={0} | all-to-all | bytes 262144 | tf_op jit(solution)/shard_map/all_to_all | solution.py:92
  50.2 2.4 %subtract_convert_fusion = bf16[1024,512]{1,0:T(8,128)(2,1)} fusion(bf16[1024,512]{1,0:T(8,128)(2,1)S(1)} %convolution_convert_fusion, bf16[1024,128]{0,1:T(8,128)(2,1)} %fusion.2, bf16[512,128]{1,0:T(8,128)(2,1)S(1)} %bitcast.28), kind=kOutput, calls=%fused_computation | convolution fusion | flops 135790592 | bytes 2490368 | tf_op jit(solution)/shard_map/dot_general | solution.py:140
  (16 shorter events, 0.0 us)
Async XLA Ops:
  0.0 4.3 %copy-start = (bf16[1024,1024]{1,0:T(8,128)(2,1)S(1)}, bf16[1024,1024]{1,0:T(8,128)(2,1)}, u32[]{:S(2)}) copy-start(bf16[1024,1024]{1,0:T(8,128)(2,1)} %param.11) | copy-start | bytes 6291460
  0.0 6.8 %copy-start.4 = (bf16[1024,128]{1,0:T(8,128)(2,1)S(1)}, bf16[1024,128]{1,0:T(8,128)(2,1)}, u32[]{:S(2)}) copy-start(bf16[1024,128]{1,0:T(8,128)(2,1)} %param.9) | copy-start | bytes 786436
  0.0 6.8 %copy-start.5 = (bf16[1,1024,128]{2,1,0:T(8,128)(2,1)S(1)}, bf16[1,1024,128]{2,1,0:T(8,128)(2,1)}, u32[]{:S(2)}) copy-start(bf16[1,1024,128]{2,1,0:T(8,128)(2,1)} %param.8) | copy-start | bytes 786436
  0.0 9.8 %collective-permute-start = (bf16[1024,128]{1,0:T(8,128)(2,1)}, bf16[1024,128]{1,0:T(8,128)(2,1)S(1)}, u32[]{:S(2)}, u32[]{:S(2)}) collective-permute-start(bf16[1024,128]{1,0:T(8,128)(2,1)} %bitcast.25), channel_id=1, source_target_pairs={{0,16},{16,0},{1,17},{17,1},{2,18},{18,2},{3,19},{19,3},{4,20},{20... | collective-permute-start | bytes 786440 | tf_op jit(solution)/shard_map/ppermute | solution.py:17
  3.0 4.4 %collective-permute-start.1 = (bf16[1024,128]{1,0:T(8,128)(2,1)}, bf16[1024,128]{1,0:T(8,128)(2,1)S(1)}, u32[]{:S(2)}, u32[]{:S(2)}) collective-permute-start(bf16[1024,128]{1,0:T(8,128)(2,1)} %param.10), channel_id=1, source_target_pairs={{1,0},{2,1},{3,2},{4,3},{5,4},{6,5},{7,6},{8,7},{9,8},{10,9},{11,1... | collective-permute-start | bytes 786440 | tf_op jit(solution)/shard_map/ppermute | solution.py:12
  7.1 2.7 %copy-start.3 = (bf16[128,128]{0,1:T(8,128)(2,1)}, bf16[128,128]{0,1:T(8,128)(2,1)S(1)}, u32[]{:S(2)}) copy-start(bf16[128,128]{0,1:T(8,128)(2,1)S(1)} %convolution_convert_fusion.3) | copy-start | bytes 98308
  7.1 4.2 %collective-permute-start.2 = (bf16[128,128]{1,0:T(8,128)(2,1)S(1)}, bf16[128,128]{1,0:T(8,128)(2,1)S(1)}, u32[]{:S(2)}, u32[]{:S(2)}) collective-permute-start(bf16[128,128]{1,0:T(8,128)(2,1)S(1)} %bitcast.30), channel_id=1, source_target_pairs={{0,16},{16,0},{1,17},{17,1},{2,18},{18,2},{3,19},{19,3},{4,20},{20... | collective-permute-start | bytes 98312 | tf_op jit(solution)/shard_map/ppermute | solution.py:17
  9.8 1.5 %copy-start.2 = (bf16[1024,128]{1,0:T(8,128)(2,1)}, bf16[1024,128]{1,0:T(8,128)(2,1)S(1)}, u32[]{:S(2)}) copy-start(bf16[1024,128]{1,0:T(8,128)(2,1)S(1)} %collective-permute-done.refs_1_) | copy-start | bytes 786436
  11.3 0.6 %copy-start.6 = (bf16[128,128]{1,0:T(8,128)(2,1)}, bf16[128,128]{1,0:T(8,128)(2,1)S(1)}, u32[]{:S(2)}) copy-start(bf16[128,128]{1,0:T(8,128)(2,1)S(1)} %collective-permute-done.2.refs_3_) | copy-start | bytes 98308
  14.4 14.6 %all-to-all-start = ((bf16[8,192,128]{2,1,0:T(8,128)(2,1)}), bf16[8,192,128]{2,1,0:T(8,128)(2,1)S(1)}, u32[]{:S(2)}, u32[]{:S(2)}) async-start(bf16[8,192,128]{2,1,0:T(8,128)(2,1)} %shard_map.73), calls=%async_computation | async-start | bytes 786432 | tf_op jit(solution)/shard_map/all_to_all | solution.py:92
  29.0 0.7 %copy-start.1 = (bf16[8,192,128]{2,1,0:T(8,128)(2,1)}, bf16[8,192,128]{2,1,0:T(8,128)(2,1)S(1)}, u32[]{:S(2)}) copy-start(bf16[8,192,128]{2,1,0:T(8,128)(2,1)S(1)} %all-to-all-done.steps_ref) | copy-start | bytes 1179652
  32.4 5.9 %collective-permute-start.3 = (bf16[64,128]{1,0:T(8,128)(2,1)}, bf16[64,128]{1,0:T(8,128)(2,1)S(1)}, u32[]{:S(2)}, u32[]{:S(2)}) collective-permute-start(bf16[64,128]{1,0:T(8,128)(2,1)} %get-tuple-element.32), channel_id=1, source_target_pairs={{0,8},{1,9},{2,10},{3,11},{4,12},{5,13},{6,14},{7,15},{16,24},{17,... | collective-permute-start | bytes 49160 | tf_op jit(solution)/shard_map/ppermute | solution.py:12
  38.3 0.6 %copy-start.7 = (bf16[64,128]{1,0:T(8,128)(2,1)}, bf16[64,128]{1,0:T(8,128)(2,1)S(1)}, u32[]{:S(2)}) copy-start(bf16[64,128]{1,0:T(8,128)(2,1)S(1)} %collective-permute-done.3.entered_ref) | copy-start | bytes 49156

commit v8 on v7

--- a/solution.py
+++ b/solution.py
@@ -54,7 +54,7 @@
 
 def compose_values(steps_ref, entry_ref, values_ref, last_ref):
     count, _, rank = steps_ref.shape
-    state = entry_ref[...]
+    state = entry_ref[...].T
     for member in range(count):
         values_ref[member] = state
         state = wide(state, steps_ref[member, :rank])
@@ -85,6 +85,7 @@
         in_specs=[VMEM] * len(inputs),
         out_specs=[VMEM] * len(outputs),
         out_shape=[jax.ShapeDtypeStruct(*output) for output in outputs],
+        compiler_params=pltpu.CompilerParams(vmem_limit_bytes=16 * 2**20),
     )(*inputs)
 
 
@@ -120,7 +121,7 @@
     )
     lefts, incoming, sent = lax.optimization_barrier((lefts, incoming, sent))
     steps = exchanged(sent, near)
-    entry = lax.dynamic_slice_in_dim(incoming, lower * share, share, 1).T
+    entry = lax.dynamic_slice_in_dim(incoming, lower * share, share, 1)
     entry = jnp.where(upper == 0, entry, 0.0)
     tile_range = -sum(product(left, core) for left, core in zip(lefts, cores))
     gain = product(inverse_diag, tile_range.astype(half)).astype(half)

time: 53.2 us -> 41.2 us (0.77)
  Pallas kernels: 9.52 us -> 3.31 us
  waiting for transfers between devices: 1.47 us -> 7.09 us
  matrix products: 12.3 us -> 8.18 us
  local copies, waits for them, and re-layouts: 3.76 us -> 0.03 us
  blocking collectives: 9.37 us -> 7.73 us
  starting transfers between devices: 14.7 us -> 13.4 us
    pallas_call x4, Pallas kernels: 9.52 us -> 3.31 us  [local(): pl.pallas_call(kernel, in_specs=[VMEM] * len(inputs), out_specs=[VMEM] *...]
    all_to_all x1, waiting for transfers between devices: 0.01 us -> 3.5 us  [exchanged(): lax.all_to_all(blocks, 'row', 0, 0, axis_index_groups=members, tiled=True)]
    all_to_all x1, starting transfers between devices: 6.63 us -> 4.5 us  [exchanged(): lax.all_to_all(blocks, 'row', 0, 0, axis_index_groups=members, tiled=True)]
    unnamed x16 -> x12, local copies, waits for them, and re-layouts: 1.97 us -> 0.03 us
    optimization_barrier x1 -> x0, local copies, waits for them, and re-layouts: 1.78 us -> none  [body(): lefts, incoming, sent = lax.optimization_barrier((lefts, incoming, sent))]
    dot_general x3, matrix products: 7.26 us -> 5.52 us  [product(): return jnp.dot(a, b, preferred_element_type=jnp.float32)]
    all_to_all x1, blocking collectives: 9.37 us -> 7.73 us  [exchanged(): lax.all_to_all(blocks, 'row', 0, 0, axis_index_groups=members, tiled=True)]
    dot_general x3, matrix products: 2.69 us -> 1.22 us  [project(): lax.dot_general(basis, vectors, (((0,), (0,)), ((), ())), preferred_eleme...]
  transfers between devices with their start and end apart: 5 -> 5, of which waited for: 1 -> 4; matrix products, arithmetic and copies ran while one was open for 25% -> 19% of each run, Pallas kernels for 5% -> 2%
where the time goes in v8:
time: 41.2 us; the launch traced here: 40.8 us
  starting transfers between devices  13.4 us (33%)
  matrix products  8.18 us (20%)
  blocking collectives  7.73 us (19%)
  waiting for transfers between devices  7.09 us (17%)
  Pallas kernels  3.31 us (8%)
  other arithmetic  0.92 us (2%)
    all_to_all x1, blocking collectives, exchanged(): lax.all_to_all(blocks, 'row', 0, 0, axis_index_groups=members, tiled=True)  7.73 us
    ppermute x2, starting transfers between devices, shifted(): lax.ppermute(value, axis, [(source, source + steps) for source in range(l...  5.65 us
    dot_general x3, matrix products, product(): return jnp.dot(a, b, preferred_element_type=jnp.float32)  5.52 us
    all_to_all x1, starting transfers between devices, exchanged(): lax.all_to_all(blocks, 'row', 0, 0, axis_index_groups=members, tiled=True)  4.5 us
    all_to_all x1, waiting for transfers between devices, exchanged(): lax.all_to_all(blocks, 'row', 0, 0, axis_index_groups=members, tiled=True)  3.5 us
    pallas_call x4, Pallas kernels, local(): pl.pallas_call(kernel, in_specs=[VMEM] * len(inputs), out_specs=[VMEM] *...  3.31 us
    ppermute x2, starting transfers between devices, rotated(): lax.ppermute(value, axis, [(source, (source + steps) % count) for source...  3.29 us
    ppermute x2, waiting for transfers between devices, rotated(): lax.ppermute(value, axis, [(source, (source + steps) % count) for source...  2.9 us
  transfers between devices with their start and end apart: 5, of which 4 were waited for; matrix products, arithmetic and copies ran while one was open for 19% of the time, Pallas kernels for 2%

profile of v8, /device:TPU:0, one launch (start us, length us, event | category | flops | bytes accessed | tf_op | source)
XLA Modules:
  0.0 40.8 jit_solution(5556688418472453690)
XLA Ops:
  0.0 3.0 %collective-permute-start = (bf16[1024,128]{1,0:T(8,128)(2,1)}, bf16[1024,128]{1,0:T(8,128)(2,1)S(1)}, u32[]{:S(2)}, u32[]{:S(2)}) collective-permute-start(bf16[1024,128]{1,0:T(8,128)(2,1)} %bitcast.23), channel_id=1, source_target_pairs={{0,16},{16,0},{1,17},{17,1},{2,18},{18,2},{3,19},{19,3},{4,20},{20... | collective-permute-start | bytes 786440 | tf_op jit(solution)/shard_map/ppermute | solution.py:17
  3.0 1.3 %collective-permute-start.1 = (bf16[1024,128]{1,0:T(8,128)(2,1)}, bf16[1024,128]{1,0:T(8,128)(2,1)S(1)}, u32[]{:S(2)}, u32[]{:S(2)}) collective-permute-start(bf16[1024,128]{1,0:T(8,128)(2,1)} %param.10), channel_id=1, source_target_pairs={{1,0},{2,1},{3,2},{4,3},{5,4},{6,5},{7,6},{8,7},{9,8},{10,9},{11,1... | collective-permute-start | bytes 786440 | tf_op jit(solution)/shard_map/ppermute | solution.py:12
  4.3 2.5 %convolution_convert_fusion = bf16[1024,512]{1,0:T(8,128)(2,1)S(1)} fusion(bf16[1024,1024]{1,0:T(8,128)(2,1)S(1)} %copy-done, bf16[1024,512]{1,0:T(8,128)(2,1)} %param.12), kind=kOutput, calls=%fused_computation.1 | convolution fusion | flops 1074266112 | bytes 4194304 | tf_op jit(solution)/shard_map/dot_general | solution.py:27
  6.8 0.0 copy-start.2
  6.8 0.3 convolution_convert_fusion.3
  7.1 0.0 copy-start.1
  7.1 0.3 collective-permute-start.2
  7.4 0.5 %fusion.4.refs_4_ = f32[128,1024]{1,0:T(8,128)S(1)} fusion(bf16[1024,128]{1,0:T(8,128)(2,1)S(1)} %collective-permute-done.1, bf16[1024,1024]{1,0:T(8,128)(2,1)S(1)} %copy-done), kind=kOutput, calls=%fused_computation.11 | convolution fusion | flops 268435456 | bytes 2883584 | tf_op jit(solution)/shard_map/dot_general | solution.py:21
  7.9 0.5 %convolution_convert_fusion.2 = bf16[512,128]{1,0:T(8,128)(2,1)S(1)} fusion(bf16[1024,512]{1,0:T(8,128)(2,1)S(1)} %convolution_convert_fusion, bf16[1024,128]{1,0:T(8,128)(2,1)S(1)} %collective-permute-done.1), kind=kOutput, calls=%fused_computation.7 | convolution fusion | flops 134283264 | bytes 1441792 | tf_op jit(solution)/shard_map/dot_general | solution.py:21
  8.4 1.2 %collective-permute-done.refs_1_ = bf16[1024,128]{1,0:T(8,128)(2,1)S(1)} collective-permute-done((bf16[1024,128]{1,0:T(8,128)(2,1)}, bf16[1024,128]{1,0:T(8,128)(2,1)S(1)}, u32[]{:S(2)}, u32[]{:S(2)}) %collective-permute-start) | collective-permute-done | bytes 262176 | tf_op jit(solution)/shard_map/ppermute | solution.py:17
  9.5 1.7 %collective-permute-done.2.refs_3_ = bf16[128,128]{1,0:T(8,128)(2,1)S(1)} collective-permute-done((bf16[128,128]{1,0:T(8,128)(2,1)S(1)}, bf16[128,128]{1,0:T(8,128)(2,1)S(1)}, u32[]{:S(2)}, u32[]{:S(2)}) %collective-permute-start.2) | collective-permute-done | bytes 32800 | tf_op jit(solution)/shard_map/ppermute | solution.py:17
  11.3 1.3 %shard_map.73 = bf16[8,192,128]{2,1,0:T(8,128)(2,1)} custom-call(bf16[1024,128]{1,0:T(8,128)(2,1)S(1)} %bitcast.24, bf16[1024,128]{1,0:T(8,128)(2,1)S(1)} %collective-permute-done.refs_1_, bf16[128,128]{1,0:T(8,128)(2,1)S(1)} %bitcast.28, bf16[128,128]{1,0:T(8,128)(2,1)S(1)} %collective-permute-done.2.refs_3_, f32[128,1024]{1,0:T(8,128)S(1)} %fusion.4.refs_4_, ...), custom_call_target="tpu_custom_call" | custom-call | tf_op jit(solution)/shard_map/pallas_call | solution.py:83
  12.6 4.5 %all-to-all-start = ((bf16[8,192,128]{2,1,0:T(8,128)(2,1)}), bf16[8,192,128]{2,1,0:T(8,128)(2,1)S(1)}, u32[]{:S(2)}, u32[]{:S(2)}) async-start(bf16[8,192,128]{2,1,0:T(8,128)(2,1)} %shard_map.73), calls=%async_computation | async-start | bytes 786432 | tf_op jit(solution)/shard_map/all_to_all | solution.py:93
  17.1 0.9 %dynamic-slice_select_fusion.entry_ref = f32[128,64]{1,0:T(8,128)S(1)} fusion(f32[128,512]{1,0:T(8,128)} %param.13, s32[]{:T(128)S(6)} %select_n.12, pred[]{:T(512)S(6)} %eq.3), kind=kLoop, calls=%fused_computation.10 | loop fusion | flops 8192 | bytes 65541 | tf_op jit(solution)/shard_map/jit(_where)/select_n | solution.py:125
  18.0 1.0 %fusion.5 = f32[1024,128]{1,0:T(8,128)} fusion(bf16[1024,128]{1,0:T(8,128)(2,1)S(1)} %collective-permute-done.refs_1_, bf16[128,128]{1,0:T(8,128)(2,1)S(1)} %collective-permute-done.2.refs_3_), kind=kOutput, calls=%fused_computation.12 | convolution fusion | flops 33554432 | bytes 819200 | tf_op jit(solution)/shard_map/dot_general | solution.py:27
  19.0 2.0 %fusion.2 = bf16[1024,128]{0,1:T(8,128)(2,1)S(1)} fusion(bf16[1024,1024]{1,0:T(8,128)(2,1)S(1)} %copy-done, f32[1024,128]{1,0:T(8,128)} %fusion.5, bf16[1024,128]{1,0:T(8,128)(2,1)S(1)} %bitcast.25, bf16[128,128]{0,1:T(8,128)(2,1)S(1)} %convolution_convert_fusion.3), kind=kOutput, calls=%fused_computation.6 | convolution fusion | flops 302514176 | bytes 3178496 | tf_op jit(solution)/shard_map/dot_general | solution.py:27
  21.1 3.5 %all-to-all-done.steps_ref = bf16[8,192,128]{2,1,0:T(8,128)(2,1)S(1)} async-done(((bf16[8,192,128]{2,1,0:T(8,128)(2,1)}), bf16[8,192,128]{2,1,0:T(8,128)(2,1)S(1)}, u32[]{:S(2)}, u32[]{:S(2)}) %all-to-all-start) | async-done | bytes 393248 | tf_op jit(solution)/shard_map/all_to_all | solution.py:93
  24.6 1.1 %shard_map.74 = (f32[8,64,128]{2,1,0:T(8,128)S(1)}, bf16[64,128]{1,0:T(8,128)(2,1)S(1)}) custom-call(bf16[8,192,128]{2,1,0:T(8,128)(2,1)S(1)} %all-to-all-done.steps_ref, f32[128,64]{1,0:T(8,128)S(1)} %dynamic-slice_select_fusion.entry_ref), custom_call_target="tpu_custom_call" | custom-call | tf_op jit(solution)/shard_map/pallas_call | solution.py:83
  25.7 4.4 %collective-permute-start.3 = (bf16[64,128]{1,0:T(8,128)(2,1)S(1)}, bf16[64,128]{1,0:T(8,128)(2,1)S(1)}, u32[]{:S(2)}, u32[]{:S(2)}) collective-permute-start(bf16[64,128]{1,0:T(8,128)(2,1)S(1)} %get-tuple-element.32), channel_id=1, source_target_pairs={{0,8},{1,9},{2,10},{3,11},{4,12},{5,13},{6,14},{7,15},{16,24},{17,... | collective-permute-start | bytes 49160 | tf_op jit(solution)/shard_map/ppermute | solution.py:12
  30.0 0.7 %shard_map.75.maps_ref = bf16[8,128,128]{2,1,0:T(8,128)(2,1)S(1)} custom-call(bf16[8,192,128]{2,1,0:T(8,128)(2,1)S(1)} %all-to-all-done.steps_ref), custom_call_target="tpu_custom_call" | custom-call | tf_op jit(solution)/shard_map/pallas_call | solution.py:83
  30.8 0.7 %collective-permute-done.3.entered_ref = bf16[64,128]{1,0:T(8,128)(2,1)S(1)} collective-permute-done((bf16[64,128]{1,0:T(8,128)(2,1)S(1)}, bf16[64,128]{1,0:T(8,128)(2,1)S(1)}, u32[]{:S(2)}, u32[]{:S(2)}) %collective-permute-start.3) | collective-permute-done | bytes 16416 | tf_op jit(solution)/shard_map/ppermute | solution.py:12
  31.5 0.2 shard_map.76
  31.7 7.7 %all_to_all.10 = bf16[8,64,128]{2,1,0:T(8,128)(2,1)S(1)} all-to-all(bf16[8,64,128]{2,1,0:T(8,128)(2,1)S(1)} %shard_map.76), channel_id=1, replica_groups={{0,1,2,3,4,5,6,7},{8,9,10,11,12,13,14,15},{16,17,18,19,20,21,22,23},{24..., dimensions={0} | all-to-all | bytes 262144 | tf_op jit(solution)/shard_map/all_to_all | solution.py:93
  39.4 1.4 %subtract_convert_fusion = bf16[1024,512]{1,0:T(8,128)(2,1)} fusion(bf16[1024,512]{1,0:T(8,128)(2,1)S(1)} %copy-done.3, bf16[1024,128]{0,1:T(8,128)(2,1)S(1)} %fusion.2, bf16[512,128]{1,0:T(8,128)(2,1)S(1)} %bitcast.29), kind=kOutput, calls=%fused_computation | convolution fusion | flops 135790592 | bytes 2490368 | tf_op jit(solution)/shard_map/dot_general | solution.py:141
  (11 shorter events, 0.0 us)
Async XLA Ops:
  0.0 4.3 %copy-start = (bf16[1024,1024]{1,0:T(8,128)(2,1)S(1)}, bf16[1024,1024]{1,0:T(8,128)(2,1)}, u32[]{:S(2)}) copy-start(bf16[1024,1024]{1,0:T(8,128)(2,1)} %param.11) | copy-start | bytes 6291460
  0.0 6.8 %copy-start.4 = (bf16[1024,128]{1,0:T(8,128)(2,1)S(1)}, bf16[1024,128]{1,0:T(8,128)(2,1)}, u32[]{:S(2)}) copy-start(bf16[1024,128]{1,0:T(8,128)(2,1)} %param.9) | copy-start | bytes 786436
  0.0 6.8 %copy-start.5 = (bf16[1,1024,128]{2,1,0:T(8,128)(2,1)S(1)}, bf16[1,1024,128]{2,1,0:T(8,128)(2,1)}, u32[]{:S(2)}) copy-start(bf16[1,1024,128]{2,1,0:T(8,128)(2,1)} %param.8) | copy-start | bytes 786436
  0.0 9.5 %collective-permute-start = (bf16[1024,128]{1,0:T(8,128)(2,1)}, bf16[1024,128]{1,0:T(8,128)(2,1)S(1)}, u32[]{:S(2)}, u32[]{:S(2)}) collective-permute-start(bf16[1024,128]{1,0:T(8,128)(2,1)} %bitcast.23), channel_id=1, source_target_pairs={{0,16},{16,0},{1,17},{17,1},{2,18},{18,2},{3,19},{19,3},{4,20},{20... | collective-permute-start | bytes 786440 | tf_op jit(solution)/shard_map/ppermute | solution.py:17
  3.0 4.4 %collective-permute-start.1 = (bf16[1024,128]{1,0:T(8,128)(2,1)}, bf16[1024,128]{1,0:T(8,128)(2,1)S(1)}, u32[]{:S(2)}, u32[]{:S(2)}) collective-permute-start(bf16[1024,128]{1,0:T(8,128)(2,1)} %param.10), channel_id=1, source_target_pairs={{1,0},{2,1},{3,2},{4,3},{5,4},{6,5},{7,6},{8,7},{9,8},{10,9},{11,1... | collective-permute-start | bytes 786440 | tf_op jit(solution)/shard_map/ppermute | solution.py:12
  6.8 1.6 %copy-start.2 = (bf16[1024,512]{1,0:T(8,128)(2,1)}, bf16[1024,512]{1,0:T(8,128)(2,1)S(1)}, u32[]{:S(2)}) copy-start(bf16[1024,512]{1,0:T(8,128)(2,1)S(1)} %convolution_convert_fusion) | copy-start | bytes 3145732
  7.1 4.2 %copy-start.1 = (bf16[1,1024,128]{2,1,0:T(8,128)(2,1)S(1)}, bf16[1,1024,128]{2,1,0:T(8,128)(2,1)}, u32[]{:S(2)}) copy-start(bf16[1,1024,128]{2,1,0:T(8,128)(2,1)} %param.7) | copy-start | bytes 786436
  7.1 4.2 %collective-permute-start.2 = (bf16[128,128]{1,0:T(8,128)(2,1)S(1)}, bf16[128,128]{1,0:T(8,128)(2,1)S(1)}, u32[]{:S(2)}, u32[]{:S(2)}) collective-permute-start(bf16[128,128]{1,0:T(8,128)(2,1)S(1)} %bitcast.27), channel_id=1, source_target_pairs={{0,16},{16,0},{1,17},{17,1},{2,18},{18,2},{3,19},{19,3},{4,20},{20... | collective-permute-start | bytes 98312 | tf_op jit(solution)/shard_map/ppermute | solution.py:17
  12.6 12.0 %all-to-all-start = ((bf16[8,192,128]{2,1,0:T(8,128)(2,1)}), bf16[8,192,128]{2,1,0:T(8,128)(2,1)S(1)}, u32[]{:S(2)}, u32[]{:S(2)}) async-start(bf16[8,192,128]{2,1,0:T(8,128)(2,1)} %shard_map.73), calls=%async_computation | async-start | bytes 786432 | tf_op jit(solution)/shard_map/all_to_all | solution.py:93
  24.6 14.8 %copy-start.3 = (bf16[1024,512]{1,0:T(8,128)(2,1)S(1)}, bf16[1024,512]{1,0:T(8,128)(2,1)}, u32[]{:S(2)}) copy-start(bf16[1024,512]{1,0:T(8,128)(2,1)} %copy-done.2) | copy-start | bytes 3145732
  25.7 5.8 %collective-permute-start.3 = (bf16[64,128]{1,0:T(8,128)(2,1)S(1)}, bf16[64,128]{1,0:T(8,128)(2,1)S(1)}, u32[]{:S(2)}, u32[]{:S(2)}) collective-permute-start(bf16[64,128]{1,0:T(8,128)(2,1)S(1)} %get-tuple-element.32), channel_id=1, source_target_pairs={{0,8},{1,9},{2,10},{3,11},{4,12},{5,13},{6,14},{7,15},{16,24},{17,... | collective-permute-start | bytes 49160 | tf_op jit(solution)/shard_map/ppermute | solution.py:12

commit v9 on v8

--- a/solution.py
+++ b/solution.py
@@ -27,6 +27,7 @@
     return jnp.dot(a, b, preferred_element_type=jnp.float32)
 
 
+SMEM = pl.BlockSpec(memory_space=pltpu.SMEM)
 VMEM = pl.BlockSpec(memory_space=pltpu.VMEM)
 FLIPPED = (((1,), (1,)), ((), ()))
 
@@ -52,23 +53,36 @@
         sent_ref[target, rank:] = shift_ref[target]
 
 
-def compose_values(steps_ref, entry_ref, values_ref, last_ref):
+def chain(steps_ref, state, values_ref):
     count, _, rank = steps_ref.shape
-    state = entry_ref[...].T
     for member in range(count):
         values_ref[member] = state
         state = wide(state, steps_ref[member, :rank])
         state = state + steps_ref[member, rank:].astype(jnp.float32)
-    last_ref[...] = state.astype(jnp.bfloat16)
+    return state
 
 
-def compose_maps(steps_ref, maps_ref):
+def first_half(upper_ref, steps_ref, entry_ref, values_ref, last_ref):
+    @pl.when(upper_ref[0] == 0)
+    def _():
+        last_ref[...] = chain(steps_ref, entry_ref[...].T, values_ref).astype(jnp.bfloat16)
+
+
+def second_half(upper_ref, steps_ref, before_ref, values_ref, maps_ref):
     count, rank, _ = maps_ref.shape
-    state = steps_ref[0, :rank]
-    for member in range(1, count):
-        maps_ref[member] = state
-        if member + 1 < count:
-            state = product(state, steps_ref[member, :rank]).astype(jnp.bfloat16)
+
+    @pl.when(upper_ref[0] == 0)
+    def _():
+        maps_ref[...] = jnp.zeros(maps_ref.shape, jnp.bfloat16)
+
+    @pl.when(upper_ref[0] > 0)
+    def _():
+        chain(steps_ref, jnp.zeros(values_ref.shape[1:], jnp.float32), values_ref)
+        state = steps_ref[0, :rank]
+        for member in range(1, count):
+            maps_ref[member] = state
+            if member + 1 < count:
+                state = product(state, steps_ref[member, :rank]).astype(jnp.bfloat16)
 
 
 def enter(entered_ref, maps_ref, values_ref, coupled_ref):
@@ -79,12 +93,14 @@
         coupled_ref[member] = (moved + values_ref[member]).astype(jnp.bfloat16)
 
 
-def local(kernel, inputs, *outputs):
+def local(kernel, inputs, *outputs, scalar=False, aliases={}):
+    specs = [SMEM] * scalar + [VMEM] * (len(inputs) - scalar)
     return pl.pallas_call(
         kernel,
-        in_specs=[VMEM] * len(inputs),
+        in_specs=specs,
         out_specs=[VMEM] * len(outputs),
         out_shape=[jax.ShapeDtypeStruct(*output) for output in outputs],
+        input_output_aliases=aliases,
         compiler_params=pltpu.CompilerParams(vmem_limit_bytes=16 * 2**20),
     )(*inputs)
 
@@ -122,20 +138,28 @@
     lefts, incoming, sent = lax.optimization_barrier((lefts, incoming, sent))
     steps = exchanged(sent, near)
     entry = lax.dynamic_slice_in_dim(incoming, lower * share, share, 1)
-    entry = jnp.where(upper == 0, entry, 0.0)
     tile_range = -sum(product(left, core) for left, core in zip(lefts, cores))
     gain = product(inverse_diag, tile_range.astype(half)).astype(half)
     gain, entry, steps = lax.optimization_barrier((gain, entry, steps))
 
+    place = upper.reshape(1)
     values, last = local(
-        compose_values,
-        (steps, entry),
+        first_half,
+        (place, steps, entry),
         ((lowers, share, rank), jnp.float32),
         ((share, rank), half),
+        scalar=True,
     )
     entered = shifted(last, "row", lowers)
     steps, _ = lax.optimization_barrier((steps, last))
-    (maps,) = local(compose_maps, (steps,), ((lowers, rank, rank), half))
+    values, maps = local(
+        second_half,
+        (place, steps, values),
+        ((lowers, share, rank), jnp.float32),
+        ((lowers, rank, rank), half),
+        scalar=True,
+        aliases={2: 0},
+    )
     (coupled,) = local(enter, (entered, maps, values), ((lowers, share, rank), half))
     coupled = exchanged(coupled, near).reshape(width, rank)
     moved = lax.dot_general(gain, coupled, FLIPPED, preferred_element_type=jnp.float32)

time: 41.2 us -> 40.3 us (0.978)
  other arithmetic: 0.92 us -> 0 us
  local copies, waits for them, and re-layouts: 0.03 us -> 0.94 us
  starting transfers between devices: 13.4 us -> 12.5 us
  waiting for transfers between devices: 7.09 us -> 7.78 us
  Pallas kernels: 3.31 us -> 2.64 us
    ppermute x2, starting transfers between devices: 5.65 us -> 4.69 us  [shifted(): lax.ppermute(value, axis, [(source, source + steps) for source in range(l...]
    select_n x1 -> x0, other arithmetic: 0.92 us -> none  [body(): entry = jnp.where(upper == 0, entry, 0.0)]
    dynamic_slice x0 -> x1, local copies, waits for them, and re-layouts: none -> 0.91 us  [body(): entry = lax.dynamic_slice_in_dim(incoming, lower * share, share, 1)]
    pallas_call x4, Pallas kernels: 3.31 us -> 2.64 us  [local(): pl.pallas_call(kernel, in_specs=specs, out_specs=[VMEM] * len(outputs), o...]
    ppermute x2, waiting for transfers between devices: 0.7 us -> 1.37 us  [shifted(): lax.ppermute(value, axis, [(source, source + steps) for source in range(l...]
  transfers between devices with their start and end apart: 5 -> 5, of which waited for: 4 -> 4; matrix products, arithmetic and copies ran while one was open for 19% -> 19% of each run, Pallas kernels for 2% -> 0%
where the time goes in v9:
time: 40.3 us; the launch traced here: 39.9 us
  starting transfers between devices  12.5 us (31%)
  matrix products  8.18 us (20%)
  waiting for transfers between devices  7.78 us (19%)
  blocking collectives  7.73 us (19%)
  Pallas kernels  2.64 us (7%)
  local copies, waits for them, and re-layouts  0.94 us (2%)
    all_to_all x1, blocking collectives, exchanged(): lax.all_to_all(blocks, 'row', 0, 0, axis_index_groups=members, tiled=True)  7.73 us
    dot_general x3, matrix products, product(): return jnp.dot(a, b, preferred_element_type=jnp.float32)  5.52 us
    ppermute x2, starting transfers between devices, shifted(): lax.ppermute(value, axis, [(source, source + steps) for source in range(l...  4.69 us
    all_to_all x1, starting transfers between devices, exchanged(): lax.all_to_all(blocks, 'row', 0, 0, axis_index_groups=members, tiled=True)  4.5 us
    all_to_all x1, waiting for transfers between devices, exchanged(): lax.all_to_all(blocks, 'row', 0, 0, axis_index_groups=members, tiled=True)  3.5 us
    ppermute x2, starting transfers between devices, rotated(): lax.ppermute(value, axis, [(source, (source + steps) % count) for source...  3.29 us
    ppermute x2, waiting for transfers between devices, rotated(): lax.ppermute(value, axis, [(source, (source + steps) % count) for source...  2.9 us
    pallas_call x4, Pallas kernels, local(): pl.pallas_call(kernel, in_specs=specs, out_specs=[VMEM] * len(outputs), o...  2.64 us
  transfers between devices with their start and end apart: 5, of which 4 were waited for; matrix products, arithmetic and copies ran while one was open for 19% of the time, Pallas kernels for 0%

profile of v9, /device:TPU:0, one launch (start us, length us, event | category | flops | bytes accessed | tf_op | source)
XLA Modules:
  0.0 39.9 jit_solution(3538783868491481846)
XLA Ops:
  0.0 3.0 %collective-permute-start = (bf16[1024,128]{1,0:T(8,128)(2,1)}, bf16[1024,128]{1,0:T(8,128)(2,1)S(1)}, u32[]{:S(2)}, u32[]{:S(2)}) collective-permute-start(bf16[1024,128]{1,0:T(8,128)(2,1)} %bitcast.24), channel_id=1, source_target_pairs={{0,16},{16,0},{1,17},{17,1},{2,18},{18,2},{3,19},{19,3},{4,20},{20... | collective-permute-start | bytes 786440 | tf_op jit(solution)/shard_map/ppermute | solution.py:17
  3.0 1.3 %collective-permute-start.1 = (bf16[1024,128]{1,0:T(8,128)(2,1)}, bf16[1024,128]{1,0:T(8,128)(2,1)S(1)}, u32[]{:S(2)}, u32[]{:S(2)}) collective-permute-start(bf16[1024,128]{1,0:T(8,128)(2,1)} %param.10), channel_id=1, source_target_pairs={{1,0},{2,1},{3,2},{4,3},{5,4},{6,5},{7,6},{8,7},{9,8},{10,9},{11,1... | collective-permute-start | bytes 786440 | tf_op jit(solution)/shard_map/ppermute | solution.py:12
  4.3 2.5 %convolution_convert_fusion = bf16[1024,512]{1,0:T(8,128)(2,1)S(1)} fusion(bf16[1024,1024]{1,0:T(8,128)(2,1)S(1)} %copy-done, bf16[1024,512]{1,0:T(8,128)(2,1)} %param.12), kind=kOutput, calls=%fused_computation.1 | convolution fusion | flops 1074266112 | bytes 4194304 | tf_op jit(solution)/shard_map/dot_general | solution.py:27
  6.8 0.0 copy-start.2
  6.8 0.3 convolution_convert_fusion.3
  7.1 0.0 copy-start.1
  7.1 0.3 collective-permute-start.2
  7.4 0.0 collective-permute-done.1
  7.4 0.5 %fusion.4.refs_4_ = f32[128,1024]{1,0:T(8,128)S(1)} fusion(bf16[1024,128]{1,0:T(8,128)(2,1)S(1)} %collective-permute-done.1, bf16[1024,1024]{1,0:T(8,128)(2,1)S(1)} %copy-done), kind=kOutput, calls=%fused_computation.11 | convolution fusion | flops 268435456 | bytes 2883584 | tf_op jit(solution)/shard_map/dot_general | solution.py:21
  7.9 0.5 %convolution_convert_fusion.2 = bf16[512,128]{1,0:T(8,128)(2,1)S(1)} fusion(bf16[1024,512]{1,0:T(8,128)(2,1)S(1)} %convolution_convert_fusion, bf16[1024,128]{1,0:T(8,128)(2,1)S(1)} %collective-permute-done.1), kind=kOutput, calls=%fused_computation.7 | convolution fusion | flops 134283264 | bytes 1441792 | tf_op jit(solution)/shard_map/dot_general | solution.py:21
  8.4 1.2 %collective-permute-done.refs_1_ = bf16[1024,128]{1,0:T(8,128)(2,1)S(1)} collective-permute-done((bf16[1024,128]{1,0:T(8,128)(2,1)}, bf16[1024,128]{1,0:T(8,128)(2,1)S(1)}, u32[]{:S(2)}, u32[]{:S(2)}) %collective-permute-start) | collective-permute-done | bytes 262176 | tf_op jit(solution)/shard_map/ppermute | solution.py:17
  9.5 1.7 %collective-permute-done.2.refs_3_ = bf16[128,128]{1,0:T(8,128)(2,1)S(1)} collective-permute-done((bf16[128,128]{1,0:T(8,128)(2,1)S(1)}, bf16[128,128]{1,0:T(8,128)(2,1)S(1)}, u32[]{:S(2)}, u32[]{:S(2)}) %collective-permute-start.2) | collective-permute-done | bytes 32800 | tf_op jit(solution)/shard_map/ppermute | solution.py:17
  11.3 1.3 %shard_map.73 = bf16[8,192,128]{2,1,0:T(8,128)(2,1)} custom-call(bf16[1024,128]{1,0:T(8,128)(2,1)S(1)} %bitcast.25, bf16[1024,128]{1,0:T(8,128)(2,1)S(1)} %collective-permute-done.refs_1_, bf16[128,128]{1,0:T(8,128)(2,1)S(1)} %bitcast.29, bf16[128,128]{1,0:T(8,128)(2,1)S(1)} %collective-permute-done.2.refs_3_, f32[128,1024]{1,0:T(8,128)S(1)} %fusion.4.refs_4_, ...), custom_call_target="tpu_custom_call" | custom-call | tf_op jit(solution)/shard_map/pallas_call | solution.py:98
  12.6 4.5 %all-to-all-start = ((bf16[8,192,128]{2,1,0:T(8,128)(2,1)}), bf16[8,192,128]{2,1,0:T(8,128)(2,1)S(1)}, u32[]{:S(2)}, u32[]{:S(2)}) async-start(bf16[8,192,128]{2,1,0:T(8,128)(2,1)} %shard_map.73), calls=%async_computation | async-start | bytes 786432 | tf_op jit(solution)/shard_map/all_to_all | solution.py:109
  17.1 0.9 %constant_dynamic-slice_fusion.entry_ref = f32[128,64]{1,0:T(8,128)S(1)} fusion(f32[128,512]{1,0:T(8,128)} %param.13, s32[]{:T(128)S(6)} %select_n.3), kind=kLoop, calls=%fused_computation.10 | loop fusion | bytes 65540 | tf_op jit(solution)/shard_map/dynamic_slice | solution.py:140
  18.0 1.0 %fusion.5 = f32[1024,128]{1,0:T(8,128)} fusion(bf16[1024,128]{1,0:T(8,128)(2,1)S(1)} %collective-permute-done.refs_1_, bf16[128,128]{1,0:T(8,128)(2,1)S(1)} %collective-permute-done.2.refs_3_), kind=kOutput, calls=%fused_computation.12 | convolution fusion | flops 33554432 | bytes 819200 | tf_op jit(solution)/shard_map/dot_general | solution.py:27
  19.0 2.0 %fusion.2 = bf16[1024,128]{0,1:T(8,128)(2,1)S(1)} fusion(bf16[1024,1024]{1,0:T(8,128)(2,1)S(1)} %copy-done, f32[1024,128]{1,0:T(8,128)} %fusion.5, bf16[1024,128]{1,0:T(8,128)(2,1)S(1)} %bitcast.26, bf16[128,128]{0,1:T(8,128)(2,1)S(1)} %convolution_convert_fusion.3), kind=kOutput, calls=%fused_computation.6 | convolution fusion | flops 302514176 | bytes 3178496 | tf_op jit(solution)/shard_map/dot_general | solution.py:27
  21.1 3.5 %all-to-all-done.steps_ref = bf16[8,192,128]{2,1,0:T(8,128)(2,1)S(1)} async-done(((bf16[8,192,128]{2,1,0:T(8,128)(2,1)}), bf16[8,192,128]{2,1,0:T(8,128)(2,1)S(1)}, u32[]{:S(2)}, u32[]{:S(2)}) %all-to-all-start) | async-done | bytes 393248 | tf_op jit(solution)/shard_map/all_to_all | solution.py:109
  24.6 1.1 %shard_map.74 = (f32[8,64,128]{2,1,0:T(8,128)S(1)}, bf16[64,128]{1,0:T(8,128)(2,1)S(1)}) custom-call(s32[1]{0:T(128)} %bitcast.5.upper_ref, bf16[8,192,128]{2,1,0:T(8,128)(2,1)S(1)} %all-to-all-done.steps_ref, f32[128,64]{1,0:T(8,128)S(1)} %constant_dynamic-slice_fusion.entry_ref), custom_call_target="tpu_custom_call" | custom-call | tf_op jit(solution)/shard_map/pallas_call | solution.py:98
  25.7 3.4 %collective-permute-start.3 = (bf16[64,128]{1,0:T(8,128)(2,1)S(1)}, bf16[64,128]{1,0:T(8,128)(2,1)S(1)}, u32[]{:S(2)}, u32[]{:S(2)}) collective-permute-start(bf16[64,128]{1,0:T(8,128)(2,1)S(1)} %get-tuple-element.34), channel_id=1, source_target_pairs={{0,8},{1,9},{2,10},{3,11},{4,12},{5,13},{6,14},{7,15},{16,24},{17,... | collective-permute-start | bytes 49160 | tf_op jit(solution)/shard_map/ppermute | solution.py:12
  29.1 1.4 %collective-permute-done.3.entered_ref = bf16[64,128]{1,0:T(8,128)(2,1)S(1)} collective-permute-done((bf16[64,128]{1,0:T(8,128)(2,1)S(1)}, bf16[64,128]{1,0:T(8,128)(2,1)S(1)}, u32[]{:S(2)}, u32[]{:S(2)}) %collective-permute-start.3) | collective-permute-done | bytes 16416 | tf_op jit(solution)/shard_map/ppermute | solution.py:12
  30.5 0.2 shard_map.76
  30.7 7.7 %all_to_all.10 = bf16[8,64,128]{2,1,0:T(8,128)(2,1)S(1)} all-to-all(bf16[8,64,128]{2,1,0:T(8,128)(2,1)S(1)} %shard_map.76), channel_id=1, replica_groups={{0,1,2,3,4,5,6,7},{8,9,10,11,12,13,14,15},{16,17,18,19,20,21,22,23},{24..., dimensions={0} | all-to-all | bytes 262144 | tf_op jit(solution)/shard_map/all_to_all | solution.py:109
  38.4 1.4 %subtract_convert_fusion = bf16[1024,512]{1,0:T(8,128)(2,1)} fusion(bf16[1024,512]{1,0:T(8,128)(2,1)S(1)} %copy-done.3, bf16[1024,128]{0,1:T(8,128)(2,1)S(1)} %fusion.2, bf16[512,128]{1,0:T(8,128)(2,1)S(1)} %bitcast.30), kind=kOutput, calls=%fused_computation | convolution fusion | flops 135790592 | bytes 2490368 | tf_op jit(solution)/shard_map/dot_general | solution.py:165
  (11 shorter events, 0.1 us)
Async XLA Ops:
  0.0 4.3 %copy-start = (bf16[1024,1024]{1,0:T(8,128)(2,1)S(1)}, bf16[1024,1024]{1,0:T(8,128)(2,1)}, u32[]{:S(2)}) copy-start(bf16[1024,1024]{1,0:T(8,128)(2,1)} %param.11) | copy-start | bytes 6291460
  0.0 6.8 %copy-start.4 = (bf16[1024,128]{1,0:T(8,128)(2,1)S(1)}, bf16[1024,128]{1,0:T(8,128)(2,1)}, u32[]{:S(2)}) copy-start(bf16[1024,128]{1,0:T(8,128)(2,1)} %param.9) | copy-start | bytes 786436
  0.0 6.8 %copy-start.5 = (bf16[1,1024,128]{2,1,0:T(8,128)(2,1)S(1)}, bf16[1,1024,128]{2,1,0:T(8,128)(2,1)}, u32[]{:S(2)}) copy-start(bf16[1,1024,128]{2,1,0:T(8,128)(2,1)} %param.8) | copy-start | bytes 786436
  0.0 9.5 %collective-permute-start = (bf16[1024,128]{1,0:T(8,128)(2,1)}, bf16[1024,128]{1,0:T(8,128)(2,1)S(1)}, u32[]{:S(2)}, u32[]{:S(2)}) collective-permute-start(bf16[1024,128]{1,0:T(8,128)(2,1)} %bitcast.24), channel_id=1, source_target_pairs={{0,16},{16,0},{1,17},{17,1},{2,18},{18,2},{3,19},{19,3},{4,20},{20... | collective-permute-start | bytes 786440 | tf_op jit(solution)/shard_map/ppermute | solution.py:17
  3.0 4.4 %collective-permute-start.1 = (bf16[1024,128]{1,0:T(8,128)(2,1)}, bf16[1024,128]{1,0:T(8,128)(2,1)S(1)}, u32[]{:S(2)}, u32[]{:S(2)}) collective-permute-start(bf16[1024,128]{1,0:T(8,128)(2,1)} %param.10), channel_id=1, source_target_pairs={{1,0},{2,1},{3,2},{4,3},{5,4},{6,5},{7,6},{8,7},{9,8},{10,9},{11,1... | collective-permute-start | bytes 786440 | tf_op jit(solution)/shard_map/ppermute | solution.py:12
  6.8 1.6 %copy-start.2 = (bf16[1024,512]{1,0:T(8,128)(2,1)}, bf16[1024,512]{1,0:T(8,128)(2,1)S(1)}, u32[]{:S(2)}) copy-start(bf16[1024,512]{1,0:T(8,128)(2,1)S(1)} %convolution_convert_fusion) | copy-start | bytes 3145732
  7.1 4.2 %copy-start.1 = (bf16[1,1024,128]{2,1,0:T(8,128)(2,1)S(1)}, bf16[1,1024,128]{2,1,0:T(8,128)(2,1)}, u32[]{:S(2)}) copy-start(bf16[1,1024,128]{2,1,0:T(8,128)(2,1)} %param.7) | copy-start | bytes 786436
  7.1 4.2 %collective-permute-start.2 = (bf16[128,128]{1,0:T(8,128)(2,1)S(1)}, bf16[128,128]{1,0:T(8,128)(2,1)S(1)}, u32[]{:S(2)}, u32[]{:S(2)}) collective-permute-start(bf16[128,128]{1,0:T(8,128)(2,1)S(1)} %bitcast.28), channel_id=1, source_target_pairs={{0,16},{16,0},{1,17},{17,1},{2,18},{18,2},{3,19},{19,3},{4,20},{20... | collective-permute-start | bytes 98312 | tf_op jit(solution)/shard_map/ppermute | solution.py:17
  12.6 12.0 %all-to-all-start = ((bf16[8,192,128]{2,1,0:T(8,128)(2,1)}), bf16[8,192,128]{2,1,0:T(8,128)(2,1)S(1)}, u32[]{:S(2)}, u32[]{:S(2)}) async-start(bf16[8,192,128]{2,1,0:T(8,128)(2,1)} %shard_map.73), calls=%async_computation | async-start | bytes 786432 | tf_op jit(solution)/shard_map/all_to_all | solution.py:109
  24.6 13.9 %copy-start.3 = (bf16[1024,512]{1,0:T(8,128)(2,1)S(1)}, bf16[1024,512]{1,0:T(8,128)(2,1)}, u32[]{:S(2)}) copy-start(bf16[1024,512]{1,0:T(8,128)(2,1)} %copy-done.2) | copy-start | bytes 3145732
  25.7 4.8 %collective-permute-start.3 = (bf16[64,128]{1,0:T(8,128)(2,1)S(1)}, bf16[64,128]{1,0:T(8,128)(2,1)S(1)}, u32[]{:S(2)}, u32[]{:S(2)}) collective-permute-start(bf16[64,128]{1,0:T(8,128)(2,1)S(1)} %get-tuple-element.34), channel_id=1, source_target_pairs={{0,8},{1,9},{2,10},{3,11},{4,12},{5,13},{6,14},{7,15},{16,24},{17,... | collective-permute-start | bytes 49160 | tf_op jit(solution)/shard_map/ppermute | solution.py:12

commit v10 on v9

--- a/solution.py
+++ b/solution.py
@@ -42,15 +42,34 @@
     return both[: value.shape[0]] + both[value.shape[0] :]
 
 
-def make_maps(layers, *refs):
+def make_applied(inverse_ref, right_ref, applied_ref):
+    rows = inverse_ref.shape[0] // 4
+
+    def part(k, _):
+        here = pl.ds(pl.multiple_of(k * rows, rows), rows)
+        applied_ref[here, :] = product(inverse_ref[here, :], right_ref[...]).astype(jnp.bfloat16)
+        return _
+
+    lax.fori_loop(0, 4, part, 0)
+
+
+def make_gain(layers, *refs):
     lefts = jnp.concatenate([ref[...] for ref in refs[:layers]], axis=1)
     cores = jnp.concatenate([ref[...] for ref in refs[layers : 2 * layers]], axis=0)
-    weights_ref, shift_ref, sent_ref = refs[2 * layers :]
-    map_t = wide(wide(weights_ref[...], lefts), cores).T.astype(jnp.bfloat16)
-    rank = map_t.shape[0]
+    inverse_ref, gain_ref = refs[2 * layers :]
+    tile_range = (-product(lefts, cores)).astype(jnp.bfloat16)
+    gain_ref[...] = product(inverse_ref[...], tile_range).astype(jnp.bfloat16)
+
+
+def make_steps(gain_ref, applied_ref, next_ref, sent_ref):
+    rank = gain_ref.shape[1]
+    share = sent_ref.shape[1] - rank
+    flipped = next_ref[...].T
+    map_t = (-product(flipped, gain_ref[...])).T.astype(jnp.bfloat16)
+    shift_t = product(flipped, applied_ref[...]).T.astype(jnp.bfloat16)
     for target in range(sent_ref.shape[0]):
         sent_ref[target, :rank] = map_t
-        sent_ref[target, rank:] = shift_ref[target]
+        sent_ref[target, rank:] = shift_t[target * share : (target + 1) * share]
 
 
 def chain(steps_ref, state, values_ref):
@@ -93,7 +112,7 @@
         coupled_ref[member] = (moved + values_ref[member]).astype(jnp.bfloat16)
 
 
-def local(kernel, inputs, *outputs, scalar=False, aliases={}):
+def local(kernel, inputs, *outputs, scalar=False, aliases={}, cost=None):
     specs = [SMEM] * scalar + [VMEM] * (len(inputs) - scalar)
     return pl.pallas_call(
         kernel,
@@ -101,6 +120,7 @@
         out_specs=[VMEM] * len(outputs),
         out_shape=[jax.ShapeDtypeStruct(*output) for output in outputs],
         input_output_aliases=aliases,
+        cost_estimate=cost,
         compiler_params=pltpu.CompilerParams(vmem_limit_bytes=16 * 2**20),
     )(*inputs)
 
@@ -111,7 +131,7 @@
 
 def body(left_factors, right_factors, sketch, row_basis, inverse_diag, right_side, incoming):
     half = jnp.bfloat16
-    rank = sketch.shape[1]
+    order, rank = sketch.shape
     width = right_side.shape[1]
     layers, groups = lax.axis_size("layer"), lax.axis_size("row")
     lowers = groups // 2
@@ -122,25 +142,28 @@
 
     lefts = [left_factors[0]] + [rotated(left_factors[0], "layer", k) for k in range(1, layers)]
     next_rows = shifted(row_basis, "row", -1)
-    applied = product(inverse_diag, right_side).astype(half)
-    sketch, applied = lax.optimization_barrier((sketch, applied))
     core = project(right_factors[0], sketch).astype(half)
+    right_side, core = lax.optimization_barrier((right_side, core))
     cores = [core] + [rotated(core, "layer", k) for k in range(1, layers)]
-
-    shift_t = project(applied, next_rows).astype(half).reshape(lowers, share, rank)
-    weights = project(next_rows, inverse_diag)
-    lefts[-1], shift_t, weights = lax.optimization_barrier((lefts[-1], shift_t, weights))
+    (applied,) = local(
+        make_applied,
+        (inverse_diag, right_side),
+        (right_side.shape, half),
+        cost=pl.CostEstimate(flops=1, bytes_accessed=1, transcendentals=0),
+    )
+    lefts[-1], applied = lax.optimization_barrier((lefts[-1], applied))
+
+    (gain,) = local(
+        lambda *refs: make_gain(layers, *refs),
+        (*lefts, *cores, inverse_diag),
+        ((order, rank), half),
+    )
     (sent,) = local(
-        lambda *refs: make_maps(layers, *refs),
-        (*lefts, *cores, weights, shift_t),
-        ((lowers, rank + share, rank), half),
-    )
-    lefts, incoming, sent = lax.optimization_barrier((lefts, incoming, sent))
+        make_steps, (gain, applied, next_rows), ((lowers, rank + share, rank), half)
+    )
+    incoming, sent = lax.optimization_barrier((incoming, sent))
     steps = exchanged(sent, near)
     entry = lax.dynamic_slice_in_dim(incoming, lower * share, share, 1)
-    tile_range = -sum(product(left, core) for left, core in zip(lefts, cores))
-    gain = product(inverse_diag, tile_range.astype(half)).astype(half)
-    gain, entry, steps = lax.optimization_barrier((gain, entry, steps))
 
     place = upper.reshape(1)
     values, last = local(

time: 40.3 us -> 40.8 us (1.012)
  matrix products: 8.18 us -> 2.62 us
  local copies, waits for them, and re-layouts: 0.94 us -> 3.74 us
  Pallas kernels: 2.64 us -> 5.42 us
    dot_general x3 -> x0, matrix products: 5.52 us -> none  [product(): return jnp.dot(a, b, preferred_element_type=jnp.float32)]
    all_to_all x1, waiting for transfers between devices: 3.5 us -> 6.57 us  [exchanged(): lax.all_to_all(blocks, 'row', 0, 0, axis_index_groups=members, tiled=True)]
    ppermute x2, waiting for transfers between devices: 2.9 us -> 0.01 us  [rotated(): lax.ppermute(value, axis, [(source, (source + steps) % count) for source...]
    unnamed x12 -> x8, local copies, waits for them, and re-layouts: 0.03 us -> 2.82 us
    pallas_call x4 -> x6, Pallas kernels: 2.64 us -> 5.42 us  [local(): pl.pallas_call(kernel, in_specs=specs, out_specs=[VMEM] * len(outputs), o...]
    dot_general x3 -> x1, matrix products: 1.22 us -> 1.21 us  [project(): lax.dot_general(basis, vectors, (((0,), (0,)), ((), ())), preferred_eleme...]
  transfers between devices with their start and end apart: 5 -> 5, of which waited for: 4 -> 2; matrix products, arithmetic and copies ran while one was open for 19% -> 5% of each run, Pallas kernels for 0% -> 7%
where the time goes in v10:
time: 40.8 us; the launch traced here: 40.3 us
  starting transfers between devices  12.8 us (31%)
  waiting for transfers between devices  7.95 us (19%)
  blocking collectives  7.72 us (19%)
  Pallas kernels  5.42 us (13%)
  local copies, waits for them, and re-layouts  3.74 us (9%)
  matrix products  2.62 us (6%)
    all_to_all x1, blocking collectives, exchanged(): lax.all_to_all(blocks, 'row', 0, 0, axis_index_groups=members, tiled=True)  7.72 us
    all_to_all x1, waiting for transfers between devices, exchanged(): lax.all_to_all(blocks, 'row', 0, 0, axis_index_groups=members, tiled=True)  6.57 us
    pallas_call x6, Pallas kernels, local(): pl.pallas_call(kernel, in_specs=specs, out_specs=[VMEM] * len(outputs), o...  5.42 us
    all_to_all x1, starting transfers between devices, exchanged(): lax.all_to_all(blocks, 'row', 0, 0, axis_index_groups=members, tiled=True)  4.82 us
    ppermute x2, starting transfers between devices, shifted(): lax.ppermute(value, axis, [(source, source + steps) for source in range(l...  4.8 us
    ppermute x2, starting transfers between devices, rotated(): lax.ppermute(value, axis, [(source, (source + steps) % count) for source...  3.15 us
    unnamed x8, local copies, waits for them, and re-layouts  2.82 us
    dot_general x1, matrix products, body(): lax.dot_general(gain, coupled, FLIPPED, preferred_element_type=jnp.float32)  1.41 us
  transfers between devices with their start and end apart: 5, of which 2 were waited for; matrix products, arithmetic and copies ran while one was open for 5% of the time, Pallas kernels for 7%

profile of v10, /device:TPU:0, one launch (start us, length us, event | category | flops | bytes accessed | tf_op | source)
XLA Modules:
  0.0 40.3 jit_solution(4041081274619291278)
XLA Ops:
  0.0 0.0 copy-start
  0.0 2.9 %collective-permute-start = (bf16[1024,128]{1,0:T(8,128)(2,1)}, bf16[1024,128]{1,0:T(8,128)(2,1)S(1)}, u32[]{:S(2)}, u32[]{:S(2)}) collective-permute-start(bf16[1024,128]{1,0:T(8,128)(2,1)} %bitcast.9), channel_id=1, source_target_pairs={{0,16},{16,0},{1,17},{17,1},{2,18},{18,2},{3,19},{19,3},{4,20},{20... | collective-permute-start | bytes 786440 | tf_op jit(solution)/shard_map/ppermute | solution.py:17
  2.9 1.3 %collective-permute-start.2 = (bf16[1024,128]{1,0:T(8,128)(2,1)}, bf16[1024,128]{1,0:T(8,128)(2,1)S(1)}, u32[]{:S(2)}, u32[]{:S(2)}) collective-permute-start(bf16[1024,128]{1,0:T(8,128)(2,1)} %param.10), channel_id=1, source_target_pairs={{1,0},{2,1},{3,2},{4,3},{5,4},{6,5},{7,6},{8,7},{9,8},{10,9},{11,1... | collective-permute-start | bytes 786440 | tf_op jit(solution)/shard_map/ppermute | solution.py:12
  4.2 0.0 copy-done
  4.2 1.2 %convolution_convert_fusion.refs_2_ = bf16[128,128]{1,0:T(8,128)(2,1)S(1)} fusion(bf16[1024,128]{1,0:T(8,128)(2,1)S(1)} %copy-done, bf16[1,1024,128]{2,1,0:T(8,128)(2,1)} %param.8), kind=kOutput, calls=%fused_computation.1 | convolution fusion | flops 33570816 | bytes 557056 | tf_op jit(solution)/shard_map/dot_general | solution.py:21
  5.5 0.2 collective-permute-start.1
  5.7 1.6 %copy-done.1 = bf16[1024,1024]{1,0:T(8,128)(2,1)S(1)} copy-done((bf16[1024,1024]{1,0:T(8,128)(2,1)S(1)}, bf16[1024,1024]{1,0:T(8,128)(2,1)}, u32[]{:S(2)}) %copy-start.1) | copy-done | bytes 2097176
  7.3 1.2 %copy-done.2 = bf16[1024,512]{1,0:T(8,128)(2,1)S(1)} copy-done((bf16[1024,512]{1,0:T(8,128)(2,1)S(1)}, bf16[1024,512]{1,0:T(8,128)(2,1)}, u32[]{:S(2)}) %copy-start.2) | copy-done | bytes 1048600
  8.5 1.7 %shard_map.73.applied_ref = bf16[1024,512]{1,0:T(8,128)(2,1)S(1)} custom-call(bf16[1024,1024]{1,0:T(8,128)(2,1)S(1)} %copy-done.1, bf16[1024,512]{1,0:T(8,128)(2,1)S(1)} %copy-done.2), custom_call_target="tpu_custom_call" | custom-call | flops 1 | bytes 1 | tf_op jit(solution)/shard_map/pallas_call | solution.py:117
  10.2 0.0 collective-permute-done.refs_1_
  10.3 0.0 collective-permute-done.1.refs_3_
  10.3 0.0 copy-done.3
  10.3 1.1 %shard_map.74.gain_ref = bf16[1024,128]{1,0:T(8,128)(2,1)S(1)} custom-call(bf16[1024,128]{1,0:T(8,128)(2,1)S(1)} %bitcast.10, bf16[1024,128]{1,0:T(8,128)(2,1)S(1)} %collective-permute-done.refs_1_, bf16[128,128]{1,0:T(8,128)(2,1)S(1)} %convolution_convert_fusion.refs_2_, bf16[128,128]{1,0:T(8,128)(2,1)S(1)} %collective-permute-done.1.refs_3_, ...), custom_call_target="tpu_custom_call" | custom-call | tf_op jit(solution)/shard_map/pallas_call | solution.py:117
  11.4 0.0 collective-permute-done.2.next_ref
  11.4 1.3 %shard_map.75 = bf16[8,192,128]{2,1,0:T(8,128)(2,1)} custom-call(bf16[1024,128]{1,0:T(8,128)(2,1)S(1)} %shard_map.74.gain_ref, bf16[1024,512]{1,0:T(8,128)(2,1)S(1)} %shard_map.73.applied_ref, bf16[1024,128]{1,0:T(8,128)(2,1)S(1)} %collective-permute-done.2.next_ref), custom_call_target="tpu_custom_call" | custom-call | tf_op jit(solution)/shard_map/pallas_call | solution.py:117
  12.6 4.8 %all-to-all-start = ((bf16[8,192,128]{2,1,0:T(8,128)(2,1)}), bf16[8,192,128]{2,1,0:T(8,128)(2,1)S(1)}, u32[]{:S(2)}, u32[]{:S(2)}) async-start(bf16[8,192,128]{2,1,0:T(8,128)(2,1)} %shard_map.75), calls=%async_computation | async-start | bytes 786432 | tf_op jit(solution)/shard_map/all_to_all | solution.py:129
  17.5 0.9 %constant_dynamic-slice_fusion.entry_ref = f32[128,64]{1,0:T(8,128)S(1)} fusion(f32[128,512]{1,0:T(8,128)} %param.13, s32[]{:T(128)S(6)} %select_n.3), kind=kLoop, calls=%fused_computation.3 | loop fusion | bytes 65540 | tf_op jit(solution)/shard_map/dynamic_slice | solution.py:166
  18.4 6.6 %all-to-all-done.steps_ref = bf16[8,192,128]{2,1,0:T(8,128)(2,1)S(1)} async-done(((bf16[8,192,128]{2,1,0:T(8,128)(2,1)}), bf16[8,192,128]{2,1,0:T(8,128)(2,1)S(1)}, u32[]{:S(2)}, u32[]{:S(2)}) %all-to-all-start) | async-done | bytes 393248 | tf_op jit(solution)/shard_map/all_to_all | solution.py:129
  25.0 1.1 %shard_map.76 = (f32[8,64,128]{2,1,0:T(8,128)S(1)}, bf16[64,128]{1,0:T(8,128)(2,1)S(1)}) custom-call(s32[1]{0:T(128)} %bitcast.2.upper_ref, bf16[8,192,128]{2,1,0:T(8,128)(2,1)S(1)} %all-to-all-done.steps_ref, f32[128,64]{1,0:T(8,128)S(1)} %constant_dynamic-slice_fusion.entry_ref), custom_call_target="tpu_custom_call" | custom-call | tf_op jit(solution)/shard_map/pallas_call | solution.py:117
  26.0 3.5 %collective-permute-start.3 = (bf16[64,128]{1,0:T(8,128)(2,1)S(1)}, bf16[64,128]{1,0:T(8,128)(2,1)S(1)}, u32[]{:S(2)}, u32[]{:S(2)}) collective-permute-start(bf16[64,128]{1,0:T(8,128)(2,1)S(1)} %get-tuple-element.22), channel_id=1, source_target_pairs={{0,8},{1,9},{2,10},{3,11},{4,12},{5,13},{6,14},{7,15},{16,24},{17,... | collective-permute-start | bytes 49160 | tf_op jit(solution)/shard_map/ppermute | solution.py:12
  29.6 1.4 %collective-permute-done.3.entered_ref = bf16[64,128]{1,0:T(8,128)(2,1)S(1)} collective-permute-done((bf16[64,128]{1,0:T(8,128)(2,1)S(1)}, bf16[64,128]{1,0:T(8,128)(2,1)S(1)}, u32[]{:S(2)}, u32[]{:S(2)}) %collective-permute-start.3) | collective-permute-done | bytes 16416 | tf_op jit(solution)/shard_map/ppermute | solution.py:12
  31.0 0.2 shard_map.78
  31.2 7.7 %all_to_all.10 = bf16[8,64,128]{2,1,0:T(8,128)(2,1)S(1)} all-to-all(bf16[8,64,128]{2,1,0:T(8,128)(2,1)S(1)} %shard_map.78), channel_id=1, replica_groups={{0,1,2,3,4,5,6,7},{8,9,10,11,12,13,14,15},{16,17,18,19,20,21,22,23},{24..., dimensions={0} | all-to-all | bytes 262144 | tf_op jit(solution)/shard_map/all_to_all | solution.py:129
  38.9 1.4 %subtract_convert_fusion = bf16[1024,512]{1,0:T(8,128)(2,1)} fusion(bf16[1024,512]{1,0:T(8,128)(2,1)S(1)} %shard_map.73.applied_ref, bf16[1024,128]{1,0:T(8,128)(2,1)S(1)} %shard_map.74.gain_ref, bf16[512,128]{1,0:T(8,128)(2,1)S(1)} %bitcast.11), kind=kOutput, calls=%fused_computation | convolution fusion | flops 135790592 | bytes 2490368 | tf_op jit(solution)/shard_map/dot_general | solution.py:188
  (4 shorter events, 0.1 us)
Async XLA Ops:
  0.0 4.2 %copy-start = (bf16[1024,128]{1,0:T(8,128)(2,1)S(1)}, bf16[1024,128]{1,0:T(8,128)(2,1)}, u32[]{:S(2)}) copy-start(bf16[1024,128]{1,0:T(8,128)(2,1)} %param.9) | copy-start | bytes 786436
  0.0 10.2 %collective-permute-start = (bf16[1024,128]{1,0:T(8,128)(2,1)}, bf16[1024,128]{1,0:T(8,128)(2,1)S(1)}, u32[]{:S(2)}, u32[]{:S(2)}) collective-permute-start(bf16[1024,128]{1,0:T(8,128)(2,1)} %bitcast.9), channel_id=1, source_target_pairs={{0,16},{16,0},{1,17},{17,1},{2,18},{18,2},{3,19},{19,3},{4,20},{20... | collective-permute-start | bytes 786440 | tf_op jit(solution)/shard_map/ppermute | solution.py:17
  2.9 8.4 %collective-permute-start.2 = (bf16[1024,128]{1,0:T(8,128)(2,1)}, bf16[1024,128]{1,0:T(8,128)(2,1)S(1)}, u32[]{:S(2)}, u32[]{:S(2)}) collective-permute-start(bf16[1024,128]{1,0:T(8,128)(2,1)} %param.10), channel_id=1, source_target_pairs={{1,0},{2,1},{3,2},{4,3},{5,4},{6,5},{7,6},{8,7},{9,8},{10,9},{11,1... | collective-permute-start | bytes 786440 | tf_op jit(solution)/shard_map/ppermute | solution.py:12
  5.5 4.8 %collective-permute-start.1 = (bf16[128,128]{1,0:T(8,128)(2,1)S(1)}, bf16[128,128]{1,0:T(8,128)(2,1)S(1)}, u32[]{:S(2)}, u32[]{:S(2)}) collective-permute-start(bf16[128,128]{1,0:T(8,128)(2,1)S(1)} %convolution_convert_fusion.refs_2_), channel_id=1, source_target_pairs={{0,16},{16,0},{1,17},{17,1},{2,18},{18,2},{3,19},{19,3},{4,20},{20... | collective-permute-start | bytes 98312 | tf_op jit(solution)/shard_map/ppermute | solution.py:17
  5.7 1.6 %copy-start.1 = (bf16[1024,1024]{1,0:T(8,128)(2,1)S(1)}, bf16[1024,1024]{1,0:T(8,128)(2,1)}, u32[]{:S(2)}) copy-start(bf16[1024,1024]{1,0:T(8,128)(2,1)} %refs_4_.1) | copy-start | bytes 6291460
  7.3 1.2 %copy-start.2 = (bf16[1024,512]{1,0:T(8,128)(2,1)S(1)}, bf16[1024,512]{1,0:T(8,128)(2,1)}, u32[]{:S(2)}) copy-start(bf16[1024,512]{1,0:T(8,128)(2,1)} %right_ref) | copy-start | bytes 3145732
  8.5 1.8 %copy-start.3 = (bf16[1,1024,128]{2,1,0:T(8,128)(2,1)S(1)}, bf16[1,1024,128]{2,1,0:T(8,128)(2,1)}, u32[]{:S(2)}) copy-start(bf16[1,1024,128]{2,1,0:T(8,128)(2,1)} %param.7) | copy-start | bytes 786436
  12.6 12.3 %all-to-all-start = ((bf16[8,192,128]{2,1,0:T(8,128)(2,1)}), bf16[8,192,128]{2,1,0:T(8,128)(2,1)S(1)}, u32[]{:S(2)}, u32[]{:S(2)}) async-start(bf16[8,192,128]{2,1,0:T(8,128)(2,1)} %shard_map.75), calls=%async_computation | async-start | bytes 786432 | tf_op jit(solution)/shard_map/all_to_all | solution.py:129
  26.0 5.0 %collective-permute-start.3 = (bf16[64,128]{1,0:T(8,128)(2,1)S(1)}, bf16[64,128]{1,0:T(8,128)(2,1)S(1)}, u32[]{:S(2)}, u32[]{:S(2)}) collective-permute-start(bf16[64,128]{1,0:T(8,128)(2,1)S(1)} %get-tuple-element.22), channel_id=1, source_target_pairs={{0,8},{1,9},{2,10},{3,11},{4,12},{5,13},{6,14},{7,15},{16,24},{17,... | collective-permute-start | bytes 49160 | tf_op jit(solution)/shard_map/ppermute | solution.py:12

commit v11 on v10

--- a/solution.py
+++ b/solution.py
@@ -28,7 +28,9 @@
 
 
 SMEM = pl.BlockSpec(memory_space=pltpu.SMEM)
+HBM = pl.BlockSpec(memory_space=pltpu.HBM)
 VMEM = pl.BlockSpec(memory_space=pltpu.VMEM)
+PARTS = 4
 FLIPPED = (((1,), (1,)), ((), ()))
 
 
@@ -42,31 +44,53 @@
     return both[: value.shape[0]] + both[value.shape[0] :]
 
 
-def make_applied(inverse_ref, right_ref, applied_ref):
-    rows = inverse_ref.shape[0] // 4
-
-    def part(k, _):
-        here = pl.ds(pl.multiple_of(k * rows, rows), rows)
-        applied_ref[here, :] = product(inverse_ref[here, :], right_ref[...]).astype(jnp.bfloat16)
-        return _
-
-    lax.fori_loop(0, 4, part, 0)
+def make_core(right_hbm, sketch_hbm, core_ref, right, sketch, arrived):
+    copies = [
+        pltpu.make_async_copy(right_hbm, right, arrived.at[0]),
+        pltpu.make_async_copy(sketch_hbm, sketch, arrived.at[1]),
+    ]
+    for copy in copies:
+        copy.start()
+    for copy in copies:
+        copy.wait()
+    core_ref[...] = project(right[...], sketch[...]).astype(jnp.bfloat16)
+
+
+def make_applied(inverse_hbm, right_hbm, applied_ref, flipped_ref, inverse, right, arrived):
+    order = inverse.shape[0]
+    rows = order // PARTS
+    pieces = [pl.ds(part * rows, rows) for part in range(PARTS)]
+    copies = [pltpu.make_async_copy(right_hbm, right, arrived.at[PARTS])]
+    for part, piece in enumerate(pieces):
+        copies.append(
+            pltpu.make_async_copy(inverse_hbm.at[piece], inverse.at[piece], arrived.at[part])
+        )
+    for copy in copies:
+        copy.start()
+    copies[0].wait()
+    for copy, piece in zip(copies[1:], pieces):
+        copy.wait()
+        applied = product(inverse[piece], right[...])
+        applied_ref[piece] = applied.astype(jnp.bfloat16)
+        flipped_ref[:, piece] = applied.T.astype(jnp.bfloat16)
 
 
 def make_gain(layers, *refs):
     lefts = jnp.concatenate([ref[...] for ref in refs[:layers]], axis=1)
     cores = jnp.concatenate([ref[...] for ref in refs[layers : 2 * layers]], axis=0)
-    inverse_ref, gain_ref = refs[2 * layers :]
+    inverse_ref, gain_ref, flipped_ref = refs[2 * layers :]
     tile_range = (-product(lefts, cores)).astype(jnp.bfloat16)
-    gain_ref[...] = product(inverse_ref[...], tile_range).astype(jnp.bfloat16)
+    gain = product(inverse_ref[...], tile_range)
+    gain_ref[...] = gain.astype(jnp.bfloat16)
+    flipped_ref[...] = gain.T.astype(jnp.bfloat16)
 
 
 def make_steps(gain_ref, applied_ref, next_ref, sent_ref):
-    rank = gain_ref.shape[1]
+    rank = gain_ref.shape[0]
     share = sent_ref.shape[1] - rank
-    flipped = next_ref[...].T
-    map_t = (-product(flipped, gain_ref[...])).T.astype(jnp.bfloat16)
-    shift_t = product(flipped, applied_ref[...]).T.astype(jnp.bfloat16)
+    basis = next_ref[...]
+    map_t = (-product(gain_ref[...], basis)).astype(jnp.bfloat16)
+    shift_t = product(applied_ref[...], basis).astype(jnp.bfloat16)
     for target in range(sent_ref.shape[0]):
         sent_ref[target, :rank] = map_t
         sent_ref[target, rank:] = shift_t[target * share : (target + 1) * share]
@@ -112,16 +136,17 @@
         coupled_ref[member] = (moved + values_ref[member]).astype(jnp.bfloat16)
 
 
-def local(kernel, inputs, *outputs, scalar=False, aliases={}, cost=None):
-    specs = [SMEM] * scalar + [VMEM] * (len(inputs) - scalar)
+def local(kernel, inputs, *outputs, scalar=False, aliases={}, cost=None, scratch=()):
+    specs = [SMEM] * scalar + [HBM if scratch else VMEM] * (len(inputs) - scalar)
     return pl.pallas_call(
         kernel,
         in_specs=specs,
         out_specs=[VMEM] * len(outputs),
         out_shape=[jax.ShapeDtypeStruct(*output) for output in outputs],
+        scratch_shapes=scratch,
         input_output_aliases=aliases,
         cost_estimate=cost,
-        compiler_params=pltpu.CompilerParams(vmem_limit_bytes=16 * 2**20),
+        compiler_params=pltpu.CompilerParams(vmem_limit_bytes=(56 if scratch else 16) * 2**20),
     )(*inputs)
 
 
@@ -142,24 +167,40 @@
 
     lefts = [left_factors[0]] + [rotated(left_factors[0], "layer", k) for k in range(1, layers)]
     next_rows = shifted(row_basis, "row", -1)
-    core = project(right_factors[0], sketch).astype(half)
+    (core,) = local(
+        make_core,
+        (right_factors[0], sketch),
+        ((rank, rank), half),
+        scratch=(
+            pltpu.VMEM(sketch.shape, half),
+            pltpu.VMEM(sketch.shape, half),
+            pltpu.SemaphoreType.DMA((2,)),
+        ),
+    )
     right_side, core = lax.optimization_barrier((right_side, core))
     cores = [core] + [rotated(core, "layer", k) for k in range(1, layers)]
-    (applied,) = local(
+    applied, applied_t = local(
         make_applied,
         (inverse_diag, right_side),
-        (right_side.shape, half),
+        ((order, width), half),
+        ((width, order), half),
         cost=pl.CostEstimate(flops=1, bytes_accessed=1, transcendentals=0),
-    )
-    lefts[-1], applied = lax.optimization_barrier((lefts[-1], applied))
-
-    (gain,) = local(
+        scratch=(
+            pltpu.VMEM((order, order), half),
+            pltpu.VMEM((order, width), half),
+            pltpu.SemaphoreType.DMA((PARTS + 1,)),
+        ),
+    )
+    lefts[-1], applied_t = lax.optimization_barrier((lefts[-1], applied_t))
+
+    gain, gain_t = local(
         lambda *refs: make_gain(layers, *refs),
         (*lefts, *cores, inverse_diag),
         ((order, rank), half),
+        ((rank, order), half),
     )
     (sent,) = local(
-        make_steps, (gain, applied, next_rows), ((lowers, rank + share, rank), half)
+        make_steps, (gain_t, applied_t, next_rows), ((lowers, rank + share, rank), half)
     )
     incoming, sent = lax.optimization_barrier((incoming, sent))
     steps = exchanged(sent, near)

time: 40.8 us -> 41.8 us (1.025)
  Pallas kernels: 5.42 us -> 10.3 us
  local copies, waits for them, and re-layouts: 3.74 us -> 0.11 us
  matrix products: 2.62 us -> 1.41 us
  waiting for transfers between devices: 7.95 us -> 8.76 us
    pallas_call x6 -> x7, Pallas kernels: 5.42 us -> 10.3 us  [local(): pl.pallas_call(kernel, in_specs=specs, out_specs=[VMEM] * len(outputs), o...]
    unnamed x8 -> x12, local copies, waits for them, and re-layouts: 2.82 us -> 0.03 us
    dot_general x1 -> x0, matrix products: 1.21 us -> none  [project(): lax.dot_general(basis, vectors, (((0,), (0,)), ((), ())), preferred_eleme...]
    dynamic_slice x1, local copies, waits for them, and re-layouts: 0.91 us -> 0.09 us  [body(): entry = lax.dynamic_slice_in_dim(incoming, lower * share, share, 1)]
    all_to_all x1, waiting for transfers between devices: 6.57 us -> 7.39 us  [exchanged(): lax.all_to_all(blocks, 'row', 0, 0, axis_index_groups=members, tiled=True)]
  transfers between devices with their start and end apart: 5 -> 5, of which waited for: 2 -> 2; matrix products, arithmetic and copies ran while one was open for 5% -> 0% of each run, Pallas kernels for 7% -> 19%
where the time goes in v11:
time: 41.8 us; the launch traced here: 41.5 us
  starting transfers between devices  13 us (31%)
  Pallas kernels  10.3 us (25%)
  waiting for transfers between devices  8.76 us (21%)
  blocking collectives  7.73 us (18%)
  matrix products  1.41 us (3%)
    pallas_call x7, Pallas kernels, local(): pl.pallas_call(kernel, in_specs=specs, out_specs=[VMEM] * len(outputs), o...  10.3 us
    all_to_all x1, blocking collectives, exchanged(): lax.all_to_all(blocks, 'row', 0, 0, axis_index_groups=members, tiled=True)  7.73 us
    all_to_all x1, waiting for transfers between devices, exchanged(): lax.all_to_all(blocks, 'row', 0, 0, axis_index_groups=members, tiled=True)  7.39 us
    all_to_all x1, starting transfers between devices, exchanged(): lax.all_to_all(blocks, 'row', 0, 0, axis_index_groups=members, tiled=True)  4.95 us
    ppermute x2, starting transfers between devices, shifted(): lax.ppermute(value, axis, [(source, source + steps) for source in range(l...  4.81 us
    ppermute x2, starting transfers between devices, rotated(): lax.ppermute(value, axis, [(source, (source + steps) % count) for source...  3.23 us
    dot_general x1, matrix products, body(): lax.dot_general(gain, coupled, FLIPPED, preferred_element_type=jnp.float32)  1.41 us
    ppermute x2, waiting for transfers between devices, shifted(): lax.ppermute(value, axis, [(source, source + steps) for source in range(l...  1.37 us
  transfers between devices with their start and end apart: 5, of which 2 were waited for; matrix products, arithmetic and copies ran while one was open for 0% of the time, Pallas kernels for 19%

profile of v11, /device:TPU:0, one launch (start us, length us, event | category | flops | bytes accessed | tf_op | source)
XLA Modules:
  0.0 41.5 jit_solution(3036100501515978635)
XLA Ops:
  0.0 0.0 copy-start
  0.0 3.0 %collective-permute-start = (bf16[1024,128]{1,0:T(8,128)(2,1)}, bf16[1024,128]{1,0:T(8,128)(2,1)S(1)}, u32[]{:S(2)}, u32[]{:S(2)}) collective-permute-start(bf16[1024,128]{1,0:T(8,128)(2,1)} %bitcast.6), channel_id=1, source_target_pairs={{0,16},{16,0},{1,17},{17,1},{2,18},{18,2},{3,19},{19,3},{4,20},{20... | collective-permute-start | bytes 786440 | tf_op jit(solution)/shard_map/ppermute | solution.py:17
  3.0 1.3 %collective-permute-start.2 = (bf16[1024,128]{1,0:T(8,128)(2,1)}, bf16[1024,128]{1,0:T(8,128)(2,1)S(1)}, u32[]{:S(2)}, u32[]{:S(2)}) collective-permute-start(bf16[1024,128]{1,0:T(8,128)(2,1)} %param.10), channel_id=1, source_target_pairs={{1,0},{2,1},{3,2},{4,3},{5,4},{6,5},{7,6},{8,7},{9,8},{10,9},{11,1... | collective-permute-start | bytes 786440 | tf_op jit(solution)/shard_map/ppermute | solution.py:12
  4.3 1.9 %shard_map.73.refs_2_ = bf16[128,128]{1,0:T(8,128)(2,1)} custom-call(bf16[1024,128]{1,0:T(8,128)(2,1)} %bitcast.9, bf16[1024,128]{1,0:T(8,128)(2,1)} %sketch_hbm.1), custom_call_target="tpu_custom_call" | custom-call | tf_op jit(solution)/shard_map/pallas_call | solution.py:141
  6.2 0.0 copy-start.4
  6.2 0.2 collective-permute-start.1
  6.5 4.7 %shard_map.74 = (bf16[1024,512]{1,0:T(8,128)(2,1)}, bf16[512,1024]{1,0:T(8,128)(2,1)}) custom-call(bf16[1024,1024]{1,0:T(8,128)(2,1)} %refs_4_.1, bf16[1024,512]{1,0:T(8,128)(2,1)} %right_hbm), custom_call_target="tpu_custom_call" | custom-call | flops 1 | bytes 1 | tf_op jit(solution)/shard_map/pallas_call | solution.py:141
  11.2 0.0 copy-start.2
  11.2 0.0 collective-permute-done.refs_1_
  11.2 0.0 collective-permute-done.1.refs_3_
  11.2 1.2 %shard_map.75 = (bf16[1024,128]{1,0:T(8,128)(2,1)S(1)}, bf16[128,1024]{1,0:T(8,128)(2,1)S(1)}) custom-call(bf16[1024,128]{1,0:T(8,128)(2,1)S(1)} %bitcast.7, bf16[1024,128]{1,0:T(8,128)(2,1)S(1)} %collective-permute-done.refs_1_, bf16[128,128]{1,0:T(8,128)(2,1)S(1)} %copy-done.4, bf16[128,128]{1,0:T(8,128)(2,1)S(1)} %collective-permute-done.1.refs_3_, ...), custom_call_target="tpu_custom_call" | custom-call | tf_op jit(solution)/shard_map/pallas_call | solution.py:141
  12.4 0.0 collective-permute-done.2.next_ref
  12.4 0.0 copy-done.2
  12.4 0.0 copy-start.5
  12.4 1.2 %shard_map.76 = bf16[8,192,128]{2,1,0:T(8,128)(2,1)} custom-call(bf16[128,1024]{1,0:T(8,128)(2,1)S(1)} %get-tuple-element.26.gain_ref, bf16[512,1024]{1,0:T(8,128)(2,1)S(1)} %copy-done.2, bf16[1024,128]{1,0:T(8,128)(2,1)S(1)} %collective-permute-done.2.next_ref), custom_call_target="tpu_custom_call" | custom-call | tf_op jit(solution)/shard_map/pallas_call | solution.py:141
  13.7 4.9 %all-to-all-start = ((bf16[8,192,128]{2,1,0:T(8,128)(2,1)}), bf16[8,192,128]{2,1,0:T(8,128)(2,1)S(1)}, u32[]{:S(2)}, u32[]{:S(2)}) async-start(bf16[8,192,128]{2,1,0:T(8,128)(2,1)} %shard_map.76), calls=%async_computation | async-start | bytes 786432 | tf_op jit(solution)/shard_map/all_to_all | solution.py:154
  18.6 0.1 constant_dynamic-slice_fusion.entry_ref
  18.7 7.4 %all-to-all-done.steps_ref = bf16[8,192,128]{2,1,0:T(8,128)(2,1)S(1)} async-done(((bf16[8,192,128]{2,1,0:T(8,128)(2,1)}), bf16[8,192,128]{2,1,0:T(8,128)(2,1)S(1)}, u32[]{:S(2)}, u32[]{:S(2)}) %all-to-all-start) | async-done | bytes 393248 | tf_op jit(solution)/shard_map/all_to_all | solution.py:154
  26.1 1.1 %shard_map.77 = (f32[8,64,128]{2,1,0:T(8,128)S(1)}, bf16[64,128]{1,0:T(8,128)(2,1)S(1)}) custom-call(s32[1]{0:T(128)} %bitcast.2.upper_ref, bf16[8,192,128]{2,1,0:T(8,128)(2,1)S(1)} %all-to-all-done.steps_ref, f32[128,64]{1,0:T(8,128)S(1)} %constant_dynamic-slice_fusion.entry_ref), custom_call_target="tpu_custom_call" | custom-call | tf_op jit(solution)/shard_map/pallas_call | solution.py:141
  27.2 3.5 %collective-permute-start.3 = (bf16[64,128]{1,0:T(8,128)(2,1)S(1)}, bf16[64,128]{1,0:T(8,128)(2,1)S(1)}, u32[]{:S(2)}, u32[]{:S(2)}) collective-permute-start(bf16[64,128]{1,0:T(8,128)(2,1)S(1)} %get-tuple-element.30), channel_id=1, source_target_pairs={{0,8},{1,9},{2,10},{3,11},{4,12},{5,13},{6,14},{7,15},{16,24},{17,... | collective-permute-start | bytes 49160 | tf_op jit(solution)/shard_map/ppermute | solution.py:12
  30.8 1.4 %collective-permute-done.3.entered_ref = bf16[64,128]{1,0:T(8,128)(2,1)S(1)} collective-permute-done((bf16[64,128]{1,0:T(8,128)(2,1)S(1)}, bf16[64,128]{1,0:T(8,128)(2,1)S(1)}, u32[]{:S(2)}, u32[]{:S(2)}) %collective-permute-start.3) | collective-permute-done | bytes 16416 | tf_op jit(solution)/shard_map/ppermute | solution.py:12
  32.1 0.2 shard_map.79
  32.3 7.7 %all_to_all.10 = bf16[8,64,128]{2,1,0:T(8,128)(2,1)S(1)} all-to-all(bf16[8,64,128]{2,1,0:T(8,128)(2,1)S(1)} %shard_map.79), channel_id=1, replica_groups={{0,1,2,3,4,5,6,7},{8,9,10,11,12,13,14,15},{16,17,18,19,20,21,22,23},{24..., dimensions={0} | all-to-all | bytes 262144 | tf_op jit(solution)/shard_map/all_to_all | solution.py:154
  40.1 1.4 %subtract_convert_fusion = bf16[1024,512]{1,0:T(8,128)(2,1)} fusion(bf16[1024,512]{1,0:T(8,128)(2,1)S(1)} %copy-done.5, bf16[1024,128]{1,0:T(8,128)(2,1)S(1)} %get-tuple-element.25, bf16[512,128]{1,0:T(8,128)(2,1)S(1)} %bitcast.8), kind=kOutput, calls=%fused_computation | convolution fusion | flops 135790592 | bytes 2490368 | tf_op jit(solution)/shard_map/dot_general | solution.py:229
  (8 shorter events, 0.1 us)
Async XLA Ops:
  0.0 18.6 %copy-start = (f32[128,512]{1,0:T(8,128)S(1)}, f32[128,512]{1,0:T(8,128)}, u32[]{:S(2)}) copy-start(f32[128,512]{1,0:T(8,128)} %param.13) | copy-start | bytes 786436
  0.0 11.2 %copy-start.3 = (bf16[1,1024,128]{2,1,0:T(8,128)(2,1)S(1)}, bf16[1,1024,128]{2,1,0:T(8,128)(2,1)}, u32[]{:S(2)}) copy-start(bf16[1,1024,128]{2,1,0:T(8,128)(2,1)} %param.7) | copy-start | bytes 786436
  0.0 11.2 %copy-start.1 = (bf16[1024,1024]{1,0:T(8,128)(2,1)S(1)}, bf16[1024,1024]{1,0:T(8,128)(2,1)}, u32[]{:S(2)}) copy-start(bf16[1024,1024]{1,0:T(8,128)(2,1)} %refs_4_.1) | copy-start | bytes 6291460
  0.0 11.2 %collective-permute-start = (bf16[1024,128]{1,0:T(8,128)(2,1)}, bf16[1024,128]{1,0:T(8,128)(2,1)S(1)}, u32[]{:S(2)}, u32[]{:S(2)}) collective-permute-start(bf16[1024,128]{1,0:T(8,128)(2,1)} %bitcast.6), channel_id=1, source_target_pairs={{0,16},{16,0},{1,17},{17,1},{2,18},{18,2},{3,19},{19,3},{4,20},{20... | collective-permute-start | bytes 786440 | tf_op jit(solution)/shard_map/ppermute | solution.py:17
  3.0 9.4 %collective-permute-start.2 = (bf16[1024,128]{1,0:T(8,128)(2,1)}, bf16[1024,128]{1,0:T(8,128)(2,1)S(1)}, u32[]{:S(2)}, u32[]{:S(2)}) collective-permute-start(bf16[1024,128]{1,0:T(8,128)(2,1)} %param.10), channel_id=1, source_target_pairs={{1,0},{2,1},{3,2},{4,3},{5,4},{6,5},{7,6},{8,7},{9,8},{10,9},{11,1... | collective-permute-start | bytes 786440 | tf_op jit(solution)/shard_map/ppermute | solution.py:12
  6.2 5.0 %copy-start.4 = (bf16[128,128]{1,0:T(8,128)(2,1)S(1)}, bf16[128,128]{1,0:T(8,128)(2,1)}, u32[]{:S(2)}) copy-start(bf16[128,128]{1,0:T(8,128)(2,1)} %shard_map.73.refs_2_) | copy-start | bytes 98308
  6.2 5.0 %collective-permute-start.1 = (bf16[128,128]{1,0:T(8,128)(2,1)}, bf16[128,128]{1,0:T(8,128)(2,1)S(1)}, u32[]{:S(2)}, u32[]{:S(2)}) collective-permute-start(bf16[128,128]{1,0:T(8,128)(2,1)} %shard_map.73.refs_2_), channel_id=1, source_target_pairs={{0,16},{16,0},{1,17},{17,1},{2,18},{18,2},{3,19},{19,3},{4,20},{20... | collective-permute-start | bytes 98312 | tf_op jit(solution)/shard_map/ppermute | solution.py:17
  11.2 1.2 %copy-start.2 = (bf16[512,1024]{1,0:T(8,128)(2,1)S(1)}, bf16[512,1024]{1,0:T(8,128)(2,1)}, u32[]{:S(2)}) copy-start(bf16[512,1024]{1,0:T(8,128)(2,1)} %get-tuple-element.27.applied_ref) | copy-start | bytes 3145732
  12.4 27.7 %copy-start.5 = (bf16[1024,512]{1,0:T(8,128)(2,1)S(1)}, bf16[1024,512]{1,0:T(8,128)(2,1)}, u32[]{:S(2)}) copy-start(bf16[1024,512]{1,0:T(8,128)(2,1)} %get-tuple-element.21) | copy-start | bytes 3145732
  13.7 12.4 %all-to-all-start = ((bf16[8,192,128]{2,1,0:T(8,128)(2,1)}), bf16[8,192,128]{2,1,0:T(8,128)(2,1)S(1)}, u32[]{:S(2)}, u32[]{:S(2)}) async-start(bf16[8,192,128]{2,1,0:T(8,128)(2,1)} %shard_map.76), calls=%async_computation | async-start | bytes 786432 | tf_op jit(solution)/shard_map/all_to_all | solution.py:154
  27.2 5.0 %collective-permute-start.3 = (bf16[64,128]{1,0:T(8,128)(2,1)S(1)}, bf16[64,128]{1,0:T(8,128)(2,1)S(1)}, u32[]{:S(2)}, u32[]{:S(2)}) collective-permute-start(bf16[64,128]{1,0:T(8,128)(2,1)S(1)} %get-tuple-element.30), channel_id=1, source_target_pairs={{0,8},{1,9},{2,10},{3,11},{4,12},{5,13},{6,14},{7,15},{16,24},{17,... | collective-permute-start | bytes 49160 | tf_op jit(solution)/shard_map/ppermute | solution.py:12

commit v12 on v10

--- a/solution.py
+++ b/solution.py
@@ -28,6 +28,7 @@
 
 
 SMEM = pl.BlockSpec(memory_space=pltpu.SMEM)
+HBM = pl.BlockSpec(memory_space=pltpu.HBM)
 VMEM = pl.BlockSpec(memory_space=pltpu.VMEM)
 FLIPPED = (((1,), (1,)), ((), ()))
 
@@ -40,6 +41,18 @@
 def wide(value, matrix):
     both = product(jnp.concatenate(split(value)), matrix)
     return both[: value.shape[0]] + both[value.shape[0] :]
+
+
+def make_core(right_hbm, sketch_hbm, core_ref, right, sketch, arrived):
+    copies = [
+        pltpu.make_async_copy(right_hbm, right, arrived.at[0]),
+        pltpu.make_async_copy(sketch_hbm, sketch, arrived.at[1]),
+    ]
+    for copy in copies:
+        copy.start()
+    for copy in copies:
+        copy.wait()
+    core_ref[...] = project(right[...], sketch[...]).astype(jnp.bfloat16)
 
 
 def make_applied(inverse_ref, right_ref, applied_ref):
@@ -112,16 +125,17 @@
         coupled_ref[member] = (moved + values_ref[member]).astype(jnp.bfloat16)
 
 
-def local(kernel, inputs, *outputs, scalar=False, aliases={}, cost=None):
-    specs = [SMEM] * scalar + [VMEM] * (len(inputs) - scalar)
+def local(kernel, inputs, *outputs, scalar=False, aliases={}, cost=None, scratch=()):
+    specs = [SMEM] * scalar + [HBM if scratch else VMEM] * (len(inputs) - scalar)
     return pl.pallas_call(
         kernel,
         in_specs=specs,
         out_specs=[VMEM] * len(outputs),
         out_shape=[jax.ShapeDtypeStruct(*output) for output in outputs],
+        scratch_shapes=scratch,
         input_output_aliases=aliases,
         cost_estimate=cost,
-        compiler_params=pltpu.CompilerParams(vmem_limit_bytes=16 * 2**20),
+        compiler_params=pltpu.CompilerParams(vmem_limit_bytes=(56 if scratch else 16) * 2**20),
     )(*inputs)
 
 
@@ -142,7 +156,17 @@
 
     lefts = [left_factors[0]] + [rotated(left_factors[0], "layer", k) for k in range(1, layers)]
     next_rows = shifted(row_basis, "row", -1)
-    core = project(right_factors[0], sketch).astype(half)
+    (core,) = local(
+        make_core,
+        (right_factors[0], sketch),
+        ((rank, rank), half),
+        scratch=(
+            pltpu.VMEM(sketch.shape, half),
+            pltpu.VMEM(sketch.shape, half),
+            pltpu.SemaphoreType.DMA((2,)),
+        ),
+        cost=pl.CostEstimate(flops=10**10, bytes_accessed=1, transcendentals=0),
+    )
     right_side, core = lax.optimization_barrier((right_side, core))
     cores = [core] + [rotated(core, "layer", k) for k in range(1, layers)]
     (applied,) = local(
@@ -151,7 +175,8 @@
         (right_side.shape, half),
         cost=pl.CostEstimate(flops=1, bytes_accessed=1, transcendentals=0),
     )
-    lefts[-1], applied = lax.optimization_barrier((lefts[-1], applied))
+    entry = lax.dynamic_slice_in_dim(incoming, lower * share, share, 1)
+    lefts[-1], applied, entry = lax.optimization_barrier((lefts[-1], applied, entry))
 
     (gain,) = local(
         lambda *refs: make_gain(layers, *refs),
@@ -161,9 +186,7 @@
     (sent,) = local(
         make_steps, (gain, applied, next_rows), ((lowers, rank + share, rank), half)
     )
-    incoming, sent = lax.optimization_barrier((incoming, sent))
     steps = exchanged(sent, near)
-    entry = lax.dynamic_slice_in_dim(incoming, lower * share, share, 1)
 
     place = upper.reshape(1)
     values, last = local(

time: 40.8 us -> 43.2 us (1.059)
  Pallas kernels: 5.42 us -> 9.4 us
  waiting for transfers between devices: 7.95 us -> 9.92 us
  local copies, waits for them, and re-layouts: 3.74 us -> 2.03 us
  matrix products: 2.62 us -> 1.41 us
  starting transfers between devices: 12.8 us -> 12.2 us
    pallas_call x6 -> x7, Pallas kernels: 5.42 us -> 9.4 us  [local(): pl.pallas_call(kernel, in_specs=specs, out_specs=[VMEM] * len(outputs), o...]
    dot_general x1 -> x0, matrix products: 1.21 us -> none  [project(): lax.dot_general(basis, vectors, (((0,), (0,)), ((), ())), preferred_eleme...]
    ppermute x2, waiting for transfers between devices: 0.01 us -> 1.07 us  [rotated(): lax.ppermute(value, axis, [(source, (source + steps) % count) for source...]
    all_to_all x1, waiting for transfers between devices: 6.57 us -> 7.48 us  [exchanged(): lax.all_to_all(blocks, 'row', 0, 0, axis_index_groups=members, tiled=True)]
    unnamed x8 -> x14, local copies, waits for them, and re-layouts: 2.82 us -> 1.94 us
    dynamic_slice x1, local copies, waits for them, and re-layouts: 0.91 us -> 0.08 us  [body(): entry = lax.dynamic_slice_in_dim(incoming, lower * share, share, 1)]
    all_to_all x1, starting transfers between devices: 4.82 us -> 4.25 us  [exchanged(): lax.all_to_all(blocks, 'row', 0, 0, axis_index_groups=members, tiled=True)]
  transfers between devices with their start and end apart: 5 -> 5, of which waited for: 2 -> 3; matrix products, arithmetic and copies ran while one was open for 5% -> 0% of each run, Pallas kernels for 7% -> 14%
where the time goes in v12:
time: 43.2 us; the launch traced here: 42.8 us
  starting transfers between devices  12.2 us (28%)
  waiting for transfers between devices  9.92 us (23%)
  Pallas kernels  9.4 us (22%)
  blocking collectives  7.73 us (18%)
  local copies, waits for them, and re-layouts  2.03 us (5%)
  matrix products  1.41 us (3%)
    pallas_call x7, Pallas kernels, local(): pl.pallas_call(kernel, in_specs=specs, out_specs=[VMEM] * len(outputs), o...  9.4 us
    all_to_all x1, blocking collectives, exchanged(): lax.all_to_all(blocks, 'row', 0, 0, axis_index_groups=members, tiled=True)  7.73 us
    all_to_all x1, waiting for transfers between devices, exchanged(): lax.all_to_all(blocks, 'row', 0, 0, axis_index_groups=members, tiled=True)  7.48 us
    ppermute x2, starting transfers between devices, shifted(): lax.ppermute(value, axis, [(source, source + steps) for source in range(l...  4.8 us
    all_to_all x1, starting transfers between devices, exchanged(): lax.all_to_all(blocks, 'row', 0, 0, axis_index_groups=members, tiled=True)  4.25 us
    ppermute x2, starting transfers between devices, rotated(): lax.ppermute(value, axis, [(source, (source + steps) % count) for source...  3.15 us
    unnamed x14, local copies, waits for them, and re-layouts  1.94 us
    dot_general x1, matrix products, body(): lax.dot_general(gain, coupled, FLIPPED, preferred_element_type=jnp.float32)  1.41 us
  transfers between devices with their start and end apart: 5, of which 3 were waited for; matrix products, arithmetic and copies ran while one was open for 0% of the time, Pallas kernels for 14%

profile of v12, /device:TPU:0, one launch (start us, length us, event | category | flops | bytes accessed | tf_op | source)
XLA Modules:
  0.0 42.8 jit_solution(17973835842435111003)
XLA Ops:
  0.0 0.0 copy-start
  0.0 2.9 %collective-permute-start = (bf16[1024,128]{1,0:T(8,128)(2,1)}, bf16[1024,128]{1,0:T(8,128)(2,1)}, u32[]{:S(2)}, u32[]{:S(2)}) collective-permute-start(bf16[1024,128]{1,0:T(8,128)(2,1)} %bitcast.6), channel_id=1, source_target_pairs={{0,16},{16,0},{1,17},{17,1},{2,18},{18,2},{3,19},{19,3},{4,20},{20... | collective-permute-start | bytes 786440 | tf_op jit(solution)/shard_map/ppermute | solution.py:17
  2.9 1.3 %collective-permute-start.2 = (bf16[1024,128]{1,0:T(8,128)(2,1)}, bf16[1024,128]{1,0:T(8,128)(2,1)}, u32[]{:S(2)}, u32[]{:S(2)}) collective-permute-start(bf16[1024,128]{1,0:T(8,128)(2,1)} %param.10), channel_id=1, source_target_pairs={{1,0},{2,1},{3,2},{4,3},{5,4},{6,5},{7,6},{8,7},{9,8},{10,9},{11,1... | collective-permute-start | bytes 786440 | tf_op jit(solution)/shard_map/ppermute | solution.py:12
  4.2 0.0 copy-start.1
  4.2 2.1 %shard_map.73.refs_2_ = bf16[128,128]{1,0:T(8,128)(2,1)} custom-call(bf16[1024,128]{1,0:T(8,128)(2,1)} %bitcast.9, bf16[1024,128]{1,0:T(8,128)(2,1)} %sketch_hbm.1), custom_call_target="tpu_custom_call" | custom-call | flops 10000000000 | bytes 1 | tf_op jit(solution)/shard_map/pallas_call | solution.py:130
  6.3 0.2 collective-permute-start.1
  6.5 0.1 constant_dynamic-slice_fusion.entry_ref
  6.6 0.0 copy-start.4
  6.7 1.2 %copy-done.4 = bf16[1024,512]{1,0:T(8,128)(2,1)S(1)} copy-done((bf16[1024,512]{1,0:T(8,128)(2,1)S(1)}, bf16[1024,512]{1,0:T(8,128)(2,1)}, u32[]{:S(2)}) %copy-start.4) | copy-done | bytes 1048600
  7.9 1.7 %shard_map.74.applied_ref = bf16[1024,512]{1,0:T(8,128)(2,1)S(1)} custom-call(bf16[1024,1024]{1,0:T(8,128)(2,1)S(1)} %copy-done.1, bf16[1024,512]{1,0:T(8,128)(2,1)S(1)} %copy-done.4), custom_call_target="tpu_custom_call" | custom-call | flops 1 | bytes 1 | tf_op jit(solution)/shard_map/pallas_call | solution.py:130
  9.6 0.0 collective-permute-done.refs_1_
  9.6 1.1 %collective-permute-done.1.refs_3_ = bf16[128,128]{1,0:T(8,128)(2,1)S(1)} collective-permute-done((bf16[128,128]{1,0:T(8,128)(2,1)}, bf16[128,128]{1,0:T(8,128)(2,1)S(1)}, u32[]{:S(2)}, u32[]{:S(2)}) %collective-permute-start.1) | collective-permute-done | bytes 32800 | tf_op jit(solution)/shard_map/ppermute | solution.py:17
  10.7 2.0 %shard_map.75.gain_ref = bf16[1024,128]{1,0:T(8,128)(2,1)S(1)} custom-call(bf16[1024,128]{1,0:T(8,128)(2,1)S(1)} %bitcast.7, bf16[1024,128]{1,0:T(8,128)(2,1)} %collective-permute-done.refs_1_, bf16[128,128]{1,0:T(8,128)(2,1)S(1)} %copy-done.6, bf16[128,128]{1,0:T(8,128)(2,1)S(1)} %collective-permute-done.1.refs_3_, bf16[1024,1024]{1,0:T(8,128)(2,1)S(1)} %copy-done.1), custom_call_target="tpu_custom_call" | custom-call | tf_op jit(solution)/shard_map/pallas_call | solution.py:130
  12.7 0.0 collective-permute-done.2.next_ref
  12.8 2.2 %shard_map.76 = bf16[8,192,128]{2,1,0:T(8,128)(2,1)} custom-call(bf16[1024,128]{1,0:T(8,128)(2,1)S(1)} %shard_map.75.gain_ref, bf16[1024,512]{1,0:T(8,128)(2,1)S(1)} %shard_map.74.applied_ref, bf16[1024,128]{1,0:T(8,128)(2,1)} %collective-permute-done.2.next_ref), custom_call_target="tpu_custom_call" | custom-call | tf_op jit(solution)/shard_map/pallas_call | solution.py:130
  15.0 0.7 %copy-done.2 = bf16[1024,128]{1,0:T(8,128)(2,1)} copy-done((bf16[1024,128]{1,0:T(8,128)(2,1)}, bf16[1024,128]{1,0:T(8,128)(2,1)S(1)}, u32[]{:S(2)}) %copy-start.2) | copy-done | bytes 262168
  15.7 4.2 %all-to-all-start = ((bf16[8,192,128]{2,1,0:T(8,128)(2,1)}), bf16[8,192,128]{2,1,0:T(8,128)(2,1)S(1)}, u32[]{:S(2)}, u32[]{:S(2)}) async-start(bf16[8,192,128]{2,1,0:T(8,128)(2,1)} %shard_map.76), calls=%async_computation | async-start | bytes 786432 | tf_op jit(solution)/shard_map/all_to_all | solution.py:143
  19.9 7.5 %all-to-all-done.steps_ref = bf16[8,192,128]{2,1,0:T(8,128)(2,1)S(1)} async-done(((bf16[8,192,128]{2,1,0:T(8,128)(2,1)}), bf16[8,192,128]{2,1,0:T(8,128)(2,1)S(1)}, u32[]{:S(2)}, u32[]{:S(2)}) %all-to-all-start) | async-done | bytes 393248 | tf_op jit(solution)/shard_map/all_to_all | solution.py:143
  27.4 1.1 %shard_map.77 = (f32[8,64,128]{2,1,0:T(8,128)S(1)}, bf16[64,128]{1,0:T(8,128)(2,1)S(1)}) custom-call(s32[1]{0:T(128)} %bitcast.2.upper_ref, bf16[8,192,128]{2,1,0:T(8,128)(2,1)S(1)} %all-to-all-done.steps_ref, f32[128,64]{1,0:T(8,128)S(1)} %constant_dynamic-slice_fusion.entry_ref), custom_call_target="tpu_custom_call" | custom-call | tf_op jit(solution)/shard_map/pallas_call | solution.py:130
  28.5 3.5 %collective-permute-start.3 = (bf16[64,128]{1,0:T(8,128)(2,1)S(1)}, bf16[64,128]{1,0:T(8,128)(2,1)S(1)}, u32[]{:S(2)}, u32[]{:S(2)}) collective-permute-start(bf16[64,128]{1,0:T(8,128)(2,1)S(1)} %get-tuple-element.20), channel_id=1, source_target_pairs={{0,8},{1,9},{2,10},{3,11},{4,12},{5,13},{6,14},{7,15},{16,24},{17,... | collective-permute-start | bytes 49160 | tf_op jit(solution)/shard_map/ppermute | solution.py:12
  32.1 1.4 %collective-permute-done.3.entered_ref = bf16[64,128]{1,0:T(8,128)(2,1)S(1)} collective-permute-done((bf16[64,128]{1,0:T(8,128)(2,1)S(1)}, bf16[64,128]{1,0:T(8,128)(2,1)S(1)}, u32[]{:S(2)}, u32[]{:S(2)}) %collective-permute-start.3) | collective-permute-done | bytes 16416 | tf_op jit(solution)/shard_map/ppermute | solution.py:12
  33.5 0.2 shard_map.79
  33.7 7.7 %all_to_all.10 = bf16[8,64,128]{2,1,0:T(8,128)(2,1)S(1)} all-to-all(bf16[8,64,128]{2,1,0:T(8,128)(2,1)S(1)} %shard_map.79), channel_id=1, replica_groups={{0,1,2,3,4,5,6,7},{8,9,10,11,12,13,14,15},{16,17,18,19,20,21,22,23},{24..., dimensions={0} | all-to-all | bytes 262144 | tf_op jit(solution)/shard_map/all_to_all | solution.py:143
  41.4 1.4 %subtract_convert_fusion = bf16[1024,512]{1,0:T(8,128)(2,1)} fusion(bf16[1024,512]{1,0:T(8,128)(2,1)S(1)} %shard_map.74.applied_ref, bf16[1024,128]{1,0:T(8,128)(2,1)S(1)} %copy-done.3, bf16[512,128]{1,0:T(8,128)(2,1)S(1)} %bitcast.8), kind=kOutput, calls=%fused_computation | convolution fusion | flops 135790592 | bytes 2490368 | tf_op jit(solution)/shard_map/dot_general | solution.py:211
  (10 shorter events, 0.1 us)
Async XLA Ops:
  0.0 6.5 %copy-start = (f32[128,512]{1,0:T(8,128)S(1)}, f32[128,512]{1,0:T(8,128)}, u32[]{:S(2)}) copy-start(f32[128,512]{1,0:T(8,128)} %param.13) | copy-start | bytes 786436
  0.0 9.6 %collective-permute-start = (bf16[1024,128]{1,0:T(8,128)(2,1)}, bf16[1024,128]{1,0:T(8,128)(2,1)}, u32[]{:S(2)}, u32[]{:S(2)}) collective-permute-start(bf16[1024,128]{1,0:T(8,128)(2,1)} %bitcast.6), channel_id=1, source_target_pairs={{0,16},{16,0},{1,17},{17,1},{2,18},{18,2},{3,19},{19,3},{4,20},{20... | collective-permute-start | bytes 786440 | tf_op jit(solution)/shard_map/ppermute | solution.py:17
  2.9 9.8 %collective-permute-start.2 = (bf16[1024,128]{1,0:T(8,128)(2,1)}, bf16[1024,128]{1,0:T(8,128)(2,1)}, u32[]{:S(2)}, u32[]{:S(2)}) collective-permute-start(bf16[1024,128]{1,0:T(8,128)(2,1)} %param.10), channel_id=1, source_target_pairs={{1,0},{2,1},{3,2},{4,3},{5,4},{6,5},{7,6},{8,7},{9,8},{10,9},{11,1... | collective-permute-start | bytes 786440 | tf_op jit(solution)/shard_map/ppermute | solution.py:12
  4.2 2.4 %copy-start.1 = (bf16[1024,1024]{1,0:T(8,128)(2,1)S(1)}, bf16[1024,1024]{1,0:T(8,128)(2,1)}, u32[]{:S(2)}) copy-start(bf16[1024,1024]{1,0:T(8,128)(2,1)} %refs_4_.1) | copy-start | bytes 6291460
  6.3 4.4 %collective-permute-start.1 = (bf16[128,128]{1,0:T(8,128)(2,1)}, bf16[128,128]{1,0:T(8,128)(2,1)S(1)}, u32[]{:S(2)}, u32[]{:S(2)}) collective-permute-start(bf16[128,128]{1,0:T(8,128)(2,1)} %shard_map.73.refs_2_), channel_id=1, source_target_pairs={{0,16},{16,0},{1,17},{17,1},{2,18},{18,2},{3,19},{19,3},{4,20},{20... | collective-permute-start | bytes 98312 | tf_op jit(solution)/shard_map/ppermute | solution.py:17
  6.6 1.2 %copy-start.4 = (bf16[1024,512]{1,0:T(8,128)(2,1)S(1)}, bf16[1024,512]{1,0:T(8,128)(2,1)}, u32[]{:S(2)}) copy-start(bf16[1024,512]{1,0:T(8,128)(2,1)} %right_ref) | copy-start | bytes 3145732
  7.9 2.8 %copy-start.5 = (bf16[1,1024,128]{2,1,0:T(8,128)(2,1)S(1)}, bf16[1,1024,128]{2,1,0:T(8,128)(2,1)}, u32[]{:S(2)}) copy-start(bf16[1,1024,128]{2,1,0:T(8,128)(2,1)} %param.7) | copy-start | bytes 786436
  7.9 2.8 %copy-start.6 = (bf16[128,128]{1,0:T(8,128)(2,1)S(1)}, bf16[128,128]{1,0:T(8,128)(2,1)}, u32[]{:S(2)}) copy-start(bf16[128,128]{1,0:T(8,128)(2,1)} %shard_map.73.refs_2_) | copy-start | bytes 98308
  15.0 0.7 %copy-start.2 = (bf16[1024,128]{1,0:T(8,128)(2,1)}, bf16[1024,128]{1,0:T(8,128)(2,1)S(1)}, u32[]{:S(2)}) copy-start(bf16[1024,128]{1,0:T(8,128)(2,1)S(1)} %shard_map.75.gain_ref) | copy-start | bytes 786436
  15.7 11.7 %all-to-all-start = ((bf16[8,192,128]{2,1,0:T(8,128)(2,1)}), bf16[8,192,128]{2,1,0:T(8,128)(2,1)S(1)}, u32[]{:S(2)}, u32[]{:S(2)}) async-start(bf16[8,192,128]{2,1,0:T(8,128)(2,1)} %shard_map.76), calls=%async_computation | async-start | bytes 786432 | tf_op jit(solution)/shard_map/all_to_all | solution.py:143
  19.9 21.5 %copy-start.3 = (bf16[1024,128]{1,0:T(8,128)(2,1)S(1)}, bf16[1024,128]{1,0:T(8,128)(2,1)}, u32[]{:S(2)}) copy-start(bf16[1024,128]{1,0:T(8,128)(2,1)} %copy-done.2) | copy-start | bytes 786436
  28.5 5.0 %collective-permute-start.3 = (bf16[64,128]{1,0:T(8,128)(2,1)S(1)}, bf16[64,128]{1,0:T(8,128)(2,1)S(1)}, u32[]{:S(2)}, u32[]{:S(2)}) collective-permute-start(bf16[64,128]{1,0:T(8,128)(2,1)S(1)} %get-tuple-element.20), channel_id=1, source_target_pairs={{0,8},{1,9},{2,10},{3,11},{4,12},{5,13},{6,14},{7,15},{16,24},{17,... | collective-permute-start | bytes 49160 | tf_op jit(solution)/shard_map/ppermute | solution.py:12

commit v13 on v9

--- a/solution.py
+++ b/solution.py
@@ -28,7 +28,9 @@
 
 
 SMEM = pl.BlockSpec(memory_space=pltpu.SMEM)
+HBM = pl.BlockSpec(memory_space=pltpu.HBM)
 VMEM = pl.BlockSpec(memory_space=pltpu.VMEM)
+PARTS = 4
 FLIPPED = (((1,), (1,)), ((), ()))
 
 
@@ -37,8 +39,9 @@
     return high, (value - high.astype(jnp.float32)).astype(jnp.bfloat16)
 
 
-def wide(value, matrix):
-    both = product(jnp.concatenate(split(value)), matrix)
+def wide(value, matrix, twice=False):
+    parts = jnp.concatenate(split(value))
+    both = product(jnp.concatenate([parts, parts], axis=1) if twice else parts, matrix)
     return both[: value.shape[0]] + both[value.shape[0] :]
 
 
@@ -62,22 +65,31 @@
     return state
 
 
-def first_half(upper_ref, steps_ref, entry_ref, values_ref, last_ref):
+def leave(upper_ref, steps_ref, entry_ref, last_ref):
+    count, _, rank = steps_ref.shape
+
     @pl.when(upper_ref[0] == 0)
     def _():
-        last_ref[...] = chain(steps_ref, entry_ref[...].T, values_ref).astype(jnp.bfloat16)
-
-
-def second_half(upper_ref, steps_ref, before_ref, values_ref, maps_ref):
+        pairs = [product(steps_ref[k], steps_ref[k + 1, :rank]) for k in range(0, count, 2)]
+        state = entry_ref[...].T
+        for index, pair in enumerate(pairs):
+            moved = wide(state, jnp.concatenate(split(pair[:rank])), twice=True)
+            shift = pair[rank:] + steps_ref[2 * index + 1, rank:].astype(jnp.float32)
+            state = moved + shift
+        last_ref[...] = state.astype(jnp.bfloat16)
+
+
+def compose(upper_ref, steps_ref, entry_ref, values_ref, maps_ref):
     count, rank, _ = maps_ref.shape
-
-    @pl.when(upper_ref[0] == 0)
+    first = upper_ref[0] == 0
+    chain(steps_ref, jnp.where(first, entry_ref[...].T, 0.0), values_ref)
+
+    @pl.when(first)
     def _():
         maps_ref[...] = jnp.zeros(maps_ref.shape, jnp.bfloat16)
 
-    @pl.when(upper_ref[0] > 0)
+    @pl.when(jnp.logical_not(first))
     def _():
-        chain(steps_ref, jnp.zeros(values_ref.shape[1:], jnp.float32), values_ref)
         state = steps_ref[0, :rank]
         for member in range(1, count):
             maps_ref[member] = state
@@ -93,14 +105,29 @@
         coupled_ref[member] = (moved + values_ref[member]).astype(jnp.bfloat16)
 
 
-def local(kernel, inputs, *outputs, scalar=False, aliases={}):
+def solve(gain_ref, coupled_ref, applied_ref, result_hbm, result, sent):
+    rows = gain_ref.shape[0] // PARTS
+    copies = []
+    for part in range(PARTS):
+        piece = pl.ds(part * rows, rows)
+        moved = lax.dot_general(
+            gain_ref[piece], coupled_ref[...], FLIPPED, preferred_element_type=jnp.float32
+        )
+        applied = applied_ref[piece].astype(jnp.float32)
+        result[piece] = (applied - moved).astype(jnp.bfloat16)
+        copies.append(pltpu.make_async_copy(result.at[piece], result_hbm.at[piece], sent.at[part]))
+        copies[-1].start()
+    for copy in copies:
+        copy.wait()
+
+
+def local(kernel, inputs, *outputs, scalar=False):
     specs = [SMEM] * scalar + [VMEM] * (len(inputs) - scalar)
     return pl.pallas_call(
         kernel,
         in_specs=specs,
         out_specs=[VMEM] * len(outputs),
         out_shape=[jax.ShapeDtypeStruct(*output) for output in outputs],
-        input_output_aliases=aliases,
         compiler_params=pltpu.CompilerParams(vmem_limit_bytes=16 * 2**20),
     )(*inputs)
 
@@ -143,27 +170,26 @@
     gain, entry, steps = lax.optimization_barrier((gain, entry, steps))
 
     place = upper.reshape(1)
-    values, last = local(
-        first_half,
-        (place, steps, entry),
-        ((lowers, share, rank), jnp.float32),
-        ((share, rank), half),
-        scalar=True,
-    )
+    (last,) = local(leave, (place, steps, entry), ((share, rank), half), scalar=True)
     entered = shifted(last, "row", lowers)
     steps, _ = lax.optimization_barrier((steps, last))
     values, maps = local(
-        second_half,
-        (place, steps, values),
+        compose,
+        (place, steps, entry),
         ((lowers, share, rank), jnp.float32),
         ((lowers, rank, rank), half),
         scalar=True,
-        aliases={2: 0},
     )
     (coupled,) = local(enter, (entered, maps, values), ((lowers, share, rank), half))
     coupled = exchanged(coupled, near).reshape(width, rank)
-    moved = lax.dot_general(gain, coupled, FLIPPED, preferred_element_type=jnp.float32)
-    return (applied.astype(jnp.float32) - moved).astype(half)
+    return pl.pallas_call(
+        solve,
+        in_specs=[VMEM] * 3,
+        out_specs=HBM,
+        out_shape=jax.ShapeDtypeStruct(applied.shape, half),
+        scratch_shapes=[pltpu.VMEM(applied.shape, half), pltpu.SemaphoreType.DMA((PARTS,))],
+        compiler_params=pltpu.CompilerParams(vmem_limit_bytes=16 * 2**20),
+    )(gain, coupled, applied)
 
 
 def solution(mesh):

time: 40.3 us -> 43.8 us (1.087)
  local copies, waits for them, and re-layouts: 0.94 us -> 6.25 us
  waiting for transfers between devices: 7.78 us -> 4.1 us
  Pallas kernels: 2.64 us -> 3.67 us
    unnamed x12 -> x22, local copies, waits for them, and re-layouts: 0.03 us -> 4.69 us
    all_to_all x1, waiting for transfers between devices: 3.5 us -> 1.18 us  [exchanged(): lax.all_to_all(blocks, 'row', 0, 0, axis_index_groups=members, tiled=True)]
    dot_general x3, matrix products: 5.52 us -> 7.22 us  [product(): return jnp.dot(a, b, preferred_element_type=jnp.float32)]
    dot_general x1 -> x0, matrix products: 1.43 us -> none  [body(): lax.dot_general(gain, coupled, FLIPPED, preferred_element_type=jnp.float32)]
    ppermute x2, waiting for transfers between devices: 1.37 us -> 0.01 us  [shifted(): lax.ppermute(value, axis, [(source, source + steps) for source in range(l...]
    pallas_call x0 -> x1, Pallas kernels: none -> 1.23 us  [body(): pl.pallas_call(solve, in_specs=[VMEM] * 3, out_specs=HBM, out_shape=jax.S...]
    dynamic_slice x1, local copies, waits for them, and re-layouts: 0.91 us -> 1.56 us  [body(): entry = lax.dynamic_slice_in_dim(incoming, lower * share, share, 1)]
  transfers between devices with their start and end apart: 5 -> 5, of which waited for: 4 -> 3; matrix products, arithmetic and copies ran while one was open for 19% -> 23% of each run, Pallas kernels for 0% -> 2%
where the time goes in v13:
time: 43.8 us; the launch traced here: 43.3 us
  starting transfers between devices  12.7 us (29%)
  matrix products  8.45 us (19%)
  blocking collectives  8.01 us (18%)
  local copies, waits for them, and re-layouts  6.25 us (14%)
  waiting for transfers between devices  4.1 us (9%)
  Pallas kernels  3.67 us (8%)
    all_to_all x1, blocking collectives, exchanged(): lax.all_to_all(blocks, 'row', 0, 0, axis_index_groups=members, tiled=True)  8.01 us
    dot_general x3, matrix products, product(): return jnp.dot(a, b, preferred_element_type=jnp.float32)  7.22 us
    ppermute x2, starting transfers between devices, shifted(): lax.ppermute(value, axis, [(source, source + steps) for source in range(l...  4.9 us
    unnamed x22, local copies, waits for them, and re-layouts  4.69 us
    all_to_all x1, starting transfers between devices, exchanged(): lax.all_to_all(blocks, 'row', 0, 0, axis_index_groups=members, tiled=True)  4.5 us
    ppermute x2, starting transfers between devices, rotated(): lax.ppermute(value, axis, [(source, (source + steps) % count) for source...  3.28 us
    ppermute x2, waiting for transfers between devices, rotated(): lax.ppermute(value, axis, [(source, (source + steps) % count) for source...  2.92 us
    pallas_call x4, Pallas kernels, local(): pl.pallas_call(kernel, in_specs=specs, out_specs=[VMEM] * len(outputs), o...  2.45 us
  transfers between devices with their start and end apart: 5, of which 3 were waited for; matrix products, arithmetic and copies ran while one was open for 23% of the time, Pallas kernels for 2%

profile of v13, /device:TPU:0, one launch (start us, length us, event | category | flops | bytes accessed | tf_op | source)
XLA Modules:
  0.0 43.3 jit_solution(4999553802624590950)
XLA Ops:
  0.0 3.0 %collective-permute-start = (bf16[1024,128]{1,0:T(8,128)(2,1)}, bf16[1024,128]{1,0:T(8,128)(2,1)S(1)}, u32[]{:S(2)}, u32[]{:S(2)}) collective-permute-start(bf16[1024,128]{1,0:T(8,128)(2,1)} %bitcast.22), channel_id=1, source_target_pairs={{0,16},{16,0},{1,17},{17,1},{2,18},{18,2},{3,19},{19,3},{4,20},{20... | collective-permute-start | bytes 786440 | tf_op jit(solution)/shard_map/ppermute | solution.py:17
  3.0 1.3 %collective-permute-start.1 = (bf16[1024,128]{1,0:T(8,128)(2,1)}, bf16[1024,128]{1,0:T(8,128)(2,1)S(1)}, u32[]{:S(2)}, u32[]{:S(2)}) collective-permute-start(bf16[1024,128]{1,0:T(8,128)(2,1)} %param.10), channel_id=1, source_target_pairs={{1,0},{2,1},{3,2},{4,3},{5,4},{6,5},{7,6},{8,7},{9,8},{10,9},{11,1... | collective-permute-start | bytes 786440 | tf_op jit(solution)/shard_map/ppermute | solution.py:12
  4.3 2.5 %convolution_convert_fusion.applied_ref = bf16[1024,512]{1,0:T(8,128)(2,1)S(1)} fusion(bf16[1024,1024]{1,0:T(8,128)(2,1)S(1)} %copy-done, bf16[1024,512]{1,0:T(8,128)(2,1)} %param.12), kind=kOutput, calls=%fused_computation | convolution fusion | flops 1074266112 | bytes 4194304 | tf_op jit(solution)/shard_map/dot_general | solution.py:27
  7.4 0.5 %fusion.4.refs_4_ = f32[128,1024]{1,0:T(8,128)S(1)} fusion(bf16[1024,128]{1,0:T(8,128)(2,1)S(1)} %collective-permute-done.1, bf16[1024,1024]{1,0:T(8,128)(2,1)S(1)} %copy-done), kind=kOutput, calls=%fused_computation.10 | convolution fusion | flops 268435456 | bytes 2883584 | tf_op jit(solution)/shard_map/dot_general | solution.py:21
  7.9 0.5 %convolution_convert_fusion.2 = bf16[512,128]{1,0:T(8,128)(2,1)S(1)} fusion(bf16[1024,512]{1,0:T(8,128)(2,1)S(1)} %convolution_convert_fusion.applied_ref, bf16[1024,128]{1,0:T(8,128)(2,1)S(1)} %collective-permute-done.1), kind=kOutput, calls=%fused_computation.6 | convolution fusion | flops 134283264 | bytes 1441792 | tf_op jit(solution)/shard_map/dot_general | solution.py:21
  8.4 1.2 %collective-permute-done.refs_1_ = bf16[1024,128]{1,0:T(8,128)(2,1)S(1)} collective-permute-done((bf16[1024,128]{1,0:T(8,128)(2,1)}, bf16[1024,128]{1,0:T(8,128)(2,1)S(1)}, u32[]{:S(2)}, u32[]{:S(2)}) %collective-permute-start) | collective-permute-done | bytes 262176 | tf_op jit(solution)/shard_map/ppermute | solution.py:17
  9.5 1.7 %collective-permute-done.2.refs_3_ = bf16[128,128]{1,0:T(8,128)(2,1)S(1)} collective-permute-done((bf16[128,128]{1,0:T(8,128)(2,1)S(1)}, bf16[128,128]{1,0:T(8,128)(2,1)S(1)}, u32[]{:S(2)}, u32[]{:S(2)}) %collective-permute-start.2) | collective-permute-done | bytes 32800 | tf_op jit(solution)/shard_map/ppermute | solution.py:17
  11.3 0.6 %shard_map.73 = bf16[8,192,128]{2,1,0:T(8,128)(2,1)S(1)} custom-call(bf16[1024,128]{1,0:T(8,128)(2,1)S(1)} %bitcast.24, bf16[1024,128]{1,0:T(8,128)(2,1)S(1)} %collective-permute-done.refs_1_, bf16[128,128]{1,0:T(8,128)(2,1)S(1)} %bitcast.28, bf16[128,128]{1,0:T(8,128)(2,1)S(1)} %collective-permute-done.2.refs_3_, f32[128,1024]{1,0:T(8,128)S(1)} %fusion.4.refs_4_, ...), custom_call_target="tpu_custom_call" | custom-call | tf_op jit(solution)/shard_map/pallas_call | solution.py:126
  11.9 0.7 %copy-done.1 = bf16[8,192,128]{2,1,0:T(8,128)(2,1)} copy-done((bf16[8,192,128]{2,1,0:T(8,128)(2,1)}, bf16[8,192,128]{2,1,0:T(8,128)(2,1)S(1)}, u32[]{:S(2)}) %copy-start.1) | copy-done | bytes 393240
  12.6 0.7 %copy-done.3 = bf16[1024,128]{1,0:T(8,128)(2,1)} copy-done((bf16[1024,128]{1,0:T(8,128)(2,1)}, bf16[1024,128]{1,0:T(8,128)(2,1)S(1)}, u32[]{:S(2)}) %copy-start.3) | copy-done | bytes 262168
  13.3 0.6 %copy-done.8 = bf16[128,128]{1,0:T(8,128)(2,1)} copy-done((bf16[128,128]{1,0:T(8,128)(2,1)}, bf16[128,128]{1,0:T(8,128)(2,1)S(1)}, u32[]{:S(2)}) %copy-start.8) | copy-done | bytes 32792
  13.9 4.5 %all-to-all-start = ((bf16[8,192,128]{2,1,0:T(8,128)(2,1)}), bf16[8,192,128]{2,1,0:T(8,128)(2,1)S(1)}, u32[]{:S(2)}, u32[]{:S(2)}) async-start(bf16[8,192,128]{2,1,0:T(8,128)(2,1)} %copy-done.1), calls=%async_computation | async-start | bytes 786432 | tf_op jit(solution)/shard_map/all_to_all | solution.py:136
  18.4 1.6 %constant_dynamic-slice_fusion.entry_ref = f32[128,64]{1,0:T(8,128)} fusion(f32[128,512]{1,0:T(8,128)} %param.13, s32[]{:T(128)S(6)} %select_n.3), kind=kLoop, calls=%fused_computation.9 | loop fusion | bytes 65540 | tf_op jit(solution)/shard_map/dynamic_slice | solution.py:167
  20.0 2.0 %fusion.5 = f32[1024,128]{1,0:T(8,128)} fusion(bf16[1024,128]{1,0:T(8,128)(2,1)} %copy-done.3, bf16[128,128]{1,0:T(8,128)(2,1)} %copy-done.8), kind=kOutput, calls=%fused_computation.11 | convolution fusion | flops 33554432 | bytes 819200 | tf_op jit(solution)/shard_map/dot_general | solution.py:27
  21.9 2.8 %fusion.2.gain_ref = bf16[1024,128]{1,0:T(8,128)(2,1)} fusion(bf16[1024,1024]{1,0:T(8,128)(2,1)S(1)} %copy-done, f32[1024,128]{1,0:T(8,128)} %fusion.5, bf16[1024,128]{1,0:T(8,128)(2,1)} %bitcast.23, bf16[128,128]{0,1:T(8,128)(2,1)} %copy-done.7), kind=kOutput, calls=%fused_computation.5 | convolution fusion | flops 302514176 | bytes 3178496 | tf_op jit(solution)/shard_map/dot_general | solution.py:27
  24.7 1.2 %all-to-all-done.steps_ref = bf16[8,192,128]{2,1,0:T(8,128)(2,1)S(1)} async-done(((bf16[8,192,128]{2,1,0:T(8,128)(2,1)}), bf16[8,192,128]{2,1,0:T(8,128)(2,1)S(1)}, u32[]{:S(2)}, u32[]{:S(2)}) %all-to-all-start) | async-done | bytes 393248 | tf_op jit(solution)/shard_map/all_to_all | solution.py:136
  25.9 0.8 %copy-done.5 = f32[128,64]{1,0:T(8,128)S(1)} copy-done((f32[128,64]{1,0:T(8,128)S(1)}, f32[128,64]{1,0:T(8,128)}, u32[]{:S(2)}) %copy-start.5) | copy-done | bytes 32792
  26.7 0.7 %shard_map.74 = bf16[64,128]{1,0:T(8,128)(2,1)S(1)} custom-call(s32[1]{0:T(128)} %bitcast.5.upper_ref, bf16[8,192,128]{2,1,0:T(8,128)(2,1)S(1)} %all-to-all-done.steps_ref, f32[128,64]{1,0:T(8,128)S(1)} %copy-done.5), custom_call_target="tpu_custom_call" | custom-call | tf_op jit(solution)/shard_map/pallas_call | solution.py:126
  27.5 3.6 %collective-permute-start.3 = (bf16[64,128]{1,0:T(8,128)(2,1)S(1)}, bf16[64,128]{1,0:T(8,128)(2,1)S(1)}, u32[]{:S(2)}, u32[]{:S(2)}) collective-permute-start(bf16[64,128]{1,0:T(8,128)(2,1)S(1)} %shard_map.74), channel_id=1, source_target_pairs={{0,8},{1,9},{2,10},{3,11},{4,12},{5,13},{6,14},{7,15},{16,24},{17,... | collective-permute-start | bytes 49160 | tf_op jit(solution)/shard_map/ppermute | solution.py:12
  31.1 0.8 %copy-done.6 = f32[128,64]{1,0:T(8,128)S(1)} copy-done((f32[128,64]{1,0:T(8,128)S(1)}, f32[128,64]{1,0:T(8,128)}, u32[]{:S(2)}) %copy-start.6) | copy-done | bytes 32792
  31.9 1.0 %shard_map.75 = (f32[8,64,128]{2,1,0:T(8,128)S(1)}, bf16[8,128,128]{2,1,0:T(8,128)(2,1)S(1)}) custom-call(s32[1]{0:T(128)} %bitcast.5.upper_ref, bf16[8,192,128]{2,1,0:T(8,128)(2,1)S(1)} %all-to-all-done.steps_ref, f32[128,64]{1,0:T(8,128)S(1)} %copy-done.6), custom_call_target="tpu_custom_call" | custom-call | tf_op jit(solution)/shard_map/pallas_call | solution.py:126
  33.1 8.0 %all_to_all.10 = bf16[8,64,128]{2,1,0:T(8,128)(2,1)S(1)} all-to-all(bf16[8,64,128]{2,1,0:T(8,128)(2,1)S(1)} %shard_map.76), channel_id=1, replica_groups={{0,1,2,3,4,5,6,7},{8,9,10,11,12,13,14,15},{16,17,18,19,20,21,22,23},{24..., dimensions={0} | all-to-all | bytes 262144 | tf_op jit(solution)/shard_map/all_to_all | solution.py:136
  41.1 0.9 %copy-done.4 = bf16[1024,128]{1,0:T(8,128)(2,1)S(1)} copy-done((bf16[1024,128]{1,0:T(8,128)(2,1)S(1)}, bf16[1024,128]{1,0:T(8,128)(2,1)}, u32[]{:S(2)}) %copy-start.4) | copy-done | bytes 262168
  42.1 1.2 %shard_map.77 = bf16[1024,512]{1,0:T(8,128)(2,1)} custom-call(bf16[1024,128]{1,0:T(8,128)(2,1)S(1)} %copy-done.4, bf16[512,128]{1,0:T(8,128)(2,1)S(1)} %bitcast.25, bf16[1024,512]{1,0:T(8,128)(2,1)S(1)} %convolution_convert_fusion.applied_ref), custom_call_target="tpu_custom_call" | custom-call | tf_op jit(solution)/shard_map/pallas_call | solution.py:185
  (21 shorter events, 0.8 us)
Async XLA Ops:
  0.0 4.3 %copy-start = (bf16[1024,1024]{1,0:T(8,128)(2,1)S(1)}, bf16[1024,1024]{1,0:T(8,128)(2,1)}, u32[]{:S(2)}) copy-start(bf16[1024,1024]{1,0:T(8,128)(2,1)} %param.11) | copy-start | bytes 6291460
  0.0 6.8 %copy-start.9 = (bf16[1024,128]{1,0:T(8,128)(2,1)S(1)}, bf16[1024,128]{1,0:T(8,128)(2,1)}, u32[]{:S(2)}) copy-start(bf16[1024,128]{1,0:T(8,128)(2,1)} %param.9) | copy-start | bytes 786436
  0.0 6.8 %copy-start.10 = (bf16[1,1024,128]{2,1,0:T(8,128)(2,1)S(1)}, bf16[1,1024,128]{2,1,0:T(8,128)(2,1)}, u32[]{:S(2)}) copy-start(bf16[1,1024,128]{2,1,0:T(8,128)(2,1)} %param.8) | copy-start | bytes 786436
  0.0 9.5 %collective-permute-start = (bf16[1024,128]{1,0:T(8,128)(2,1)}, bf16[1024,128]{1,0:T(8,128)(2,1)S(1)}, u32[]{:S(2)}, u32[]{:S(2)}) collective-permute-start(bf16[1024,128]{1,0:T(8,128)(2,1)} %bitcast.22), channel_id=1, source_target_pairs={{0,16},{16,0},{1,17},{17,1},{2,18},{18,2},{3,19},{19,3},{4,20},{20... | collective-permute-start | bytes 786440 | tf_op jit(solution)/shard_map/ppermute | solution.py:17
  3.0 4.4 %collective-permute-start.1 = (bf16[1024,128]{1,0:T(8,128)(2,1)}, bf16[1024,128]{1,0:T(8,128)(2,1)S(1)}, u32[]{:S(2)}, u32[]{:S(2)}) collective-permute-start(bf16[1024,128]{1,0:T(8,128)(2,1)} %param.10), channel_id=1, source_target_pairs={{1,0},{2,1},{3,2},{4,3},{5,4},{6,5},{7,6},{8,7},{9,8},{10,9},{11,1... | collective-permute-start | bytes 786440 | tf_op jit(solution)/shard_map/ppermute | solution.py:12
  7.1 4.2 %copy-start.7 = (bf16[128,128]{0,1:T(8,128)(2,1)}, bf16[128,128]{0,1:T(8,128)(2,1)S(1)}, u32[]{:S(2)}) copy-start(bf16[128,128]{0,1:T(8,128)(2,1)S(1)} %convolution_convert_fusion.3) | copy-start | bytes 98308
  7.1 4.2 %copy-start.2 = (bf16[1,1024,128]{2,1,0:T(8,128)(2,1)S(1)}, bf16[1,1024,128]{2,1,0:T(8,128)(2,1)}, u32[]{:S(2)}) copy-start(bf16[1,1024,128]{2,1,0:T(8,128)(2,1)} %param.7) | copy-start | bytes 786436
  7.1 4.2 %collective-permute-start.2 = (bf16[128,128]{1,0:T(8,128)(2,1)S(1)}, bf16[128,128]{1,0:T(8,128)(2,1)S(1)}, u32[]{:S(2)}, u32[]{:S(2)}) collective-permute-start(bf16[128,128]{1,0:T(8,128)(2,1)S(1)} %bitcast.27), channel_id=1, source_target_pairs={{0,16},{16,0},{1,17},{17,1},{2,18},{18,2},{3,19},{19,3},{4,20},{20... | collective-permute-start | bytes 98312 | tf_op jit(solution)/shard_map/ppermute | solution.py:17
  11.9 0.8 %copy-start.1 = (bf16[8,192,128]{2,1,0:T(8,128)(2,1)}, bf16[8,192,128]{2,1,0:T(8,128)(2,1)S(1)}, u32[]{:S(2)}) copy-start(bf16[8,192,128]{2,1,0:T(8,128)(2,1)S(1)} %shard_map.73) | copy-start | bytes 1179652
  12.6 0.7 %copy-start.3 = (bf16[1024,128]{1,0:T(8,128)(2,1)}, bf16[1024,128]{1,0:T(8,128)(2,1)S(1)}, u32[]{:S(2)}) copy-start(bf16[1024,128]{1,0:T(8,128)(2,1)S(1)} %collective-permute-done.refs_1_) | copy-start | bytes 786436
  13.3 0.6 %copy-start.8 = (bf16[128,128]{1,0:T(8,128)(2,1)}, bf16[128,128]{1,0:T(8,128)(2,1)S(1)}, u32[]{:S(2)}) copy-start(bf16[128,128]{1,0:T(8,128)(2,1)S(1)} %collective-permute-done.2.refs_3_) | copy-start | bytes 98308
  13.9 12.0 %all-to-all-start = ((bf16[8,192,128]{2,1,0:T(8,128)(2,1)}), bf16[8,192,128]{2,1,0:T(8,128)(2,1)S(1)}, u32[]{:S(2)}, u32[]{:S(2)}) async-start(bf16[8,192,128]{2,1,0:T(8,128)(2,1)} %copy-done.1), calls=%async_computation | async-start | bytes 786432 | tf_op jit(solution)/shard_map/all_to_all | solution.py:136
  25.9 0.8 %copy-start.5 = (f32[128,64]{1,0:T(8,128)S(1)}, f32[128,64]{1,0:T(8,128)}, u32[]{:S(2)}) copy-start(f32[128,64]{1,0:T(8,128)} %constant_dynamic-slice_fusion.entry_ref) | copy-start | bytes 98308
  27.5 5.4 %collective-permute-start.3 = (bf16[64,128]{1,0:T(8,128)(2,1)S(1)}, bf16[64,128]{1,0:T(8,128)(2,1)S(1)}, u32[]{:S(2)}, u32[]{:S(2)}) collective-permute-start(bf16[64,128]{1,0:T(8,128)(2,1)S(1)} %shard_map.74), channel_id=1, source_target_pairs={{0,8},{1,9},{2,10},{3,11},{4,12},{5,13},{6,14},{7,15},{16,24},{17,... | collective-permute-start | bytes 49160 | tf_op jit(solution)/shard_map/ppermute | solution.py:12
  31.1 0.8 %copy-start.6 = (f32[128,64]{1,0:T(8,128)S(1)}, f32[128,64]{1,0:T(8,128)}, u32[]{:S(2)}) copy-start(f32[128,64]{1,0:T(8,128)} %constant_dynamic-slice_fusion.entry_ref) | copy-start | bytes 98308
  41.1 1.0 %copy-start.4 = (bf16[1024,128]{1,0:T(8,128)(2,1)S(1)}, bf16[1024,128]{1,0:T(8,128)(2,1)}, u32[]{:S(2)}) copy-start(bf16[1024,128]{1,0:T(8,128)(2,1)} %fusion.2.gain_ref) | copy-start | bytes 786436

commit v14 on v13

--- a/solution.py
+++ b/solution.py
@@ -28,9 +28,7 @@
 
 
 SMEM = pl.BlockSpec(memory_space=pltpu.SMEM)
-HBM = pl.BlockSpec(memory_space=pltpu.HBM)
 VMEM = pl.BlockSpec(memory_space=pltpu.VMEM)
-PARTS = 4
 FLIPPED = (((1,), (1,)), ((), ()))
 
 
@@ -54,6 +52,14 @@
     for target in range(sent_ref.shape[0]):
         sent_ref[target, :rank] = map_t
         sent_ref[target, rank:] = shift_ref[target]
+
+
+def make_gain(layers, *refs):
+    lefts = jnp.concatenate([ref[...] for ref in refs[:layers]], axis=1)
+    cores = jnp.concatenate([ref[...] for ref in refs[layers : 2 * layers]], axis=0)
+    inverse_ref, gain_ref = refs[2 * layers :]
+    tile_range = (-product(lefts, cores)).astype(jnp.bfloat16)
+    gain_ref[...] = product(inverse_ref[...], tile_range).astype(jnp.bfloat16)
 
 
 def chain(steps_ref, state, values_ref):
@@ -105,22 +111,6 @@
         coupled_ref[member] = (moved + values_ref[member]).astype(jnp.bfloat16)
 
 
-def solve(gain_ref, coupled_ref, applied_ref, result_hbm, result, sent):
-    rows = gain_ref.shape[0] // PARTS
-    copies = []
-    for part in range(PARTS):
-        piece = pl.ds(part * rows, rows)
-        moved = lax.dot_general(
-            gain_ref[piece], coupled_ref[...], FLIPPED, preferred_element_type=jnp.float32
-        )
-        applied = applied_ref[piece].astype(jnp.float32)
-        result[piece] = (applied - moved).astype(jnp.bfloat16)
-        copies.append(pltpu.make_async_copy(result.at[piece], result_hbm.at[piece], sent.at[part]))
-        copies[-1].start()
-    for copy in copies:
-        copy.wait()
-
-
 def local(kernel, inputs, *outputs, scalar=False):
     specs = [SMEM] * scalar + [VMEM] * (len(inputs) - scalar)
     return pl.pallas_call(
@@ -138,7 +128,7 @@
 
 def body(left_factors, right_factors, sketch, row_basis, inverse_diag, right_side, incoming):
     half = jnp.bfloat16
-    rank = sketch.shape[1]
+    order, rank = sketch.shape
     width = right_side.shape[1]
     layers, groups = lax.axis_size("layer"), lax.axis_size("row")
     lowers = groups // 2
@@ -156,23 +146,21 @@
 
     shift_t = project(applied, next_rows).astype(half).reshape(lowers, share, rank)
     weights = project(next_rows, inverse_diag)
-    lefts[-1], shift_t, weights = lax.optimization_barrier((lefts[-1], shift_t, weights))
+    entry = lax.dynamic_slice_in_dim(incoming, lower * share, share, 1)
+    lefts[-1], shift_t, weights, entry = lax.optimization_barrier(
+        (lefts[-1], shift_t, weights, entry)
+    )
     (sent,) = local(
         lambda *refs: make_maps(layers, *refs),
         (*lefts, *cores, weights, shift_t),
         ((lowers, rank + share, rank), half),
     )
-    lefts, incoming, sent = lax.optimization_barrier((lefts, incoming, sent))
     steps = exchanged(sent, near)
-    entry = lax.dynamic_slice_in_dim(incoming, lower * share, share, 1)
-    tile_range = -sum(product(left, core) for left, core in zip(lefts, cores))
-    gain = product(inverse_diag, tile_range.astype(half)).astype(half)
-    gain, entry, steps = lax.optimization_barrier((gain, entry, steps))
 
     place = upper.reshape(1)
     (last,) = local(leave, (place, steps, entry), ((share, rank), half), scalar=True)
     entered = shifted(last, "row", lowers)
-    steps, _ = lax.optimization_barrier((steps, last))
+    steps, lefts, _ = lax.optimization_barrier((steps, lefts, last))
     values, maps = local(
         compose,
         (place, steps, entry),
@@ -180,16 +168,16 @@
         ((lowers, rank, rank), half),
         scalar=True,
     )
+    (gain,) = local(
+        lambda *refs: make_gain(layers, *refs),
+        (*lefts, *cores, inverse_diag),
+        ((order, rank), half),
+    )
+    gain, maps = lax.optimization_barrier((gain, maps))
     (coupled,) = local(enter, (entered, maps, values), ((lowers, share, rank), half))
     coupled = exchanged(coupled, near).reshape(width, rank)
-    return pl.pallas_call(
-        solve,
-        in_specs=[VMEM] * 3,
-        out_specs=HBM,
-        out_shape=jax.ShapeDtypeStruct(applied.shape, half),
-        scratch_shapes=[pltpu.VMEM(applied.shape, half), pltpu.SemaphoreType.DMA((PARTS,))],
-        compiler_params=pltpu.CompilerParams(vmem_limit_bytes=16 * 2**20),
-    )(gain, coupled, applied)
+    moved = lax.dot_general(gain, coupled, FLIPPED, preferred_element_type=jnp.float32)
+    return (applied.astype(jnp.float32) - moved).astype(half)
 
 
 def solution(mesh):

time: 43.8 us -> 49.2 us (1.12)
  waiting for transfers between devices: 4.1 us -> 7.49 us
  local copies, waits for them, and re-layouts: 6.25 us -> 7.49 us
  starting transfers between devices: 12.7 us -> 13.7 us
    all_to_all x1, waiting for transfers between devices: 1.18 us -> 7.48 us  [exchanged(): lax.all_to_all(blocks, 'row', 0, 0, axis_index_groups=members, tiled=True)]
    dot_general x3 -> x1, matrix products: 7.22 us -> 3.81 us  [product(): return jnp.dot(a, b, preferred_element_type=jnp.float32)]
    ppermute x2, waiting for transfers between devices: 2.92 us -> 0.01 us  [rotated(): lax.ppermute(value, axis, [(source, (source + steps) % count) for source...]
    dot_general x3, matrix products: 1.23 us -> 3.16 us  [project(): lax.dot_general(basis, vectors, (((0,), (0,)), ((), ())), preferred_eleme...]
    dot_general x0 -> x1, matrix products: none -> 1.41 us  [body(): lax.dot_general(gain, coupled, FLIPPED, preferred_element_type=jnp.float32)]
    pallas_call x1 -> x0, Pallas kernels: 1.23 us -> none  [body(): pl.pallas_call(solve, in_specs=[VMEM] * 3, out_specs=HBM, out_shape=jax.S...]
    unnamed x22 -> x34, local copies, waits for them, and re-layouts: 4.69 us -> 5.86 us
    pallas_call x4 -> x5, Pallas kernels: 2.45 us -> 3.53 us  [local(): pl.pallas_call(kernel, in_specs=specs, out_specs=[VMEM] * len(outputs), o...]
  transfers between devices with their start and end apart: 5 -> 5, of which waited for: 3 -> 1; matrix products, arithmetic and copies ran while one was open for 23% -> 18% of each run, Pallas kernels for 2% -> 4%
where the time goes in v14:
time: 49.2 us; the launch traced here: 48.5 us
  starting transfers between devices  13.7 us (28%)
  matrix products  8.38 us (17%)
  blocking collectives  7.72 us (16%)
  local copies, waits for them, and re-layouts  7.49 us (15%)
  waiting for transfers between devices  7.49 us (15%)
  Pallas kernels  3.53 us (7%)
    all_to_all x1, blocking collectives, exchanged(): lax.all_to_all(blocks, 'row', 0, 0, axis_index_groups=members, tiled=True)  7.72 us
    all_to_all x1, waiting for transfers between devices, exchanged(): lax.all_to_all(blocks, 'row', 0, 0, axis_index_groups=members, tiled=True)  7.48 us
    unnamed x34, local copies, waits for them, and re-layouts  5.86 us
    ppermute x2, starting transfers between devices, shifted(): lax.ppermute(value, axis, [(source, source + steps) for source in range(l...  5.52 us
    all_to_all x1, starting transfers between devices, exchanged(): lax.all_to_all(blocks, 'row', 0, 0, axis_index_groups=members, tiled=True)  4.82 us
    dot_general x1, matrix products, product(): return jnp.dot(a, b, preferred_element_type=jnp.float32)  3.81 us
    pallas_call x5, Pallas kernels, local(): pl.pallas_call(kernel, in_specs=specs, out_specs=[VMEM] * len(outputs), o...  3.53 us
    ppermute x2, starting transfers between devices, rotated(): lax.ppermute(value, axis, [(source, (source + steps) % count) for source...  3.38 us
  transfers between devices with their start and end apart: 5, of which 1 were waited for; matrix products, arithmetic and copies ran while one was open for 18% of the time, Pallas kernels for 4%

profile of v14, /device:TPU:0, one launch (start us, length us, event | category | flops | bytes accessed | tf_op | source)
XLA Modules:
  0.0 48.5 jit_solution(17222199747575258196)
XLA Ops:
  0.0 3.0 %collective-permute-start = (bf16[1024,128]{1,0:T(8,128)(2,1)}, bf16[1024,128]{1,0:T(8,128)(2,1)S(1)}, u32[]{:S(2)}, u32[]{:S(2)}) collective-permute-start(bf16[1024,128]{1,0:T(8,128)(2,1)} %bitcast.18), channel_id=1, source_target_pairs={{0,16},{16,0},{1,17},{17,1},{2,18},{18,2},{3,19},{19,3},{4,20},{20... | collective-permute-start | bytes 786440 | tf_op jit(solution)/shard_map/ppermute | solution.py:17
  3.0 1.3 %collective-permute-start.1 = (bf16[1024,128]{1,0:T(8,128)(2,1)}, bf16[1024,128]{1,0:T(8,128)(2,1)}, u32[]{:S(2)}, u32[]{:S(2)}) collective-permute-start(bf16[1024,128]{1,0:T(8,128)(2,1)} %param.10), channel_id=1, source_target_pairs={{1,0},{2,1},{3,2},{4,3},{5,4},{6,5},{7,6},{8,7},{9,8},{10,9},{11,1... | collective-permute-start | bytes 786440 | tf_op jit(solution)/shard_map/ppermute | solution.py:12
  4.3 3.8 %convolution_convert_fusion = bf16[1024,512]{1,0:T(8,128)(2,1)} fusion(bf16[1024,1024]{1,0:T(8,128)(2,1)} %refs_4_.1, bf16[1024,512]{1,0:T(8,128)(2,1)S(1)} %copy-done), kind=kOutput, calls=%fused_computation.1 | convolution fusion | flops 1074266112 | bytes 4194304 | tf_op jit(solution)/shard_map/dot_general | solution.py:27
  8.1 0.3 fusion.refs_2_
  8.4 0.4 collective-permute-start.2
  8.8 1.6 %constant_dynamic-slice_fusion.entry_ref = f32[128,64]{1,0:T(8,128)} fusion(f32[128,512]{1,0:T(8,128)} %param.13, s32[]{:T(128)S(6)} %select_n.3), kind=kLoop, calls=%fused_computation.6 | loop fusion | bytes 65540 | tf_op jit(solution)/shard_map/dynamic_slice | solution.py:149
  10.4 1.5 %fusion.2.refs_4_ = f32[128,1024]{1,0:T(8,128)S(1)} fusion(bf16[1024,128]{1,0:T(8,128)(2,1)} %collective-permute-done.1, bf16[1024,1024]{1,0:T(8,128)(2,1)S(1)} %copy-done.1), kind=kOutput, calls=%fused_computation.7 | convolution fusion | flops 268435456 | bytes 2883584 | tf_op jit(solution)/shard_map/dot_general | solution.py:21
  11.9 1.4 %convolution_convert_fusion.1 = bf16[512,128]{1,0:T(8,128)(2,1)S(1)} fusion(bf16[1024,512]{1,0:T(8,128)(2,1)S(1)} %copy-done.13, bf16[1024,128]{1,0:T(8,128)(2,1)} %collective-permute-done.1), kind=kOutput, calls=%fused_computation.2 | convolution fusion | flops 134283264 | bytes 1441792 | tf_op jit(solution)/shard_map/dot_general | solution.py:21
  13.4 0.6 %shard_map.73 = bf16[8,192,128]{2,1,0:T(8,128)(2,1)S(1)} custom-call(bf16[1024,128]{1,0:T(8,128)(2,1)S(1)} %bitcast.19, bf16[1024,128]{1,0:T(8,128)(2,1)S(1)} %collective-permute-done.refs_1_, bf16[128,128]{1,0:T(8,128)(2,1)S(1)} %fusion.refs_2_, bf16[128,128]{1,0:T(8,128)(2,1)S(1)} %collective-permute-done.2.refs_3_, f32[128,1024]{1,0:T(8,128)S(1)} %fusion.2.refs_4_, ...), custom_call_target="tpu_custom_call" | custom-call | tf_op jit(solution)/shard_map/pallas_call | solution.py:116
  14.0 0.7 %copy-done.2 = bf16[8,192,128]{2,1,0:T(8,128)(2,1)} copy-done((bf16[8,192,128]{2,1,0:T(8,128)(2,1)}, bf16[8,192,128]{2,1,0:T(8,128)(2,1)S(1)}, u32[]{:S(2)}) %copy-start.2) | copy-done | bytes 393240
  14.7 4.8 %all-to-all-start = ((bf16[8,192,128]{2,1,0:T(8,128)(2,1)}), bf16[8,192,128]{2,1,0:T(8,128)(2,1)S(1)}, u32[]{:S(2)}, u32[]{:S(2)}) async-start(bf16[8,192,128]{2,1,0:T(8,128)(2,1)} %copy-done.2), calls=%async_computation | async-start | bytes 786432 | tf_op jit(solution)/shard_map/all_to_all | solution.py:126
  19.6 7.5 %all-to-all-done.steps_ref = bf16[8,192,128]{2,1,0:T(8,128)(2,1)S(1)} async-done(((bf16[8,192,128]{2,1,0:T(8,128)(2,1)}), bf16[8,192,128]{2,1,0:T(8,128)(2,1)S(1)}, u32[]{:S(2)}, u32[]{:S(2)}) %all-to-all-start) | async-done | bytes 393248 | tf_op jit(solution)/shard_map/all_to_all | solution.py:126
  27.0 0.8 %copy-done.7 = f32[128,64]{1,0:T(8,128)S(1)} copy-done((f32[128,64]{1,0:T(8,128)S(1)}, f32[128,64]{1,0:T(8,128)}, u32[]{:S(2)}) %copy-start.7) | copy-done | bytes 32792
  27.9 0.7 %shard_map.74 = bf16[64,128]{1,0:T(8,128)(2,1)S(1)} custom-call(s32[1]{0:T(128)} %bitcast.4.upper_ref, bf16[8,192,128]{2,1,0:T(8,128)(2,1)S(1)} %all-to-all-done.steps_ref, f32[128,64]{1,0:T(8,128)S(1)} %copy-done.7), custom_call_target="tpu_custom_call" | custom-call | tf_op jit(solution)/shard_map/pallas_call | solution.py:116
  28.6 4.2 %collective-permute-start.3 = (bf16[64,128]{1,0:T(8,128)(2,1)S(1)}, bf16[64,128]{1,0:T(8,128)(2,1)S(1)}, u32[]{:S(2)}, u32[]{:S(2)}) collective-permute-start(bf16[64,128]{1,0:T(8,128)(2,1)S(1)} %shard_map.74), channel_id=1, source_target_pairs={{0,8},{1,9},{2,10},{3,11},{4,12},{5,13},{6,14},{7,15},{16,24},{17,... | collective-permute-start | bytes 49160 | tf_op jit(solution)/shard_map/ppermute | solution.py:12
  32.9 0.8 %copy-done.8 = f32[128,64]{1,0:T(8,128)S(1)} copy-done((f32[128,64]{1,0:T(8,128)S(1)}, f32[128,64]{1,0:T(8,128)}, u32[]{:S(2)}) %copy-start.8) | copy-done | bytes 32792
  33.7 1.0 %shard_map.76 = (f32[8,64,128]{2,1,0:T(8,128)S(1)}, bf16[8,128,128]{2,1,0:T(8,128)(2,1)S(1)}) custom-call(s32[1]{0:T(128)} %bitcast.4.upper_ref, bf16[8,192,128]{2,1,0:T(8,128)(2,1)S(1)} %all-to-all-done.steps_ref, f32[128,64]{1,0:T(8,128)S(1)} %copy-done.8), custom_call_target="tpu_custom_call" | custom-call | tf_op jit(solution)/shard_map/pallas_call | solution.py:116
  34.7 0.9 %copy-done.4 = bf16[1,1024,128]{2,1,0:T(8,128)(2,1)S(1)} copy-done((bf16[1,1024,128]{2,1,0:T(8,128)(2,1)S(1)}, bf16[1,1024,128]{2,1,0:T(8,128)(2,1)}, u32[]{:S(2)}) %copy-start.4) | copy-done | bytes 262168
  35.6 0.9 %copy-done.6 = bf16[1024,128]{1,0:T(8,128)(2,1)S(1)} copy-done((bf16[1024,128]{1,0:T(8,128)(2,1)S(1)}, bf16[1024,128]{1,0:T(8,128)(2,1)}, u32[]{:S(2)}) %copy-start.6) | copy-done | bytes 262168
  36.6 0.8 %copy-done.10 = bf16[128,128]{1,0:T(8,128)(2,1)S(1)} copy-done((bf16[128,128]{1,0:T(8,128)(2,1)S(1)}, bf16[128,128]{1,0:T(8,128)(2,1)}, u32[]{:S(2)}) %copy-start.10) | copy-done | bytes 32792
  37.3 0.8 %copy-done.12 = bf16[128,128]{1,0:T(8,128)(2,1)S(1)} copy-done((bf16[128,128]{1,0:T(8,128)(2,1)S(1)}, bf16[128,128]{1,0:T(8,128)(2,1)}, u32[]{:S(2)}) %copy-start.12) | copy-done | bytes 32792
  38.1 1.1 %shard_map.75 = bf16[1024,128]{1,0:T(8,128)(2,1)S(1)} custom-call(bf16[1024,128]{1,0:T(8,128)(2,1)S(1)} %bitcast.20, bf16[1024,128]{1,0:T(8,128)(2,1)S(1)} %copy-done.6, bf16[128,128]{1,0:T(8,128)(2,1)S(1)} %copy-done.10, bf16[128,128]{1,0:T(8,128)(2,1)S(1)} %copy-done.12, bf16[1024,1024]{1,0:T(8,128)(2,1)S(1)} %copy-done.1), custom_call_target="tpu_custom_call" | custom-call | tf_op jit(solution)/shard_map/pallas_call | solution.py:116
  39.4 7.7 %all_to_all.10 = bf16[8,64,128]{2,1,0:T(8,128)(2,1)S(1)} all-to-all(bf16[8,64,128]{2,1,0:T(8,128)(2,1)S(1)} %shard_map.77), channel_id=1, replica_groups={{0,1,2,3,4,5,6,7},{8,9,10,11,12,13,14,15},{16,17,18,19,20,21,22,23},{24..., dimensions={0} | all-to-all | bytes 262144 | tf_op jit(solution)/shard_map/all_to_all | solution.py:126
  47.1 1.4 %subtract_convert_fusion = bf16[1024,512]{1,0:T(8,128)(2,1)} fusion(bf16[1024,512]{1,0:T(8,128)(2,1)S(1)} %copy-done.14, bf16[1024,128]{1,0:T(8,128)(2,1)S(1)} %shard_map.75, bf16[512,128]{1,0:T(8,128)(2,1)S(1)} %bitcast.22), kind=kOutput, calls=%fused_computation | convolution fusion | flops 135790592 | bytes 2490368 | tf_op jit(solution)/shard_map/dot_general | solution.py:179
  (32 shorter events, 0.3 us)
Async XLA Ops:
  0.0 4.3 %copy-start = (bf16[1024,512]{1,0:T(8,128)(2,1)S(1)}, bf16[1024,512]{1,0:T(8,128)(2,1)}, u32[]{:S(2)}) copy-start(bf16[1024,512]{1,0:T(8,128)(2,1)} %param.12) | copy-start | bytes 3145732
  0.0 8.1 %copy-start.15 = (bf16[1024,128]{1,0:T(8,128)(2,1)S(1)}, bf16[1024,128]{1,0:T(8,128)(2,1)}, u32[]{:S(2)}) copy-start(bf16[1024,128]{1,0:T(8,128)(2,1)} %param.9) | copy-start | bytes 786436
  0.0 8.1 %copy-start.16 = (bf16[1,1024,128]{2,1,0:T(8,128)(2,1)S(1)}, bf16[1,1024,128]{2,1,0:T(8,128)(2,1)}, u32[]{:S(2)}) copy-start(bf16[1,1024,128]{2,1,0:T(8,128)(2,1)} %param.8) | copy-start | bytes 786436
  0.0 10.4 %copy-start.1 = (bf16[1024,1024]{1,0:T(8,128)(2,1)S(1)}, bf16[1024,1024]{1,0:T(8,128)(2,1)}, u32[]{:S(2)}) copy-start(bf16[1024,1024]{1,0:T(8,128)(2,1)} %refs_4_.1) | copy-start | bytes 6291460
  0.0 13.3 %collective-permute-start = (bf16[1024,128]{1,0:T(8,128)(2,1)}, bf16[1024,128]{1,0:T(8,128)(2,1)S(1)}, u32[]{:S(2)}, u32[]{:S(2)}) collective-permute-start(bf16[1024,128]{1,0:T(8,128)(2,1)} %bitcast.18), channel_id=1, source_target_pairs={{0,16},{16,0},{1,17},{17,1},{2,18},{18,2},{3,19},{19,3},{4,20},{20... | collective-permute-start | bytes 786440 | tf_op jit(solution)/shard_map/ppermute | solution.py:17
  3.0 7.4 %collective-permute-start.1 = (bf16[1024,128]{1,0:T(8,128)(2,1)}, bf16[1024,128]{1,0:T(8,128)(2,1)}, u32[]{:S(2)}, u32[]{:S(2)}) collective-permute-start(bf16[1024,128]{1,0:T(8,128)(2,1)} %param.10), channel_id=1, source_target_pairs={{1,0},{2,1},{3,2},{4,3},{5,4},{6,5},{7,6},{8,7},{9,8},{10,9},{11,1... | collective-permute-start | bytes 786440 | tf_op jit(solution)/shard_map/ppermute | solution.py:12
  8.4 5.0 %copy-start.9 = (bf16[128,128]{1,0:T(8,128)(2,1)}, bf16[128,128]{1,0:T(8,128)(2,1)S(1)}, u32[]{:S(2)}) copy-start(bf16[128,128]{1,0:T(8,128)(2,1)S(1)} %fusion.refs_2_) | copy-start | bytes 98308
  8.4 4.9 %collective-permute-start.2 = (bf16[128,128]{1,0:T(8,128)(2,1)S(1)}, bf16[128,128]{1,0:T(8,128)(2,1)S(1)}, u32[]{:S(2)}, u32[]{:S(2)}) collective-permute-start(bf16[128,128]{1,0:T(8,128)(2,1)S(1)} %fusion.refs_2_), channel_id=1, source_target_pairs={{0,16},{16,0},{1,17},{17,1},{2,18},{18,2},{3,19},{19,3},{4,20},{20... | collective-permute-start | bytes 98312 | tf_op jit(solution)/shard_map/ppermute | solution.py:17
  8.8 3.1 %copy-start.13 = (bf16[1024,512]{1,0:T(8,128)(2,1)S(1)}, bf16[1024,512]{1,0:T(8,128)(2,1)}, u32[]{:S(2)}) copy-start(bf16[1024,512]{1,0:T(8,128)(2,1)} %convolution_convert_fusion) | copy-start | bytes 3145732
  10.4 3.0 %copy-start.3 = (bf16[1,1024,128]{2,1,0:T(8,128)(2,1)S(1)}, bf16[1,1024,128]{2,1,0:T(8,128)(2,1)}, u32[]{:S(2)}) copy-start(bf16[1,1024,128]{2,1,0:T(8,128)(2,1)} %param.7) | copy-start | bytes 786436
  13.4 1.4 %copy-start.5 = (bf16[1024,128]{1,0:T(8,128)(2,1)}, bf16[1024,128]{1,0:T(8,128)(2,1)S(1)}, u32[]{:S(2)}) copy-start(bf16[1024,128]{1,0:T(8,128)(2,1)S(1)} %collective-permute-done.refs_1_) | copy-start | bytes 786436
  13.4 1.3 %copy-start.11 = (bf16[128,128]{1,0:T(8,128)(2,1)}, bf16[128,128]{1,0:T(8,128)(2,1)S(1)}, u32[]{:S(2)}) copy-start(bf16[128,128]{1,0:T(8,128)(2,1)S(1)} %collective-permute-done.2.refs_3_) | copy-start | bytes 98308
  14.0 0.7 %copy-start.2 = (bf16[8,192,128]{2,1,0:T(8,128)(2,1)}, bf16[8,192,128]{2,1,0:T(8,128)(2,1)S(1)}, u32[]{:S(2)}) copy-start(bf16[8,192,128]{2,1,0:T(8,128)(2,1)S(1)} %shard_map.73) | copy-start | bytes 1179652
  14.7 12.3 %all-to-all-start = ((bf16[8,192,128]{2,1,0:T(8,128)(2,1)}), bf16[8,192,128]{2,1,0:T(8,128)(2,1)S(1)}, u32[]{:S(2)}, u32[]{:S(2)}) async-start(bf16[8,192,128]{2,1,0:T(8,128)(2,1)} %copy-done.2), calls=%async_computation | async-start | bytes 786432 | tf_op jit(solution)/shard_map/all_to_all | solution.py:126
  27.0 0.8 %copy-start.7 = (f32[128,64]{1,0:T(8,128)S(1)}, f32[128,64]{1,0:T(8,128)}, u32[]{:S(2)}) copy-start(f32[128,64]{1,0:T(8,128)} %constant_dynamic-slice_fusion.entry_ref) | copy-start | bytes 98308
  28.6 10.6 %collective-permute-start.3 = (bf16[64,128]{1,0:T(8,128)(2,1)S(1)}, bf16[64,128]{1,0:T(8,128)(2,1)S(1)}, u32[]{:S(2)}, u32[]{:S(2)}) collective-permute-start(bf16[64,128]{1,0:T(8,128)(2,1)S(1)} %shard_map.74), channel_id=1, source_target_pairs={{0,8},{1,9},{2,10},{3,11},{4,12},{5,13},{6,14},{7,15},{16,24},{17,... | collective-permute-start | bytes 49160 | tf_op jit(solution)/shard_map/ppermute | solution.py:12
  32.9 0.8 %copy-start.8 = (f32[128,64]{1,0:T(8,128)S(1)}, f32[128,64]{1,0:T(8,128)}, u32[]{:S(2)}) copy-start(f32[128,64]{1,0:T(8,128)} %constant_dynamic-slice_fusion.entry_ref) | copy-start | bytes 98308
  34.7 1.0 %copy-start.4 = (bf16[1,1024,128]{2,1,0:T(8,128)(2,1)S(1)}, bf16[1,1024,128]{2,1,0:T(8,128)(2,1)}, u32[]{:S(2)}) copy-start(bf16[1,1024,128]{2,1,0:T(8,128)(2,1)} %param.7) | copy-start | bytes 786436
  35.6 0.9 %copy-start.6 = (bf16[1024,128]{1,0:T(8,128)(2,1)S(1)}, bf16[1024,128]{1,0:T(8,128)(2,1)}, u32[]{:S(2)}) copy-start(bf16[1024,128]{1,0:T(8,128)(2,1)} %copy-done.5) | copy-start | bytes 786436
  36.6 0.8 %copy-start.10 = (bf16[128,128]{1,0:T(8,128)(2,1)S(1)}, bf16[128,128]{1,0:T(8,128)(2,1)}, u32[]{:S(2)}) copy-start(bf16[128,128]{1,0:T(8,128)(2,1)} %copy-done.9) | copy-start | bytes 98308
  37.3 0.8 %copy-start.12 = (bf16[128,128]{1,0:T(8,128)(2,1)S(1)}, bf16[128,128]{1,0:T(8,128)(2,1)}, u32[]{:S(2)}) copy-start(bf16[128,128]{1,0:T(8,128)(2,1)} %copy-done.11) | copy-start | bytes 98308
  38.1 9.0 %copy-start.14 = (bf16[1024,512]{1,0:T(8,128)(2,1)S(1)}, bf16[1024,512]{1,0:T(8,128)(2,1)}, u32[]{:S(2)}) copy-start(bf16[1024,512]{1,0:T(8,128)(2,1)} %convolution_convert_fusion) | copy-start | bytes 3145732

commit v15 on v14

--- a/solution.py
+++ b/solution.py
@@ -147,17 +147,22 @@
     shift_t = project(applied, next_rows).astype(half).reshape(lowers, share, rank)
     weights = project(next_rows, inverse_diag)
     entry = lax.dynamic_slice_in_dim(incoming, lower * share, share, 1)
-    lefts[-1], shift_t, weights, entry = lax.optimization_barrier(
-        (lefts[-1], shift_t, weights, entry)
+    place = upper.reshape(1)
+    lefts[-1], shift_t, weights, entry, place = lax.optimization_barrier(
+        (lefts[-1], shift_t, weights, entry, place)
     )
     (sent,) = local(
         lambda *refs: make_maps(layers, *refs),
         (*lefts, *cores, weights, shift_t),
         ((lowers, rank + share, rank), half),
     )
+    sent, lefts, cores, entry, place, applied, inverse_diag = lax.optimization_barrier(
+        (sent, lefts, cores, entry, place, applied, inverse_diag)
+    )
     steps = exchanged(sent, near)
-
-    place = upper.reshape(1)
+    steps, lefts, cores, entry, place, applied, inverse_diag = lax.optimization_barrier(
+        (steps, lefts, cores, entry, place, applied, inverse_diag)
+    )
     (last,) = local(leave, (place, steps, entry), ((share, rank), half), scalar=True)
     entered = shifted(last, "row", lowers)
     steps, lefts, _ = lax.optimization_barrier((steps, lefts, last))

time: 49.2 us -> 42.6 us (0.87)
  blocking collectives: 7.72 us -> 20.4 us
  waiting for transfers between devices: 7.49 us -> 0.01 us
  local copies, waits for them, and re-layouts: 7.49 us -> 1.03 us
  starting transfers between devices: 13.7 us -> 8.72 us
    all_to_all x1 -> x2, blocking collectives: 7.72 us -> 20.4 us  [exchanged(): lax.all_to_all(blocks, 'row', 0, 0, axis_index_groups=members, tiled=True)]
    all_to_all x1 -> x0, waiting for transfers between devices: 7.48 us -> none  [exchanged(): lax.all_to_all(blocks, 'row', 0, 0, axis_index_groups=members, tiled=True)]
    unnamed x34 -> x12, local copies, waits for them, and re-layouts: 5.86 us -> 0.02 us
    all_to_all x1 -> x0, starting transfers between devices: 4.82 us -> none  [exchanged(): lax.all_to_all(blocks, 'row', 0, 0, axis_index_groups=members, tiled=True)]
    dynamic_slice x1, local copies, waits for them, and re-layouts: 1.63 us -> 1 us  [body(): entry = lax.dynamic_slice_in_dim(incoming, lower * share, share, 1)]
  transfers between devices with their start and end apart: 5 -> 4, of which waited for: 1 -> 0; matrix products, arithmetic and copies ran while one was open for 18% -> 19% of each run, Pallas kernels for 4% -> 5%
where the time goes in v15:
time: 42.6 us; the launch traced here: 42.3 us
  blocking collectives  20.4 us (48%)
  starting transfers between devices  8.72 us (20%)
  matrix products  8.38 us (20%)
  Pallas kernels  3.53 us (8%)
  local copies, waits for them, and re-layouts  1.03 us (2%)
    all_to_all x2, blocking collectives, exchanged(): lax.all_to_all(blocks, 'row', 0, 0, axis_index_groups=members, tiled=True)  20.4 us
    ppermute x2, starting transfers between devices, shifted(): lax.ppermute(value, axis, [(source, source + steps) for source in range(l...  5.34 us
    dot_general x1, matrix products, product(): return jnp.dot(a, b, preferred_element_type=jnp.float32)  3.81 us
    pallas_call x5, Pallas kernels, local(): pl.pallas_call(kernel, in_specs=specs, out_specs=[VMEM] * len(outputs), o...  3.53 us
    ppermute x2, starting transfers between devices, rotated(): lax.ppermute(value, axis, [(source, (source + steps) % count) for source...  3.38 us
    dot_general x3, matrix products, project(): lax.dot_general(basis, vectors, (((0,), (0,)), ((), ())), preferred_eleme...  3.17 us
    dot_general x1, matrix products, body(): lax.dot_general(gain, coupled, FLIPPED, preferred_element_type=jnp.float32)  1.41 us
    dynamic_slice x1, local copies, waits for them, and re-layouts, body(): entry = lax.dynamic_slice_in_dim(incoming, lower * share, share, 1)  1 us
  transfers between devices with their start and end apart: 4, of which 0 were waited for; matrix products, arithmetic and copies ran while one was open for 19% of the time, Pallas kernels for 5%

profile of v15, /device:TPU:0, one launch (start us, length us, event | category | flops | bytes accessed | tf_op | source)
XLA Modules:
  0.0 42.3 jit_solution(2328220203654069149)
XLA Ops:
  0.0 0.0 copy-start
  0.0 3.0 %collective-permute-start = (bf16[1024,128]{1,0:T(8,128)(2,1)}, bf16[1024,128]{1,0:T(8,128)(2,1)S(1)}, u32[]{:S(2)}, u32[]{:S(2)}) collective-permute-start(bf16[1024,128]{1,0:T(8,128)(2,1)} %bitcast.18), channel_id=1, source_target_pairs={{0,16},{16,0},{1,17},{17,1},{2,18},{18,2},{3,19},{19,3},{4,20},{20... | collective-permute-start | bytes 786440 | tf_op jit(solution)/shard_map/ppermute | solution.py:17
  3.0 1.3 %collective-permute-start.1 = (bf16[1024,128]{1,0:T(8,128)(2,1)}, bf16[1024,128]{1,0:T(8,128)(2,1)}, u32[]{:S(2)}, u32[]{:S(2)}) collective-permute-start(bf16[1024,128]{1,0:T(8,128)(2,1)} %param.10), channel_id=1, source_target_pairs={{1,0},{2,1},{3,2},{4,3},{5,4},{6,5},{7,6},{8,7},{9,8},{10,9},{11,1... | collective-permute-start | bytes 786440 | tf_op jit(solution)/shard_map/ppermute | solution.py:12
  4.3 0.0 copy-done
  4.3 3.8 %convolution_convert_fusion = bf16[1024,512]{1,0:T(8,128)(2,1)} fusion(bf16[1024,1024]{1,0:T(8,128)(2,1)} %refs_4_, bf16[1024,512]{1,0:T(8,128)(2,1)S(1)} %copy-done), kind=kOutput, calls=%fused_computation.1 | convolution fusion | flops 1074266112 | bytes 4194304 | tf_op jit(solution)/shard_map/dot_general | solution.py:27
  8.1 0.0 copy-done.4
  8.1 0.3 fusion.refs_2_
  8.4 0.4 collective-permute-start.2
  8.8 1.0 %constant_dynamic-slice_fusion.entry_ref = f32[128,64]{1,0:T(8,128)S(1)} fusion(f32[128,512]{1,0:T(8,128)} %param.13, s32[]{:T(128)S(6)} %select_n.3), kind=kLoop, calls=%fused_computation.6 | loop fusion | bytes 65540 | tf_op jit(solution)/shard_map/dynamic_slice | solution.py:149
  9.8 0.0 collective-permute-done.1
  9.8 1.5 %fusion.2.refs_4_ = f32[128,1024]{1,0:T(8,128)S(1)} fusion(bf16[1024,128]{1,0:T(8,128)(2,1)} %collective-permute-done.1, bf16[1024,1024]{1,0:T(8,128)(2,1)S(1)} %copy-done.1), kind=kOutput, calls=%fused_computation.7 | convolution fusion | flops 268435456 | bytes 2883584 | tf_op jit(solution)/shard_map/dot_general | solution.py:21
  11.3 1.4 %convolution_convert_fusion.1 = bf16[512,128]{1,0:T(8,128)(2,1)S(1)} fusion(bf16[1024,512]{1,0:T(8,128)(2,1)S(1)} %copy-done.3, bf16[1024,128]{1,0:T(8,128)(2,1)} %collective-permute-done.1), kind=kOutput, calls=%fused_computation.2 | convolution fusion | flops 134283264 | bytes 1441792 | tf_op jit(solution)/shard_map/dot_general | solution.py:21
  12.7 0.0 collective-permute-done.refs_1_
  12.7 0.0 collective-permute-done.2.refs_3_
  12.8 0.6 %shard_map.73 = bf16[8,192,128]{2,1,0:T(8,128)(2,1)S(1)} custom-call(bf16[1024,128]{1,0:T(8,128)(2,1)S(1)} %bitcast.19, bf16[1024,128]{1,0:T(8,128)(2,1)S(1)} %collective-permute-done.refs_1_, bf16[128,128]{1,0:T(8,128)(2,1)S(1)} %fusion.refs_2_, bf16[128,128]{1,0:T(8,128)(2,1)S(1)} %collective-permute-done.2.refs_3_, f32[128,1024]{1,0:T(8,128)S(1)} %fusion.2.refs_4_, ...), custom_call_target="tpu_custom_call" | custom-call | tf_op jit(solution)/shard_map/pallas_call | solution.py:116
  13.3 12.9 %all_to_all.10.steps_ref = bf16[8,192,128]{2,1,0:T(8,128)(2,1)S(1)} all-to-all(bf16[8,192,128]{2,1,0:T(8,128)(2,1)S(1)} %shard_map.73), channel_id=1, replica_groups={{0,1,2,3,4,5,6,7},{8,9,10,11,12,13,14,15},{16,17,18,19,20,21,22,23},{24..., dimensions={0} | all-to-all | bytes 786432 | tf_op jit(solution)/shard_map/all_to_all | solution.py:126
  26.2 0.7 %shard_map.74 = bf16[64,128]{1,0:T(8,128)(2,1)S(1)} custom-call(s32[1]{0:T(128)} %bitcast.2.upper_ref, bf16[8,192,128]{2,1,0:T(8,128)(2,1)S(1)} %all_to_all.10.steps_ref, f32[128,64]{1,0:T(8,128)S(1)} %constant_dynamic-slice_fusion.entry_ref), custom_call_target="tpu_custom_call" | custom-call | tf_op jit(solution)/shard_map/pallas_call | solution.py:116
  26.9 4.1 %collective-permute-start.3 = (bf16[64,128]{1,0:T(8,128)(2,1)S(1)}, bf16[64,128]{1,0:T(8,128)(2,1)S(1)}, u32[]{:S(2)}, u32[]{:S(2)}) collective-permute-start(bf16[64,128]{1,0:T(8,128)(2,1)S(1)} %shard_map.74), channel_id=1, source_target_pairs={{0,8},{1,9},{2,10},{3,11},{4,12},{5,13},{6,14},{7,15},{16,24},{17,... | collective-permute-start | bytes 49160 | tf_op jit(solution)/shard_map/ppermute | solution.py:12
  31.0 1.0 %shard_map.76 = (f32[8,64,128]{2,1,0:T(8,128)S(1)}, bf16[8,128,128]{2,1,0:T(8,128)(2,1)S(1)}) custom-call(s32[1]{0:T(128)} %bitcast.2.upper_ref, bf16[8,192,128]{2,1,0:T(8,128)(2,1)S(1)} %all_to_all.10.steps_ref, f32[128,64]{1,0:T(8,128)S(1)} %constant_dynamic-slice_fusion.entry_ref), custom_call_target="tpu_custom_call" | custom-call | tf_op jit(solution)/shard_map/pallas_call | solution.py:116
  32.0 1.1 %shard_map.75 = bf16[1024,128]{1,0:T(8,128)(2,1)S(1)} custom-call(bf16[1024,128]{1,0:T(8,128)(2,1)S(1)} %bitcast.20, bf16[1024,128]{1,0:T(8,128)(2,1)S(1)} %collective-permute-done.refs_1_, bf16[128,128]{1,0:T(8,128)(2,1)S(1)} %fusion.refs_2_, bf16[128,128]{1,0:T(8,128)(2,1)S(1)} %collective-permute-done.2.refs_3_, bf16[1024,1024]{1,0:T(8,128)(2,1)S(1)} %copy-done.1), custom_call_target="tpu_custom_call" | custom-call | tf_op jit(solution)/shard_map/pallas_call | solution.py:116
  33.1 0.0 collective-permute-done.3.entered_ref
  33.1 0.2 shard_map.77
  33.3 7.6 %all_to_all.11 = bf16[8,64,128]{2,1,0:T(8,128)(2,1)S(1)} all-to-all(bf16[8,64,128]{2,1,0:T(8,128)(2,1)S(1)} %shard_map.77), channel_id=1, replica_groups={{0,1,2,3,4,5,6,7},{8,9,10,11,12,13,14,15},{16,17,18,19,20,21,22,23},{24..., dimensions={0} | all-to-all | bytes 262144 | tf_op jit(solution)/shard_map/all_to_all | solution.py:126
  40.8 1.4 %subtract_convert_fusion = bf16[1024,512]{1,0:T(8,128)(2,1)} fusion(bf16[1024,512]{1,0:T(8,128)(2,1)S(1)} %copy-done.3, bf16[1024,128]{1,0:T(8,128)(2,1)S(1)} %shard_map.75, bf16[512,128]{1,0:T(8,128)(2,1)S(1)} %bitcast.22), kind=kOutput, calls=%fused_computation | convolution fusion | flops 135790592 | bytes 2490368 | tf_op jit(solution)/shard_map/dot_general | solution.py:184
  (9 shorter events, 0.0 us)
Async XLA Ops:
  0.0 4.3 %copy-start = (bf16[1024,512]{1,0:T(8,128)(2,1)S(1)}, bf16[1024,512]{1,0:T(8,128)(2,1)}, u32[]{:S(2)}) copy-start(bf16[1024,512]{1,0:T(8,128)(2,1)} %param.12) | copy-start | bytes 3145732
  0.0 8.1 %copy-start.4 = (bf16[1024,128]{1,0:T(8,128)(2,1)S(1)}, bf16[1024,128]{1,0:T(8,128)(2,1)}, u32[]{:S(2)}) copy-start(bf16[1024,128]{1,0:T(8,128)(2,1)} %param.9) | copy-start | bytes 786436
  0.0 8.1 %copy-start.5 = (bf16[1,1024,128]{2,1,0:T(8,128)(2,1)S(1)}, bf16[1,1024,128]{2,1,0:T(8,128)(2,1)}, u32[]{:S(2)}) copy-start(bf16[1,1024,128]{2,1,0:T(8,128)(2,1)} %param.8) | copy-start | bytes 786436
  0.0 9.8 %copy-start.1 = (bf16[1024,1024]{1,0:T(8,128)(2,1)S(1)}, bf16[1024,1024]{1,0:T(8,128)(2,1)}, u32[]{:S(2)}) copy-start(bf16[1024,1024]{1,0:T(8,128)(2,1)} %refs_4_) | copy-start | bytes 6291460
  0.0 12.7 %collective-permute-start = (bf16[1024,128]{1,0:T(8,128)(2,1)}, bf16[1024,128]{1,0:T(8,128)(2,1)S(1)}, u32[]{:S(2)}, u32[]{:S(2)}) collective-permute-start(bf16[1024,128]{1,0:T(8,128)(2,1)} %bitcast.18), channel_id=1, source_target_pairs={{0,16},{16,0},{1,17},{17,1},{2,18},{18,2},{3,19},{19,3},{4,20},{20... | collective-permute-start | bytes 786440 | tf_op jit(solution)/shard_map/ppermute | solution.py:17
  3.0 6.8 %collective-permute-start.1 = (bf16[1024,128]{1,0:T(8,128)(2,1)}, bf16[1024,128]{1,0:T(8,128)(2,1)}, u32[]{:S(2)}, u32[]{:S(2)}) collective-permute-start(bf16[1024,128]{1,0:T(8,128)(2,1)} %param.10), channel_id=1, source_target_pairs={{1,0},{2,1},{3,2},{4,3},{5,4},{6,5},{7,6},{8,7},{9,8},{10,9},{11,1... | collective-permute-start | bytes 786440 | tf_op jit(solution)/shard_map/ppermute | solution.py:12
  8.4 4.3 %collective-permute-start.2 = (bf16[128,128]{1,0:T(8,128)(2,1)S(1)}, bf16[128,128]{1,0:T(8,128)(2,1)S(1)}, u32[]{:S(2)}, u32[]{:S(2)}) collective-permute-start(bf16[128,128]{1,0:T(8,128)(2,1)S(1)} %fusion.refs_2_), channel_id=1, source_target_pairs={{0,16},{16,0},{1,17},{17,1},{2,18},{18,2},{3,19},{19,3},{4,20},{20... | collective-permute-start | bytes 98312 | tf_op jit(solution)/shard_map/ppermute | solution.py:17
  8.8 2.5 %copy-start.3 = (bf16[1024,512]{1,0:T(8,128)(2,1)S(1)}, bf16[1024,512]{1,0:T(8,128)(2,1)}, u32[]{:S(2)}) copy-start(bf16[1024,512]{1,0:T(8,128)(2,1)} %convolution_convert_fusion) | copy-start | bytes 3145732
  9.8 3.0 %copy-start.2 = (bf16[1,1024,128]{2,1,0:T(8,128)(2,1)S(1)}, bf16[1,1024,128]{2,1,0:T(8,128)(2,1)}, u32[]{:S(2)}) copy-start(bf16[1,1024,128]{2,1,0:T(8,128)(2,1)} %param.7) | copy-start | bytes 786436
  26.9 6.1 %collective-permute-start.3 = (bf16[64,128]{1,0:T(8,128)(2,1)S(1)}, bf16[64,128]{1,0:T(8,128)(2,1)S(1)}, u32[]{:S(2)}, u32[]{:S(2)}) collective-permute-start(bf16[64,128]{1,0:T(8,128)(2,1)S(1)} %shard_map.74), channel_id=1, source_target_pairs={{0,8},{1,9},{2,10},{3,11},{4,12},{5,13},{6,14},{7,15},{16,24},{17,... | collective-permute-start | bytes 49160 | tf_op jit(solution)/shard_map/ppermute | solution.py:12

commit v16 on v10

--- a/solution.py
+++ b/solution.py
@@ -37,8 +37,9 @@
     return high, (value - high.astype(jnp.float32)).astype(jnp.bfloat16)
 
 
-def wide(value, matrix):
-    both = product(jnp.concatenate(split(value)), matrix)
+def wide(value, matrix, twice=False):
+    parts = jnp.concatenate(split(value))
+    both = product(jnp.concatenate([parts, parts], axis=1) if twice else parts, matrix)
     return both[: value.shape[0]] + both[value.shape[0] :]
 
 
@@ -81,22 +82,31 @@
     return state
 
 
-def first_half(upper_ref, steps_ref, entry_ref, values_ref, last_ref):
+def leave(upper_ref, steps_ref, entry_ref, last_ref):
+    count, _, rank = steps_ref.shape
+
     @pl.when(upper_ref[0] == 0)
     def _():
-        last_ref[...] = chain(steps_ref, entry_ref[...].T, values_ref).astype(jnp.bfloat16)
-
-
-def second_half(upper_ref, steps_ref, before_ref, values_ref, maps_ref):
+        pairs = [product(steps_ref[k], steps_ref[k + 1, :rank]) for k in range(0, count, 2)]
+        state = entry_ref[...].T
+        for index, pair in enumerate(pairs):
+            moved = wide(state, jnp.concatenate(split(pair[:rank])), twice=True)
+            shift = pair[rank:] + steps_ref[2 * index + 1, rank:].astype(jnp.float32)
+            state = moved + shift
+        last_ref[...] = state.astype(jnp.bfloat16)
+
+
+def compose(upper_ref, steps_ref, entry_ref, values_ref, maps_ref):
     count, rank, _ = maps_ref.shape
-
-    @pl.when(upper_ref[0] == 0)
+    first = upper_ref[0] == 0
+    chain(steps_ref, jnp.where(first, entry_ref[...].T, 0.0), values_ref)
+
+    @pl.when(first)
     def _():
         maps_ref[...] = jnp.zeros(maps_ref.shape, jnp.bfloat16)
 
-    @pl.when(upper_ref[0] > 0)
+    @pl.when(jnp.logical_not(first))
     def _():
-        chain(steps_ref, jnp.zeros(values_ref.shape[1:], jnp.float32), values_ref)
         state = steps_ref[0, :rank]
         for member in range(1, count):
             maps_ref[member] = state
@@ -112,14 +122,13 @@
         coupled_ref[member] = (moved + values_ref[member]).astype(jnp.bfloat16)
 
 
-def local(kernel, inputs, *outputs, scalar=False, aliases={}, cost=None):
+def local(kernel, inputs, *outputs, scalar=False, cost=None):
     specs = [SMEM] * scalar + [VMEM] * (len(inputs) - scalar)
     return pl.pallas_call(
         kernel,
         in_specs=specs,
         out_specs=[VMEM] * len(outputs),
         out_shape=[jax.ShapeDtypeStruct(*output) for output in outputs],
-        input_output_aliases=aliases,
         cost_estimate=cost,
         compiler_params=pltpu.CompilerParams(vmem_limit_bytes=16 * 2**20),
     )(*inputs)
@@ -151,7 +160,11 @@
         (right_side.shape, half),
         cost=pl.CostEstimate(flops=1, bytes_accessed=1, transcendentals=0),
     )
-    lefts[-1], applied = lax.optimization_barrier((lefts[-1], applied))
+    entry = lax.dynamic_slice_in_dim(incoming, lower * share, share, 1)
+    place = upper.reshape(1)
+    lefts[-1], applied, entry, place = lax.optimization_barrier(
+        (lefts[-1], applied, entry, place)
+    )
 
     (gain,) = local(
         lambda *refs: make_gain(layers, *refs),
@@ -161,27 +174,18 @@
     (sent,) = local(
         make_steps, (gain, applied, next_rows), ((lowers, rank + share, rank), half)
     )
-    incoming, sent = lax.optimization_barrier((incoming, sent))
+    sent, entry, place = lax.optimization_barrier((sent, entry, place))
     steps = exchanged(sent, near)
-    entry = lax.dynamic_slice_in_dim(incoming, lower * share, share, 1)
-
-    place = upper.reshape(1)
-    values, last = local(
-        first_half,
-        (place, steps, entry),
-        ((lowers, share, rank), jnp.float32),
-        ((share, rank), half),
-        scalar=True,
-    )
+    steps, entry, place = lax.optimization_barrier((steps, entry, place))
+    (last,) = local(leave, (place, steps, entry), ((share, rank), half), scalar=True)
     entered = shifted(last, "row", lowers)
     steps, _ = lax.optimization_barrier((steps, last))
     values, maps = local(
-        second_half,
-        (place, steps, values),
+        compose,
+        (place, steps, entry),
         ((lowers, share, rank), jnp.float32),
         ((lowers, rank, rank), half),
         scalar=True,
-        aliases={2: 0},
     )
     (coupled,) = local(enter, (entered, maps, values), ((lowers, share, rank), half))
     coupled = exchanged(coupled, near).reshape(width, rank)

time: 40.8 us -> 44.4 us (1.088)
  blocking collectives: 7.72 us -> 20.2 us
  waiting for transfers between devices: 7.95 us -> 0.46 us
  starting transfers between devices: 12.8 us -> 8.68 us
  Pallas kernels: 5.42 us -> 7.14 us
  local copies, waits for them, and re-layouts: 3.74 us -> 4.69 us
    all_to_all x1 -> x2, blocking collectives: 7.72 us -> 20.2 us  [exchanged(): lax.all_to_all(blocks, 'row', 0, 0, axis_index_groups=members, tiled=True)]
    all_to_all x1 -> x0, waiting for transfers between devices: 6.57 us -> none  [exchanged(): lax.all_to_all(blocks, 'row', 0, 0, axis_index_groups=members, tiled=True)]
    all_to_all x1 -> x0, starting transfers between devices: 4.82 us -> none  [exchanged(): lax.all_to_all(blocks, 'row', 0, 0, axis_index_groups=members, tiled=True)]
    pallas_call x6, Pallas kernels: 5.42 us -> 7.14 us  [local(): pl.pallas_call(kernel, in_specs=specs, out_specs=[VMEM] * len(outputs), o...]
    unnamed x8 -> x10, local copies, waits for them, and re-layouts: 2.82 us -> 3.77 us
    ppermute x2, waiting for transfers between devices: 1.37 us -> 0.45 us  [shifted(): lax.ppermute(value, axis, [(source, source + steps) for source in range(l...]
    ppermute x2, starting transfers between devices: 4.8 us -> 5.53 us  [shifted(): lax.ppermute(value, axis, [(source, source + steps) for source in range(l...]
  transfers between devices with their start and end apart: 5 -> 4, of which waited for: 2 -> 1; matrix products, arithmetic and copies ran while one was open for 5% -> 5% of each run, Pallas kernels for 7% -> 11%
where the time goes in v16:
time: 44.4 us; the launch traced here: 43.9 us
  blocking collectives  20.2 us (45%)
  starting transfers between devices  8.68 us (20%)
  Pallas kernels  7.14 us (16%)
  local copies, waits for them, and re-layouts  4.69 us (11%)
  matrix products  2.62 us (6%)
  waiting for transfers between devices  0.46 us (1%)
    all_to_all x2, blocking collectives, exchanged(): lax.all_to_all(blocks, 'row', 0, 0, axis_index_groups=members, tiled=True)  20.2 us
    pallas_call x6, Pallas kernels, local(): pl.pallas_call(kernel, in_specs=specs, out_specs=[VMEM] * len(outputs), o...  7.14 us
    ppermute x2, starting transfers between devices, shifted(): lax.ppermute(value, axis, [(source, source + steps) for source in range(l...  5.53 us
    unnamed x10, local copies, waits for them, and re-layouts  3.77 us
    ppermute x2, starting transfers between devices, rotated(): lax.ppermute(value, axis, [(source, (source + steps) % count) for source...  3.15 us
    dot_general x1, matrix products, body(): lax.dot_general(gain, coupled, FLIPPED, preferred_element_type=jnp.float32)  1.41 us
    dot_general x1, matrix products, project(): lax.dot_general(basis, vectors, (((0,), (0,)), ((), ())), preferred_eleme...  1.21 us
    dynamic_slice x1, local copies, waits for them, and re-layouts, body(): entry = lax.dynamic_slice_in_dim(incoming, lower * share, share, 1)  0.91 us
  transfers between devices with their start and end apart: 4, of which 1 were waited for; matrix products, arithmetic and copies ran while one was open for 5% of the time, Pallas kernels for 11%

profile of v16, /device:TPU:0, one launch (start us, length us, event | category | flops | bytes accessed | tf_op | source)
XLA Modules:
  0.0 43.9 jit_solution(4448892096183416757)
XLA Ops:
  0.0 2.9 %collective-permute-start = (bf16[1024,128]{1,0:T(8,128)(2,1)}, bf16[1024,128]{1,0:T(8,128)(2,1)}, u32[]{:S(2)}, u32[]{:S(2)}) collective-permute-start(bf16[1024,128]{1,0:T(8,128)(2,1)} %bitcast.9), channel_id=1, source_target_pairs={{0,16},{16,0},{1,17},{17,1},{2,18},{18,2},{3,19},{19,3},{4,20},{20... | collective-permute-start | bytes 786440 | tf_op jit(solution)/shard_map/ppermute | solution.py:17
  2.9 1.3 %collective-permute-start.2 = (bf16[1024,128]{1,0:T(8,128)(2,1)}, bf16[1024,128]{1,0:T(8,128)(2,1)}, u32[]{:S(2)}, u32[]{:S(2)}) collective-permute-start(bf16[1024,128]{1,0:T(8,128)(2,1)} %param.10), channel_id=1, source_target_pairs={{1,0},{2,1},{3,2},{4,3},{5,4},{6,5},{7,6},{8,7},{9,8},{10,9},{11,1... | collective-permute-start | bytes 786440 | tf_op jit(solution)/shard_map/ppermute | solution.py:12
  4.2 0.0 copy-done
  4.2 1.2 %convolution_convert_fusion.refs_2_ = bf16[128,128]{1,0:T(8,128)(2,1)S(1)} fusion(bf16[1024,128]{1,0:T(8,128)(2,1)S(1)} %copy-done, bf16[1,1024,128]{2,1,0:T(8,128)(2,1)} %param.8), kind=kOutput, calls=%fused_computation.1 | convolution fusion | flops 33570816 | bytes 557056 | tf_op jit(solution)/shard_map/dot_general | solution.py:21
  5.5 0.2 collective-permute-start.1
  5.7 0.9 %constant_dynamic-slice_fusion.entry_ref = f32[128,64]{1,0:T(8,128)S(1)} fusion(f32[128,512]{1,0:T(8,128)} %param.13, s32[]{:T(128)S(6)} %select_n.3), kind=kLoop, calls=%fused_computation.3 | loop fusion | bytes 65540 | tf_op jit(solution)/shard_map/dynamic_slice | solution.py:163
  6.6 1.6 %copy-done.1 = bf16[1024,1024]{1,0:T(8,128)(2,1)S(1)} copy-done((bf16[1024,1024]{1,0:T(8,128)(2,1)S(1)}, bf16[1024,1024]{1,0:T(8,128)(2,1)}, u32[]{:S(2)}) %copy-start.1) | copy-done | bytes 2097176
  8.2 1.2 %copy-done.3 = bf16[1024,512]{1,0:T(8,128)(2,1)S(1)} copy-done((bf16[1024,512]{1,0:T(8,128)(2,1)S(1)}, bf16[1024,512]{1,0:T(8,128)(2,1)}, u32[]{:S(2)}) %copy-start.3) | copy-done | bytes 1048600
  9.4 1.7 %shard_map.73.applied_ref = bf16[1024,512]{1,0:T(8,128)(2,1)S(1)} custom-call(bf16[1024,1024]{1,0:T(8,128)(2,1)S(1)} %copy-done.1, bf16[1024,512]{1,0:T(8,128)(2,1)S(1)} %copy-done.3), custom_call_target="tpu_custom_call" | custom-call | flops 1 | bytes 1 | tf_op jit(solution)/shard_map/pallas_call | solution.py:127
  11.2 0.0 collective-permute-done.refs_1_
  11.2 0.0 collective-permute-done.1.refs_3_
  11.2 0.0 copy-start.4
  11.2 0.9 %copy-done.4 = bf16[1,1024,128]{2,1,0:T(8,128)(2,1)S(1)} copy-done((bf16[1,1024,128]{2,1,0:T(8,128)(2,1)S(1)}, bf16[1,1024,128]{2,1,0:T(8,128)(2,1)}, u32[]{:S(2)}) %copy-start.4) | copy-done | bytes 262168
  12.2 2.0 %shard_map.74.gain_ref = bf16[1024,128]{1,0:T(8,128)(2,1)S(1)} custom-call(bf16[1024,128]{1,0:T(8,128)(2,1)S(1)} %bitcast.10, bf16[1024,128]{1,0:T(8,128)(2,1)} %collective-permute-done.refs_1_, bf16[128,128]{1,0:T(8,128)(2,1)S(1)} %convolution_convert_fusion.refs_2_, bf16[128,128]{1,0:T(8,128)(2,1)S(1)} %collective-permute-done.1.refs_3_, ...), custom_call_target="tpu_custom_call" | custom-call | tf_op jit(solution)/shard_map/pallas_call | solution.py:127
  14.2 0.0 collective-permute-done.2.next_ref
  14.2 1.5 %shard_map.75 = bf16[8,192,128]{2,1,0:T(8,128)(2,1)S(1)} custom-call(bf16[1024,128]{1,0:T(8,128)(2,1)S(1)} %shard_map.74.gain_ref, bf16[1024,512]{1,0:T(8,128)(2,1)S(1)} %shard_map.73.applied_ref, bf16[1024,128]{1,0:T(8,128)(2,1)} %collective-permute-done.2.next_ref), custom_call_target="tpu_custom_call" | custom-call | tf_op jit(solution)/shard_map/pallas_call | solution.py:127
  15.7 12.7 %all_to_all.10.steps_ref = bf16[8,192,128]{2,1,0:T(8,128)(2,1)S(1)} all-to-all(bf16[8,192,128]{2,1,0:T(8,128)(2,1)S(1)} %shard_map.75), channel_id=1, replica_groups={{0,1,2,3,4,5,6,7},{8,9,10,11,12,13,14,15},{16,17,18,19,20,21,22,23},{24..., dimensions={0} | all-to-all | bytes 786432 | tf_op jit(solution)/shard_map/all_to_all | solution.py:138
  28.3 0.7 %shard_map.76 = bf16[64,128]{1,0:T(8,128)(2,1)S(1)} custom-call(s32[1]{0:T(128)} %bitcast.2.upper_ref, bf16[8,192,128]{2,1,0:T(8,128)(2,1)S(1)} %all_to_all.10.steps_ref, f32[128,64]{1,0:T(8,128)S(1)} %constant_dynamic-slice_fusion.entry_ref), custom_call_target="tpu_custom_call" | custom-call | tf_op jit(solution)/shard_map/pallas_call | solution.py:127
  29.1 4.3 %collective-permute-start.3 = (bf16[64,128]{1,0:T(8,128)(2,1)S(1)}, bf16[64,128]{1,0:T(8,128)(2,1)S(1)}, u32[]{:S(2)}, u32[]{:S(2)}) collective-permute-start(bf16[64,128]{1,0:T(8,128)(2,1)S(1)} %shard_map.76), channel_id=1, source_target_pairs={{0,8},{1,9},{2,10},{3,11},{4,12},{5,13},{6,14},{7,15},{16,24},{17,... | collective-permute-start | bytes 49160 | tf_op jit(solution)/shard_map/ppermute | solution.py:12
  33.3 1.0 %shard_map.77 = (f32[8,64,128]{2,1,0:T(8,128)S(1)}, bf16[8,128,128]{2,1,0:T(8,128)(2,1)S(1)}) custom-call(s32[1]{0:T(128)} %bitcast.2.upper_ref, bf16[8,192,128]{2,1,0:T(8,128)(2,1)S(1)} %all_to_all.10.steps_ref, f32[128,64]{1,0:T(8,128)S(1)} %constant_dynamic-slice_fusion.entry_ref), custom_call_target="tpu_custom_call" | custom-call | tf_op jit(solution)/shard_map/pallas_call | solution.py:127
  34.3 0.5 %collective-permute-done.3.entered_ref = bf16[64,128]{1,0:T(8,128)(2,1)S(1)} collective-permute-done((bf16[64,128]{1,0:T(8,128)(2,1)S(1)}, bf16[64,128]{1,0:T(8,128)(2,1)S(1)}, u32[]{:S(2)}, u32[]{:S(2)}) %collective-permute-start.3) | collective-permute-done | bytes 16416 | tf_op jit(solution)/shard_map/ppermute | solution.py:12
  34.8 0.2 shard_map.78
  35.0 7.6 %all_to_all.11 = bf16[8,64,128]{2,1,0:T(8,128)(2,1)S(1)} all-to-all(bf16[8,64,128]{2,1,0:T(8,128)(2,1)S(1)} %shard_map.78), channel_id=1, replica_groups={{0,1,2,3,4,5,6,7},{8,9,10,11,12,13,14,15},{16,17,18,19,20,21,22,23},{24..., dimensions={0} | all-to-all | bytes 262144 | tf_op jit(solution)/shard_map/all_to_all | solution.py:138
  42.5 1.4 %subtract_convert_fusion = bf16[1024,512]{1,0:T(8,128)(2,1)} fusion(bf16[1024,512]{1,0:T(8,128)(2,1)S(1)} %shard_map.73.applied_ref, bf16[1024,128]{1,0:T(8,128)(2,1)S(1)} %shard_map.74.gain_ref, bf16[512,128]{1,0:T(8,128)(2,1)S(1)} %bitcast.11), kind=kOutput, calls=%fused_computation | convolution fusion | flops 135790592 | bytes 2490368 | tf_op jit(solution)/shard_map/dot_general | solution.py:192
  (5 shorter events, 0.0 us)
Async XLA Ops:
  0.0 4.2 %copy-start = (bf16[1024,128]{1,0:T(8,128)(2,1)S(1)}, bf16[1024,128]{1,0:T(8,128)(2,1)}, u32[]{:S(2)}) copy-start(bf16[1024,128]{1,0:T(8,128)(2,1)} %param.9) | copy-start | bytes 786436
  0.0 11.2 %collective-permute-start = (bf16[1024,128]{1,0:T(8,128)(2,1)}, bf16[1024,128]{1,0:T(8,128)(2,1)}, u32[]{:S(2)}, u32[]{:S(2)}) collective-permute-start(bf16[1024,128]{1,0:T(8,128)(2,1)} %bitcast.9), channel_id=1, source_target_pairs={{0,16},{16,0},{1,17},{17,1},{2,18},{18,2},{3,19},{19,3},{4,20},{20... | collective-permute-start | bytes 786440 | tf_op jit(solution)/shard_map/ppermute | solution.py:17
  2.9 11.2 %collective-permute-start.2 = (bf16[1024,128]{1,0:T(8,128)(2,1)}, bf16[1024,128]{1,0:T(8,128)(2,1)}, u32[]{:S(2)}, u32[]{:S(2)}) collective-permute-start(bf16[1024,128]{1,0:T(8,128)(2,1)} %param.10), channel_id=1, source_target_pairs={{1,0},{2,1},{3,2},{4,3},{5,4},{6,5},{7,6},{8,7},{9,8},{10,9},{11,1... | collective-permute-start | bytes 786440 | tf_op jit(solution)/shard_map/ppermute | solution.py:12
  5.5 5.7 %collective-permute-start.1 = (bf16[128,128]{1,0:T(8,128)(2,1)S(1)}, bf16[128,128]{1,0:T(8,128)(2,1)S(1)}, u32[]{:S(2)}, u32[]{:S(2)}) collective-permute-start(bf16[128,128]{1,0:T(8,128)(2,1)S(1)} %convolution_convert_fusion.refs_2_), channel_id=1, source_target_pairs={{0,16},{16,0},{1,17},{17,1},{2,18},{18,2},{3,19},{19,3},{4,20},{20... | collective-permute-start | bytes 98312 | tf_op jit(solution)/shard_map/ppermute | solution.py:17
  6.6 1.6 %copy-start.1 = (bf16[1024,1024]{1,0:T(8,128)(2,1)S(1)}, bf16[1024,1024]{1,0:T(8,128)(2,1)}, u32[]{:S(2)}) copy-start(bf16[1024,1024]{1,0:T(8,128)(2,1)} %refs_4_.1) | copy-start | bytes 6291460
  8.2 1.2 %copy-start.3 = (bf16[1024,512]{1,0:T(8,128)(2,1)S(1)}, bf16[1024,512]{1,0:T(8,128)(2,1)}, u32[]{:S(2)}) copy-start(bf16[1024,512]{1,0:T(8,128)(2,1)} %right_ref) | copy-start | bytes 3145732
  9.4 1.8 %copy-start.2 = (bf16[1024,1024]{1,0:T(8,128)(2,1)S(1)}, bf16[1024,1024]{1,0:T(8,128)(2,1)}, u32[]{:S(2)}) copy-start(bf16[1024,1024]{1,0:T(8,128)(2,1)} %refs_4_.1) | copy-start | bytes 6291460
  11.2 1.0 %copy-start.4 = (bf16[1,1024,128]{2,1,0:T(8,128)(2,1)S(1)}, bf16[1,1024,128]{2,1,0:T(8,128)(2,1)}, u32[]{:S(2)}) copy-start(bf16[1,1024,128]{2,1,0:T(8,128)(2,1)} %param.7) | copy-start | bytes 786436
  29.1 5.7 %collective-permute-start.3 = (bf16[64,128]{1,0:T(8,128)(2,1)S(1)}, bf16[64,128]{1,0:T(8,128)(2,1)S(1)}, u32[]{:S(2)}, u32[]{:S(2)}) collective-permute-start(bf16[64,128]{1,0:T(8,128)(2,1)S(1)} %shard_map.76), channel_id=1, source_target_pairs={{0,8},{1,9},{2,10},{3,11},{4,12},{5,13},{6,14},{7,15},{16,24},{17,... | collective-permute-start | bytes 49160 | tf_op jit(solution)/shard_map/ppermute | solution.py:12

commit v17 on v9

--- a/solution.py
+++ b/solution.py
@@ -45,7 +45,8 @@
 def make_maps(layers, *refs):
     lefts = jnp.concatenate([ref[...] for ref in refs[:layers]], axis=1)
     cores = jnp.concatenate([ref[...] for ref in refs[layers : 2 * layers]], axis=0)
-    weights_ref, shift_ref, sent_ref = refs[2 * layers :]
+    weights_ref, shift_ref, range_ref, sent_ref = refs[2 * layers :]
+    range_ref[...] = (-product(lefts, cores)).astype(jnp.bfloat16)
     map_t = wide(wide(weights_ref[...], lefts), cores).T.astype(jnp.bfloat16)
     rank = map_t.shape[0]
     for target in range(sent_ref.shape[0]):
@@ -111,7 +112,7 @@
 
 def body(left_factors, right_factors, sketch, row_basis, inverse_diag, right_side, incoming):
     half = jnp.bfloat16
-    rank = sketch.shape[1]
+    order, rank = sketch.shape
     width = right_side.shape[1]
     layers, groups = lax.axis_size("layer"), lax.axis_size("row")
     lowers = groups // 2
@@ -129,20 +130,20 @@
 
     shift_t = project(applied, next_rows).astype(half).reshape(lowers, share, rank)
     weights = project(next_rows, inverse_diag)
-    lefts[-1], shift_t, weights = lax.optimization_barrier((lefts[-1], shift_t, weights))
-    (sent,) = local(
+    entry = lax.dynamic_slice_in_dim(incoming, lower * share, share, 1)
+    place = upper.reshape(1)
+    lefts[-1], shift_t, weights, entry, place = lax.optimization_barrier(
+        (lefts[-1], shift_t, weights, entry, place)
+    )
+    tile_range, sent = local(
         lambda *refs: make_maps(layers, *refs),
         (*lefts, *cores, weights, shift_t),
+        ((order, rank), half),
         ((lowers, rank + share, rank), half),
     )
-    lefts, incoming, sent = lax.optimization_barrier((lefts, incoming, sent))
+    sent, tile_range, entry, place = lax.optimization_barrier((sent, tile_range, entry, place))
     steps = exchanged(sent, near)
-    entry = lax.dynamic_slice_in_dim(incoming, lower * share, share, 1)
-    tile_range = -sum(product(left, core) for left, core in zip(lefts, cores))
-    gain = product(inverse_diag, tile_range.astype(half)).astype(half)
-    gain, entry, steps = lax.optimization_barrier((gain, entry, steps))
-
-    place = upper.reshape(1)
+    steps, tile_range, entry, place = lax.optimization_barrier((steps, tile_range, entry, place))
     values, last = local(
         first_half,
         (place, steps, entry),
@@ -151,7 +152,8 @@
         scalar=True,
     )
     entered = shifted(last, "row", lowers)
-    steps, _ = lax.optimization_barrier((steps, last))
+    steps, tile_range, _ = lax.optimization_barrier((steps, tile_range, last))
+    gain = product(inverse_diag, tile_range).astype(half)
     values, maps = local(
         second_half,
         (place, steps, values),
@@ -160,6 +162,7 @@
         scalar=True,
         aliases={2: 0},
     )
+    gain, maps = lax.optimization_barrier((gain, maps))
     (coupled,) = local(enter, (entered, maps, values), ((lowers, share, rank), half))
     coupled = exchanged(coupled, near).reshape(width, rank)
     moved = lax.dot_general(gain, coupled, FLIPPED, preferred_element_type=jnp.float32)

time: 40.3 us -> 40.8 us (1.012)
  blocking collectives: 7.73 us -> 21.9 us
  waiting for transfers between devices: 7.78 us -> 0.57 us
  starting transfers between devices: 12.5 us -> 6.95 us
  Pallas kernels: 2.64 us -> 2.03 us
    all_to_all x1 -> x2, blocking collectives: 7.73 us -> 21.9 us  [exchanged(): lax.all_to_all(blocks, 'row', 0, 0, axis_index_groups=members, tiled=True)]
    all_to_all x1 -> x0, starting transfers between devices: 4.5 us -> none  [exchanged(): lax.all_to_all(blocks, 'row', 0, 0, axis_index_groups=members, tiled=True)]
    all_to_all x1 -> x0, waiting for transfers between devices: 3.5 us -> none  [exchanged(): lax.all_to_all(blocks, 'row', 0, 0, axis_index_groups=members, tiled=True)]
    ppermute x2, waiting for transfers between devices: 2.9 us -> 0.05 us  [rotated(): lax.ppermute(value, axis, [(source, (source + steps) % count) for source...]
    dot_general x3 -> x2, matrix products: 5.52 us -> 3.31 us  [product(): return jnp.dot(a, b, preferred_element_type=jnp.float32)]
    dot_general x3, matrix products: 1.22 us -> 3.17 us  [project(): lax.dot_general(basis, vectors, (((0,), (0,)), ((), ())), preferred_eleme...]
    ppermute x2, starting transfers between devices: 4.69 us -> 3.67 us  [shifted(): lax.ppermute(value, axis, [(source, source + steps) for source in range(l...]
    ppermute x2, waiting for transfers between devices: 1.37 us -> 0.53 us  [shifted(): lax.ppermute(value, axis, [(source, source + steps) for source in range(l...]
  transfers between devices with their start and end apart: 5 -> 4, of which waited for: 4 -> 1; matrix products, arithmetic and copies ran while one was open for 19% -> 18% of each run, Pallas kernels for 0% -> 0%
where the time goes in v17:
time: 40.8 us; the launch traced here: 40.4 us
  blocking collectives  21.9 us (54%)
  matrix products  7.91 us (19%)
  starting transfers between devices  6.95 us (17%)
  Pallas kernels  2.03 us (5%)
  local copies, waits for them, and re-layouts  0.93 us (2%)
  waiting for transfers between devices  0.57 us (1%)
    all_to_all x2, blocking collectives, exchanged(): lax.all_to_all(blocks, 'row', 0, 0, axis_index_groups=members, tiled=True)  21.9 us
    ppermute x2, starting transfers between devices, shifted(): lax.ppermute(value, axis, [(source, source + steps) for source in range(l...  3.67 us
    dot_general x2, matrix products, product(): return jnp.dot(a, b, preferred_element_type=jnp.float32)  3.31 us
    ppermute x2, starting transfers between devices, rotated(): lax.ppermute(value, axis, [(source, (source + steps) % count) for source...  3.28 us
    dot_general x3, matrix products, project(): lax.dot_general(basis, vectors, (((0,), (0,)), ((), ())), preferred_eleme...  3.17 us
    pallas_call x4, Pallas kernels, local(): pl.pallas_call(kernel, in_specs=specs, out_specs=[VMEM] * len(outputs), o...  2.03 us
    dot_general x1, matrix products, body(): lax.dot_general(gain, coupled, FLIPPED, preferred_element_type=jnp.float32)  1.44 us
    dynamic_slice x1, local copies, waits for them, and re-layouts, body(): entry = lax.dynamic_slice_in_dim(incoming, lower * share, share, 1)  0.91 us
  transfers between devices with their start and end apart: 4, of which 1 were waited for; matrix products, arithmetic and copies ran while one was open for 18% of the time, Pallas kernels for 0%

profile of v17, /device:TPU:0, one launch (start us, length us, event | category | flops | bytes accessed | tf_op | source)
XLA Modules:
  0.0 40.4 jit_solution(10246477128456550279)
XLA Ops:
  0.0 0.0 copy-start
  0.0 3.0 %collective-permute-start = (bf16[1024,128]{1,0:T(8,128)(2,1)}, bf16[1024,128]{1,0:T(8,128)(2,1)S(1)}, u32[]{:S(2)}, u32[]{:S(2)}) collective-permute-start(bf16[1024,128]{1,0:T(8,128)(2,1)} %bitcast.23), channel_id=1, source_target_pairs={{0,16},{16,0},{1,17},{17,1},{2,18},{18,2},{3,19},{19,3},{4,20},{20... | collective-permute-start | bytes 786440 | tf_op jit(solution)/shard_map/ppermute | solution.py:17
  3.0 1.3 %collective-permute-start.1 = (bf16[1024,128]{1,0:T(8,128)(2,1)}, bf16[1024,128]{1,0:T(8,128)(2,1)}, u32[]{:S(2)}, u32[]{:S(2)}) collective-permute-start(bf16[1024,128]{1,0:T(8,128)(2,1)} %param.10), channel_id=1, source_target_pairs={{1,0},{2,1},{3,2},{4,3},{5,4},{6,5},{7,6},{8,7},{9,8},{10,9},{11,1... | collective-permute-start | bytes 786440 | tf_op jit(solution)/shard_map/ppermute | solution.py:12
  4.3 0.0 copy-done
  4.3 2.5 %convolution_convert_fusion = bf16[1024,512]{1,0:T(8,128)(2,1)S(1)} fusion(bf16[1024,1024]{1,0:T(8,128)(2,1)S(1)} %copy-done, bf16[1024,512]{1,0:T(8,128)(2,1)} %param.12), kind=kOutput, calls=%fused_computation.1 | convolution fusion | flops 1074266112 | bytes 4194304 | tf_op jit(solution)/shard_map/dot_general | solution.py:27
  6.8 0.0 copy-done.2
  6.8 0.0 copy-done.3
  6.8 0.3 fusion.1.refs_2_
  7.1 0.3 collective-permute-start.2
  7.4 0.9 %constant_dynamic-slice_fusion.entry_ref = f32[128,64]{1,0:T(8,128)S(1)} fusion(f32[128,512]{1,0:T(8,128)} %param.13, s32[]{:T(128)S(6)} %select_n.3), kind=kLoop, calls=%fused_computation.8 | loop fusion | bytes 65540 | tf_op jit(solution)/shard_map/dynamic_slice | solution.py:133
  8.3 0.0 collective-permute-done.1
  8.3 1.5 %fusion.3.refs_4_ = f32[128,1024]{1,0:T(8,128)S(1)} fusion(bf16[1024,128]{1,0:T(8,128)(2,1)} %collective-permute-done.1, bf16[1024,1024]{1,0:T(8,128)(2,1)S(1)} %copy-done), kind=kOutput, calls=%fused_computation.9 | convolution fusion | flops 268435456 | bytes 2883584 | tf_op jit(solution)/shard_map/dot_general | solution.py:21
  9.8 1.4 %convolution_convert_fusion.2 = bf16[512,128]{1,0:T(8,128)(2,1)S(1)} fusion(bf16[1024,512]{1,0:T(8,128)(2,1)S(1)} %convolution_convert_fusion, bf16[1024,128]{1,0:T(8,128)(2,1)} %collective-permute-done.1), kind=kOutput, calls=%fused_computation.4 | convolution fusion | flops 134283264 | bytes 1441792 | tf_op jit(solution)/shard_map/dot_general | solution.py:21
  11.2 0.0 collective-permute-done.refs_1_
  11.2 0.0 collective-permute-done.2.refs_3_
  11.3 0.7 %shard_map.73 = (bf16[1024,128]{1,0:T(8,128)(2,1)S(1)}, bf16[8,192,128]{2,1,0:T(8,128)(2,1)S(1)}) custom-call(bf16[1024,128]{1,0:T(8,128)(2,1)S(1)} %bitcast.24, bf16[1024,128]{1,0:T(8,128)(2,1)S(1)} %collective-permute-done.refs_1_, bf16[128,128]{1,0:T(8,128)(2,1)S(1)} %fusion.1.refs_2_, bf16[128,128]{1,0:T(8,128)(2,1)S(1)} %collective-permute-done.2.refs_3_, ...), custom_call_target="tpu_custom_call" | custom-call | tf_op jit(solution)/shard_map/pallas_call | solution.py:99
  12.0 14.3 %all_to_all.10.steps_ref = bf16[8,192,128]{2,1,0:T(8,128)(2,1)S(1)} all-to-all(bf16[8,192,128]{2,1,0:T(8,128)(2,1)S(1)} %get-tuple-element.39), channel_id=1, replica_groups={{0,1,2,3,4,5,6,7},{8,9,10,11,12,13,14,15},{16,17,18,19,20,21,22,23},{24..., dimensions={0} | all-to-all | bytes 786432 | tf_op jit(solution)/shard_map/all_to_all | solution.py:110
  26.3 1.1 %shard_map.74 = (f32[8,64,128]{2,1,0:T(8,128)S(1)}, bf16[64,128]{1,0:T(8,128)(2,1)S(1)}) custom-call(s32[1]{0:T(128)} %bitcast.2.upper_ref, bf16[8,192,128]{2,1,0:T(8,128)(2,1)S(1)} %all_to_all.10.steps_ref, f32[128,64]{1,0:T(8,128)S(1)} %constant_dynamic-slice_fusion.entry_ref), custom_call_target="tpu_custom_call" | custom-call | tf_op jit(solution)/shard_map/pallas_call | solution.py:99
  27.4 2.4 %collective-permute-start.3 = (bf16[64,128]{1,0:T(8,128)(2,1)S(1)}, bf16[64,128]{1,0:T(8,128)(2,1)S(1)}, u32[]{:S(2)}, u32[]{:S(2)}) collective-permute-start(bf16[64,128]{1,0:T(8,128)(2,1)S(1)} %get-tuple-element.47), channel_id=1, source_target_pairs={{0,8},{1,9},{2,10},{3,11},{4,12},{5,13},{6,14},{7,15},{16,24},{17,... | collective-permute-start | bytes 49160 | tf_op jit(solution)/shard_map/ppermute | solution.py:12
  29.8 0.8 %fusion = bf16[1024,128]{0,1:T(8,128)(2,1)S(1)} fusion(bf16[1024,128]{1,0:T(8,128)(2,1)S(1)} %get-tuple-element.48, bf16[1024,1024]{1,0:T(8,128)(2,1)S(1)} %copy-done), kind=kOutput, calls=%fused_computation.3 | convolution fusion | flops 268566528 | bytes 2621440 | tf_op jit(solution)/shard_map/dot_general | solution.py:27
  30.7 0.5 %collective-permute-done.3.entered_ref = bf16[64,128]{1,0:T(8,128)(2,1)S(1)} collective-permute-done((bf16[64,128]{1,0:T(8,128)(2,1)S(1)}, bf16[64,128]{1,0:T(8,128)(2,1)S(1)}, u32[]{:S(2)}, u32[]{:S(2)}) %collective-permute-start.3) | collective-permute-done | bytes 16416 | tf_op jit(solution)/shard_map/ppermute | solution.py:12
  31.2 0.2 shard_map.76
  31.4 7.6 %all_to_all.11 = bf16[8,64,128]{2,1,0:T(8,128)(2,1)S(1)} all-to-all(bf16[8,64,128]{2,1,0:T(8,128)(2,1)S(1)} %shard_map.76), channel_id=1, replica_groups={{0,1,2,3,4,5,6,7},{8,9,10,11,12,13,14,15},{16,17,18,19,20,21,22,23},{24..., dimensions={0} | all-to-all | bytes 262144 | tf_op jit(solution)/shard_map/all_to_all | solution.py:110
  39.0 1.4 %subtract_convert_fusion = bf16[1024,512]{1,0:T(8,128)(2,1)} fusion(bf16[1024,512]{1,0:T(8,128)(2,1)S(1)} %convolution_convert_fusion, bf16[1024,128]{0,1:T(8,128)(2,1)S(1)} %fusion, bf16[512,128]{1,0:T(8,128)(2,1)S(1)} %bitcast.25), kind=kOutput, calls=%fused_computation | convolution fusion | flops 135790592 | bytes 2490368 | tf_op jit(solution)/shard_map/dot_general | solution.py:168
  (5 shorter events, 0.1 us)
Async XLA Ops:
  0.0 4.3 %copy-start = (bf16[1024,1024]{1,0:T(8,128)(2,1)S(1)}, bf16[1024,1024]{1,0:T(8,128)(2,1)}, u32[]{:S(2)}) copy-start(bf16[1024,1024]{1,0:T(8,128)(2,1)} %param.11) | copy-start | bytes 6291460
  0.0 6.8 %copy-start.2 = (bf16[1024,128]{1,0:T(8,128)(2,1)S(1)}, bf16[1024,128]{1,0:T(8,128)(2,1)}, u32[]{:S(2)}) copy-start(bf16[1024,128]{1,0:T(8,128)(2,1)} %param.9) | copy-start | bytes 786436
  0.0 6.8 %copy-start.3 = (bf16[1,1024,128]{2,1,0:T(8,128)(2,1)S(1)}, bf16[1,1024,128]{2,1,0:T(8,128)(2,1)}, u32[]{:S(2)}) copy-start(bf16[1,1024,128]{2,1,0:T(8,128)(2,1)} %param.8) | copy-start | bytes 786436
  0.0 11.2 %collective-permute-start = (bf16[1024,128]{1,0:T(8,128)(2,1)}, bf16[1024,128]{1,0:T(8,128)(2,1)S(1)}, u32[]{:S(2)}, u32[]{:S(2)}) collective-permute-start(bf16[1024,128]{1,0:T(8,128)(2,1)} %bitcast.23), channel_id=1, source_target_pairs={{0,16},{16,0},{1,17},{17,1},{2,18},{18,2},{3,19},{19,3},{4,20},{20... | collective-permute-start | bytes 786440 | tf_op jit(solution)/shard_map/ppermute | solution.py:17
  3.0 5.3 %collective-permute-start.1 = (bf16[1024,128]{1,0:T(8,128)(2,1)}, bf16[1024,128]{1,0:T(8,128)(2,1)}, u32[]{:S(2)}, u32[]{:S(2)}) collective-permute-start(bf16[1024,128]{1,0:T(8,128)(2,1)} %param.10), channel_id=1, source_target_pairs={{1,0},{2,1},{3,2},{4,3},{5,4},{6,5},{7,6},{8,7},{9,8},{10,9},{11,1... | collective-permute-start | bytes 786440 | tf_op jit(solution)/shard_map/ppermute | solution.py:12
  7.1 4.2 %collective-permute-start.2 = (bf16[128,128]{1,0:T(8,128)(2,1)S(1)}, bf16[128,128]{1,0:T(8,128)(2,1)S(1)}, u32[]{:S(2)}, u32[]{:S(2)}) collective-permute-start(bf16[128,128]{1,0:T(8,128)(2,1)S(1)} %fusion.1.refs_2_), channel_id=1, source_target_pairs={{0,16},{16,0},{1,17},{17,1},{2,18},{18,2},{3,19},{19,3},{4,20},{20... | collective-permute-start | bytes 98312 | tf_op jit(solution)/shard_map/ppermute | solution.py:17
  8.3 3.0 %copy-start.1 = (bf16[1,1024,128]{2,1,0:T(8,128)(2,1)S(1)}, bf16[1,1024,128]{2,1,0:T(8,128)(2,1)}, u32[]{:S(2)}) copy-start(bf16[1,1024,128]{2,1,0:T(8,128)(2,1)} %param.7) | copy-start | bytes 786436
  27.4 3.8 %collective-permute-start.3 = (bf16[64,128]{1,0:T(8,128)(2,1)S(1)}, bf16[64,128]{1,0:T(8,128)(2,1)S(1)}, u32[]{:S(2)}, u32[]{:S(2)}) collective-permute-start(bf16[64,128]{1,0:T(8,128)(2,1)S(1)} %get-tuple-element.47), channel_id=1, source_target_pairs={{0,8},{1,9},{2,10},{3,11},{4,12},{5,13},{6,14},{7,15},{16,24},{17,... | collective-permute-start | bytes 49160 | tf_op jit(solution)/shard_map/ppermute | solution.py:12

commit v18 on v17

--- a/solution.py
+++ b/solution.py
@@ -42,16 +42,24 @@
     return both[: value.shape[0]] + both[value.shape[0] :]
 
 
+def use_basis(next_ref, inverse_ref, applied_ref, high_ref, low_ref, shift_ref):
+    flipped = next_ref[...].T
+    high_ref[...], low_ref[...] = split(product(flipped, inverse_ref[...]))
+    shift_ref[...] = product(flipped, applied_ref[...]).T.astype(jnp.bfloat16)
+
+
 def make_maps(layers, *refs):
     lefts = jnp.concatenate([ref[...] for ref in refs[:layers]], axis=1)
     cores = jnp.concatenate([ref[...] for ref in refs[layers : 2 * layers]], axis=0)
-    weights_ref, shift_ref, range_ref, sent_ref = refs[2 * layers :]
+    high_ref, low_ref, shift_ref, range_ref, sent_ref = refs[2 * layers :]
     range_ref[...] = (-product(lefts, cores)).astype(jnp.bfloat16)
-    map_t = wide(wide(weights_ref[...], lefts), cores).T.astype(jnp.bfloat16)
-    rank = map_t.shape[0]
+    parts = product(jnp.concatenate([high_ref[...], low_ref[...]]), lefts)
+    rank = parts.shape[0] // 2
+    map_t = wide(parts[:rank] + parts[rank:], cores).T.astype(jnp.bfloat16)
+    share = sent_ref.shape[1] - rank
     for target in range(sent_ref.shape[0]):
         sent_ref[target, :rank] = map_t
-        sent_ref[target, rank:] = shift_ref[target]
+        sent_ref[target, rank:] = shift_ref[target * share : (target + 1) * share]
 
 
 def chain(steps_ref, state, values_ref):
@@ -128,16 +136,21 @@
     core = project(right_factors[0], sketch).astype(half)
     cores = [core] + [rotated(core, "layer", k) for k in range(1, layers)]
 
-    shift_t = project(applied, next_rows).astype(half).reshape(lowers, share, rank)
-    weights = project(next_rows, inverse_diag)
+    high, low, shift_t = local(
+        use_basis,
+        (next_rows, inverse_diag, applied),
+        ((rank, order), half),
+        ((rank, order), half),
+        ((width, rank), half),
+    )
     entry = lax.dynamic_slice_in_dim(incoming, lower * share, share, 1)
     place = upper.reshape(1)
-    lefts[-1], shift_t, weights, entry, place = lax.optimization_barrier(
-        (lefts[-1], shift_t, weights, entry, place)
+    lefts[-1], shift_t, entry, place = lax.optimization_barrier(
+        (lefts[-1], shift_t, entry, place)
     )
     tile_range, sent = local(
         lambda *refs: make_maps(layers, *refs),
-        (*lefts, *cores, weights, shift_t),
+        (*lefts, *cores, high, low, shift_t),
         ((order, rank), half),
         ((lowers, rank + share, rank), half),
     )

time: 40.8 us -> 43.1 us (1.056)
  Pallas kernels: 2.03 us -> 4.61 us
  blocking collectives: 21.9 us -> 20.4 us
  matrix products: 7.91 us -> 6.52 us
  starting transfers between devices: 6.95 us -> 8.2 us
  local copies, waits for them, and re-layouts: 0.93 us -> 2.17 us
    dot_general x3 -> x1, matrix products: 3.17 us -> 0.28 us  [project(): lax.dot_general(basis, vectors, (((0,), (0,)), ((), ())), preferred_eleme...]
    pallas_call x4 -> x5, Pallas kernels: 2.03 us -> 4.61 us  [local(): pl.pallas_call(kernel, in_specs=specs, out_specs=[VMEM] * len(outputs), o...]
    dot_general x2, matrix products: 3.31 us -> 4.8 us  [product(): return jnp.dot(a, b, preferred_element_type=jnp.float32)]
    all_to_all x2, blocking collectives: 21.9 us -> 20.4 us  [exchanged(): lax.all_to_all(blocks, 'row', 0, 0, axis_index_groups=members, tiled=True)]
    ppermute x2, starting transfers between devices: 3.67 us -> 4.97 us  [shifted(): lax.ppermute(value, axis, [(source, source + steps) for source in range(l...]
    unnamed x8 -> x14, local copies, waits for them, and re-layouts: 0.02 us -> 1.25 us
  transfers between devices with their start and end apart: 4 -> 4, of which waited for: 1 -> 2; matrix products, arithmetic and copies ran while one was open for 18% -> 14% of each run, Pallas kernels for 0% -> 4%
where the time goes in v18:
time: 43.1 us; the launch traced here: 42.7 us
  blocking collectives  20.4 us (47%)
  starting transfers between devices  8.2 us (19%)
  matrix products  6.52 us (15%)
  Pallas kernels  4.61 us (11%)
  local copies, waits for them, and re-layouts  2.17 us (5%)
  waiting for transfers between devices  0.67 us (2%)
    all_to_all x2, blocking collectives, exchanged(): lax.all_to_all(blocks, 'row', 0, 0, axis_index_groups=members, tiled=True)  20.4 us
    ppermute x2, starting transfers between devices, shifted(): lax.ppermute(value, axis, [(source, source + steps) for source in range(l...  4.97 us
    dot_general x2, matrix products, product(): return jnp.dot(a, b, preferred_element_type=jnp.float32)  4.8 us
    pallas_call x5, Pallas kernels, local(): pl.pallas_call(kernel, in_specs=specs, out_specs=[VMEM] * len(outputs), o...  4.61 us
    ppermute x2, starting transfers between devices, rotated(): lax.ppermute(value, axis, [(source, (source + steps) % count) for source...  3.23 us
    dot_general x1, matrix products, body(): lax.dot_general(gain, coupled, FLIPPED, preferred_element_type=jnp.float32)  1.43 us
    unnamed x14, local copies, waits for them, and re-layouts  1.25 us
    dynamic_slice x1, local copies, waits for them, and re-layouts, body(): entry = lax.dynamic_slice_in_dim(incoming, lower * share, share, 1)  0.91 us
  transfers between devices with their start and end apart: 4, of which 2 were waited for; matrix products, arithmetic and copies ran while one was open for 14% of the time, Pallas kernels for 4%

profile of v18, /device:TPU:0, one launch (start us, length us, event | category | flops | bytes accessed | tf_op | source)
XLA Modules:
  0.0 42.7 jit_solution(363096002006705715)
XLA Ops:
  0.0 0.0 copy-start
  0.0 3.0 %collective-permute-start = (bf16[1024,128]{1,0:T(8,128)(2,1)}, bf16[1024,128]{1,0:T(8,128)(2,1)}, u32[]{:S(2)}, u32[]{:S(2)}) collective-permute-start(bf16[1024,128]{1,0:T(8,128)(2,1)} %bitcast.17), channel_id=1, source_target_pairs={{0,16},{16,0},{1,17},{17,1},{2,18},{18,2},{3,19},{19,3},{4,20},{20... | collective-permute-start | bytes 786440 | tf_op jit(solution)/shard_map/ppermute | solution.py:17
  3.0 1.3 %collective-permute-start.1 = (bf16[1024,128]{1,0:T(8,128)(2,1)}, bf16[1024,128]{1,0:T(8,128)(2,1)}, u32[]{:S(2)}, u32[]{:S(2)}) collective-permute-start(bf16[1024,128]{1,0:T(8,128)(2,1)} %param.10), channel_id=1, source_target_pairs={{1,0},{2,1},{3,2},{4,3},{5,4},{6,5},{7,6},{8,7},{9,8},{10,9},{11,1... | collective-permute-start | bytes 786440 | tf_op jit(solution)/shard_map/ppermute | solution.py:12
  4.3 4.0 %convolution_convert_fusion.applied_ref = bf16[1024,512]{1,0:T(8,128)(2,1)} fusion(bf16[1024,1024]{1,0:T(8,128)(2,1)} %inverse_ref.1, bf16[1024,512]{1,0:T(8,128)(2,1)S(1)} %copy-done), kind=kOutput, calls=%fused_computation.1 | convolution fusion | flops 1074266112 | bytes 4194304 | tf_op jit(solution)/shard_map/dot_general | solution.py:27
  8.3 0.0 copy-done.5
  8.3 0.3 fusion.1.refs_2_
  8.6 0.2 collective-permute-start.2
  8.8 0.9 %constant_dynamic-slice_fusion.entry_ref = f32[128,64]{1,0:T(8,128)S(1)} fusion(f32[128,512]{1,0:T(8,128)} %param.13, s32[]{:T(128)S(6)} %select_n.3), kind=kLoop, calls=%fused_computation.7 | loop fusion | bytes 65540 | tf_op jit(solution)/shard_map/dynamic_slice | solution.py:146
  9.7 0.0 collective-permute-done.1.next_ref
  9.7 0.0 copy-start.2
  9.7 1.2 %copy-done.2 = bf16[1024,512]{1,0:T(8,128)(2,1)S(1)} copy-done((bf16[1024,512]{1,0:T(8,128)(2,1)S(1)}, bf16[1024,512]{1,0:T(8,128)(2,1)}, u32[]{:S(2)}) %copy-start.2) | copy-done | bytes 1048600
  11.0 1.6 %shard_map.73 = (bf16[128,1024]{1,0:T(8,128)(2,1)S(1)}, bf16[128,1024]{1,0:T(8,128)(2,1)S(1)}, bf16[512,128]{1,0:T(8,128)(2,1)S(1)}) custom-call(bf16[1024,128]{1,0:T(8,128)(2,1)} %collective-permute-done.1.next_ref, bf16[1024,1024]{1,0:T(8,128)(2,1)S(1)} %copy-done.1, bf16[1024,512]{1,0:T(8,128)(2,1)S(1)} %copy-done.2), custom_call_target="tpu_custom_call" | custom-call | tf_op jit(solution)/shard_map/pallas_call | solution.py:107
  12.6 0.0 collective-permute-done.refs_1_
  12.6 0.1 collective-permute-done.2.refs_3_
  12.8 1.7 %shard_map.74 = (bf16[1024,128]{1,0:T(8,128)(2,1)S(1)}, bf16[8,192,128]{2,1,0:T(8,128)(2,1)S(1)}) custom-call(bf16[1024,128]{1,0:T(8,128)(2,1)S(1)} %bitcast.18, bf16[1024,128]{1,0:T(8,128)(2,1)} %collective-permute-done.refs_1_, bf16[128,128]{1,0:T(8,128)(2,1)S(1)} %fusion.1.refs_2_, bf16[128,128]{1,0:T(8,128)(2,1)S(1)} %collective-permute-done.2.refs_3_, ...), custom_call_target="tpu_custom_call" | custom-call | tf_op jit(solution)/shard_map/pallas_call | solution.py:107
  14.4 12.9 %all_to_all.10.steps_ref = bf16[8,192,128]{2,1,0:T(8,128)(2,1)S(1)} all-to-all(bf16[8,192,128]{2,1,0:T(8,128)(2,1)S(1)} %get-tuple-element.43), channel_id=1, replica_groups={{0,1,2,3,4,5,6,7},{8,9,10,11,12,13,14,15},{16,17,18,19,20,21,22,23},{24..., dimensions={0} | all-to-all | bytes 786432 | tf_op jit(solution)/shard_map/all_to_all | solution.py:118
  27.3 1.1 %shard_map.75 = (f32[8,64,128]{2,1,0:T(8,128)S(1)}, bf16[64,128]{1,0:T(8,128)(2,1)S(1)}) custom-call(s32[1]{0:T(128)} %bitcast.1.upper_ref, bf16[8,192,128]{2,1,0:T(8,128)(2,1)S(1)} %all_to_all.10.steps_ref, f32[128,64]{1,0:T(8,128)S(1)} %constant_dynamic-slice_fusion.entry_ref), custom_call_target="tpu_custom_call" | custom-call | tf_op jit(solution)/shard_map/pallas_call | solution.py:107
  28.4 0.0 copy-start.3
  28.4 3.7 %collective-permute-start.3 = (bf16[64,128]{1,0:T(8,128)(2,1)S(1)}, bf16[64,128]{1,0:T(8,128)(2,1)S(1)}, u32[]{:S(2)}, u32[]{:S(2)}) collective-permute-start(bf16[64,128]{1,0:T(8,128)(2,1)S(1)} %get-tuple-element.51), channel_id=1, source_target_pairs={{0,8},{1,9},{2,10},{3,11},{4,12},{5,13},{6,14},{7,15},{16,24},{17,... | collective-permute-start | bytes 49160 | tf_op jit(solution)/shard_map/ppermute | solution.py:12
  32.1 0.8 %fusion = bf16[1024,128]{0,1:T(8,128)(2,1)S(1)} fusion(bf16[1024,128]{1,0:T(8,128)(2,1)S(1)} %get-tuple-element.52, bf16[1024,1024]{1,0:T(8,128)(2,1)S(1)} %copy-done.1), kind=kOutput, calls=%fused_computation.3 | convolution fusion | flops 268566528 | bytes 2621440 | tf_op jit(solution)/shard_map/dot_general | solution.py:27
  33.0 0.5 %collective-permute-done.3.entered_ref = bf16[64,128]{1,0:T(8,128)(2,1)S(1)} collective-permute-done((bf16[64,128]{1,0:T(8,128)(2,1)S(1)}, bf16[64,128]{1,0:T(8,128)(2,1)S(1)}, u32[]{:S(2)}, u32[]{:S(2)}) %collective-permute-start.3) | collective-permute-done | bytes 16416 | tf_op jit(solution)/shard_map/ppermute | solution.py:12
  33.5 0.2 shard_map.77
  33.7 7.6 %all_to_all.11 = bf16[8,64,128]{2,1,0:T(8,128)(2,1)S(1)} all-to-all(bf16[8,64,128]{2,1,0:T(8,128)(2,1)S(1)} %shard_map.77), channel_id=1, replica_groups={{0,1,2,3,4,5,6,7},{8,9,10,11,12,13,14,15},{16,17,18,19,20,21,22,23},{24..., dimensions={0} | all-to-all | bytes 262144 | tf_op jit(solution)/shard_map/all_to_all | solution.py:118
  41.3 1.4 %subtract_convert_fusion = bf16[1024,512]{1,0:T(8,128)(2,1)} fusion(bf16[1024,512]{1,0:T(8,128)(2,1)S(1)} %copy-done.3, bf16[1024,128]{0,1:T(8,128)(2,1)S(1)} %fusion, bf16[512,128]{1,0:T(8,128)(2,1)S(1)} %bitcast.19), kind=kOutput, calls=%fused_computation | convolution fusion | flops 135790592 | bytes 2490368 | tf_op jit(solution)/shard_map/dot_general | solution.py:181
  (10 shorter events, 0.1 us)
Async XLA Ops:
  0.0 4.3 %copy-start = (bf16[1024,512]{1,0:T(8,128)(2,1)S(1)}, bf16[1024,512]{1,0:T(8,128)(2,1)}, u32[]{:S(2)}) copy-start(bf16[1024,512]{1,0:T(8,128)(2,1)} %param.12) | copy-start | bytes 3145732
  0.0 8.3 %copy-start.5 = (bf16[1024,128]{1,0:T(8,128)(2,1)S(1)}, bf16[1024,128]{1,0:T(8,128)(2,1)}, u32[]{:S(2)}) copy-start(bf16[1024,128]{1,0:T(8,128)(2,1)} %param.9) | copy-start | bytes 786436
  0.0 8.3 %copy-start.6 = (bf16[1,1024,128]{2,1,0:T(8,128)(2,1)S(1)}, bf16[1,1024,128]{2,1,0:T(8,128)(2,1)}, u32[]{:S(2)}) copy-start(bf16[1,1024,128]{2,1,0:T(8,128)(2,1)} %param.8) | copy-start | bytes 786436
  0.0 12.6 %collective-permute-start = (bf16[1024,128]{1,0:T(8,128)(2,1)}, bf16[1024,128]{1,0:T(8,128)(2,1)}, u32[]{:S(2)}, u32[]{:S(2)}) collective-permute-start(bf16[1024,128]{1,0:T(8,128)(2,1)} %bitcast.17), channel_id=1, source_target_pairs={{0,16},{16,0},{1,17},{17,1},{2,18},{18,2},{3,19},{19,3},{4,20},{20... | collective-permute-start | bytes 786440 | tf_op jit(solution)/shard_map/ppermute | solution.py:17
  3.0 6.7 %collective-permute-start.1 = (bf16[1024,128]{1,0:T(8,128)(2,1)}, bf16[1024,128]{1,0:T(8,128)(2,1)}, u32[]{:S(2)}, u32[]{:S(2)}) collective-permute-start(bf16[1024,128]{1,0:T(8,128)(2,1)} %param.10), channel_id=1, source_target_pairs={{1,0},{2,1},{3,2},{4,3},{5,4},{6,5},{7,6},{8,7},{9,8},{10,9},{11,1... | collective-permute-start | bytes 786440 | tf_op jit(solution)/shard_map/ppermute | solution.py:12
  4.3 5.4 %copy-start.1 = (bf16[1024,1024]{1,0:T(8,128)(2,1)S(1)}, bf16[1024,1024]{1,0:T(8,128)(2,1)}, u32[]{:S(2)}) copy-start(bf16[1024,1024]{1,0:T(8,128)(2,1)} %inverse_ref.1) | copy-start | bytes 6291460
  8.3 4.5 %copy-start.4 = (bf16[1,1024,128]{2,1,0:T(8,128)(2,1)S(1)}, bf16[1,1024,128]{2,1,0:T(8,128)(2,1)}, u32[]{:S(2)}) copy-start(bf16[1,1024,128]{2,1,0:T(8,128)(2,1)} %param.7) | copy-start | bytes 786436
  8.6 4.2 %collective-permute-start.2 = (bf16[128,128]{1,0:T(8,128)(2,1)S(1)}, bf16[128,128]{1,0:T(8,128)(2,1)S(1)}, u32[]{:S(2)}, u32[]{:S(2)}) collective-permute-start(bf16[128,128]{1,0:T(8,128)(2,1)S(1)} %fusion.1.refs_2_), channel_id=1, source_target_pairs={{0,16},{16,0},{1,17},{17,1},{2,18},{18,2},{3,19},{19,3},{4,20},{20... | collective-permute-start | bytes 98312 | tf_op jit(solution)/shard_map/ppermute | solution.py:17
  9.7 1.2 %copy-start.2 = (bf16[1024,512]{1,0:T(8,128)(2,1)S(1)}, bf16[1024,512]{1,0:T(8,128)(2,1)}, u32[]{:S(2)}) copy-start(bf16[1024,512]{1,0:T(8,128)(2,1)} %convolution_convert_fusion.applied_ref) | copy-start | bytes 3145732
  28.4 12.9 %copy-start.3 = (bf16[1024,512]{1,0:T(8,128)(2,1)S(1)}, bf16[1024,512]{1,0:T(8,128)(2,1)}, u32[]{:S(2)}) copy-start(bf16[1024,512]{1,0:T(8,128)(2,1)} %convolution_convert_fusion.applied_ref) | copy-start | bytes 3145732
  28.4 5.1 %collective-permute-start.3 = (bf16[64,128]{1,0:T(8,128)(2,1)S(1)}, bf16[64,128]{1,0:T(8,128)(2,1)S(1)}, u32[]{:S(2)}, u32[]{:S(2)}) collective-permute-start(bf16[64,128]{1,0:T(8,128)(2,1)S(1)} %get-tuple-element.51), channel_id=1, source_target_pairs={{0,8},{1,9},{2,10},{3,11},{4,12},{5,13},{6,14},{7,15},{16,24},{17,... | collective-permute-start | bytes 49160 | tf_op jit(solution)/shard_map/ppermute | solution.py:12

commit v19 on v17

--- a/solution.py
+++ b/solution.py
@@ -42,6 +42,10 @@
     return both[: value.shape[0]] + both[value.shape[0] :]
 
 
+def make_shift(next_ref, applied_ref, shift_ref):
+    shift_ref[...] = project(next_ref[...], applied_ref[...]).T.astype(jnp.bfloat16)
+
+
 def make_maps(layers, *refs):
     lefts = jnp.concatenate([ref[...] for ref in refs[:layers]], axis=1)
     cores = jnp.concatenate([ref[...] for ref in refs[layers : 2 * layers]], axis=0)
@@ -49,9 +53,10 @@
     range_ref[...] = (-product(lefts, cores)).astype(jnp.bfloat16)
     map_t = wide(wide(weights_ref[...], lefts), cores).T.astype(jnp.bfloat16)
     rank = map_t.shape[0]
+    share = sent_ref.shape[1] - rank
     for target in range(sent_ref.shape[0]):
         sent_ref[target, :rank] = map_t
-        sent_ref[target, rank:] = shift_ref[target]
+        sent_ref[target, rank:] = shift_ref[target * share : (target + 1) * share]
 
 
 def chain(steps_ref, state, values_ref):
@@ -128,7 +133,7 @@
     core = project(right_factors[0], sketch).astype(half)
     cores = [core] + [rotated(core, "layer", k) for k in range(1, layers)]
 
-    shift_t = project(applied, next_rows).astype(half).reshape(lowers, share, rank)
+    (shift_t,) = local(make_shift, (next_rows, applied), ((width, rank), half))
     weights = project(next_rows, inverse_diag)
     entry = lax.dynamic_slice_in_dim(incoming, lower * share, share, 1)
     place = upper.reshape(1)

time: 40.8 us -> 40.4 us (level)
  matrix products: 7.91 us -> 5.49 us
  blocking collectives: 21.9 us -> 19.8 us
  waiting for transfers between devices: 0.57 us -> 2.6 us
  Pallas kernels: 2.03 us -> 3.37 us
  starting transfers between devices: 6.95 us -> 7.79 us
    dot_general x3 -> x2, matrix products: 3.17 us -> 0.74 us  [project(): lax.dot_general(basis, vectors, (((0,), (0,)), ((), ())), preferred_eleme...]
    all_to_all x2, blocking collectives: 21.9 us -> 19.8 us  [exchanged(): lax.all_to_all(blocks, 'row', 0, 0, axis_index_groups=members, tiled=True)]
    ppermute x2, waiting for transfers between devices: 0.05 us -> 2.08 us  [rotated(): lax.ppermute(value, axis, [(source, (source + steps) % count) for source...]
    pallas_call x4 -> x5, Pallas kernels: 2.03 us -> 3.37 us  [local(): pl.pallas_call(kernel, in_specs=specs, out_specs=[VMEM] * len(outputs), o...]
    ppermute x2, starting transfers between devices: 3.67 us -> 4.51 us  [shifted(): lax.ppermute(value, axis, [(source, source + steps) for source in range(l...]
  transfers between devices with their start and end apart: 4 -> 4, of which waited for: 1 -> 3; matrix products, arithmetic and copies ran while one was open for 18% -> 12% of each run, Pallas kernels for 0% -> 1%
where the time goes in v19:
time: 40.4 us; the launch traced here: 40.1 us
  blocking collectives  19.8 us (49%)
  starting transfers between devices  7.79 us (19%)
  matrix products  5.49 us (14%)
  Pallas kernels  3.37 us (8%)
  waiting for transfers between devices  2.6 us (6%)
  local copies, waits for them, and re-layouts  0.93 us (2%)
    all_to_all x2, blocking collectives, exchanged(): lax.all_to_all(blocks, 'row', 0, 0, axis_index_groups=members, tiled=True)  19.8 us
    ppermute x2, starting transfers between devices, shifted(): lax.ppermute(value, axis, [(source, source + steps) for source in range(l...  4.51 us
    pallas_call x5, Pallas kernels, local(): pl.pallas_call(kernel, in_specs=specs, out_specs=[VMEM] * len(outputs), o...  3.37 us
    dot_general x2, matrix products, product(): return jnp.dot(a, b, preferred_element_type=jnp.float32)  3.31 us
    ppermute x2, starting transfers between devices, rotated(): lax.ppermute(value, axis, [(source, (source + steps) % count) for source...  3.28 us
    ppermute x2, waiting for transfers between devices, rotated(): lax.ppermute(value, axis, [(source, (source + steps) % count) for source...  2.08 us
    dot_general x1, matrix products, body(): lax.dot_general(gain, coupled, FLIPPED, preferred_element_type=jnp.float32)  1.44 us
    dynamic_slice x1, local copies, waits for them, and re-layouts, body(): entry = lax.dynamic_slice_in_dim(incoming, lower * share, share, 1)  0.91 us
  transfers between devices with their start and end apart: 4, of which 3 were waited for; matrix products, arithmetic and copies ran while one was open for 12% of the time, Pallas kernels for 1%

profile of v19, /device:TPU:0, one launch (start us, length us, event | category | flops | bytes accessed | tf_op | source)
XLA Modules:
  0.0 40.1 jit_solution(6506828366396278966)
XLA Ops:
  0.0 0.0 copy-start
  0.0 3.0 %collective-permute-start = (bf16[1024,128]{1,0:T(8,128)(2,1)}, bf16[1024,128]{1,0:T(8,128)(2,1)}, u32[]{:S(2)}, u32[]{:S(2)}) collective-permute-start(bf16[1024,128]{1,0:T(8,128)(2,1)} %bitcast.19), channel_id=1, source_target_pairs={{0,16},{16,0},{1,17},{17,1},{2,18},{18,2},{3,19},{19,3},{4,20},{20... | collective-permute-start | bytes 786440 | tf_op jit(solution)/shard_map/ppermute | solution.py:17
  3.0 1.3 %collective-permute-start.1 = (bf16[1024,128]{1,0:T(8,128)(2,1)}, bf16[1024,128]{1,0:T(8,128)(2,1)S(1)}, u32[]{:S(2)}, u32[]{:S(2)}) collective-permute-start(bf16[1024,128]{1,0:T(8,128)(2,1)} %param.10), channel_id=1, source_target_pairs={{1,0},{2,1},{3,2},{4,3},{5,4},{6,5},{7,6},{8,7},{9,8},{10,9},{11,1... | collective-permute-start | bytes 786440 | tf_op jit(solution)/shard_map/ppermute | solution.py:12
  4.3 0.0 copy-done
  4.3 2.5 %convolution_convert_fusion.applied_ref = bf16[1024,512]{1,0:T(8,128)(2,1)S(1)} fusion(bf16[1024,1024]{1,0:T(8,128)(2,1)S(1)} %copy-done, bf16[1024,512]{1,0:T(8,128)(2,1)} %param.12), kind=kOutput, calls=%fused_computation.1 | convolution fusion | flops 1074266112 | bytes 4194304 | tf_op jit(solution)/shard_map/dot_general | solution.py:27
  6.8 0.0 copy-done.2
  6.8 0.0 copy-done.3
  6.8 0.3 fusion.1.refs_2_
  7.1 0.3 collective-permute-start.2
  7.4 0.9 %constant_dynamic-slice_fusion.entry_ref = f32[128,64]{1,0:T(8,128)S(1)} fusion(f32[128,512]{1,0:T(8,128)} %param.13, s32[]{:T(128)S(6)} %select_n.3), kind=kLoop, calls=%fused_computation.7 | loop fusion | bytes 65540 | tf_op jit(solution)/shard_map/dynamic_slice | solution.py:138
  8.3 0.0 collective-permute-done.1.next_ref
  8.3 0.5 %fusion.3.refs_4_ = f32[128,1024]{1,0:T(8,128)S(1)} fusion(bf16[1024,128]{1,0:T(8,128)(2,1)S(1)} %collective-permute-done.1.next_ref, bf16[1024,1024]{1,0:T(8,128)(2,1)S(1)} %copy-done), kind=kOutput, calls=%fused_computation.8 | convolution fusion | flops 268435456 | bytes 2883584 | tf_op jit(solution)/shard_map/dot_general | solution.py:21
  8.8 0.4 shard_map.73.refs_5_
  9.2 0.5 %collective-permute-done.refs_1_ = bf16[1024,128]{1,0:T(8,128)(2,1)} collective-permute-done((bf16[1024,128]{1,0:T(8,128)(2,1)}, bf16[1024,128]{1,0:T(8,128)(2,1)}, u32[]{:S(2)}, u32[]{:S(2)}) %collective-permute-start) | collective-permute-done | bytes 262176 | tf_op jit(solution)/shard_map/ppermute | solution.py:17
  9.6 1.6 %collective-permute-done.2.refs_3_ = bf16[128,128]{1,0:T(8,128)(2,1)S(1)} collective-permute-done((bf16[128,128]{1,0:T(8,128)(2,1)S(1)}, bf16[128,128]{1,0:T(8,128)(2,1)S(1)}, u32[]{:S(2)}, u32[]{:S(2)}) %collective-permute-start.2) | collective-permute-done | bytes 32800 | tf_op jit(solution)/shard_map/ppermute | solution.py:17
  11.3 1.6 %shard_map.74 = (bf16[1024,128]{1,0:T(8,128)(2,1)S(1)}, bf16[8,192,128]{2,1,0:T(8,128)(2,1)S(1)}) custom-call(bf16[1024,128]{1,0:T(8,128)(2,1)S(1)} %bitcast.20, bf16[1024,128]{1,0:T(8,128)(2,1)} %collective-permute-done.refs_1_, bf16[128,128]{1,0:T(8,128)(2,1)S(1)} %fusion.1.refs_2_, bf16[128,128]{1,0:T(8,128)(2,1)S(1)} %collective-permute-done.2.refs_3_, ...), custom_call_target="tpu_custom_call" | custom-call | tf_op jit(solution)/shard_map/pallas_call | solution.py:104
  12.9 12.3 %all_to_all.10.steps_ref = bf16[8,192,128]{2,1,0:T(8,128)(2,1)S(1)} all-to-all(bf16[8,192,128]{2,1,0:T(8,128)(2,1)S(1)} %get-tuple-element.39), channel_id=1, replica_groups={{0,1,2,3,4,5,6,7},{8,9,10,11,12,13,14,15},{16,17,18,19,20,21,22,23},{24..., dimensions={0} | all-to-all | bytes 786432 | tf_op jit(solution)/shard_map/all_to_all | solution.py:115
  25.2 1.1 %shard_map.75 = (f32[8,64,128]{2,1,0:T(8,128)S(1)}, bf16[64,128]{1,0:T(8,128)(2,1)S(1)}) custom-call(s32[1]{0:T(128)} %bitcast.1.upper_ref, bf16[8,192,128]{2,1,0:T(8,128)(2,1)S(1)} %all_to_all.10.steps_ref, f32[128,64]{1,0:T(8,128)S(1)} %constant_dynamic-slice_fusion.entry_ref), custom_call_target="tpu_custom_call" | custom-call | tf_op jit(solution)/shard_map/pallas_call | solution.py:104
  26.2 3.2 %collective-permute-start.3 = (bf16[64,128]{1,0:T(8,128)(2,1)S(1)}, bf16[64,128]{1,0:T(8,128)(2,1)S(1)}, u32[]{:S(2)}, u32[]{:S(2)}) collective-permute-start(bf16[64,128]{1,0:T(8,128)(2,1)S(1)} %get-tuple-element.47), channel_id=1, source_target_pairs={{0,8},{1,9},{2,10},{3,11},{4,12},{5,13},{6,14},{7,15},{16,24},{17,... | collective-permute-start | bytes 49160 | tf_op jit(solution)/shard_map/ppermute | solution.py:12
  29.5 0.8 %fusion = bf16[1024,128]{0,1:T(8,128)(2,1)S(1)} fusion(bf16[1024,128]{1,0:T(8,128)(2,1)S(1)} %get-tuple-element.48, bf16[1024,1024]{1,0:T(8,128)(2,1)S(1)} %copy-done), kind=kOutput, calls=%fused_computation.3 | convolution fusion | flops 268566528 | bytes 2621440 | tf_op jit(solution)/shard_map/dot_general | solution.py:27
  30.4 0.5 %collective-permute-done.3.entered_ref = bf16[64,128]{1,0:T(8,128)(2,1)S(1)} collective-permute-done((bf16[64,128]{1,0:T(8,128)(2,1)S(1)}, bf16[64,128]{1,0:T(8,128)(2,1)S(1)}, u32[]{:S(2)}, u32[]{:S(2)}) %collective-permute-start.3) | collective-permute-done | bytes 16416 | tf_op jit(solution)/shard_map/ppermute | solution.py:12
  30.9 0.2 shard_map.77
  31.1 7.6 %all_to_all.11 = bf16[8,64,128]{2,1,0:T(8,128)(2,1)S(1)} all-to-all(bf16[8,64,128]{2,1,0:T(8,128)(2,1)S(1)} %shard_map.77), channel_id=1, replica_groups={{0,1,2,3,4,5,6,7},{8,9,10,11,12,13,14,15},{16,17,18,19,20,21,22,23},{24..., dimensions={0} | all-to-all | bytes 262144 | tf_op jit(solution)/shard_map/all_to_all | solution.py:115
  38.7 1.4 %subtract_convert_fusion = bf16[1024,512]{1,0:T(8,128)(2,1)} fusion(bf16[1024,512]{1,0:T(8,128)(2,1)S(1)} %convolution_convert_fusion.applied_ref, bf16[1024,128]{0,1:T(8,128)(2,1)S(1)} %fusion, bf16[512,128]{1,0:T(8,128)(2,1)S(1)} %bitcast.21), kind=kOutput, calls=%fused_computation | convolution fusion | flops 135790592 | bytes 2490368 | tf_op jit(solution)/shard_map/dot_general | solution.py:173
  (5 shorter events, 0.1 us)
Async XLA Ops:
  0.0 4.3 %copy-start = (bf16[1024,1024]{1,0:T(8,128)(2,1)S(1)}, bf16[1024,1024]{1,0:T(8,128)(2,1)}, u32[]{:S(2)}) copy-start(bf16[1024,1024]{1,0:T(8,128)(2,1)} %param.11) | copy-start | bytes 6291460
  0.0 6.8 %copy-start.2 = (bf16[1024,128]{1,0:T(8,128)(2,1)S(1)}, bf16[1024,128]{1,0:T(8,128)(2,1)}, u32[]{:S(2)}) copy-start(bf16[1024,128]{1,0:T(8,128)(2,1)} %param.9) | copy-start | bytes 786436
  0.0 6.8 %copy-start.3 = (bf16[1,1024,128]{2,1,0:T(8,128)(2,1)S(1)}, bf16[1,1024,128]{2,1,0:T(8,128)(2,1)}, u32[]{:S(2)}) copy-start(bf16[1,1024,128]{2,1,0:T(8,128)(2,1)} %param.8) | copy-start | bytes 786436
  0.0 9.6 %collective-permute-start = (bf16[1024,128]{1,0:T(8,128)(2,1)}, bf16[1024,128]{1,0:T(8,128)(2,1)}, u32[]{:S(2)}, u32[]{:S(2)}) collective-permute-start(bf16[1024,128]{1,0:T(8,128)(2,1)} %bitcast.19), channel_id=1, source_target_pairs={{0,16},{16,0},{1,17},{17,1},{2,18},{18,2},{3,19},{19,3},{4,20},{20... | collective-permute-start | bytes 786440 | tf_op jit(solution)/shard_map/ppermute | solution.py:17
  3.0 5.3 %collective-permute-start.1 = (bf16[1024,128]{1,0:T(8,128)(2,1)}, bf16[1024,128]{1,0:T(8,128)(2,1)S(1)}, u32[]{:S(2)}, u32[]{:S(2)}) collective-permute-start(bf16[1024,128]{1,0:T(8,128)(2,1)} %param.10), channel_id=1, source_target_pairs={{1,0},{2,1},{3,2},{4,3},{5,4},{6,5},{7,6},{8,7},{9,8},{10,9},{11,1... | collective-permute-start | bytes 786440 | tf_op jit(solution)/shard_map/ppermute | solution.py:12
  7.1 4.2 %collective-permute-start.2 = (bf16[128,128]{1,0:T(8,128)(2,1)S(1)}, bf16[128,128]{1,0:T(8,128)(2,1)S(1)}, u32[]{:S(2)}, u32[]{:S(2)}) collective-permute-start(bf16[128,128]{1,0:T(8,128)(2,1)S(1)} %fusion.1.refs_2_), channel_id=1, source_target_pairs={{0,16},{16,0},{1,17},{17,1},{2,18},{18,2},{3,19},{19,3},{4,20},{20... | collective-permute-start | bytes 98312 | tf_op jit(solution)/shard_map/ppermute | solution.py:17
  8.3 3.0 %copy-start.1 = (bf16[1,1024,128]{2,1,0:T(8,128)(2,1)S(1)}, bf16[1,1024,128]{2,1,0:T(8,128)(2,1)}, u32[]{:S(2)}) copy-start(bf16[1,1024,128]{2,1,0:T(8,128)(2,1)} %param.7) | copy-start | bytes 786436
  26.2 4.7 %collective-permute-start.3 = (bf16[64,128]{1,0:T(8,128)(2,1)S(1)}, bf16[64,128]{1,0:T(8,128)(2,1)S(1)}, u32[]{:S(2)}, u32[]{:S(2)}) collective-permute-start(bf16[64,128]{1,0:T(8,128)(2,1)S(1)} %get-tuple-element.47), channel_id=1, source_target_pairs={{0,8},{1,9},{2,10},{3,11},{4,12},{5,13},{6,14},{7,15},{16,24},{17,... | collective-permute-start | bytes 49160 | tf_op jit(solution)/shard_map/ppermute | solution.py:12

commit v20 on v19

--- a/solution.py
+++ b/solution.py
@@ -107,7 +107,7 @@
         out_specs=[VMEM] * len(outputs),
         out_shape=[jax.ShapeDtypeStruct(*output) for output in outputs],
         input_output_aliases=aliases,
-        compiler_params=pltpu.CompilerParams(vmem_limit_bytes=16 * 2**20),
+        compiler_params=pltpu.CompilerParams(vmem_limit_bytes=6 * 2**20),
     )(*inputs)
 
 

time: 40.4 us -> 40.4 us (level)
  no operation moved by 1% of the time
where the time goes in v20:
time: 40.4 us; the launch traced here: 40.1 us
  blocking collectives  19.8 us (49%)
  starting transfers between devices  7.79 us (19%)
  matrix products  5.49 us (14%)
  Pallas kernels  3.37 us (8%)
  waiting for transfers between devices  2.6 us (6%)
  local copies, waits for them, and re-layouts  0.93 us (2%)
    all_to_all x2, blocking collectives, exchanged(): lax.all_to_all(blocks, 'row', 0, 0, axis_index_groups=members, tiled=True)  19.8 us
    ppermute x2, starting transfers between devices, shifted(): lax.ppermute(value, axis, [(source, source + steps) for source in range(l...  4.51 us
    pallas_call x5, Pallas kernels, local(): pl.pallas_call(kernel, in_specs=specs, out_specs=[VMEM] * len(outputs), o...  3.37 us
    dot_general x2, matrix products, product(): return jnp.dot(a, b, preferred_element_type=jnp.float32)  3.31 us
    ppermute x2, starting transfers between devices, rotated(): lax.ppermute(value, axis, [(source, (source + steps) % count) for source...  3.28 us
    ppermute x2, waiting for transfers between devices, rotated(): lax.ppermute(value, axis, [(source, (source + steps) % count) for source...  2.08 us
    dot_general x1, matrix products, body(): lax.dot_general(gain, coupled, FLIPPED, preferred_element_type=jnp.float32)  1.44 us
    dynamic_slice x1, local copies, waits for them, and re-layouts, body(): entry = lax.dynamic_slice_in_dim(incoming, lower * share, share, 1)  0.91 us
  transfers between devices with their start and end apart: 4, of which 3 were waited for; matrix products, arithmetic and copies ran while one was open for 12% of the time, Pallas kernels for 1%

profile of v20, /device:TPU:0, one launch (start us, length us, event | category | flops | bytes accessed | tf_op | source)
XLA Modules:
  0.0 40.1 jit_solution(4289494085506712714)
XLA Ops:
  0.0 0.0 copy-start
  0.0 3.0 %collective-permute-start = (bf16[1024,128]{1,0:T(8,128)(2,1)}, bf16[1024,128]{1,0:T(8,128)(2,1)}, u32[]{:S(2)}, u32[]{:S(2)}) collective-permute-start(bf16[1024,128]{1,0:T(8,128)(2,1)} %bitcast.19), channel_id=1, source_target_pairs={{0,16},{16,0},{1,17},{17,1},{2,18},{18,2},{3,19},{19,3},{4,20},{20... | collective-permute-start | bytes 786440 | tf_op jit(solution)/shard_map/ppermute | solution.py:17
  3.0 1.3 %collective-permute-start.1 = (bf16[1024,128]{1,0:T(8,128)(2,1)}, bf16[1024,128]{1,0:T(8,128)(2,1)S(1)}, u32[]{:S(2)}, u32[]{:S(2)}) collective-permute-start(bf16[1024,128]{1,0:T(8,128)(2,1)} %param.10), channel_id=1, source_target_pairs={{1,0},{2,1},{3,2},{4,3},{5,4},{6,5},{7,6},{8,7},{9,8},{10,9},{11,1... | collective-permute-start | bytes 786440 | tf_op jit(solution)/shard_map/ppermute | solution.py:12
  4.3 0.0 copy-done
  4.3 2.5 %convolution_convert_fusion.applied_ref = bf16[1024,512]{1,0:T(8,128)(2,1)S(1)} fusion(bf16[1024,1024]{1,0:T(8,128)(2,1)S(1)} %copy-done, bf16[1024,512]{1,0:T(8,128)(2,1)} %param.12), kind=kOutput, calls=%fused_computation.1 | convolution fusion | flops 1074266112 | bytes 4194304 | tf_op jit(solution)/shard_map/dot_general | solution.py:27
  6.8 0.0 copy-done.2
  6.8 0.0 copy-done.3
  6.8 0.3 fusion.1.refs_2_
  7.1 0.3 collective-permute-start.2
  7.4 0.9 %constant_dynamic-slice_fusion.entry_ref = f32[128,64]{1,0:T(8,128)S(1)} fusion(f32[128,512]{1,0:T(8,128)} %param.13, s32[]{:T(128)S(6)} %select_n.3), kind=kLoop, calls=%fused_computation.7 | loop fusion | bytes 65540 | tf_op jit(solution)/shard_map/dynamic_slice | solution.py:138
  8.3 0.0 collective-permute-done.1.next_ref
  8.3 0.5 %fusion.3.refs_4_ = f32[128,1024]{1,0:T(8,128)S(1)} fusion(bf16[1024,128]{1,0:T(8,128)(2,1)S(1)} %collective-permute-done.1.next_ref, bf16[1024,1024]{1,0:T(8,128)(2,1)S(1)} %copy-done), kind=kOutput, calls=%fused_computation.8 | convolution fusion | flops 268435456 | bytes 2883584 | tf_op jit(solution)/shard_map/dot_general | solution.py:21
  8.8 0.4 shard_map.73.refs_5_
  9.2 0.5 %collective-permute-done.refs_1_ = bf16[1024,128]{1,0:T(8,128)(2,1)} collective-permute-done((bf16[1024,128]{1,0:T(8,128)(2,1)}, bf16[1024,128]{1,0:T(8,128)(2,1)}, u32[]{:S(2)}, u32[]{:S(2)}) %collective-permute-start) | collective-permute-done | bytes 262176 | tf_op jit(solution)/shard_map/ppermute | solution.py:17
  9.6 1.6 %collective-permute-done.2.refs_3_ = bf16[128,128]{1,0:T(8,128)(2,1)S(1)} collective-permute-done((bf16[128,128]{1,0:T(8,128)(2,1)S(1)}, bf16[128,128]{1,0:T(8,128)(2,1)S(1)}, u32[]{:S(2)}, u32[]{:S(2)}) %collective-permute-start.2) | collective-permute-done | bytes 32800 | tf_op jit(solution)/shard_map/ppermute | solution.py:17
  11.3 1.6 %shard_map.74 = (bf16[1024,128]{1,0:T(8,128)(2,1)S(1)}, bf16[8,192,128]{2,1,0:T(8,128)(2,1)S(1)}) custom-call(bf16[1024,128]{1,0:T(8,128)(2,1)S(1)} %bitcast.20, bf16[1024,128]{1,0:T(8,128)(2,1)} %collective-permute-done.refs_1_, bf16[128,128]{1,0:T(8,128)(2,1)S(1)} %fusion.1.refs_2_, bf16[128,128]{1,0:T(8,128)(2,1)S(1)} %collective-permute-done.2.refs_3_, ...), custom_call_target="tpu_custom_call" | custom-call | tf_op jit(solution)/shard_map/pallas_call | solution.py:104
  12.9 12.3 %all_to_all.10.steps_ref = bf16[8,192,128]{2,1,0:T(8,128)(2,1)S(1)} all-to-all(bf16[8,192,128]{2,1,0:T(8,128)(2,1)S(1)} %get-tuple-element.39), channel_id=1, replica_groups={{0,1,2,3,4,5,6,7},{8,9,10,11,12,13,14,15},{16,17,18,19,20,21,22,23},{24..., dimensions={0} | all-to-all | bytes 786432 | tf_op jit(solution)/shard_map/all_to_all | solution.py:115
  25.2 1.1 %shard_map.75 = (f32[8,64,128]{2,1,0:T(8,128)S(1)}, bf16[64,128]{1,0:T(8,128)(2,1)S(1)}) custom-call(s32[1]{0:T(128)} %bitcast.1.upper_ref, bf16[8,192,128]{2,1,0:T(8,128)(2,1)S(1)} %all_to_all.10.steps_ref, f32[128,64]{1,0:T(8,128)S(1)} %constant_dynamic-slice_fusion.entry_ref), custom_call_target="tpu_custom_call" | custom-call | tf_op jit(solution)/shard_map/pallas_call | solution.py:104
  26.2 3.2 %collective-permute-start.3 = (bf16[64,128]{1,0:T(8,128)(2,1)S(1)}, bf16[64,128]{1,0:T(8,128)(2,1)S(1)}, u32[]{:S(2)}, u32[]{:S(2)}) collective-permute-start(bf16[64,128]{1,0:T(8,128)(2,1)S(1)} %get-tuple-element.47), channel_id=1, source_target_pairs={{0,8},{1,9},{2,10},{3,11},{4,12},{5,13},{6,14},{7,15},{16,24},{17,... | collective-permute-start | bytes 49160 | tf_op jit(solution)/shard_map/ppermute | solution.py:12
  29.5 0.8 %fusion = bf16[1024,128]{0,1:T(8,128)(2,1)S(1)} fusion(bf16[1024,128]{1,0:T(8,128)(2,1)S(1)} %get-tuple-element.48, bf16[1024,1024]{1,0:T(8,128)(2,1)S(1)} %copy-done), kind=kOutput, calls=%fused_computation.3 | convolution fusion | flops 268566528 | bytes 2621440 | tf_op jit(solution)/shard_map/dot_general | solution.py:27
  30.4 0.5 %collective-permute-done.3.entered_ref = bf16[64,128]{1,0:T(8,128)(2,1)S(1)} collective-permute-done((bf16[64,128]{1,0:T(8,128)(2,1)S(1)}, bf16[64,128]{1,0:T(8,128)(2,1)S(1)}, u32[]{:S(2)}, u32[]{:S(2)}) %collective-permute-start.3) | collective-permute-done | bytes 16416 | tf_op jit(solution)/shard_map/ppermute | solution.py:12
  30.9 0.2 shard_map.77
  31.1 7.6 %all_to_all.11 = bf16[8,64,128]{2,1,0:T(8,128)(2,1)S(1)} all-to-all(bf16[8,64,128]{2,1,0:T(8,128)(2,1)S(1)} %shard_map.77), channel_id=1, replica_groups={{0,1,2,3,4,5,6,7},{8,9,10,11,12,13,14,15},{16,17,18,19,20,21,22,23},{24..., dimensions={0} | all-to-all | bytes 262144 | tf_op jit(solution)/shard_map/all_to_all | solution.py:115
  38.7 1.4 %subtract_convert_fusion = bf16[1024,512]{1,0:T(8,128)(2,1)} fusion(bf16[1024,512]{1,0:T(8,128)(2,1)S(1)} %convolution_convert_fusion.applied_ref, bf16[1024,128]{0,1:T(8,128)(2,1)S(1)} %fusion, bf16[512,128]{1,0:T(8,128)(2,1)S(1)} %bitcast.21), kind=kOutput, calls=%fused_computation | convolution fusion | flops 135790592 | bytes 2490368 | tf_op jit(solution)/shard_map/dot_general | solution.py:173
  (5 shorter events, 0.1 us)
Async XLA Ops:
  0.0 4.3 %copy-start = (bf16[1024,1024]{1,0:T(8,128)(2,1)S(1)}, bf16[1024,1024]{1,0:T(8,128)(2,1)}, u32[]{:S(2)}) copy-start(bf16[1024,1024]{1,0:T(8,128)(2,1)} %param.11) | copy-start | bytes 6291460
  0.0 6.8 %copy-start.2 = (bf16[1024,128]{1,0:T(8,128)(2,1)S(1)}, bf16[1024,128]{1,0:T(8,128)(2,1)}, u32[]{:S(2)}) copy-start(bf16[1024,128]{1,0:T(8,128)(2,1)} %param.9) | copy-start | bytes 786436
  0.0 6.8 %copy-start.3 = (bf16[1,1024,128]{2,1,0:T(8,128)(2,1)S(1)}, bf16[1,1024,128]{2,1,0:T(8,128)(2,1)}, u32[]{:S(2)}) copy-start(bf16[1,1024,128]{2,1,0:T(8,128)(2,1)} %param.8) | copy-start | bytes 786436
  0.0 9.6 %collective-permute-start = (bf16[1024,128]{1,0:T(8,128)(2,1)}, bf16[1024,128]{1,0:T(8,128)(2,1)}, u32[]{:S(2)}, u32[]{:S(2)}) collective-permute-start(bf16[1024,128]{1,0:T(8,128)(2,1)} %bitcast.19), channel_id=1, source_target_pairs={{0,16},{16,0},{1,17},{17,1},{2,18},{18,2},{3,19},{19,3},{4,20},{20... | collective-permute-start | bytes 786440 | tf_op jit(solution)/shard_map/ppermute | solution.py:17
  3.0 5.3 %collective-permute-start.1 = (bf16[1024,128]{1,0:T(8,128)(2,1)}, bf16[1024,128]{1,0:T(8,128)(2,1)S(1)}, u32[]{:S(2)}, u32[]{:S(2)}) collective-permute-start(bf16[1024,128]{1,0:T(8,128)(2,1)} %param.10), channel_id=1, source_target_pairs={{1,0},{2,1},{3,2},{4,3},{5,4},{6,5},{7,6},{8,7},{9,8},{10,9},{11,1... | collective-permute-start | bytes 786440 | tf_op jit(solution)/shard_map/ppermute | solution.py:12
  7.1 4.2 %collective-permute-start.2 = (bf16[128,128]{1,0:T(8,128)(2,1)S(1)}, bf16[128,128]{1,0:T(8,128)(2,1)S(1)}, u32[]{:S(2)}, u32[]{:S(2)}) collective-permute-start(bf16[128,128]{1,0:T(8,128)(2,1)S(1)} %fusion.1.refs_2_), channel_id=1, source_target_pairs={{0,16},{16,0},{1,17},{17,1},{2,18},{18,2},{3,19},{19,3},{4,20},{20... | collective-permute-start | bytes 98312 | tf_op jit(solution)/shard_map/ppermute | solution.py:17
  8.3 3.0 %copy-start.1 = (bf16[1,1024,128]{2,1,0:T(8,128)(2,1)S(1)}, bf16[1,1024,128]{2,1,0:T(8,128)(2,1)}, u32[]{:S(2)}) copy-start(bf16[1,1024,128]{2,1,0:T(8,128)(2,1)} %param.7) | copy-start | bytes 786436
  26.2 4.7 %collective-permute-start.3 = (bf16[64,128]{1,0:T(8,128)(2,1)S(1)}, bf16[64,128]{1,0:T(8,128)(2,1)S(1)}, u32[]{:S(2)}, u32[]{:S(2)}) collective-permute-start(bf16[64,128]{1,0:T(8,128)(2,1)S(1)} %get-tuple-element.47), channel_id=1, source_target_pairs={{0,8},{1,9},{2,10},{3,11},{4,12},{5,13},{6,14},{7,15},{16,24},{17,... | collective-permute-start | bytes 49160 | tf_op jit(solution)/shard_map/ppermute | solution.py:12

commit v21 on v19

--- a/solution.py
+++ b/solution.py
@@ -46,10 +46,16 @@
     shift_ref[...] = project(next_ref[...], applied_ref[...]).T.astype(jnp.bfloat16)
 
 
+def lay(*refs):
+    rank = refs[0].shape[1]
+    for layer, ref in enumerate(refs[:-1]):
+        refs[-1][:, layer * rank : (layer + 1) * rank] = ref[...]
+
+
 def make_maps(layers, *refs):
-    lefts = jnp.concatenate([ref[...] for ref in refs[:layers]], axis=1)
-    cores = jnp.concatenate([ref[...] for ref in refs[layers : 2 * layers]], axis=0)
-    weights_ref, shift_ref, range_ref, sent_ref = refs[2 * layers :]
+    cores = jnp.concatenate([ref[...] for ref in refs[:layers]], axis=0)
+    lefts_ref, weights_ref, shift_ref, range_ref, sent_ref = refs[layers:]
+    lefts = lefts_ref[...]
     range_ref[...] = (-product(lefts, cores)).astype(jnp.bfloat16)
     map_t = wide(wide(weights_ref[...], lefts), cores).T.astype(jnp.bfloat16)
     rank = map_t.shape[0]
@@ -133,16 +139,18 @@
     core = project(right_factors[0], sketch).astype(half)
     cores = [core] + [rotated(core, "layer", k) for k in range(1, layers)]
 
+    (side,) = local(lay, lefts, ((order, layers * rank), half))
+    next_rows, side = lax.optimization_barrier((next_rows, side))
     (shift_t,) = local(make_shift, (next_rows, applied), ((width, rank), half))
     weights = project(next_rows, inverse_diag)
     entry = lax.dynamic_slice_in_dim(incoming, lower * share, share, 1)
     place = upper.reshape(1)
-    lefts[-1], shift_t, weights, entry, place = lax.optimization_barrier(
-        (lefts[-1], shift_t, weights, entry, place)
+    side, shift_t, weights, entry, place = lax.optimization_barrier(
+        (side, shift_t, weights, entry, place)
     )
     tile_range, sent = local(
         lambda *refs: make_maps(layers, *refs),
-        (*lefts, *cores, weights, shift_t),
+        (*cores, side, weights, shift_t),
         ((order, rank), half),
         ((lowers, rank + share, rank), half),
     )

time: 40.4 us -> 40.6 us (level)
  local copies, waits for them, and re-layouts: 0.93 us -> 1.88 us
  waiting for transfers between devices: 2.6 us -> 1.9 us
    unnamed x8, local copies, waits for them, and re-layouts: 0.02 us -> 0.96 us
    ppermute x2, waiting for transfers between devices: 2.08 us -> 1.36 us  [rotated(): lax.ppermute(value, axis, [(source, (source + steps) % count) for source...]
    pallas_call x5 -> x6, Pallas kernels: 3.37 us -> 3.47 us  [local(): pl.pallas_call(kernel, in_specs=specs, out_specs=[VMEM] * len(outputs), o...]
  transfers between devices with their start and end apart: 4 -> 4, of which waited for: 3 -> 2; matrix products, arithmetic and copies ran while one was open for 12% -> 12% of each run, Pallas kernels for 1% -> 4%
where the time goes in v21:
time: 40.6 us; the launch traced here: 40.3 us
  blocking collectives  19.5 us (48%)
  starting transfers between devices  7.96 us (20%)
  matrix products  5.47 us (13%)
  Pallas kernels  3.47 us (9%)
  waiting for transfers between devices  1.9 us (5%)
  local copies, waits for them, and re-layouts  1.88 us (5%)
    all_to_all x2, blocking collectives, exchanged(): lax.all_to_all(blocks, 'row', 0, 0, axis_index_groups=members, tiled=True)  19.5 us
    ppermute x2, starting transfers between devices, shifted(): lax.ppermute(value, axis, [(source, source + steps) for source in range(l...  4.68 us
    pallas_call x6, Pallas kernels, local(): pl.pallas_call(kernel, in_specs=specs, out_specs=[VMEM] * len(outputs), o...  3.47 us
    dot_general x2, matrix products, product(): return jnp.dot(a, b, preferred_element_type=jnp.float32)  3.3 us
    ppermute x2, starting transfers between devices, rotated(): lax.ppermute(value, axis, [(source, (source + steps) % count) for source...  3.28 us
    dot_general x1, matrix products, body(): lax.dot_general(gain, coupled, FLIPPED, preferred_element_type=jnp.float32)  1.44 us
    ppermute x2, waiting for transfers between devices, rotated(): lax.ppermute(value, axis, [(source, (source + steps) % count) for source...  1.36 us
    unnamed x8, local copies, waits for them, and re-layouts  0.96 us
  transfers between devices with their start and end apart: 4, of which 2 were waited for; matrix products, arithmetic and copies ran while one was open for 12% of the time, Pallas kernels for 4%

profile of v21, /device:TPU:0, one launch (start us, length us, event | category | flops | bytes accessed | tf_op | source)
XLA Modules:
  0.0 40.3 jit_solution(10473830002398444917)
XLA Ops:
  0.0 0.0 copy-start
  0.0 3.0 %collective-permute-start.2 = (bf16[1024,128]{1,0:T(8,128)(2,1)}, bf16[1024,128]{1,0:T(8,128)(2,1)}, u32[]{:S(2)}, u32[]{:S(2)}) collective-permute-start(bf16[1024,128]{1,0:T(8,128)(2,1)} %bitcast.19), channel_id=1, source_target_pairs={{0,16},{16,0},{1,17},{17,1},{2,18},{18,2},{3,19},{19,3},{4,20},{20... | collective-permute-start | bytes 786440 | tf_op jit(solution)/shard_map/ppermute | solution.py:17
  3.0 1.3 %collective-permute-start.1 = (bf16[1024,128]{1,0:T(8,128)(2,1)}, bf16[1024,128]{1,0:T(8,128)(2,1)S(1)}, u32[]{:S(2)}, u32[]{:S(2)}) collective-permute-start(bf16[1024,128]{1,0:T(8,128)(2,1)} %param.10), channel_id=1, source_target_pairs={{1,0},{2,1},{3,2},{4,3},{5,4},{6,5},{7,6},{8,7},{9,8},{10,9},{11,1... | collective-permute-start | bytes 786440 | tf_op jit(solution)/shard_map/ppermute | solution.py:12
  4.3 0.0 copy-done
  4.3 2.5 %convolution_convert_fusion.applied_ref = bf16[1024,512]{1,0:T(8,128)(2,1)S(1)} fusion(bf16[1024,1024]{1,0:T(8,128)(2,1)S(1)} %copy-done, bf16[1024,512]{1,0:T(8,128)(2,1)} %param.12), kind=kOutput, calls=%fused_computation.1 | convolution fusion | flops 1074266112 | bytes 4194304 | tf_op jit(solution)/shard_map/dot_general | solution.py:27
  6.8 0.3 fusion.1.refs_0_
  7.1 0.3 collective-permute-start
  7.4 0.9 %constant_dynamic-slice_fusion.entry_ref = f32[128,64]{1,0:T(8,128)S(1)} fusion(f32[128,512]{1,0:T(8,128)} %param.13, s32[]{:T(128)S(6)} %select_n.3), kind=kLoop, calls=%fused_computation.7 | loop fusion | bytes 65540 | tf_op jit(solution)/shard_map/dynamic_slice | solution.py:146
  8.3 1.4 %collective-permute-done.2.refs_1_ = bf16[1024,128]{1,0:T(8,128)(2,1)} collective-permute-done((bf16[1024,128]{1,0:T(8,128)(2,1)}, bf16[1024,128]{1,0:T(8,128)(2,1)}, u32[]{:S(2)}, u32[]{:S(2)}) %collective-permute-start.2) | collective-permute-done | bytes 262176 | tf_op jit(solution)/shard_map/ppermute | solution.py:17
  9.6 0.9 %copy-done.1 = bf16[1,1024,128]{2,1,0:T(8,128)(2,1)S(1)} copy-done((bf16[1,1024,128]{2,1,0:T(8,128)(2,1)S(1)}, bf16[1,1024,128]{2,1,0:T(8,128)(2,1)}, u32[]{:S(2)}) %copy-start.1) | copy-done | bytes 262168
  10.6 1.0 %shard_map.73.refs_2_ = bf16[1024,256]{1,0:T(8,128)(2,1)S(1)} custom-call(bf16[1024,128]{1,0:T(8,128)(2,1)S(1)} %bitcast.20, bf16[1024,128]{1,0:T(8,128)(2,1)} %collective-permute-done.2.refs_1_), custom_call_target="tpu_custom_call" | custom-call | tf_op jit(solution)/shard_map/pallas_call | solution.py:110
  11.6 0.0 collective-permute-done.1.next_ref
  11.6 0.5 %fusion.3.refs_3_ = f32[128,1024]{1,0:T(8,128)S(1)} fusion(bf16[1024,128]{1,0:T(8,128)(2,1)S(1)} %collective-permute-done.1.next_ref, bf16[1024,1024]{1,0:T(8,128)(2,1)S(1)} %copy-done), kind=kOutput, calls=%fused_computation.8 | convolution fusion | flops 268435456 | bytes 2883584 | tf_op jit(solution)/shard_map/dot_general | solution.py:21
  12.1 0.4 shard_map.74.refs_4_
  12.5 0.0 collective-permute-done.refs_1_
  12.5 0.7 %shard_map.75 = (bf16[1024,128]{1,0:T(8,128)(2,1)S(1)}, bf16[8,192,128]{2,1,0:T(8,128)(2,1)S(1)}) custom-call(bf16[128,128]{1,0:T(8,128)(2,1)S(1)} %fusion.1.refs_0_, bf16[128,128]{1,0:T(8,128)(2,1)S(1)} %collective-permute-done.refs_1_, bf16[1024,256]{1,0:T(8,128)(2,1)S(1)} %shard_map.73.refs_2_, f32[128,1024]{1,0:T(8,128)S(1)} %fusion.3.refs_3_, ...), custom_call_target="tpu_custom_call" | custom-call | tf_op jit(solution)/shard_map/pallas_call | solution.py:110
  13.2 11.9 %all_to_all.10.steps_ref = bf16[8,192,128]{2,1,0:T(8,128)(2,1)S(1)} all-to-all(bf16[8,192,128]{2,1,0:T(8,128)(2,1)S(1)} %get-tuple-element.43), channel_id=1, replica_groups={{0,1,2,3,4,5,6,7},{8,9,10,11,12,13,14,15},{16,17,18,19,20,21,22,23},{24..., dimensions={0} | all-to-all | bytes 786432 | tf_op jit(solution)/shard_map/all_to_all | solution.py:121
  25.1 1.1 %shard_map.76 = (f32[8,64,128]{2,1,0:T(8,128)S(1)}, bf16[64,128]{1,0:T(8,128)(2,1)S(1)}) custom-call(s32[1]{0:T(128)} %bitcast.3.upper_ref, bf16[8,192,128]{2,1,0:T(8,128)(2,1)S(1)} %all_to_all.10.steps_ref, f32[128,64]{1,0:T(8,128)S(1)} %constant_dynamic-slice_fusion.entry_ref), custom_call_target="tpu_custom_call" | custom-call | tf_op jit(solution)/shard_map/pallas_call | solution.py:110
  26.2 3.4 %collective-permute-start.3 = (bf16[64,128]{1,0:T(8,128)(2,1)S(1)}, bf16[64,128]{1,0:T(8,128)(2,1)S(1)}, u32[]{:S(2)}, u32[]{:S(2)}) collective-permute-start(bf16[64,128]{1,0:T(8,128)(2,1)S(1)} %get-tuple-element.51), channel_id=1, source_target_pairs={{0,8},{1,9},{2,10},{3,11},{4,12},{5,13},{6,14},{7,15},{16,24},{17,... | collective-permute-start | bytes 49160 | tf_op jit(solution)/shard_map/ppermute | solution.py:12
  29.6 0.8 %fusion = bf16[1024,128]{0,1:T(8,128)(2,1)S(1)} fusion(bf16[1024,128]{1,0:T(8,128)(2,1)S(1)} %get-tuple-element.52, bf16[1024,1024]{1,0:T(8,128)(2,1)S(1)} %copy-done), kind=kOutput, calls=%fused_computation.3 | convolution fusion | flops 268566528 | bytes 2621440 | tf_op jit(solution)/shard_map/dot_general | solution.py:27
  30.5 0.5 %collective-permute-done.3.entered_ref = bf16[64,128]{1,0:T(8,128)(2,1)S(1)} collective-permute-done((bf16[64,128]{1,0:T(8,128)(2,1)S(1)}, bf16[64,128]{1,0:T(8,128)(2,1)S(1)}, u32[]{:S(2)}, u32[]{:S(2)}) %collective-permute-start.3) | collective-permute-done | bytes 16416 | tf_op jit(solution)/shard_map/ppermute | solution.py:12
  31.0 0.2 shard_map.78
  31.2 7.6 %all_to_all.11 = bf16[8,64,128]{2,1,0:T(8,128)(2,1)S(1)} all-to-all(bf16[8,64,128]{2,1,0:T(8,128)(2,1)S(1)} %shard_map.78), channel_id=1, replica_groups={{0,1,2,3,4,5,6,7},{8,9,10,11,12,13,14,15},{16,17,18,19,20,21,22,23},{24..., dimensions={0} | all-to-all | bytes 262144 | tf_op jit(solution)/shard_map/all_to_all | solution.py:121
  38.8 1.4 %subtract_convert_fusion = bf16[1024,512]{1,0:T(8,128)(2,1)} fusion(bf16[1024,512]{1,0:T(8,128)(2,1)S(1)} %convolution_convert_fusion.applied_ref, bf16[1024,128]{0,1:T(8,128)(2,1)S(1)} %fusion, bf16[512,128]{1,0:T(8,128)(2,1)S(1)} %bitcast.21), kind=kOutput, calls=%fused_computation | convolution fusion | flops 135790592 | bytes 2490368 | tf_op jit(solution)/shard_map/dot_general | solution.py:181
  (6 shorter events, 0.1 us)
Async XLA Ops:
  0.0 4.3 %copy-start = (bf16[1024,1024]{1,0:T(8,128)(2,1)S(1)}, bf16[1024,1024]{1,0:T(8,128)(2,1)}, u32[]{:S(2)}) copy-start(bf16[1024,1024]{1,0:T(8,128)(2,1)} %param.11) | copy-start | bytes 6291460
  0.0 6.8 %copy-start.2 = (bf16[1024,128]{1,0:T(8,128)(2,1)S(1)}, bf16[1024,128]{1,0:T(8,128)(2,1)}, u32[]{:S(2)}) copy-start(bf16[1024,128]{1,0:T(8,128)(2,1)} %param.9) | copy-start | bytes 786436
  0.0 6.8 %copy-start.3 = (bf16[1,1024,128]{2,1,0:T(8,128)(2,1)S(1)}, bf16[1,1024,128]{2,1,0:T(8,128)(2,1)}, u32[]{:S(2)}) copy-start(bf16[1,1024,128]{2,1,0:T(8,128)(2,1)} %param.8) | copy-start | bytes 786436
  0.0 9.6 %collective-permute-start.2 = (bf16[1024,128]{1,0:T(8,128)(2,1)}, bf16[1024,128]{1,0:T(8,128)(2,1)}, u32[]{:S(2)}, u32[]{:S(2)}) collective-permute-start(bf16[1024,128]{1,0:T(8,128)(2,1)} %bitcast.19), channel_id=1, source_target_pairs={{0,16},{16,0},{1,17},{17,1},{2,18},{18,2},{3,19},{19,3},{4,20},{20... | collective-permute-start | bytes 786440 | tf_op jit(solution)/shard_map/ppermute | solution.py:17
  3.0 8.6 %collective-permute-start.1 = (bf16[1024,128]{1,0:T(8,128)(2,1)}, bf16[1024,128]{1,0:T(8,128)(2,1)S(1)}, u32[]{:S(2)}, u32[]{:S(2)}) collective-permute-start(bf16[1024,128]{1,0:T(8,128)(2,1)} %param.10), channel_id=1, source_target_pairs={{1,0},{2,1},{3,2},{4,3},{5,4},{6,5},{7,6},{8,7},{9,8},{10,9},{11,1... | collective-permute-start | bytes 786440 | tf_op jit(solution)/shard_map/ppermute | solution.py:12
  7.1 5.4 %collective-permute-start = (bf16[128,128]{1,0:T(8,128)(2,1)S(1)}, bf16[128,128]{1,0:T(8,128)(2,1)S(1)}, u32[]{:S(2)}, u32[]{:S(2)}) collective-permute-start(bf16[128,128]{1,0:T(8,128)(2,1)S(1)} %fusion.1.refs_0_), channel_id=1, source_target_pairs={{0,16},{16,0},{1,17},{17,1},{2,18},{18,2},{3,19},{19,3},{4,20},{20... | collective-permute-start | bytes 98312 | tf_op jit(solution)/shard_map/ppermute | solution.py:17
  9.6 1.0 %copy-start.1 = (bf16[1,1024,128]{2,1,0:T(8,128)(2,1)S(1)}, bf16[1,1024,128]{2,1,0:T(8,128)(2,1)}, u32[]{:S(2)}) copy-start(bf16[1,1024,128]{2,1,0:T(8,128)(2,1)} %param.7) | copy-start | bytes 786436
  26.2 4.8 %collective-permute-start.3 = (bf16[64,128]{1,0:T(8,128)(2,1)S(1)}, bf16[64,128]{1,0:T(8,128)(2,1)S(1)}, u32[]{:S(2)}, u32[]{:S(2)}) collective-permute-start(bf16[64,128]{1,0:T(8,128)(2,1)S(1)} %get-tuple-element.51), channel_id=1, source_target_pairs={{0,8},{1,9},{2,10},{3,11},{4,12},{5,13},{6,14},{7,15},{16,24},{17,... | collective-permute-start | bytes 49160 | tf_op jit(solution)/shard_map/ppermute | solution.py:12

commit v22 on v21

--- a/solution.py
+++ b/solution.py
@@ -54,8 +54,8 @@
 
 def make_maps(layers, *refs):
     cores = jnp.concatenate([ref[...] for ref in refs[:layers]], axis=0)
-    lefts_ref, weights_ref, shift_ref, range_ref, sent_ref = refs[layers:]
-    lefts = lefts_ref[...]
+    left_ref, others_ref, weights_ref, shift_ref, range_ref, sent_ref = refs[layers:]
+    lefts = jnp.concatenate([left_ref[...], others_ref[...]], axis=1)
     range_ref[...] = (-product(lefts, cores)).astype(jnp.bfloat16)
     map_t = wide(wide(weights_ref[...], lefts), cores).T.astype(jnp.bfloat16)
     rank = map_t.shape[0]
@@ -139,18 +139,18 @@
     core = project(right_factors[0], sketch).astype(half)
     cores = [core] + [rotated(core, "layer", k) for k in range(1, layers)]
 
-    (side,) = local(lay, lefts, ((order, layers * rank), half))
-    next_rows, side = lax.optimization_barrier((next_rows, side))
+    (others,) = local(lay, lefts[1:], ((order, (layers - 1) * rank), half))
+    next_rows, others = lax.optimization_barrier((next_rows, others))
     (shift_t,) = local(make_shift, (next_rows, applied), ((width, rank), half))
     weights = project(next_rows, inverse_diag)
     entry = lax.dynamic_slice_in_dim(incoming, lower * share, share, 1)
     place = upper.reshape(1)
-    side, shift_t, weights, entry, place = lax.optimization_barrier(
-        (side, shift_t, weights, entry, place)
+    others, shift_t, weights, entry, place = lax.optimization_barrier(
+        (others, shift_t, weights, entry, place)
     )
     tile_range, sent = local(
         lambda *refs: make_maps(layers, *refs),
-        (*cores, side, weights, shift_t),
+        (*cores, lefts[0], others, weights, shift_t),
         ((order, rank), half),
         ((lowers, rank + share, rank), half),
     )

time: 40.6 us -> 39.6 us (0.975)
  local copies, waits for them, and re-layouts: 1.88 us -> 0.97 us
    unnamed x8, local copies, waits for them, and re-layouts: 0.96 us -> 0.06 us
  transfers between devices with their start and end apart: 4 -> 4, of which waited for: 2 -> 2; matrix products, arithmetic and copies ran while one was open for 12% -> 13% of each run, Pallas kernels for 4% -> 4%
where the time goes in v22:
time: 39.6 us; the launch traced here: 39.3 us
  blocking collectives  19.5 us (49%)
  starting transfers between devices  7.92 us (20%)
  matrix products  5.47 us (14%)
  Pallas kernels  3.39 us (9%)
  waiting for transfers between devices  1.9 us (5%)
  local copies, waits for them, and re-layouts  0.97 us (2%)
    all_to_all x2, blocking collectives, exchanged(): lax.all_to_all(blocks, 'row', 0, 0, axis_index_groups=members, tiled=True)  19.5 us
    ppermute x2, starting transfers between devices, shifted(): lax.ppermute(value, axis, [(source, source + steps) for source in range(l...  4.63 us
    pallas_call x6, Pallas kernels, local(): pl.pallas_call(kernel, in_specs=specs, out_specs=[VMEM] * len(outputs), o...  3.39 us
    dot_general x2, matrix products, product(): return jnp.dot(a, b, preferred_element_type=jnp.float32)  3.3 us
    ppermute x2, starting transfers between devices, rotated(): lax.ppermute(value, axis, [(source, (source + steps) % count) for source...  3.28 us
    dot_general x1, matrix products, body(): lax.dot_general(gain, coupled, FLIPPED, preferred_element_type=jnp.float32)  1.44 us
    ppermute x2, waiting for transfers between devices, rotated(): lax.ppermute(value, axis, [(source, (source + steps) % count) for source...  1.36 us
    dynamic_slice x1, local copies, waits for them, and re-layouts, body(): entry = lax.dynamic_slice_in_dim(incoming, lower * share, share, 1)  0.91 us
  transfers between devices with their start and end apart: 4, of which 2 were waited for; matrix products, arithmetic and copies ran while one was open for 13% of the time, Pallas kernels for 4%

profile of v22, /device:TPU:0, one launch (start us, length us, event | category | flops | bytes accessed | tf_op | source)
XLA Modules:
  0.0 39.3 jit_solution(7747850805891395147)
XLA Ops:
  0.0 0.0 copy-start
  0.0 3.0 %collective-permute-start.2 = (bf16[1024,128]{1,0:T(8,128)(2,1)}, bf16[1024,128]{1,0:T(8,128)(2,1)}, u32[]{:S(2)}, u32[]{:S(2)}) collective-permute-start(bf16[1024,128]{1,0:T(8,128)(2,1)} %bitcast.19), channel_id=1, source_target_pairs={{0,16},{16,0},{1,17},{17,1},{2,18},{18,2},{3,19},{19,3},{4,20},{20... | collective-permute-start | bytes 786440 | tf_op jit(solution)/shard_map/ppermute | solution.py:17
  3.0 1.3 %collective-permute-start.1 = (bf16[1024,128]{1,0:T(8,128)(2,1)}, bf16[1024,128]{1,0:T(8,128)(2,1)S(1)}, u32[]{:S(2)}, u32[]{:S(2)}) collective-permute-start(bf16[1024,128]{1,0:T(8,128)(2,1)} %param.10), channel_id=1, source_target_pairs={{1,0},{2,1},{3,2},{4,3},{5,4},{6,5},{7,6},{8,7},{9,8},{10,9},{11,1... | collective-permute-start | bytes 786440 | tf_op jit(solution)/shard_map/ppermute | solution.py:12
  4.3 2.5 %convolution_convert_fusion.applied_ref = bf16[1024,512]{1,0:T(8,128)(2,1)S(1)} fusion(bf16[1024,1024]{1,0:T(8,128)(2,1)S(1)} %copy-done, bf16[1024,512]{1,0:T(8,128)(2,1)} %param.12), kind=kOutput, calls=%fused_computation.1 | convolution fusion | flops 1074266112 | bytes 4194304 | tf_op jit(solution)/shard_map/dot_general | solution.py:27
  6.8 0.3 fusion.1.refs_0_
  7.1 0.3 collective-permute-start
  7.4 0.9 %constant_dynamic-slice_fusion.entry_ref = f32[128,64]{1,0:T(8,128)S(1)} fusion(f32[128,512]{1,0:T(8,128)} %param.13, s32[]{:T(128)S(6)} %select_n.3), kind=kLoop, calls=%fused_computation.7 | loop fusion | bytes 65540 | tf_op jit(solution)/shard_map/dynamic_slice | solution.py:146
  8.3 1.4 %collective-permute-done.2.refs_0_ = bf16[1024,128]{1,0:T(8,128)(2,1)} collective-permute-done((bf16[1024,128]{1,0:T(8,128)(2,1)}, bf16[1024,128]{1,0:T(8,128)(2,1)}, u32[]{:S(2)}, u32[]{:S(2)}) %collective-permute-start.2) | collective-permute-done | bytes 262176 | tf_op jit(solution)/shard_map/ppermute | solution.py:17
  9.6 1.0 %shard_map.73.refs_3_ = bf16[1024,128]{1,0:T(8,128)(2,1)S(1)} custom-call(bf16[1024,128]{1,0:T(8,128)(2,1)} %collective-permute-done.2.refs_0_), custom_call_target="tpu_custom_call" | custom-call | tf_op jit(solution)/shard_map/pallas_call | solution.py:110
  10.6 0.0 copy-start.1
  10.6 0.0 collective-permute-done.1.next_ref
  10.6 0.5 %fusion.3.refs_4_ = f32[128,1024]{1,0:T(8,128)S(1)} fusion(bf16[1024,128]{1,0:T(8,128)(2,1)S(1)} %collective-permute-done.1.next_ref, bf16[1024,1024]{1,0:T(8,128)(2,1)S(1)} %copy-done), kind=kOutput, calls=%fused_computation.8 | convolution fusion | flops 268435456 | bytes 2883584 | tf_op jit(solution)/shard_map/dot_general | solution.py:21
  11.1 0.4 %shard_map.74.refs_5_ = bf16[512,128]{1,0:T(8,128)(2,1)S(1)} custom-call(bf16[1024,128]{1,0:T(8,128)(2,1)S(1)} %collective-permute-done.1.next_ref, bf16[1024,512]{1,0:T(8,128)(2,1)S(1)} %convolution_convert_fusion.applied_ref), custom_call_target="tpu_custom_call" | custom-call | tf_op jit(solution)/shard_map/pallas_call | solution.py:110
  11.5 0.0 collective-permute-done.refs_1_
  11.5 0.0 copy-done.1
  11.6 0.7 %shard_map.75 = (bf16[1024,128]{1,0:T(8,128)(2,1)S(1)}, bf16[8,192,128]{2,1,0:T(8,128)(2,1)S(1)}) custom-call(bf16[128,128]{1,0:T(8,128)(2,1)S(1)} %fusion.1.refs_0_, bf16[128,128]{1,0:T(8,128)(2,1)S(1)} %collective-permute-done.refs_1_, bf16[1024,128]{1,0:T(8,128)(2,1)S(1)} %bitcast.20, bf16[1024,128]{1,0:T(8,128)(2,1)S(1)} %shard_map.73.refs_3_, ...), custom_call_target="tpu_custom_call" | custom-call | tf_op jit(solution)/shard_map/pallas_call | solution.py:110
  12.3 11.9 %all_to_all.10.steps_ref = bf16[8,192,128]{2,1,0:T(8,128)(2,1)S(1)} all-to-all(bf16[8,192,128]{2,1,0:T(8,128)(2,1)S(1)} %get-tuple-element.43), channel_id=1, replica_groups={{0,1,2,3,4,5,6,7},{8,9,10,11,12,13,14,15},{16,17,18,19,20,21,22,23},{24..., dimensions={0} | all-to-all | bytes 786432 | tf_op jit(solution)/shard_map/all_to_all | solution.py:121
  24.2 1.1 %shard_map.76 = (f32[8,64,128]{2,1,0:T(8,128)S(1)}, bf16[64,128]{1,0:T(8,128)(2,1)S(1)}) custom-call(s32[1]{0:T(128)} %bitcast.3.upper_ref, bf16[8,192,128]{2,1,0:T(8,128)(2,1)S(1)} %all_to_all.10.steps_ref, f32[128,64]{1,0:T(8,128)S(1)} %constant_dynamic-slice_fusion.entry_ref), custom_call_target="tpu_custom_call" | custom-call | tf_op jit(solution)/shard_map/pallas_call | solution.py:110
  25.3 3.4 %collective-permute-start.3 = (bf16[64,128]{1,0:T(8,128)(2,1)S(1)}, bf16[64,128]{1,0:T(8,128)(2,1)S(1)}, u32[]{:S(2)}, u32[]{:S(2)}) collective-permute-start(bf16[64,128]{1,0:T(8,128)(2,1)S(1)} %get-tuple-element.51), channel_id=1, source_target_pairs={{0,8},{1,9},{2,10},{3,11},{4,12},{5,13},{6,14},{7,15},{16,24},{17,... | collective-permute-start | bytes 49160 | tf_op jit(solution)/shard_map/ppermute | solution.py:12
  28.6 0.8 %fusion = bf16[1024,128]{0,1:T(8,128)(2,1)S(1)} fusion(bf16[1024,128]{1,0:T(8,128)(2,1)S(1)} %get-tuple-element.52, bf16[1024,1024]{1,0:T(8,128)(2,1)S(1)} %copy-done), kind=kOutput, calls=%fused_computation.3 | convolution fusion | flops 268566528 | bytes 2621440 | tf_op jit(solution)/shard_map/dot_general | solution.py:27
  29.5 0.5 %collective-permute-done.3.entered_ref = bf16[64,128]{1,0:T(8,128)(2,1)S(1)} collective-permute-done((bf16[64,128]{1,0:T(8,128)(2,1)S(1)}, bf16[64,128]{1,0:T(8,128)(2,1)S(1)}, u32[]{:S(2)}, u32[]{:S(2)}) %collective-permute-start.3) | collective-permute-done | bytes 16416 | tf_op jit(solution)/shard_map/ppermute | solution.py:12
  30.1 0.2 shard_map.78
  30.3 7.6 %all_to_all.11 = bf16[8,64,128]{2,1,0:T(8,128)(2,1)S(1)} all-to-all(bf16[8,64,128]{2,1,0:T(8,128)(2,1)S(1)} %shard_map.78), channel_id=1, replica_groups={{0,1,2,3,4,5,6,7},{8,9,10,11,12,13,14,15},{16,17,18,19,20,21,22,23},{24..., dimensions={0} | all-to-all | bytes 262144 | tf_op jit(solution)/shard_map/all_to_all | solution.py:121
  37.8 1.4 %subtract_convert_fusion = bf16[1024,512]{1,0:T(8,128)(2,1)} fusion(bf16[1024,512]{1,0:T(8,128)(2,1)S(1)} %convolution_convert_fusion.applied_ref, bf16[1024,128]{0,1:T(8,128)(2,1)S(1)} %fusion, bf16[512,128]{1,0:T(8,128)(2,1)S(1)} %bitcast.21), kind=kOutput, calls=%fused_computation | convolution fusion | flops 135790592 | bytes 2490368 | tf_op jit(solution)/shard_map/dot_general | solution.py:181
  (6 shorter events, 0.1 us)
Async XLA Ops:
  0.0 4.3 %copy-start = (bf16[1024,1024]{1,0:T(8,128)(2,1)S(1)}, bf16[1024,1024]{1,0:T(8,128)(2,1)}, u32[]{:S(2)}) copy-start(bf16[1024,1024]{1,0:T(8,128)(2,1)} %param.11) | copy-start | bytes 6291460
  0.0 6.8 %copy-start.2 = (bf16[1024,128]{1,0:T(8,128)(2,1)S(1)}, bf16[1024,128]{1,0:T(8,128)(2,1)}, u32[]{:S(2)}) copy-start(bf16[1024,128]{1,0:T(8,128)(2,1)} %param.9) | copy-start | bytes 786436
  0.0 6.8 %copy-start.3 = (bf16[1,1024,128]{2,1,0:T(8,128)(2,1)S(1)}, bf16[1,1024,128]{2,1,0:T(8,128)(2,1)}, u32[]{:S(2)}) copy-start(bf16[1,1024,128]{2,1,0:T(8,128)(2,1)} %param.8) | copy-start | bytes 786436
  0.0 9.6 %collective-permute-start.2 = (bf16[1024,128]{1,0:T(8,128)(2,1)}, bf16[1024,128]{1,0:T(8,128)(2,1)}, u32[]{:S(2)}, u32[]{:S(2)}) collective-permute-start(bf16[1024,128]{1,0:T(8,128)(2,1)} %bitcast.19), channel_id=1, source_target_pairs={{0,16},{16,0},{1,17},{17,1},{2,18},{18,2},{3,19},{19,3},{4,20},{20... | collective-permute-start | bytes 786440 | tf_op jit(solution)/shard_map/ppermute | solution.py:17
  3.0 7.6 %collective-permute-start.1 = (bf16[1024,128]{1,0:T(8,128)(2,1)}, bf16[1024,128]{1,0:T(8,128)(2,1)S(1)}, u32[]{:S(2)}, u32[]{:S(2)}) collective-permute-start(bf16[1024,128]{1,0:T(8,128)(2,1)} %param.10), channel_id=1, source_target_pairs={{1,0},{2,1},{3,2},{4,3},{5,4},{6,5},{7,6},{8,7},{9,8},{10,9},{11,1... | collective-permute-start | bytes 786440 | tf_op jit(solution)/shard_map/ppermute | solution.py:12
  7.1 4.4 %collective-permute-start = (bf16[128,128]{1,0:T(8,128)(2,1)S(1)}, bf16[128,128]{1,0:T(8,128)(2,1)S(1)}, u32[]{:S(2)}, u32[]{:S(2)}) collective-permute-start(bf16[128,128]{1,0:T(8,128)(2,1)S(1)} %fusion.1.refs_0_), channel_id=1, source_target_pairs={{0,16},{16,0},{1,17},{17,1},{2,18},{18,2},{3,19},{19,3},{4,20},{20... | collective-permute-start | bytes 98312 | tf_op jit(solution)/shard_map/ppermute | solution.py:17
  10.6 1.0 %copy-start.1 = (bf16[1,1024,128]{2,1,0:T(8,128)(2,1)S(1)}, bf16[1,1024,128]{2,1,0:T(8,128)(2,1)}, u32[]{:S(2)}) copy-start(bf16[1,1024,128]{2,1,0:T(8,128)(2,1)} %param.7) | copy-start | bytes 786436
  25.3 4.8 %collective-permute-start.3 = (bf16[64,128]{1,0:T(8,128)(2,1)S(1)}, bf16[64,128]{1,0:T(8,128)(2,1)S(1)}, u32[]{:S(2)}, u32[]{:S(2)}) collective-permute-start(bf16[64,128]{1,0:T(8,128)(2,1)S(1)} %get-tuple-element.51), channel_id=1, source_target_pairs={{0,8},{1,9},{2,10},{3,11},{4,12},{5,13},{6,14},{7,15},{16,24},{17,... | collective-permute-start | bytes 49160 | tf_op jit(solution)/shard_map/ppermute | solution.py:12

commit v23 on v17

--- a/solution.py
+++ b/solution.py
@@ -63,10 +63,14 @@
     return state
 
 
-def first_half(upper_ref, steps_ref, entry_ref, values_ref, last_ref):
-    @pl.when(upper_ref[0] == 0)
+def first_half(place_ref, steps_ref, incoming_ref, values_ref, last_ref, flipped):
+    share = last_ref.shape[0]
+
+    @pl.when(place_ref[0] == 0)
     def _():
-        last_ref[...] = chain(steps_ref, entry_ref[...].T, values_ref).astype(jnp.bfloat16)
+        flipped[...] = incoming_ref[...].T
+        entry = flipped[pl.ds(pl.multiple_of(place_ref[1] * share, share), share), :]
+        last_ref[...] = chain(steps_ref, entry, values_ref).astype(jnp.bfloat16)
 
 
 def second_half(upper_ref, steps_ref, before_ref, values_ref, maps_ref):
@@ -94,7 +98,7 @@
         coupled_ref[member] = (moved + values_ref[member]).astype(jnp.bfloat16)
 
 
-def local(kernel, inputs, *outputs, scalar=False, aliases={}):
+def local(kernel, inputs, *outputs, scalar=False, aliases={}, scratch=()):
     specs = [SMEM] * scalar + [VMEM] * (len(inputs) - scalar)
     return pl.pallas_call(
         kernel,
@@ -102,6 +106,7 @@
         out_specs=[VMEM] * len(outputs),
         out_shape=[jax.ShapeDtypeStruct(*output) for output in outputs],
         input_output_aliases=aliases,
+        scratch_shapes=scratch,
         compiler_params=pltpu.CompilerParams(vmem_limit_bytes=16 * 2**20),
     )(*inputs)
 
@@ -130,10 +135,9 @@
 
     shift_t = project(applied, next_rows).astype(half).reshape(lowers, share, rank)
     weights = project(next_rows, inverse_diag)
-    entry = lax.dynamic_slice_in_dim(incoming, lower * share, share, 1)
-    place = upper.reshape(1)
-    lefts[-1], shift_t, weights, entry, place = lax.optimization_barrier(
-        (lefts[-1], shift_t, weights, entry, place)
+    place = jnp.stack([upper, lower])
+    lefts[-1], shift_t, weights, place = lax.optimization_barrier(
+        (lefts[-1], shift_t, weights, place)
     )
     tile_range, sent = local(
         lambda *refs: make_maps(layers, *refs),
@@ -141,15 +145,16 @@
         ((order, rank), half),
         ((lowers, rank + share, rank), half),
     )
-    sent, tile_range, entry, place = lax.optimization_barrier((sent, tile_range, entry, place))
+    sent, tile_range, place = lax.optimization_barrier((sent, tile_range, place))
     steps = exchanged(sent, near)
-    steps, tile_range, entry, place = lax.optimization_barrier((steps, tile_range, entry, place))
+    steps, tile_range, place = lax.optimization_barrier((steps, tile_range, place))
     values, last = local(
         first_half,
-        (place, steps, entry),
+        (place, steps, incoming),
         ((lowers, share, rank), jnp.float32),
         ((share, rank), half),
         scalar=True,
+        scratch=[pltpu.VMEM((width, rank), jnp.float32)],
     )
     entered = shifted(last, "row", lowers)
     steps, tile_range, _ = lax.optimization_barrier((steps, tile_range, last))

time: 40.8 us -> 41.4 us (1.015)
  Pallas kernels: 2.03 us -> 3.17 us
  local copies, waits for them, and re-layouts: 0.93 us -> 0.02 us
    pallas_call x4, Pallas kernels: 2.03 us -> 3.17 us  [local(): pl.pallas_call(kernel, in_specs=specs, out_specs=[VMEM] * len(outputs), o...]
    dynamic_slice x1 -> x0, local copies, waits for them, and re-layouts: 0.91 us -> none  [body(): entry = lax.dynamic_slice_in_dim(incoming, lower * share, share, 1)]
    ppermute x2, waiting for transfers between devices: 0.05 us -> 0.85 us  [rotated(): lax.ppermute(value, axis, [(source, (source + steps) % count) for source...]
    ppermute x2, waiting for transfers between devices: 0.53 us -> 0.01 us  [shifted(): lax.ppermute(value, axis, [(source, source + steps) for source in range(l...]
  transfers between devices with their start and end apart: 4 -> 4, of which waited for: 1 -> 1; matrix products, arithmetic and copies ran while one was open for 18% -> 16% of each run, Pallas kernels for 0% -> 1%
where the time goes in v23:
time: 41.4 us; the launch traced here: 41.1 us
  blocking collectives  22 us (53%)
  matrix products  7.94 us (19%)
  starting transfers between devices  6.91 us (17%)
  Pallas kernels  3.17 us (8%)
  waiting for transfers between devices  0.85 us (2%)
    all_to_all x2, blocking collectives, exchanged(): lax.all_to_all(blocks, 'row', 0, 0, axis_index_groups=members, tiled=True)  22 us
    ppermute x2, starting transfers between devices, shifted(): lax.ppermute(value, axis, [(source, source + steps) for source in range(l...  3.62 us
    dot_general x2, matrix products, product(): return jnp.dot(a, b, preferred_element_type=jnp.float32)  3.29 us
    ppermute x2, starting transfers between devices, rotated(): lax.ppermute(value, axis, [(source, (source + steps) % count) for source...  3.28 us
    dot_general x3, matrix products, project(): lax.dot_general(basis, vectors, (((0,), (0,)), ((), ())), preferred_eleme...  3.21 us
    pallas_call x4, Pallas kernels, local(): pl.pallas_call(kernel, in_specs=specs, out_specs=[VMEM] * len(outputs), o...  3.17 us
    dot_general x1, matrix products, body(): lax.dot_general(gain, coupled, FLIPPED, preferred_element_type=jnp.float32)  1.43 us
    ppermute x2, waiting for transfers between devices, rotated(): lax.ppermute(value, axis, [(source, (source + steps) % count) for source...  0.85 us
  transfers between devices with their start and end apart: 4, of which 1 were waited for; matrix products, arithmetic and copies ran while one was open for 16% of the time, Pallas kernels for 1%

profile of v23, /device:TPU:0, one launch (start us, length us, event | category | flops | bytes accessed | tf_op | source)
XLA Modules:
  0.0 41.1 jit_solution(4024905075757085783)
XLA Ops:
  0.0 0.0 copy-start
  0.0 3.0 %collective-permute-start = (bf16[1024,128]{1,0:T(8,128)(2,1)}, bf16[1024,128]{1,0:T(8,128)(2,1)S(1)}, u32[]{:S(2)}, u32[]{:S(2)}) collective-permute-start(bf16[1024,128]{1,0:T(8,128)(2,1)} %bitcast.24), channel_id=1, source_target_pairs={{0,16},{16,0},{1,17},{17,1},{2,18},{18,2},{3,19},{19,3},{4,20},{20... | collective-permute-start | bytes 786440 | tf_op jit(solution)/shard_map/ppermute | solution.py:17
  3.0 1.3 %collective-permute-start.1 = (bf16[1024,128]{1,0:T(8,128)(2,1)}, bf16[1024,128]{1,0:T(8,128)(2,1)}, u32[]{:S(2)}, u32[]{:S(2)}) collective-permute-start(bf16[1024,128]{1,0:T(8,128)(2,1)} %param.10), channel_id=1, source_target_pairs={{1,0},{2,1},{3,2},{4,3},{5,4},{6,5},{7,6},{8,7},{9,8},{10,9},{11,1... | collective-permute-start | bytes 786440 | tf_op jit(solution)/shard_map/ppermute | solution.py:12
  4.3 2.5 %convolution_convert_fusion = bf16[1024,512]{1,0:T(8,128)(2,1)S(1)} fusion(bf16[1024,1024]{1,0:T(8,128)(2,1)S(1)} %copy-done, bf16[1024,512]{1,0:T(8,128)(2,1)} %param.12), kind=kOutput, calls=%fused_computation.1 | convolution fusion | flops 1074266112 | bytes 4194304 | tf_op jit(solution)/shard_map/dot_general | solution.py:27
  6.8 0.3 fusion.1.refs_2_
  7.1 0.3 collective-permute-start.2
  7.4 0.1 pad_add_fusion.place_ref.upper_ref
  7.4 0.0 collective-permute-done.1
  7.4 1.5 %fusion.3.refs_4_ = f32[128,1024]{1,0:T(8,128)S(1)} fusion(bf16[1024,128]{1,0:T(8,128)(2,1)} %collective-permute-done.1, bf16[1024,1024]{1,0:T(8,128)(2,1)S(1)} %copy-done), kind=kOutput, calls=%fused_computation.9 | convolution fusion | flops 268435456 | bytes 2883584 | tf_op jit(solution)/shard_map/dot_general | solution.py:21
  8.9 0.0 copy-start.2
  8.9 1.5 %convolution_convert_fusion.2 = bf16[512,128]{1,0:T(8,128)(2,1)S(1)} fusion(bf16[1024,512]{1,0:T(8,128)(2,1)S(1)} %convolution_convert_fusion, bf16[1024,128]{1,0:T(8,128)(2,1)} %collective-permute-done.1), kind=kOutput, calls=%fused_computation.4 | convolution fusion | flops 134283264 | bytes 1441792 | tf_op jit(solution)/shard_map/dot_general | solution.py:21
  10.4 0.0 collective-permute-done.refs_1_
  10.4 0.8 %collective-permute-done.2.refs_3_ = bf16[128,128]{1,0:T(8,128)(2,1)S(1)} collective-permute-done((bf16[128,128]{1,0:T(8,128)(2,1)S(1)}, bf16[128,128]{1,0:T(8,128)(2,1)S(1)}, u32[]{:S(2)}, u32[]{:S(2)}) %collective-permute-start.2) | collective-permute-done | bytes 32800 | tf_op jit(solution)/shard_map/ppermute | solution.py:17
  11.3 0.7 %shard_map.73 = (bf16[1024,128]{1,0:T(8,128)(2,1)S(1)}, bf16[8,192,128]{2,1,0:T(8,128)(2,1)S(1)}) custom-call(bf16[1024,128]{1,0:T(8,128)(2,1)S(1)} %bitcast.25, bf16[1024,128]{1,0:T(8,128)(2,1)S(1)} %collective-permute-done.refs_1_, bf16[128,128]{1,0:T(8,128)(2,1)S(1)} %fusion.1.refs_2_, bf16[128,128]{1,0:T(8,128)(2,1)S(1)} %collective-permute-done.2.refs_3_, ...), custom_call_target="tpu_custom_call" | custom-call | tf_op jit(solution)/shard_map/pallas_call | solution.py:103
  12.0 14.4 %all_to_all.10.steps_ref = bf16[8,192,128]{2,1,0:T(8,128)(2,1)S(1)} all-to-all(bf16[8,192,128]{2,1,0:T(8,128)(2,1)S(1)} %get-tuple-element.35), channel_id=1, replica_groups={{0,1,2,3,4,5,6,7},{8,9,10,11,12,13,14,15},{16,17,18,19,20,21,22,23},{24..., dimensions={0} | all-to-all | bytes 786432 | tf_op jit(solution)/shard_map/all_to_all | solution.py:115
  26.4 0.0 copy-done.2
  26.4 1.7 %shard_map.74 = (f32[8,64,128]{2,1,0:T(8,128)S(1)}, bf16[64,128]{1,0:T(8,128)(2,1)S(1)}) custom-call(s32[2]{0:T(128)S(1)} %pad_add_fusion.place_ref.upper_ref, bf16[8,192,128]{2,1,0:T(8,128)(2,1)S(1)} %all_to_all.10.steps_ref, f32[128,512]{1,0:T(8,128)S(1)} %copy-done.2), custom_call_target="tpu_custom_call" | custom-call | tf_op jit(solution)/shard_map/pallas_call | solution.py:103
  28.1 2.3 %collective-permute-start.3 = (bf16[64,128]{1,0:T(8,128)(2,1)S(1)}, bf16[64,128]{1,0:T(8,128)(2,1)S(1)}, u32[]{:S(2)}, u32[]{:S(2)}) collective-permute-start(bf16[64,128]{1,0:T(8,128)(2,1)S(1)} %get-tuple-element.41), channel_id=1, source_target_pairs={{0,8},{1,9},{2,10},{3,11},{4,12},{5,13},{6,14},{7,15},{16,24},{17,... | collective-permute-start | bytes 49160 | tf_op jit(solution)/shard_map/ppermute | solution.py:12
  30.4 0.8 %fusion = bf16[1024,128]{0,1:T(8,128)(2,1)S(1)} fusion(bf16[1024,128]{1,0:T(8,128)(2,1)S(1)} %get-tuple-element.42, bf16[1024,1024]{1,0:T(8,128)(2,1)S(1)} %copy-done), kind=kOutput, calls=%fused_computation.3 | convolution fusion | flops 268566528 | bytes 2621440 | tf_op jit(solution)/shard_map/dot_general | solution.py:27
  31.3 0.6 %shard_map.75 = (f32[8,64,128]{2,1,0:T(8,128)S(1)}, bf16[8,128,128]{2,1,0:T(8,128)(2,1)S(1)}) custom-call(s32[2]{0:T(128)S(1)} %pad_add_fusion.place_ref.upper_ref, bf16[8,192,128]{2,1,0:T(8,128)(2,1)S(1)} %all_to_all.10.steps_ref, f32[8,64,128]{2,1,0:T(8,128)S(1)} %get-tuple-element.44.before_ref), custom_call_target="tpu_custom_call", output_to_operand_aliasing={{0}: (2, {})} | custom-call | tf_op jit(solution)/shard_map/pallas_call | solution.py:103
  31.8 0.0 collective-permute-done.3.entered_ref
  31.9 0.2 shard_map.76
  32.1 7.6 %all_to_all.11 = bf16[8,64,128]{2,1,0:T(8,128)(2,1)S(1)} all-to-all(bf16[8,64,128]{2,1,0:T(8,128)(2,1)S(1)} %shard_map.76), channel_id=1, replica_groups={{0,1,2,3,4,5,6,7},{8,9,10,11,12,13,14,15},{16,17,18,19,20,21,22,23},{24..., dimensions={0} | all-to-all | bytes 262144 | tf_op jit(solution)/shard_map/all_to_all | solution.py:115
  39.6 1.4 %subtract_convert_fusion = bf16[1024,512]{1,0:T(8,128)(2,1)} fusion(bf16[1024,512]{1,0:T(8,128)(2,1)S(1)} %convolution_convert_fusion, bf16[1024,128]{0,1:T(8,128)(2,1)S(1)} %fusion, bf16[512,128]{1,0:T(8,128)(2,1)S(1)} %bitcast.26), kind=kOutput, calls=%fused_computation | convolution fusion | flops 135790592 | bytes 2490368 | tf_op jit(solution)/shard_map/dot_general | solution.py:173
  (7 shorter events, 0.0 us)
Async XLA Ops:
  0.0 4.3 %copy-start = (bf16[1024,1024]{1,0:T(8,128)(2,1)S(1)}, bf16[1024,1024]{1,0:T(8,128)(2,1)}, u32[]{:S(2)}) copy-start(bf16[1024,1024]{1,0:T(8,128)(2,1)} %param.11) | copy-start | bytes 6291460
  0.0 6.8 %copy-start.3 = (bf16[1024,128]{1,0:T(8,128)(2,1)S(1)}, bf16[1024,128]{1,0:T(8,128)(2,1)}, u32[]{:S(2)}) copy-start(bf16[1024,128]{1,0:T(8,128)(2,1)} %param.9) | copy-start | bytes 786436
  0.0 6.8 %copy-start.4 = (bf16[1,1024,128]{2,1,0:T(8,128)(2,1)S(1)}, bf16[1,1024,128]{2,1,0:T(8,128)(2,1)}, u32[]{:S(2)}) copy-start(bf16[1,1024,128]{2,1,0:T(8,128)(2,1)} %param.8) | copy-start | bytes 786436
  0.0 10.4 %collective-permute-start = (bf16[1024,128]{1,0:T(8,128)(2,1)}, bf16[1024,128]{1,0:T(8,128)(2,1)S(1)}, u32[]{:S(2)}, u32[]{:S(2)}) collective-permute-start(bf16[1024,128]{1,0:T(8,128)(2,1)} %bitcast.24), channel_id=1, source_target_pairs={{0,16},{16,0},{1,17},{17,1},{2,18},{18,2},{3,19},{19,3},{4,20},{20... | collective-permute-start | bytes 786440 | tf_op jit(solution)/shard_map/ppermute | solution.py:17
  3.0 4.4 %collective-permute-start.1 = (bf16[1024,128]{1,0:T(8,128)(2,1)}, bf16[1024,128]{1,0:T(8,128)(2,1)}, u32[]{:S(2)}, u32[]{:S(2)}) collective-permute-start(bf16[1024,128]{1,0:T(8,128)(2,1)} %param.10), channel_id=1, source_target_pairs={{1,0},{2,1},{3,2},{4,3},{5,4},{6,5},{7,6},{8,7},{9,8},{10,9},{11,1... | collective-permute-start | bytes 786440 | tf_op jit(solution)/shard_map/ppermute | solution.py:12
  7.1 4.2 %collective-permute-start.2 = (bf16[128,128]{1,0:T(8,128)(2,1)S(1)}, bf16[128,128]{1,0:T(8,128)(2,1)S(1)}, u32[]{:S(2)}, u32[]{:S(2)}) collective-permute-start(bf16[128,128]{1,0:T(8,128)(2,1)S(1)} %fusion.1.refs_2_), channel_id=1, source_target_pairs={{0,16},{16,0},{1,17},{17,1},{2,18},{18,2},{3,19},{19,3},{4,20},{20... | collective-permute-start | bytes 98312 | tf_op jit(solution)/shard_map/ppermute | solution.py:17
  7.4 3.8 %copy-start.1 = (bf16[1,1024,128]{2,1,0:T(8,128)(2,1)S(1)}, bf16[1,1024,128]{2,1,0:T(8,128)(2,1)}, u32[]{:S(2)}) copy-start(bf16[1,1024,128]{2,1,0:T(8,128)(2,1)} %param.7) | copy-start | bytes 786436
  8.9 17.5 %copy-start.2 = (f32[128,512]{1,0:T(8,128)S(1)}, f32[128,512]{1,0:T(8,128)}, u32[]{:S(2)}) copy-start(f32[128,512]{1,0:T(8,128)} %incoming_ref.1) | copy-start | bytes 786436
  28.1 3.8 %collective-permute-start.3 = (bf16[64,128]{1,0:T(8,128)(2,1)S(1)}, bf16[64,128]{1,0:T(8,128)(2,1)S(1)}, u32[]{:S(2)}, u32[]{:S(2)}) collective-permute-start(bf16[64,128]{1,0:T(8,128)(2,1)S(1)} %get-tuple-element.41), channel_id=1, source_target_pairs={{0,8},{1,9},{2,10},{3,11},{4,12},{5,13},{6,14},{7,15},{16,24},{17,... | collective-permute-start | bytes 49160 | tf_op jit(solution)/shard_map/ppermute | solution.py:12

commit v24 on v22

--- a/solution.py
+++ b/solution.py
@@ -47,9 +47,16 @@
 
 
 def lay(*refs):
-    rank = refs[0].shape[1]
-    for layer, ref in enumerate(refs[:-1]):
-        refs[-1][:, layer * rank : (layer + 1) * rank] = ref[...]
+    arrived, target, sources = refs[-1], refs[-2], refs[:-2]
+    rank = sources[0].shape[1]
+    copies = [
+        pltpu.make_async_copy(source, target.at[:, pl.ds(k * rank, rank)], arrived.at[k])
+        for k, source in enumerate(sources)
+    ]
+    for copy in copies:
+        copy.start()
+    for copy in copies:
+        copy.wait()
 
 
 def make_maps(layers, *refs):
@@ -139,7 +146,14 @@
     core = project(right_factors[0], sketch).astype(half)
     cores = [core] + [rotated(core, "layer", k) for k in range(1, layers)]
 
-    (others,) = local(lay, lefts[1:], ((order, (layers - 1) * rank), half))
+    others = pl.pallas_call(
+        lay,
+        in_specs=[pl.BlockSpec(memory_space=pl.ANY)] * (layers - 1),
+        out_specs=VMEM,
+        out_shape=jax.ShapeDtypeStruct((order, (layers - 1) * rank), half),
+        scratch_shapes=[pltpu.SemaphoreType.DMA((layers - 1,))],
+        compiler_params=pltpu.CompilerParams(vmem_limit_bytes=16 * 2**20),
+    )(*lefts[1:])
     next_rows, others = lax.optimization_barrier((next_rows, others))
     (shift_t,) = local(make_shift, (next_rows, applied), ((width, rank), half))
     weights = project(next_rows, inverse_diag)

time: 39.6 us -> 39.6 us (level)
    pallas_call x6 -> x5, Pallas kernels: 3.39 us -> 2.42 us  [local(): pl.pallas_call(kernel, in_specs=specs, out_specs=[VMEM] * len(outputs), o...]
    pallas_call x0 -> x1, Pallas kernels: none -> 0.96 us  [body(): pl.pallas_call(lay, in_specs=[pl.BlockSpec(memory_space=pl.ANY)] * (layer...]
where the time goes in v24:
time: 39.6 us; the launch traced here: 39.3 us
  blocking collectives  19.5 us (49%)
  starting transfers between devices  7.91 us (20%)
  matrix products  5.48 us (14%)
  Pallas kernels  3.38 us (9%)
  waiting for transfers between devices  1.9 us (5%)
  local copies, waits for them, and re-layouts  0.97 us (2%)
    all_to_all x2, blocking collectives, exchanged(): lax.all_to_all(blocks, 'row', 0, 0, axis_index_groups=members, tiled=True)  19.5 us
    ppermute x2, starting transfers between devices, shifted(): lax.ppermute(value, axis, [(source, source + steps) for source in range(l...  4.62 us
    dot_general x2, matrix products, product(): return jnp.dot(a, b, preferred_element_type=jnp.float32)  3.3 us
    ppermute x2, starting transfers between devices, rotated(): lax.ppermute(value, axis, [(source, (source + steps) % count) for source...  3.28 us
    pallas_call x5, Pallas kernels, local(): pl.pallas_call(kernel, in_specs=specs, out_specs=[VMEM] * len(outputs), o...  2.42 us
    dot_general x1, matrix products, body(): lax.dot_general(gain, coupled, FLIPPED, preferred_element_type=jnp.float32)  1.44 us
    ppermute x2, waiting for transfers between devices, rotated(): lax.ppermute(value, axis, [(source, (source + steps) % count) for source...  1.36 us
    pallas_call x1, Pallas kernels, body(): pl.pallas_call(lay, in_specs=[pl.BlockSpec(memory_space=pl.ANY)] * (layer...  0.96 us
  transfers between devices with their start and end apart: 4, of which 2 were waited for; matrix products, arithmetic and copies ran while one was open for 13% of the time, Pallas kernels for 4%

profile of v24, /device:TPU:0, one launch (start us, length us, event | category | flops | bytes accessed | tf_op | source)
XLA Modules:
  0.0 39.3 jit_solution(10303960077277192399)
XLA Ops:
  0.0 0.0 copy-start
  0.0 3.0 %collective-permute-start.2 = (bf16[1024,128]{1,0:T(8,128)(2,1)}, bf16[1024,128]{1,0:T(8,128)(2,1)}, u32[]{:S(2)}, u32[]{:S(2)}) collective-permute-start(bf16[1024,128]{1,0:T(8,128)(2,1)} %bitcast.19), channel_id=1, source_target_pairs={{0,16},{16,0},{1,17},{17,1},{2,18},{18,2},{3,19},{19,3},{4,20},{20... | collective-permute-start | bytes 786440 | tf_op jit(solution)/shard_map/ppermute | solution.py:17
  3.0 1.3 %collective-permute-start.1 = (bf16[1024,128]{1,0:T(8,128)(2,1)}, bf16[1024,128]{1,0:T(8,128)(2,1)S(1)}, u32[]{:S(2)}, u32[]{:S(2)}) collective-permute-start(bf16[1024,128]{1,0:T(8,128)(2,1)} %param.10), channel_id=1, source_target_pairs={{1,0},{2,1},{3,2},{4,3},{5,4},{6,5},{7,6},{8,7},{9,8},{10,9},{11,1... | collective-permute-start | bytes 786440 | tf_op jit(solution)/shard_map/ppermute | solution.py:12
  4.3 2.5 %convolution_convert_fusion.applied_ref = bf16[1024,512]{1,0:T(8,128)(2,1)S(1)} fusion(bf16[1024,1024]{1,0:T(8,128)(2,1)S(1)} %copy-done, bf16[1024,512]{1,0:T(8,128)(2,1)} %param.12), kind=kOutput, calls=%fused_computation.1 | convolution fusion | flops 1074266112 | bytes 4194304 | tf_op jit(solution)/shard_map/dot_general | solution.py:27
  6.8 0.3 fusion.1.refs_0_
  7.1 0.3 collective-permute-start
  7.4 0.9 %constant_dynamic-slice_fusion.entry_ref = f32[128,64]{1,0:T(8,128)S(1)} fusion(f32[128,512]{1,0:T(8,128)} %param.13, s32[]{:T(128)S(6)} %select_n.3), kind=kLoop, calls=%fused_computation.7 | loop fusion | bytes 65540 | tf_op jit(solution)/shard_map/dynamic_slice | solution.py:160
  8.3 1.4 %collective-permute-done.2.refs_0_ = bf16[1024,128]{1,0:T(8,128)(2,1)} collective-permute-done((bf16[1024,128]{1,0:T(8,128)(2,1)}, bf16[1024,128]{1,0:T(8,128)(2,1)}, u32[]{:S(2)}, u32[]{:S(2)}) %collective-permute-start.2) | collective-permute-done | bytes 262176 | tf_op jit(solution)/shard_map/ppermute | solution.py:17
  9.6 1.0 %shard_map.73.refs_3_ = bf16[1024,128]{1,0:T(8,128)(2,1)S(1)} custom-call(bf16[1024,128]{1,0:T(8,128)(2,1)} %collective-permute-done.2.refs_0_), custom_call_target="tpu_custom_call" | custom-call | tf_op jit(solution)/shard_map/pallas_call | solution.py:149
  10.6 0.0 copy-start.1
  10.6 0.0 collective-permute-done.1.next_ref
  10.6 0.5 %fusion.3.refs_4_ = f32[128,1024]{1,0:T(8,128)S(1)} fusion(bf16[1024,128]{1,0:T(8,128)(2,1)S(1)} %collective-permute-done.1.next_ref, bf16[1024,1024]{1,0:T(8,128)(2,1)S(1)} %copy-done), kind=kOutput, calls=%fused_computation.8 | convolution fusion | flops 268435456 | bytes 2883584 | tf_op jit(solution)/shard_map/dot_general | solution.py:21
  11.1 0.4 %shard_map.74.refs_5_ = bf16[512,128]{1,0:T(8,128)(2,1)S(1)} custom-call(bf16[1024,128]{1,0:T(8,128)(2,1)S(1)} %collective-permute-done.1.next_ref, bf16[1024,512]{1,0:T(8,128)(2,1)S(1)} %convolution_convert_fusion.applied_ref), custom_call_target="tpu_custom_call" | custom-call | tf_op jit(solution)/shard_map/pallas_call | solution.py:117
  11.5 0.0 collective-permute-done.refs_1_
  11.5 0.0 copy-done.1
  11.6 0.7 %shard_map.75 = (bf16[1024,128]{1,0:T(8,128)(2,1)S(1)}, bf16[8,192,128]{2,1,0:T(8,128)(2,1)S(1)}) custom-call(bf16[128,128]{1,0:T(8,128)(2,1)S(1)} %fusion.1.refs_0_, bf16[128,128]{1,0:T(8,128)(2,1)S(1)} %collective-permute-done.refs_1_, bf16[1024,128]{1,0:T(8,128)(2,1)S(1)} %bitcast.20, bf16[1024,128]{1,0:T(8,128)(2,1)S(1)} %shard_map.73.refs_3_, ...), custom_call_target="tpu_custom_call" | custom-call | tf_op jit(solution)/shard_map/pallas_call | solution.py:117
  12.3 11.9 %all_to_all.10.steps_ref = bf16[8,192,128]{2,1,0:T(8,128)(2,1)S(1)} all-to-all(bf16[8,192,128]{2,1,0:T(8,128)(2,1)S(1)} %get-tuple-element.43), channel_id=1, replica_groups={{0,1,2,3,4,5,6,7},{8,9,10,11,12,13,14,15},{16,17,18,19,20,21,22,23},{24..., dimensions={0} | all-to-all | bytes 786432 | tf_op jit(solution)/shard_map/all_to_all | solution.py:128
  24.2 1.1 %shard_map.76 = (f32[8,64,128]{2,1,0:T(8,128)S(1)}, bf16[64,128]{1,0:T(8,128)(2,1)S(1)}) custom-call(s32[1]{0:T(128)} %bitcast.3.upper_ref, bf16[8,192,128]{2,1,0:T(8,128)(2,1)S(1)} %all_to_all.10.steps_ref, f32[128,64]{1,0:T(8,128)S(1)} %constant_dynamic-slice_fusion.entry_ref), custom_call_target="tpu_custom_call" | custom-call | tf_op jit(solution)/shard_map/pallas_call | solution.py:117
  25.3 3.3 %collective-permute-start.3 = (bf16[64,128]{1,0:T(8,128)(2,1)S(1)}, bf16[64,128]{1,0:T(8,128)(2,1)S(1)}, u32[]{:S(2)}, u32[]{:S(2)}) collective-permute-start(bf16[64,128]{1,0:T(8,128)(2,1)S(1)} %get-tuple-element.51), channel_id=1, source_target_pairs={{0,8},{1,9},{2,10},{3,11},{4,12},{5,13},{6,14},{7,15},{16,24},{17,... | collective-permute-start | bytes 49160 | tf_op jit(solution)/shard_map/ppermute | solution.py:12
  28.6 0.8 %fusion = bf16[1024,128]{0,1:T(8,128)(2,1)S(1)} fusion(bf16[1024,128]{1,0:T(8,128)(2,1)S(1)} %get-tuple-element.52, bf16[1024,1024]{1,0:T(8,128)(2,1)S(1)} %copy-done), kind=kOutput, calls=%fused_computation.3 | convolution fusion | flops 268566528 | bytes 2621440 | tf_op jit(solution)/shard_map/dot_general | solution.py:27
  29.5 0.5 %collective-permute-done.3.entered_ref = bf16[64,128]{1,0:T(8,128)(2,1)S(1)} collective-permute-done((bf16[64,128]{1,0:T(8,128)(2,1)S(1)}, bf16[64,128]{1,0:T(8,128)(2,1)S(1)}, u32[]{:S(2)}, u32[]{:S(2)}) %collective-permute-start.3) | collective-permute-done | bytes 16416 | tf_op jit(solution)/shard_map/ppermute | solution.py:12
  30.1 0.2 shard_map.78
  30.3 7.6 %all_to_all.11 = bf16[8,64,128]{2,1,0:T(8,128)(2,1)S(1)} all-to-all(bf16[8,64,128]{2,1,0:T(8,128)(2,1)S(1)} %shard_map.78), channel_id=1, replica_groups={{0,1,2,3,4,5,6,7},{8,9,10,11,12,13,14,15},{16,17,18,19,20,21,22,23},{24..., dimensions={0} | all-to-all | bytes 262144 | tf_op jit(solution)/shard_map/all_to_all | solution.py:128
  37.8 1.4 %subtract_convert_fusion = bf16[1024,512]{1,0:T(8,128)(2,1)} fusion(bf16[1024,512]{1,0:T(8,128)(2,1)S(1)} %convolution_convert_fusion.applied_ref, bf16[1024,128]{0,1:T(8,128)(2,1)S(1)} %fusion, bf16[512,128]{1,0:T(8,128)(2,1)S(1)} %bitcast.21), kind=kOutput, calls=%fused_computation | convolution fusion | flops 135790592 | bytes 2490368 | tf_op jit(solution)/shard_map/dot_general | solution.py:195
  (6 shorter events, 0.1 us)
Async XLA Ops:
  0.0 4.3 %copy-start = (bf16[1024,1024]{1,0:T(8,128)(2,1)S(1)}, bf16[1024,1024]{1,0:T(8,128)(2,1)}, u32[]{:S(2)}) copy-start(bf16[1024,1024]{1,0:T(8,128)(2,1)} %param.11) | copy-start | bytes 6291460
  0.0 6.8 %copy-start.2 = (bf16[1024,128]{1,0:T(8,128)(2,1)S(1)}, bf16[1024,128]{1,0:T(8,128)(2,1)}, u32[]{:S(2)}) copy-start(bf16[1024,128]{1,0:T(8,128)(2,1)} %param.9) | copy-start | bytes 786436
  0.0 6.8 %copy-start.3 = (bf16[1,1024,128]{2,1,0:T(8,128)(2,1)S(1)}, bf16[1,1024,128]{2,1,0:T(8,128)(2,1)}, u32[]{:S(2)}) copy-start(bf16[1,1024,128]{2,1,0:T(8,128)(2,1)} %param.8) | copy-start | bytes 786436
  0.0 9.6 %collective-permute-start.2 = (bf16[1024,128]{1,0:T(8,128)(2,1)}, bf16[1024,128]{1,0:T(8,128)(2,1)}, u32[]{:S(2)}, u32[]{:S(2)}) collective-permute-start(bf16[1024,128]{1,0:T(8,128)(2,1)} %bitcast.19), channel_id=1, source_target_pairs={{0,16},{16,0},{1,17},{17,1},{2,18},{18,2},{3,19},{19,3},{4,20},{20... | collective-permute-start | bytes 786440 | tf_op jit(solution)/shard_map/ppermute | solution.py:17
  3.0 7.6 %collective-permute-start.1 = (bf16[1024,128]{1,0:T(8,128)(2,1)}, bf16[1024,128]{1,0:T(8,128)(2,1)S(1)}, u32[]{:S(2)}, u32[]{:S(2)}) collective-permute-start(bf16[1024,128]{1,0:T(8,128)(2,1)} %param.10), channel_id=1, source_target_pairs={{1,0},{2,1},{3,2},{4,3},{5,4},{6,5},{7,6},{8,7},{9,8},{10,9},{11,1... | collective-permute-start | bytes 786440 | tf_op jit(solution)/shard_map/ppermute | solution.py:12
  7.1 4.4 %collective-permute-start = (bf16[128,128]{1,0:T(8,128)(2,1)S(1)}, bf16[128,128]{1,0:T(8,128)(2,1)S(1)}, u32[]{:S(2)}, u32[]{:S(2)}) collective-permute-start(bf16[128,128]{1,0:T(8,128)(2,1)S(1)} %fusion.1.refs_0_), channel_id=1, source_target_pairs={{0,16},{16,0},{1,17},{17,1},{2,18},{18,2},{3,19},{19,3},{4,20},{20... | collective-permute-start | bytes 98312 | tf_op jit(solution)/shard_map/ppermute | solution.py:17
  10.6 1.0 %copy-start.1 = (bf16[1,1024,128]{2,1,0:T(8,128)(2,1)S(1)}, bf16[1,1024,128]{2,1,0:T(8,128)(2,1)}, u32[]{:S(2)}) copy-start(bf16[1,1024,128]{2,1,0:T(8,128)(2,1)} %param.7) | copy-start | bytes 786436
  25.3 4.8 %collective-permute-start.3 = (bf16[64,128]{1,0:T(8,128)(2,1)S(1)}, bf16[64,128]{1,0:T(8,128)(2,1)S(1)}, u32[]{:S(2)}, u32[]{:S(2)}) collective-permute-start(bf16[64,128]{1,0:T(8,128)(2,1)S(1)} %get-tuple-element.51), channel_id=1, source_target_pairs={{0,8},{1,9},{2,10},{3,11},{4,12},{5,13},{6,14},{7,15},{16,24},{17,... | collective-permute-start | bytes 49160 | tf_op jit(solution)/shard_map/ppermute | solution.py:12

commit v25 on v17

--- a/solution.py
+++ b/solution.py
@@ -43,15 +43,17 @@
 
 
 def make_maps(layers, *refs):
-    lefts = jnp.concatenate([ref[...] for ref in refs[:layers]], axis=1)
-    cores = jnp.concatenate([ref[...] for ref in refs[layers : 2 * layers]], axis=0)
-    weights_ref, shift_ref, range_ref, sent_ref = refs[2 * layers :]
+    cores = jnp.concatenate([ref[...] for ref in refs[:layers]], axis=0)
+    lefts = jnp.concatenate([ref[...] for ref in refs[layers : 2 * layers]], axis=1)
+    weights_ref, next_ref, applied_ref, range_ref, sent_ref = refs[2 * layers :]
+    shift_t = project(next_ref[...], applied_ref[...]).T.astype(jnp.bfloat16)
     range_ref[...] = (-product(lefts, cores)).astype(jnp.bfloat16)
     map_t = wide(wide(weights_ref[...], lefts), cores).T.astype(jnp.bfloat16)
     rank = map_t.shape[0]
+    share = sent_ref.shape[1] - rank
     for target in range(sent_ref.shape[0]):
         sent_ref[target, :rank] = map_t
-        sent_ref[target, rank:] = shift_ref[target]
+        sent_ref[target, rank:] = shift_t[target * share : (target + 1) * share]
 
 
 def chain(steps_ref, state, values_ref):
@@ -128,16 +130,14 @@
     core = project(right_factors[0], sketch).astype(half)
     cores = [core] + [rotated(core, "layer", k) for k in range(1, layers)]
 
-    shift_t = project(applied, next_rows).astype(half).reshape(lowers, share, rank)
+    next_rows, *others = lax.optimization_barrier((next_rows, *lefts[1:]))
     weights = project(next_rows, inverse_diag)
     entry = lax.dynamic_slice_in_dim(incoming, lower * share, share, 1)
     place = upper.reshape(1)
-    lefts[-1], shift_t, weights, entry, place = lax.optimization_barrier(
-        (lefts[-1], shift_t, weights, entry, place)
-    )
+    weights, entry, place = lax.optimization_barrier((weights, entry, place))
     tile_range, sent = local(
         lambda *refs: make_maps(layers, *refs),
-        (*lefts, *cores, weights, shift_t),
+        (*cores, lefts[0], *others, weights, next_rows, applied),
         ((order, rank), half),
         ((lowers, rank + share, rank), half),
     )

time: 40.8 us -> 40.6 us (level)
  matrix products: 7.91 us -> 5.49 us
  waiting for transfers between devices: 0.57 us -> 2.98 us
  blocking collectives: 21.9 us -> 19.6 us
  Pallas kernels: 2.03 us -> 3.13 us
  starting transfers between devices: 6.95 us -> 7.97 us
    dot_general x3 -> x2, matrix products: 3.17 us -> 0.74 us  [project(): lax.dot_general(basis, vectors, (((0,), (0,)), ((), ())), preferred_eleme...]
    ppermute x2, waiting for transfers between devices: 0.05 us -> 2.46 us  [rotated(): lax.ppermute(value, axis, [(source, (source + steps) % count) for source...]
    all_to_all x2, blocking collectives: 21.9 us -> 19.6 us  [exchanged(): lax.all_to_all(blocks, 'row', 0, 0, axis_index_groups=members, tiled=True)]
    pallas_call x4, Pallas kernels: 2.03 us -> 3.13 us  [local(): pl.pallas_call(kernel, in_specs=specs, out_specs=[VMEM] * len(outputs), o...]
    ppermute x2, starting transfers between devices: 3.67 us -> 4.68 us  [shifted(): lax.ppermute(value, axis, [(source, source + steps) for source in range(l...]
  transfers between devices with their start and end apart: 4 -> 4, of which waited for: 1 -> 3; matrix products, arithmetic and copies ran while one was open for 18% -> 12% of each run, Pallas kernels for 0% -> 0%
where the time goes in v25:
time: 40.6 us; the launch traced here: 40.3 us
  blocking collectives  19.6 us (48%)
  starting transfers between devices  7.97 us (20%)
  matrix products  5.49 us (14%)
  Pallas kernels  3.13 us (8%)
  waiting for transfers between devices  2.98 us (7%)
  local copies, waits for them, and re-layouts  0.97 us (2%)
    all_to_all x2, blocking collectives, exchanged(): lax.all_to_all(blocks, 'row', 0, 0, axis_index_groups=members, tiled=True)  19.6 us
    ppermute x2, starting transfers between devices, shifted(): lax.ppermute(value, axis, [(source, source + steps) for source in range(l...  4.68 us
    dot_general x2, matrix products, product(): return jnp.dot(a, b, preferred_element_type=jnp.float32)  3.31 us
    ppermute x2, starting transfers between devices, rotated(): lax.ppermute(value, axis, [(source, (source + steps) % count) for source...  3.28 us
    pallas_call x4, Pallas kernels, local(): pl.pallas_call(kernel, in_specs=specs, out_specs=[VMEM] * len(outputs), o...  3.13 us
    ppermute x2, waiting for transfers between devices, rotated(): lax.ppermute(value, axis, [(source, (source + steps) % count) for source...  2.46 us
    dot_general x1, matrix products, body(): lax.dot_general(gain, coupled, FLIPPED, preferred_element_type=jnp.float32)  1.44 us
    dynamic_slice x1, local copies, waits for them, and re-layouts, body(): entry = lax.dynamic_slice_in_dim(incoming, lower * share, share, 1)  0.96 us
  transfers between devices with their start and end apart: 4, of which 3 were waited for; matrix products, arithmetic and copies ran while one was open for 12% of the time, Pallas kernels for 0%

profile of v25, /device:TPU:0, one launch (start us, length us, event | category | flops | bytes accessed | tf_op | source)
XLA Modules:
  0.0 40.3 jit_solution(6447323021225566632)
XLA Ops:
  0.0 0.0 copy-start
  0.0 3.0 %collective-permute-start.2 = (bf16[1024,128]{1,0:T(8,128)(2,1)}, bf16[1024,128]{1,0:T(8,128)(2,1)}, u32[]{:S(2)}, u32[]{:S(2)}) collective-permute-start(bf16[1024,128]{1,0:T(8,128)(2,1)} %bitcast.19), channel_id=1, source_target_pairs={{0,16},{16,0},{1,17},{17,1},{2,18},{18,2},{3,19},{19,3},{4,20},{20... | collective-permute-start | bytes 786440 | tf_op jit(solution)/shard_map/ppermute | solution.py:17
  3.0 1.3 %collective-permute-start.1 = (bf16[1024,128]{1,0:T(8,128)(2,1)}, bf16[1024,128]{1,0:T(8,128)(2,1)S(1)}, u32[]{:S(2)}, u32[]{:S(2)}) collective-permute-start(bf16[1024,128]{1,0:T(8,128)(2,1)} %param.10), channel_id=1, source_target_pairs={{1,0},{2,1},{3,2},{4,3},{5,4},{6,5},{7,6},{8,7},{9,8},{10,9},{11,1... | collective-permute-start | bytes 786440 | tf_op jit(solution)/shard_map/ppermute | solution.py:12
  4.3 0.0 copy-done
  4.3 2.5 %convolution_convert_fusion.refs_6_ = bf16[1024,512]{1,0:T(8,128)(2,1)S(1)} fusion(bf16[1024,1024]{1,0:T(8,128)(2,1)S(1)} %copy-done, bf16[1024,512]{1,0:T(8,128)(2,1)} %param.12), kind=kOutput, calls=%fused_computation.1 | convolution fusion | flops 1074266112 | bytes 4194304 | tf_op jit(solution)/shard_map/dot_general | solution.py:27
  6.8 0.0 copy-done.2
  6.8 0.0 copy-done.3
  6.8 0.3 fusion.1.refs_0_
  7.1 0.3 collective-permute-start
  7.4 1.0 %constant_dynamic-slice_fusion.entry_ref = f32[128,64]{1,0:T(8,128)S(1)} fusion(f32[128,512]{1,0:T(8,128)} %param.13, s32[]{:T(128)S(6)} %select_n.3), kind=kLoop, calls=%fused_computation.7 | loop fusion | bytes 65540 | tf_op jit(solution)/shard_map/dynamic_slice | solution.py:135
  8.3 1.3 %collective-permute-done.2.refs_3_ = bf16[1024,128]{1,0:T(8,128)(2,1)} collective-permute-done((bf16[1024,128]{1,0:T(8,128)(2,1)}, bf16[1024,128]{1,0:T(8,128)(2,1)}, u32[]{:S(2)}, u32[]{:S(2)}) %collective-permute-start.2) | collective-permute-done | bytes 262176 | tf_op jit(solution)/shard_map/ppermute | solution.py:17
  9.6 0.0 collective-permute-done.1.refs_5_
  9.6 0.5 %fusion.3.refs_4_ = f32[128,1024]{1,0:T(8,128)S(1)} fusion(bf16[1024,128]{1,0:T(8,128)(2,1)S(1)} %collective-permute-done.1.refs_5_, bf16[1024,1024]{1,0:T(8,128)(2,1)S(1)} %copy-done), kind=kOutput, calls=%fused_computation.8 | convolution fusion | flops 268435456 | bytes 2883584 | tf_op jit(solution)/shard_map/dot_general | solution.py:21
  10.1 1.1 %collective-permute-done.refs_1_ = bf16[128,128]{1,0:T(8,128)(2,1)S(1)} collective-permute-done((bf16[128,128]{1,0:T(8,128)(2,1)S(1)}, bf16[128,128]{1,0:T(8,128)(2,1)S(1)}, u32[]{:S(2)}, u32[]{:S(2)}) %collective-permute-start) | collective-permute-done | bytes 32800 | tf_op jit(solution)/shard_map/ppermute | solution.py:17
  11.3 0.0 copy-done.1
  11.3 1.8 %shard_map.73 = (bf16[1024,128]{1,0:T(8,128)(2,1)S(1)}, bf16[8,192,128]{2,1,0:T(8,128)(2,1)S(1)}) custom-call(bf16[128,128]{1,0:T(8,128)(2,1)S(1)} %fusion.1.refs_0_, bf16[128,128]{1,0:T(8,128)(2,1)S(1)} %collective-permute-done.refs_1_, bf16[1024,128]{1,0:T(8,128)(2,1)S(1)} %bitcast.20, bf16[1024,128]{1,0:T(8,128)(2,1)} %collective-permute-done.2.refs_3_, ...), custom_call_target="tpu_custom_call" | custom-call | tf_op jit(solution)/shard_map/pallas_call | solution.py:101
  13.1 12.1 %all_to_all.10.steps_ref = bf16[8,192,128]{2,1,0:T(8,128)(2,1)S(1)} all-to-all(bf16[8,192,128]{2,1,0:T(8,128)(2,1)S(1)} %get-tuple-element.39), channel_id=1, replica_groups={{0,1,2,3,4,5,6,7},{8,9,10,11,12,13,14,15},{16,17,18,19,20,21,22,23},{24..., dimensions={0} | all-to-all | bytes 786432 | tf_op jit(solution)/shard_map/all_to_all | solution.py:112
  25.1 1.1 %shard_map.74 = (f32[8,64,128]{2,1,0:T(8,128)S(1)}, bf16[64,128]{1,0:T(8,128)(2,1)S(1)}) custom-call(s32[1]{0:T(128)} %bitcast.3.upper_ref, bf16[8,192,128]{2,1,0:T(8,128)(2,1)S(1)} %all_to_all.10.steps_ref, f32[128,64]{1,0:T(8,128)S(1)} %constant_dynamic-slice_fusion.entry_ref), custom_call_target="tpu_custom_call" | custom-call | tf_op jit(solution)/shard_map/pallas_call | solution.py:101
  26.2 3.4 %collective-permute-start.3 = (bf16[64,128]{1,0:T(8,128)(2,1)S(1)}, bf16[64,128]{1,0:T(8,128)(2,1)S(1)}, u32[]{:S(2)}, u32[]{:S(2)}) collective-permute-start(bf16[64,128]{1,0:T(8,128)(2,1)S(1)} %get-tuple-element.47), channel_id=1, source_target_pairs={{0,8},{1,9},{2,10},{3,11},{4,12},{5,13},{6,14},{7,15},{16,24},{17,... | collective-permute-start | bytes 49160 | tf_op jit(solution)/shard_map/ppermute | solution.py:12
  29.6 0.8 %fusion = bf16[1024,128]{0,1:T(8,128)(2,1)S(1)} fusion(bf16[1024,128]{1,0:T(8,128)(2,1)S(1)} %get-tuple-element.48, bf16[1024,1024]{1,0:T(8,128)(2,1)S(1)} %copy-done), kind=kOutput, calls=%fused_computation.3 | convolution fusion | flops 268566528 | bytes 2621440 | tf_op jit(solution)/shard_map/dot_general | solution.py:27
  30.5 0.5 %collective-permute-done.3.entered_ref = bf16[64,128]{1,0:T(8,128)(2,1)S(1)} collective-permute-done((bf16[64,128]{1,0:T(8,128)(2,1)S(1)}, bf16[64,128]{1,0:T(8,128)(2,1)S(1)}, u32[]{:S(2)}, u32[]{:S(2)}) %collective-permute-start.3) | collective-permute-done | bytes 16416 | tf_op jit(solution)/shard_map/ppermute | solution.py:12
  31.1 0.2 shard_map.76
  31.3 7.6 %all_to_all.11 = bf16[8,64,128]{2,1,0:T(8,128)(2,1)S(1)} all-to-all(bf16[8,64,128]{2,1,0:T(8,128)(2,1)S(1)} %shard_map.76), channel_id=1, replica_groups={{0,1,2,3,4,5,6,7},{8,9,10,11,12,13,14,15},{16,17,18,19,20,21,22,23},{24..., dimensions={0} | all-to-all | bytes 262144 | tf_op jit(solution)/shard_map/all_to_all | solution.py:112
  38.8 1.4 %subtract_convert_fusion = bf16[1024,512]{1,0:T(8,128)(2,1)} fusion(bf16[1024,512]{1,0:T(8,128)(2,1)S(1)} %convolution_convert_fusion.refs_6_, bf16[1024,128]{0,1:T(8,128)(2,1)S(1)} %fusion, bf16[512,128]{1,0:T(8,128)(2,1)S(1)} %bitcast.21), kind=kOutput, calls=%fused_computation | convolution fusion | flops 135790592 | bytes 2490368 | tf_op jit(solution)/shard_map/dot_general | solution.py:168
  (4 shorter events, 0.1 us)
Async XLA Ops:
  0.0 4.3 %copy-start = (bf16[1024,1024]{1,0:T(8,128)(2,1)S(1)}, bf16[1024,1024]{1,0:T(8,128)(2,1)}, u32[]{:S(2)}) copy-start(bf16[1024,1024]{1,0:T(8,128)(2,1)} %param.11) | copy-start | bytes 6291460
  0.0 6.8 %copy-start.2 = (bf16[1024,128]{1,0:T(8,128)(2,1)S(1)}, bf16[1024,128]{1,0:T(8,128)(2,1)}, u32[]{:S(2)}) copy-start(bf16[1024,128]{1,0:T(8,128)(2,1)} %param.9) | copy-start | bytes 786436
  0.0 6.8 %copy-start.3 = (bf16[1,1024,128]{2,1,0:T(8,128)(2,1)S(1)}, bf16[1,1024,128]{2,1,0:T(8,128)(2,1)}, u32[]{:S(2)}) copy-start(bf16[1,1024,128]{2,1,0:T(8,128)(2,1)} %param.8) | copy-start | bytes 786436
  0.0 9.6 %collective-permute-start.2 = (bf16[1024,128]{1,0:T(8,128)(2,1)}, bf16[1024,128]{1,0:T(8,128)(2,1)}, u32[]{:S(2)}, u32[]{:S(2)}) collective-permute-start(bf16[1024,128]{1,0:T(8,128)(2,1)} %bitcast.19), channel_id=1, source_target_pairs={{0,16},{16,0},{1,17},{17,1},{2,18},{18,2},{3,19},{19,3},{4,20},{20... | collective-permute-start | bytes 786440 | tf_op jit(solution)/shard_map/ppermute | solution.py:17
  3.0 6.6 %collective-permute-start.1 = (bf16[1024,128]{1,0:T(8,128)(2,1)}, bf16[1024,128]{1,0:T(8,128)(2,1)S(1)}, u32[]{:S(2)}, u32[]{:S(2)}) collective-permute-start(bf16[1024,128]{1,0:T(8,128)(2,1)} %param.10), channel_id=1, source_target_pairs={{1,0},{2,1},{3,2},{4,3},{5,4},{6,5},{7,6},{8,7},{9,8},{10,9},{11,1... | collective-permute-start | bytes 786440 | tf_op jit(solution)/shard_map/ppermute | solution.py:12
  7.1 4.2 %collective-permute-start = (bf16[128,128]{1,0:T(8,128)(2,1)S(1)}, bf16[128,128]{1,0:T(8,128)(2,1)S(1)}, u32[]{:S(2)}, u32[]{:S(2)}) collective-permute-start(bf16[128,128]{1,0:T(8,128)(2,1)S(1)} %fusion.1.refs_0_), channel_id=1, source_target_pairs={{0,16},{16,0},{1,17},{17,1},{2,18},{18,2},{3,19},{19,3},{4,20},{20... | collective-permute-start | bytes 98312 | tf_op jit(solution)/shard_map/ppermute | solution.py:17
  7.4 3.9 %copy-start.1 = (bf16[1,1024,128]{2,1,0:T(8,128)(2,1)S(1)}, bf16[1,1024,128]{2,1,0:T(8,128)(2,1)}, u32[]{:S(2)}) copy-start(bf16[1,1024,128]{2,1,0:T(8,128)(2,1)} %param.7) | copy-start | bytes 786436
  26.2 4.8 %collective-permute-start.3 = (bf16[64,128]{1,0:T(8,128)(2,1)S(1)}, bf16[64,128]{1,0:T(8,128)(2,1)S(1)}, u32[]{:S(2)}, u32[]{:S(2)}) collective-permute-start(bf16[64,128]{1,0:T(8,128)(2,1)S(1)} %get-tuple-element.47), channel_id=1, source_target_pairs={{0,8},{1,9},{2,10},{3,11},{4,12},{5,13},{6,14},{7,15},{16,24},{17,... | collective-permute-start | bytes 49160 | tf_op jit(solution)/shard_map/ppermute | solution.py:12

commit v26 on v25

--- a/solution.py
+++ b/solution.py
@@ -42,10 +42,16 @@
     return both[: value.shape[0]] + both[value.shape[0] :]
 
 
+def lay(*refs):
+    rank = refs[0].shape[1]
+    for layer, ref in enumerate(refs[:-1]):
+        refs[-1][:, layer * rank : (layer + 1) * rank] = ref[...]
+
+
 def make_maps(layers, *refs):
     cores = jnp.concatenate([ref[...] for ref in refs[:layers]], axis=0)
-    lefts = jnp.concatenate([ref[...] for ref in refs[layers : 2 * layers]], axis=1)
-    weights_ref, next_ref, applied_ref, range_ref, sent_ref = refs[2 * layers :]
+    left_ref, others_ref, weights_ref, next_ref, applied_ref, range_ref, sent_ref = refs[layers:]
+    lefts = jnp.concatenate([left_ref[...], others_ref[...]], axis=1)
     shift_t = project(next_ref[...], applied_ref[...]).T.astype(jnp.bfloat16)
     range_ref[...] = (-product(lefts, cores)).astype(jnp.bfloat16)
     map_t = wide(wide(weights_ref[...], lefts), cores).T.astype(jnp.bfloat16)
@@ -130,14 +136,15 @@
     core = project(right_factors[0], sketch).astype(half)
     cores = [core] + [rotated(core, "layer", k) for k in range(1, layers)]
 
-    next_rows, *others = lax.optimization_barrier((next_rows, *lefts[1:]))
+    (others,) = local(lay, lefts[1:], ((order, (layers - 1) * rank), half))
+    next_rows, others = lax.optimization_barrier((next_rows, others))
     weights = project(next_rows, inverse_diag)
     entry = lax.dynamic_slice_in_dim(incoming, lower * share, share, 1)
     place = upper.reshape(1)
     weights, entry, place = lax.optimization_barrier((weights, entry, place))
     tile_range, sent = local(
         lambda *refs: make_maps(layers, *refs),
-        (*cores, lefts[0], *others, weights, next_rows, applied),
+        (*cores, lefts[0], others, weights, next_rows, applied),
         ((order, rank), half),
         ((lowers, rank + share, rank), half),
     )

time: 40.6 us -> 39.6 us (0.975)
  waiting for transfers between devices: 2.98 us -> 2 us
    ppermute x2, waiting for transfers between devices: 2.46 us -> 1.47 us  [rotated(): lax.ppermute(value, axis, [(source, (source + steps) % count) for source...]
    pallas_call x4 -> x5, Pallas kernels: 3.13 us -> 3.15 us  [local(): pl.pallas_call(kernel, in_specs=specs, out_specs=[VMEM] * len(outputs), o...]
  transfers between devices with their start and end apart: 4 -> 4, of which waited for: 3 -> 3; matrix products, arithmetic and copies ran while one was open for 12% -> 13% of each run, Pallas kernels for 0% -> 3%
where the time goes in v26:
time: 39.6 us; the launch traced here: 39.3 us
  blocking collectives  19.6 us (49%)
  starting transfers between devices  7.97 us (20%)
  matrix products  5.49 us (14%)
  Pallas kernels  3.15 us (8%)
  waiting for transfers between devices  2 us (5%)
  local copies, waits for them, and re-layouts  0.97 us (2%)
    all_to_all x2, blocking collectives, exchanged(): lax.all_to_all(blocks, 'row', 0, 0, axis_index_groups=members, tiled=True)  19.6 us
    ppermute x2, starting transfers between devices, shifted(): lax.ppermute(value, axis, [(source, source + steps) for source in range(l...  4.68 us
    dot_general x2, matrix products, product(): return jnp.dot(a, b, preferred_element_type=jnp.float32)  3.31 us
    ppermute x2, starting transfers between devices, rotated(): lax.ppermute(value, axis, [(source, (source + steps) % count) for source...  3.28 us
    pallas_call x5, Pallas kernels, local(): pl.pallas_call(kernel, in_specs=specs, out_specs=[VMEM] * len(outputs), o...  3.15 us
    ppermute x2, waiting for transfers between devices, rotated(): lax.ppermute(value, axis, [(source, (source + steps) % count) for source...  1.47 us
    dot_general x1, matrix products, body(): lax.dot_general(gain, coupled, FLIPPED, preferred_element_type=jnp.float32)  1.44 us
    dynamic_slice x1, local copies, waits for them, and re-layouts, body(): entry = lax.dynamic_slice_in_dim(incoming, lower * share, share, 1)  0.96 us
  transfers between devices with their start and end apart: 4, of which 3 were waited for; matrix products, arithmetic and copies ran while one was open for 13% of the time, Pallas kernels for 3%

profile of v26, /device:TPU:0, one launch (start us, length us, event | category | flops | bytes accessed | tf_op | source)
XLA Modules:
  0.0 39.3 jit_solution(4645338146212677677)
XLA Ops:
  0.0 0.0 copy-start
  0.0 3.0 %collective-permute-start.2 = (bf16[1024,128]{1,0:T(8,128)(2,1)}, bf16[1024,128]{1,0:T(8,128)(2,1)}, u32[]{:S(2)}, u32[]{:S(2)}) collective-permute-start(bf16[1024,128]{1,0:T(8,128)(2,1)} %bitcast.19), channel_id=1, source_target_pairs={{0,16},{16,0},{1,17},{17,1},{2,18},{18,2},{3,19},{19,3},{4,20},{20... | collective-permute-start | bytes 786440 | tf_op jit(solution)/shard_map/ppermute | solution.py:17
  3.0 1.3 %collective-permute-start.1 = (bf16[1024,128]{1,0:T(8,128)(2,1)}, bf16[1024,128]{1,0:T(8,128)(2,1)S(1)}, u32[]{:S(2)}, u32[]{:S(2)}) collective-permute-start(bf16[1024,128]{1,0:T(8,128)(2,1)} %param.10), channel_id=1, source_target_pairs={{1,0},{2,1},{3,2},{4,3},{5,4},{6,5},{7,6},{8,7},{9,8},{10,9},{11,1... | collective-permute-start | bytes 786440 | tf_op jit(solution)/shard_map/ppermute | solution.py:12
  4.3 0.0 copy-done
  4.3 2.5 %convolution_convert_fusion.refs_6_ = bf16[1024,512]{1,0:T(8,128)(2,1)S(1)} fusion(bf16[1024,1024]{1,0:T(8,128)(2,1)S(1)} %copy-done, bf16[1024,512]{1,0:T(8,128)(2,1)} %param.12), kind=kOutput, calls=%fused_computation.1 | convolution fusion | flops 1074266112 | bytes 4194304 | tf_op jit(solution)/shard_map/dot_general | solution.py:27
  6.8 0.0 copy-done.2
  6.8 0.0 copy-done.3
  6.8 0.3 fusion.1.refs_0_
  7.1 0.3 collective-permute-start
  7.4 1.0 %constant_dynamic-slice_fusion.entry_ref = f32[128,64]{1,0:T(8,128)S(1)} fusion(f32[128,512]{1,0:T(8,128)} %param.13, s32[]{:T(128)S(6)} %select_n.3), kind=kLoop, calls=%fused_computation.7 | loop fusion | bytes 65540 | tf_op jit(solution)/shard_map/dynamic_slice | solution.py:142
  8.3 1.3 %collective-permute-done.2.refs_0_ = bf16[1024,128]{1,0:T(8,128)(2,1)} collective-permute-done((bf16[1024,128]{1,0:T(8,128)(2,1)}, bf16[1024,128]{1,0:T(8,128)(2,1)}, u32[]{:S(2)}, u32[]{:S(2)}) %collective-permute-start.2) | collective-permute-done | bytes 262176 | tf_op jit(solution)/shard_map/ppermute | solution.py:17
  9.6 1.0 %shard_map.73.refs_3_ = bf16[1024,128]{1,0:T(8,128)(2,1)S(1)} custom-call(bf16[1024,128]{1,0:T(8,128)(2,1)} %collective-permute-done.2.refs_0_), custom_call_target="tpu_custom_call" | custom-call | tf_op jit(solution)/shard_map/pallas_call | solution.py:107
  10.6 0.0 collective-permute-done.1.refs_5_
  10.6 0.5 %fusion.3.refs_4_ = f32[128,1024]{1,0:T(8,128)S(1)} fusion(bf16[1024,128]{1,0:T(8,128)(2,1)S(1)} %collective-permute-done.1.refs_5_, bf16[1024,1024]{1,0:T(8,128)(2,1)S(1)} %copy-done), kind=kOutput, calls=%fused_computation.8 | convolution fusion | flops 268435456 | bytes 2883584 | tf_op jit(solution)/shard_map/dot_general | solution.py:21
  11.1 0.2 collective-permute-done.refs_1_
  11.3 0.9 %shard_map.74 = (bf16[1024,128]{1,0:T(8,128)(2,1)S(1)}, bf16[8,192,128]{2,1,0:T(8,128)(2,1)S(1)}) custom-call(bf16[128,128]{1,0:T(8,128)(2,1)S(1)} %fusion.1.refs_0_, bf16[128,128]{1,0:T(8,128)(2,1)S(1)} %collective-permute-done.refs_1_, bf16[1024,128]{1,0:T(8,128)(2,1)S(1)} %bitcast.20, bf16[1024,128]{1,0:T(8,128)(2,1)S(1)} %shard_map.73.refs_3_, ...), custom_call_target="tpu_custom_call" | custom-call | tf_op jit(solution)/shard_map/pallas_call | solution.py:107
  12.1 12.1 %all_to_all.10.steps_ref = bf16[8,192,128]{2,1,0:T(8,128)(2,1)S(1)} all-to-all(bf16[8,192,128]{2,1,0:T(8,128)(2,1)S(1)} %get-tuple-element.39), channel_id=1, replica_groups={{0,1,2,3,4,5,6,7},{8,9,10,11,12,13,14,15},{16,17,18,19,20,21,22,23},{24..., dimensions={0} | all-to-all | bytes 786432 | tf_op jit(solution)/shard_map/all_to_all | solution.py:118
  24.2 1.1 %shard_map.75 = (f32[8,64,128]{2,1,0:T(8,128)S(1)}, bf16[64,128]{1,0:T(8,128)(2,1)S(1)}) custom-call(s32[1]{0:T(128)} %bitcast.3.upper_ref, bf16[8,192,128]{2,1,0:T(8,128)(2,1)S(1)} %all_to_all.10.steps_ref, f32[128,64]{1,0:T(8,128)S(1)} %constant_dynamic-slice_fusion.entry_ref), custom_call_target="tpu_custom_call" | custom-call | tf_op jit(solution)/shard_map/pallas_call | solution.py:107
  25.3 3.4 %collective-permute-start.3 = (bf16[64,128]{1,0:T(8,128)(2,1)S(1)}, bf16[64,128]{1,0:T(8,128)(2,1)S(1)}, u32[]{:S(2)}, u32[]{:S(2)}) collective-permute-start(bf16[64,128]{1,0:T(8,128)(2,1)S(1)} %get-tuple-element.47), channel_id=1, source_target_pairs={{0,8},{1,9},{2,10},{3,11},{4,12},{5,13},{6,14},{7,15},{16,24},{17,... | collective-permute-start | bytes 49160 | tf_op jit(solution)/shard_map/ppermute | solution.py:12
  28.7 0.8 %fusion = bf16[1024,128]{0,1:T(8,128)(2,1)S(1)} fusion(bf16[1024,128]{1,0:T(8,128)(2,1)S(1)} %get-tuple-element.48, bf16[1024,1024]{1,0:T(8,128)(2,1)S(1)} %copy-done), kind=kOutput, calls=%fused_computation.3 | convolution fusion | flops 268566528 | bytes 2621440 | tf_op jit(solution)/shard_map/dot_general | solution.py:27
  29.6 0.5 %collective-permute-done.3.entered_ref = bf16[64,128]{1,0:T(8,128)(2,1)S(1)} collective-permute-done((bf16[64,128]{1,0:T(8,128)(2,1)S(1)}, bf16[64,128]{1,0:T(8,128)(2,1)S(1)}, u32[]{:S(2)}, u32[]{:S(2)}) %collective-permute-start.3) | collective-permute-done | bytes 16416 | tf_op jit(solution)/shard_map/ppermute | solution.py:12
  30.1 0.2 shard_map.77
  30.3 7.6 %all_to_all.11 = bf16[8,64,128]{2,1,0:T(8,128)(2,1)S(1)} all-to-all(bf16[8,64,128]{2,1,0:T(8,128)(2,1)S(1)} %shard_map.77), channel_id=1, replica_groups={{0,1,2,3,4,5,6,7},{8,9,10,11,12,13,14,15},{16,17,18,19,20,21,22,23},{24..., dimensions={0} | all-to-all | bytes 262144 | tf_op jit(solution)/shard_map/all_to_all | solution.py:118
  37.9 1.4 %subtract_convert_fusion = bf16[1024,512]{1,0:T(8,128)(2,1)} fusion(bf16[1024,512]{1,0:T(8,128)(2,1)S(1)} %convolution_convert_fusion.refs_6_, bf16[1024,128]{0,1:T(8,128)(2,1)S(1)} %fusion, bf16[512,128]{1,0:T(8,128)(2,1)S(1)} %bitcast.21), kind=kOutput, calls=%fused_computation | convolution fusion | flops 135790592 | bytes 2490368 | tf_op jit(solution)/shard_map/dot_general | solution.py:175
  (5 shorter events, 0.1 us)
Async XLA Ops:
  0.0 4.3 %copy-start = (bf16[1024,1024]{1,0:T(8,128)(2,1)S(1)}, bf16[1024,1024]{1,0:T(8,128)(2,1)}, u32[]{:S(2)}) copy-start(bf16[1024,1024]{1,0:T(8,128)(2,1)} %param.11) | copy-start | bytes 6291460
  0.0 6.8 %copy-start.2 = (bf16[1024,128]{1,0:T(8,128)(2,1)S(1)}, bf16[1024,128]{1,0:T(8,128)(2,1)}, u32[]{:S(2)}) copy-start(bf16[1024,128]{1,0:T(8,128)(2,1)} %param.9) | copy-start | bytes 786436
  0.0 6.8 %copy-start.3 = (bf16[1,1024,128]{2,1,0:T(8,128)(2,1)S(1)}, bf16[1,1024,128]{2,1,0:T(8,128)(2,1)}, u32[]{:S(2)}) copy-start(bf16[1,1024,128]{2,1,0:T(8,128)(2,1)} %param.8) | copy-start | bytes 786436
  0.0 9.6 %collective-permute-start.2 = (bf16[1024,128]{1,0:T(8,128)(2,1)}, bf16[1024,128]{1,0:T(8,128)(2,1)}, u32[]{:S(2)}, u32[]{:S(2)}) collective-permute-start(bf16[1024,128]{1,0:T(8,128)(2,1)} %bitcast.19), channel_id=1, source_target_pairs={{0,16},{16,0},{1,17},{17,1},{2,18},{18,2},{3,19},{19,3},{4,20},{20... | collective-permute-start | bytes 786440 | tf_op jit(solution)/shard_map/ppermute | solution.py:17
  3.0 7.6 %collective-permute-start.1 = (bf16[1024,128]{1,0:T(8,128)(2,1)}, bf16[1024,128]{1,0:T(8,128)(2,1)S(1)}, u32[]{:S(2)}, u32[]{:S(2)}) collective-permute-start(bf16[1024,128]{1,0:T(8,128)(2,1)} %param.10), channel_id=1, source_target_pairs={{1,0},{2,1},{3,2},{4,3},{5,4},{6,5},{7,6},{8,7},{9,8},{10,9},{11,1... | collective-permute-start | bytes 786440 | tf_op jit(solution)/shard_map/ppermute | solution.py:12
  7.1 4.2 %collective-permute-start = (bf16[128,128]{1,0:T(8,128)(2,1)S(1)}, bf16[128,128]{1,0:T(8,128)(2,1)S(1)}, u32[]{:S(2)}, u32[]{:S(2)}) collective-permute-start(bf16[128,128]{1,0:T(8,128)(2,1)S(1)} %fusion.1.refs_0_), channel_id=1, source_target_pairs={{0,16},{16,0},{1,17},{17,1},{2,18},{18,2},{3,19},{19,3},{4,20},{20... | collective-permute-start | bytes 98312 | tf_op jit(solution)/shard_map/ppermute | solution.py:17
  7.4 3.9 %copy-start.1 = (bf16[1,1024,128]{2,1,0:T(8,128)(2,1)S(1)}, bf16[1,1024,128]{2,1,0:T(8,128)(2,1)}, u32[]{:S(2)}) copy-start(bf16[1,1024,128]{2,1,0:T(8,128)(2,1)} %param.7) | copy-start | bytes 786436
  25.3 4.8 %collective-permute-start.3 = (bf16[64,128]{1,0:T(8,128)(2,1)S(1)}, bf16[64,128]{1,0:T(8,128)(2,1)S(1)}, u32[]{:S(2)}, u32[]{:S(2)}) collective-permute-start(bf16[64,128]{1,0:T(8,128)(2,1)S(1)} %get-tuple-element.47), channel_id=1, source_target_pairs={{0,8},{1,9},{2,10},{3,11},{4,12},{5,13},{6,14},{7,15},{16,24},{17,... | collective-permute-start | bytes 49160 | tf_op jit(solution)/shard_map/ppermute | solution.py:12

commit v27 on v22

--- a/solution.py
+++ b/solution.py
@@ -65,19 +65,19 @@
         sent_ref[target, rank:] = shift_ref[target * share : (target + 1) * share]
 
 
-def chain(steps_ref, state, values_ref):
+def chain(steps_ref, state, values_ref, swap):
     count, _, rank = steps_ref.shape
     for member in range(count):
-        values_ref[member] = state
-        state = wide(state, steps_ref[member, :rank])
-        state = state + steps_ref[member, rank:].astype(jnp.float32)
+        values_ref[member ^ swap] = state
+        state = wide(state, steps_ref[member ^ swap, :rank])
+        state = state + steps_ref[member ^ swap, rank:].astype(jnp.float32)
     return state
 
 
 def first_half(upper_ref, steps_ref, entry_ref, values_ref, last_ref):
     @pl.when(upper_ref[0] == 0)
     def _():
-        last_ref[...] = chain(steps_ref, entry_ref[...].T, values_ref).astype(jnp.bfloat16)
+        last_ref[...] = chain(steps_ref, entry_ref[...].T, values_ref, 0).astype(jnp.bfloat16)
 
 
 def second_half(upper_ref, steps_ref, before_ref, values_ref, maps_ref):
@@ -89,18 +89,20 @@
 
     @pl.when(upper_ref[0] > 0)
     def _():
-        chain(steps_ref, jnp.zeros(values_ref.shape[1:], jnp.float32), values_ref)
-        state = steps_ref[0, :rank]
+        chain(steps_ref, jnp.zeros(values_ref.shape[1:], jnp.float32), values_ref, 1)
+        rows = lax.broadcasted_iota(jnp.int32, (rank, rank), 0)
+        cols = lax.broadcasted_iota(jnp.int32, (rank, rank), 1)
+        maps_ref[1] = jnp.where(rows == cols, 1.0, 0.0).astype(jnp.bfloat16)
+        state = steps_ref[1, :rank]
         for member in range(1, count):
-            maps_ref[member] = state
+            maps_ref[member ^ 1] = state
             if member + 1 < count:
-                state = product(state, steps_ref[member, :rank]).astype(jnp.bfloat16)
+                state = product(state, steps_ref[member ^ 1, :rank]).astype(jnp.bfloat16)
 
 
 def enter(entered_ref, maps_ref, values_ref, coupled_ref):
     entered = entered_ref[...]
-    coupled_ref[0] = (entered.astype(jnp.float32) + values_ref[0]).astype(jnp.bfloat16)
-    for member in range(1, coupled_ref.shape[0]):
+    for member in range(coupled_ref.shape[0]):
         moved = product(entered, maps_ref[member])
         coupled_ref[member] = (moved + values_ref[member]).astype(jnp.bfloat16)
 
@@ -130,7 +132,8 @@
     here = lax.axis_index("row")
     upper, lower = lax.div(here, lowers), lax.rem(here, lowers)
     share = width // lowers
-    near = [list(range(lowers)), list(range(lowers, groups))]
+    across = [lowers + (place ^ 1) for place in range(lowers)]
+    near = [list(range(lowers)), across]
 
     lefts = [left_factors[0]] + [rotated(left_factors[0], "layer", k) for k in range(1, layers)]
     next_rows = shifted(row_basis, "row", -1)
@@ -164,7 +167,7 @@
         ((share, rank), half),
         scalar=True,
     )
-    entered = shifted(last, "row", lowers)
+    entered = lax.ppermute(last, "row", list(enumerate(across)))
     steps, tile_range, _ = lax.optimization_barrier((steps, tile_range, last))
     gain = product(inverse_diag, tile_range).astype(half)
     values, maps = local(

time: 39.6 us -> 39 us (0.985)
  starting transfers between devices: 7.92 us -> 7.27 us
    ppermute x2 -> x1, starting transfers between devices: 4.63 us -> 1.28 us  [shifted(): lax.ppermute(value, axis, [(source, source + steps) for source in range(l...]
    ppermute x0 -> x1, starting transfers between devices: none -> 2.71 us  [body(): entered = lax.ppermute(last, 'row', list(enumerate(across)))]
    ppermute x2 -> x1, waiting for transfers between devices: 0.53 us -> 0.01 us  [shifted(): lax.ppermute(value, axis, [(source, source + steps) for source in range(l...]
    ppermute x0 -> x1, waiting for transfers between devices: none -> 0.53 us  [body(): entered = lax.ppermute(last, 'row', list(enumerate(across)))]
where the time goes in v27:
time: 39 us; the launch traced here: 38.6 us
  blocking collectives  19.5 us (50%)
  starting transfers between devices  7.27 us (19%)
  matrix products  5.47 us (14%)
  Pallas kernels  3.4 us (9%)
  waiting for transfers between devices  1.9 us (5%)
  local copies, waits for them, and re-layouts  0.97 us (2%)
    all_to_all x2, blocking collectives, exchanged(): lax.all_to_all(blocks, 'row', 0, 0, axis_index_groups=members, tiled=True)  19.5 us
    pallas_call x6, Pallas kernels, local(): pl.pallas_call(kernel, in_specs=specs, out_specs=[VMEM] * len(outputs), o...  3.4 us
    dot_general x2, matrix products, product(): return jnp.dot(a, b, preferred_element_type=jnp.float32)  3.3 us
    ppermute x2, starting transfers between devices, rotated(): lax.ppermute(value, axis, [(source, (source + steps) % count) for source...  3.28 us
    ppermute x1, starting transfers between devices, body(): entered = lax.ppermute(last, 'row', list(enumerate(across)))  2.71 us
    dot_general x1, matrix products, body(): lax.dot_general(gain, coupled, FLIPPED, preferred_element_type=jnp.float32)  1.44 us
    ppermute x2, waiting for transfers between devices, rotated(): lax.ppermute(value, axis, [(source, (source + steps) % count) for source...  1.36 us
    ppermute x1, starting transfers between devices, shifted(): lax.ppermute(value, axis, [(source, source + steps) for source in range(l...  1.28 us
  transfers between devices with their start and end apart: 4, of which 2 were waited for; matrix products, arithmetic and copies ran while one was open for 13% of the time, Pallas kernels for 4%

profile of v27, /device:TPU:0, one launch (start us, length us, event | category | flops | bytes accessed | tf_op | source)
XLA Modules:
  0.0 38.6 jit_solution(13568218341599141111)
XLA Ops:
  0.0 0.0 copy-start
  0.0 3.0 %collective-permute-start.2 = (bf16[1024,128]{1,0:T(8,128)(2,1)}, bf16[1024,128]{1,0:T(8,128)(2,1)}, u32[]{:S(2)}, u32[]{:S(2)}) collective-permute-start(bf16[1024,128]{1,0:T(8,128)(2,1)} %bitcast.19), channel_id=1, source_target_pairs={{0,16},{16,0},{1,17},{17,1},{2,18},{18,2},{3,19},{19,3},{4,20},{20... | collective-permute-start | bytes 786440 | tf_op jit(solution)/shard_map/ppermute | solution.py:17
  3.0 1.3 %collective-permute-start.1 = (bf16[1024,128]{1,0:T(8,128)(2,1)}, bf16[1024,128]{1,0:T(8,128)(2,1)S(1)}, u32[]{:S(2)}, u32[]{:S(2)}) collective-permute-start(bf16[1024,128]{1,0:T(8,128)(2,1)} %param.10), channel_id=1, source_target_pairs={{1,0},{2,1},{3,2},{4,3},{5,4},{6,5},{7,6},{8,7},{9,8},{10,9},{11,1... | collective-permute-start | bytes 786440 | tf_op jit(solution)/shard_map/ppermute | solution.py:12
  4.3 2.5 %convolution_convert_fusion.applied_ref = bf16[1024,512]{1,0:T(8,128)(2,1)S(1)} fusion(bf16[1024,1024]{1,0:T(8,128)(2,1)S(1)} %copy-done, bf16[1024,512]{1,0:T(8,128)(2,1)} %param.12), kind=kOutput, calls=%fused_computation.1 | convolution fusion | flops 1074266112 | bytes 4194304 | tf_op jit(solution)/shard_map/dot_general | solution.py:27
  6.8 0.3 fusion.1.refs_0_
  7.1 0.3 collective-permute-start
  7.4 0.9 %constant_dynamic-slice_fusion.entry_ref = f32[128,64]{1,0:T(8,128)S(1)} fusion(f32[128,512]{1,0:T(8,128)} %param.13, s32[]{:T(128)S(6)} %select_n.3), kind=kLoop, calls=%fused_computation.7 | loop fusion | bytes 65540 | tf_op jit(solution)/shard_map/dynamic_slice | solution.py:149
  8.3 1.4 %collective-permute-done.2.refs_0_ = bf16[1024,128]{1,0:T(8,128)(2,1)} collective-permute-done((bf16[1024,128]{1,0:T(8,128)(2,1)}, bf16[1024,128]{1,0:T(8,128)(2,1)}, u32[]{:S(2)}, u32[]{:S(2)}) %collective-permute-start.2) | collective-permute-done | bytes 262176 | tf_op jit(solution)/shard_map/ppermute | solution.py:17
  9.6 1.0 %shard_map.73.refs_3_ = bf16[1024,128]{1,0:T(8,128)(2,1)S(1)} custom-call(bf16[1024,128]{1,0:T(8,128)(2,1)} %collective-permute-done.2.refs_0_), custom_call_target="tpu_custom_call" | custom-call | tf_op jit(solution)/shard_map/pallas_call | solution.py:112
  10.6 0.0 copy-start.1
  10.6 0.0 collective-permute-done.1.next_ref
  10.6 0.5 %fusion.3.refs_4_ = f32[128,1024]{1,0:T(8,128)S(1)} fusion(bf16[1024,128]{1,0:T(8,128)(2,1)S(1)} %collective-permute-done.1.next_ref, bf16[1024,1024]{1,0:T(8,128)(2,1)S(1)} %copy-done), kind=kOutput, calls=%fused_computation.8 | convolution fusion | flops 268435456 | bytes 2883584 | tf_op jit(solution)/shard_map/dot_general | solution.py:21
  11.1 0.4 %shard_map.74.refs_5_ = bf16[512,128]{1,0:T(8,128)(2,1)S(1)} custom-call(bf16[1024,128]{1,0:T(8,128)(2,1)S(1)} %collective-permute-done.1.next_ref, bf16[1024,512]{1,0:T(8,128)(2,1)S(1)} %convolution_convert_fusion.applied_ref), custom_call_target="tpu_custom_call" | custom-call | tf_op jit(solution)/shard_map/pallas_call | solution.py:112
  11.5 0.0 collective-permute-done.refs_1_
  11.5 0.0 copy-done.1
  11.6 0.7 %shard_map.75 = (bf16[1024,128]{1,0:T(8,128)(2,1)S(1)}, bf16[8,192,128]{2,1,0:T(8,128)(2,1)S(1)}) custom-call(bf16[128,128]{1,0:T(8,128)(2,1)S(1)} %fusion.1.refs_0_, bf16[128,128]{1,0:T(8,128)(2,1)S(1)} %collective-permute-done.refs_1_, bf16[1024,128]{1,0:T(8,128)(2,1)S(1)} %bitcast.20, bf16[1024,128]{1,0:T(8,128)(2,1)S(1)} %shard_map.73.refs_3_, ...), custom_call_target="tpu_custom_call" | custom-call | tf_op jit(solution)/shard_map/pallas_call | solution.py:112
  12.3 11.9 %all_to_all.10.steps_ref = bf16[8,192,128]{2,1,0:T(8,128)(2,1)S(1)} all-to-all(bf16[8,192,128]{2,1,0:T(8,128)(2,1)S(1)} %get-tuple-element.43), channel_id=1, replica_groups={{0,1,2,3,4,5,6,7},{9,8,11,10,13,12,15,14},{16,17,18,19,20,21,22,23},{25..., dimensions={0} | all-to-all | bytes 786432 | tf_op jit(solution)/shard_map/all_to_all | solution.py:123
  24.2 1.1 %shard_map.76 = (f32[8,64,128]{2,1,0:T(8,128)S(1)}, bf16[64,128]{1,0:T(8,128)(2,1)S(1)}) custom-call(s32[1]{0:T(128)} %bitcast.3.upper_ref, bf16[8,192,128]{2,1,0:T(8,128)(2,1)S(1)} %all_to_all.10.steps_ref, f32[128,64]{1,0:T(8,128)S(1)} %constant_dynamic-slice_fusion.entry_ref), custom_call_target="tpu_custom_call" | custom-call | tf_op jit(solution)/shard_map/pallas_call | solution.py:112
  25.3 2.7 %collective-permute-start.3 = (bf16[64,128]{1,0:T(8,128)(2,1)S(1)}, bf16[64,128]{1,0:T(8,128)(2,1)S(1)}, u32[]{:S(2)}, u32[]{:S(2)}) collective-permute-start(bf16[64,128]{1,0:T(8,128)(2,1)S(1)} %get-tuple-element.51), channel_id=1, source_target_pairs={{0,9},{1,8},{2,11},{3,10},{4,13},{5,12},{6,15},{7,14},{16,25},{17,... | collective-permute-start | bytes 49160 | tf_op jit(solution)/shard_map/ppermute | solution.py:170
  28.0 0.8 %fusion = bf16[1024,128]{0,1:T(8,128)(2,1)S(1)} fusion(bf16[1024,128]{1,0:T(8,128)(2,1)S(1)} %get-tuple-element.52, bf16[1024,1024]{1,0:T(8,128)(2,1)S(1)} %copy-done), kind=kOutput, calls=%fused_computation.3 | convolution fusion | flops 268566528 | bytes 2621440 | tf_op jit(solution)/shard_map/dot_general | solution.py:27
  28.9 0.5 %collective-permute-done.3.entered_ref = bf16[64,128]{1,0:T(8,128)(2,1)S(1)} collective-permute-done((bf16[64,128]{1,0:T(8,128)(2,1)S(1)}, bf16[64,128]{1,0:T(8,128)(2,1)S(1)}, u32[]{:S(2)}, u32[]{:S(2)}) %collective-permute-start.3) | collective-permute-done | bytes 16416 | tf_op jit(solution)/shard_map/ppermute | solution.py:170
  29.4 0.2 shard_map.78
  29.6 7.6 %all_to_all.11 = bf16[8,64,128]{2,1,0:T(8,128)(2,1)S(1)} all-to-all(bf16[8,64,128]{2,1,0:T(8,128)(2,1)S(1)} %shard_map.78), channel_id=1, replica_groups={{0,1,2,3,4,5,6,7},{9,8,11,10,13,12,15,14},{16,17,18,19,20,21,22,23},{25..., dimensions={0} | all-to-all | bytes 262144 | tf_op jit(solution)/shard_map/all_to_all | solution.py:123
  37.2 1.4 %subtract_convert_fusion = bf16[1024,512]{1,0:T(8,128)(2,1)} fusion(bf16[1024,512]{1,0:T(8,128)(2,1)S(1)} %convolution_convert_fusion.applied_ref, bf16[1024,128]{0,1:T(8,128)(2,1)S(1)} %fusion, bf16[512,128]{1,0:T(8,128)(2,1)S(1)} %bitcast.21), kind=kOutput, calls=%fused_computation | convolution fusion | flops 135790592 | bytes 2490368 | tf_op jit(solution)/shard_map/dot_general | solution.py:184
  (6 shorter events, 0.1 us)
Async XLA Ops:
  0.0 4.3 %copy-start = (bf16[1024,1024]{1,0:T(8,128)(2,1)S(1)}, bf16[1024,1024]{1,0:T(8,128)(2,1)}, u32[]{:S(2)}) copy-start(bf16[1024,1024]{1,0:T(8,128)(2,1)} %param.11) | copy-start | bytes 6291460
  0.0 6.8 %copy-start.2 = (bf16[1024,128]{1,0:T(8,128)(2,1)S(1)}, bf16[1024,128]{1,0:T(8,128)(2,1)}, u32[]{:S(2)}) copy-start(bf16[1024,128]{1,0:T(8,128)(2,1)} %param.9) | copy-start | bytes 786436
  0.0 6.8 %copy-start.3 = (bf16[1,1024,128]{2,1,0:T(8,128)(2,1)S(1)}, bf16[1,1024,128]{2,1,0:T(8,128)(2,1)}, u32[]{:S(2)}) copy-start(bf16[1,1024,128]{2,1,0:T(8,128)(2,1)} %param.8) | copy-start | bytes 786436
  0.0 9.6 %collective-permute-start.2 = (bf16[1024,128]{1,0:T(8,128)(2,1)}, bf16[1024,128]{1,0:T(8,128)(2,1)}, u32[]{:S(2)}, u32[]{:S(2)}) collective-permute-start(bf16[1024,128]{1,0:T(8,128)(2,1)} %bitcast.19), channel_id=1, source_target_pairs={{0,16},{16,0},{1,17},{17,1},{2,18},{18,2},{3,19},{19,3},{4,20},{20... | collective-permute-start | bytes 786440 | tf_op jit(solution)/shard_map/ppermute | solution.py:17
  3.0 7.6 %collective-permute-start.1 = (bf16[1024,128]{1,0:T(8,128)(2,1)}, bf16[1024,128]{1,0:T(8,128)(2,1)S(1)}, u32[]{:S(2)}, u32[]{:S(2)}) collective-permute-start(bf16[1024,128]{1,0:T(8,128)(2,1)} %param.10), channel_id=1, source_target_pairs={{1,0},{2,1},{3,2},{4,3},{5,4},{6,5},{7,6},{8,7},{9,8},{10,9},{11,1... | collective-permute-start | bytes 786440 | tf_op jit(solution)/shard_map/ppermute | solution.py:12
  7.1 4.4 %collective-permute-start = (bf16[128,128]{1,0:T(8,128)(2,1)S(1)}, bf16[128,128]{1,0:T(8,128)(2,1)S(1)}, u32[]{:S(2)}, u32[]{:S(2)}) collective-permute-start(bf16[128,128]{1,0:T(8,128)(2,1)S(1)} %fusion.1.refs_0_), channel_id=1, source_target_pairs={{0,16},{16,0},{1,17},{17,1},{2,18},{18,2},{3,19},{19,3},{4,20},{20... | collective-permute-start | bytes 98312 | tf_op jit(solution)/shard_map/ppermute | solution.py:17
  10.6 1.0 %copy-start.1 = (bf16[1,1024,128]{2,1,0:T(8,128)(2,1)S(1)}, bf16[1,1024,128]{2,1,0:T(8,128)(2,1)}, u32[]{:S(2)}) copy-start(bf16[1,1024,128]{2,1,0:T(8,128)(2,1)} %param.7) | copy-start | bytes 786436
  25.3 4.1 %collective-permute-start.3 = (bf16[64,128]{1,0:T(8,128)(2,1)S(1)}, bf16[64,128]{1,0:T(8,128)(2,1)S(1)}, u32[]{:S(2)}, u32[]{:S(2)}) collective-permute-start(bf16[64,128]{1,0:T(8,128)(2,1)S(1)} %get-tuple-element.51), channel_id=1, source_target_pairs={{0,9},{1,8},{2,11},{3,10},{4,13},{5,12},{6,15},{7,14},{16,25},{17,... | collective-permute-start | bytes 49160 | tf_op jit(solution)/shard_map/ppermute | solution.py:170

commit v28 on v27

--- a/solution.py
+++ b/solution.py
@@ -29,7 +29,7 @@
 
 SMEM = pl.BlockSpec(memory_space=pltpu.SMEM)
 VMEM = pl.BlockSpec(memory_space=pltpu.VMEM)
-FLIPPED = (((1,), (1,)), ((), ()))
+PARTS = 4
 
 
 def split(value):
@@ -107,6 +107,21 @@
         coupled_ref[member] = (moved + values_ref[member]).astype(jnp.bfloat16)
 
 
+def solve(gain_ref, coupled_ref, applied_ref, result_hbm, result, sent):
+    rows = gain_ref.shape[0] // PARTS
+    coupled = coupled_ref[...].T
+    copies = []
+    for part in range(PARTS):
+        piece = pl.ds(part * rows, rows)
+        moved = product(gain_ref[piece], coupled)
+        applied = applied_ref[piece].astype(jnp.float32)
+        result[piece] = (applied - moved).astype(jnp.bfloat16)
+        copies.append(pltpu.make_async_copy(result.at[piece], result_hbm.at[piece], sent.at[part]))
+        copies[-1].start()
+    for copy in copies:
+        copy.wait()
+
+
 def local(kernel, inputs, *outputs, scalar=False, aliases={}):
     specs = [SMEM] * scalar + [VMEM] * (len(inputs) - scalar)
     return pl.pallas_call(
@@ -181,8 +196,14 @@
     gain, maps = lax.optimization_barrier((gain, maps))
     (coupled,) = local(enter, (entered, maps, values), ((lowers, share, rank), half))
     coupled = exchanged(coupled, near).reshape(width, rank)
-    moved = lax.dot_general(gain, coupled, FLIPPED, preferred_element_type=jnp.float32)
-    return (applied.astype(jnp.float32) - moved).astype(half)
+    return pl.pallas_call(
+        solve,
+        in_specs=[VMEM] * 3,
+        out_specs=pl.BlockSpec(memory_space=pl.ANY),
+        out_shape=jax.ShapeDtypeStruct(applied.shape, half),
+        scratch_shapes=[pltpu.VMEM(applied.shape, half), pltpu.SemaphoreType.DMA((PARTS,))],
+        compiler_params=pltpu.CompilerParams(vmem_limit_bytes=16 * 2**20),
+    )(gain, coupled, applied)
 
 
 def solution(mesh):

time: 39 us -> 38.8 us (level)
  matrix products: 5.47 us -> 3.91 us
  Pallas kernels: 3.4 us -> 4.62 us
    dot_general x1 -> x0, matrix products: 1.44 us -> none  [body(): lax.dot_general(gain, coupled, FLIPPED, preferred_element_type=jnp.float32)]
    pallas_call x0 -> x1, Pallas kernels: none -> 1.23 us  [body(): pl.pallas_call(solve, in_specs=[VMEM] * 3, out_specs=pl.BlockSpec(memory_...]
where the time goes in v28:
time: 38.8 us; the launch traced here: 38.4 us
  blocking collectives  19.5 us (50%)
  starting transfers between devices  7.28 us (19%)
  Pallas kernels  4.62 us (12%)
  matrix products  3.91 us (10%)
  waiting for transfers between devices  2.02 us (5%)
  local copies, waits for them, and re-layouts  0.97 us (2%)
    all_to_all x2, blocking collectives, exchanged(): lax.all_to_all(blocks, 'row', 0, 0, axis_index_groups=members, tiled=True)  19.5 us
    pallas_call x6, Pallas kernels, local(): pl.pallas_call(kernel, in_specs=specs, out_specs=[VMEM] * len(outputs), o...  3.39 us
    ppermute x2, starting transfers between devices, rotated(): lax.ppermute(value, axis, [(source, (source + steps) % count) for source...  3.28 us
    dot_general x2, matrix products, product(): return jnp.dot(a, b, preferred_element_type=jnp.float32)  3.17 us
    ppermute x1, starting transfers between devices, body(): entered = lax.ppermute(last, 'row', list(enumerate(across)))  2.71 us
    ppermute x2, waiting for transfers between devices, rotated(): lax.ppermute(value, axis, [(source, (source + steps) % count) for source...  1.36 us
    ppermute x1, starting transfers between devices, shifted(): lax.ppermute(value, axis, [(source, source + steps) for source in range(l...  1.28 us
    pallas_call x1, Pallas kernels, body(): pl.pallas_call(solve, in_specs=[VMEM] * 3, out_specs=pl.BlockSpec(memory_...  1.23 us
  transfers between devices with their start and end apart: 4, of which 2 were waited for; matrix products, arithmetic and copies ran while one was open for 13% of the time, Pallas kernels for 4%

profile of v28, /device:TPU:0, one launch (start us, length us, event | category | flops | bytes accessed | tf_op | source)
XLA Modules:
  0.0 38.4 jit_solution(12273297671804516081)
XLA Ops:
  0.0 3.0 %collective-permute-start.2 = (bf16[1024,128]{1,0:T(8,128)(2,1)}, bf16[1024,128]{1,0:T(8,128)(2,1)}, u32[]{:S(2)}, u32[]{:S(2)}) collective-permute-start(bf16[1024,128]{1,0:T(8,128)(2,1)} %bitcast.18), channel_id=1, source_target_pairs={{0,16},{16,0},{1,17},{17,1},{2,18},{18,2},{3,19},{19,3},{4,20},{20... | collective-permute-start | bytes 786440 | tf_op jit(solution)/shard_map/ppermute | solution.py:17
  3.0 1.3 %collective-permute-start.1 = (bf16[1024,128]{1,0:T(8,128)(2,1)}, bf16[1024,128]{1,0:T(8,128)(2,1)S(1)}, u32[]{:S(2)}, u32[]{:S(2)}) collective-permute-start(bf16[1024,128]{1,0:T(8,128)(2,1)} %param.10), channel_id=1, source_target_pairs={{1,0},{2,1},{3,2},{4,3},{5,4},{6,5},{7,6},{8,7},{9,8},{10,9},{11,1... | collective-permute-start | bytes 786440 | tf_op jit(solution)/shard_map/ppermute | solution.py:12
  4.3 2.5 %convolution_convert_fusion.applied_ref = bf16[1024,512]{1,0:T(8,128)(2,1)S(1)} fusion(bf16[1024,1024]{1,0:T(8,128)(2,1)S(1)} %copy-done, bf16[1024,512]{1,0:T(8,128)(2,1)} %param.12), kind=kOutput, calls=%fused_computation | convolution fusion | flops 1074266112 | bytes 4194304 | tf_op jit(solution)/shard_map/dot_general | solution.py:27
  6.8 0.0 copy-done.2
  6.8 0.3 fusion.1.refs_0_
  7.1 0.3 collective-permute-start
  7.4 0.9 %constant_dynamic-slice_fusion.entry_ref = f32[128,64]{1,0:T(8,128)S(1)} fusion(f32[128,512]{1,0:T(8,128)} %param.13, s32[]{:T(128)S(6)} %select_n.3), kind=kLoop, calls=%fused_computation.6 | loop fusion | bytes 65540 | tf_op jit(solution)/shard_map/dynamic_slice | solution.py:164
  8.3 1.4 %collective-permute-done.2.refs_0_ = bf16[1024,128]{1,0:T(8,128)(2,1)} collective-permute-done((bf16[1024,128]{1,0:T(8,128)(2,1)}, bf16[1024,128]{1,0:T(8,128)(2,1)}, u32[]{:S(2)}, u32[]{:S(2)}) %collective-permute-start.2) | collective-permute-done | bytes 262176 | tf_op jit(solution)/shard_map/ppermute | solution.py:17
  9.6 1.0 %shard_map.73.refs_3_ = bf16[1024,128]{1,0:T(8,128)(2,1)S(1)} custom-call(bf16[1024,128]{1,0:T(8,128)(2,1)} %collective-permute-done.2.refs_0_), custom_call_target="tpu_custom_call" | custom-call | tf_op jit(solution)/shard_map/pallas_call | solution.py:127
  10.6 0.0 copy-start.1
  10.6 0.0 collective-permute-done.1.next_ref
  10.6 0.5 %fusion.3.refs_4_ = f32[128,1024]{1,0:T(8,128)S(1)} fusion(bf16[1024,128]{1,0:T(8,128)(2,1)S(1)} %collective-permute-done.1.next_ref, bf16[1024,1024]{1,0:T(8,128)(2,1)S(1)} %copy-done), kind=kOutput, calls=%fused_computation.7 | convolution fusion | flops 268435456 | bytes 2883584 | tf_op jit(solution)/shard_map/dot_general | solution.py:21
  11.1 0.4 %shard_map.74.refs_5_ = bf16[512,128]{1,0:T(8,128)(2,1)S(1)} custom-call(bf16[1024,128]{1,0:T(8,128)(2,1)S(1)} %collective-permute-done.1.next_ref, bf16[1024,512]{1,0:T(8,128)(2,1)S(1)} %convolution_convert_fusion.applied_ref), custom_call_target="tpu_custom_call" | custom-call | tf_op jit(solution)/shard_map/pallas_call | solution.py:127
  11.5 0.0 collective-permute-done.refs_1_
  11.5 0.0 copy-done.1
  11.6 0.7 %shard_map.75 = (bf16[1024,128]{1,0:T(8,128)(2,1)S(1)}, bf16[8,192,128]{2,1,0:T(8,128)(2,1)S(1)}) custom-call(bf16[128,128]{1,0:T(8,128)(2,1)S(1)} %fusion.1.refs_0_, bf16[128,128]{1,0:T(8,128)(2,1)S(1)} %collective-permute-done.refs_1_, bf16[1024,128]{1,0:T(8,128)(2,1)S(1)} %bitcast.19, bf16[1024,128]{1,0:T(8,128)(2,1)S(1)} %shard_map.73.refs_3_, ...), custom_call_target="tpu_custom_call" | custom-call | tf_op jit(solution)/shard_map/pallas_call | solution.py:127
  12.3 11.9 %all_to_all.10.steps_ref = bf16[8,192,128]{2,1,0:T(8,128)(2,1)S(1)} all-to-all(bf16[8,192,128]{2,1,0:T(8,128)(2,1)S(1)} %get-tuple-element.43), channel_id=1, replica_groups={{0,1,2,3,4,5,6,7},{9,8,11,10,13,12,15,14},{16,17,18,19,20,21,22,23},{25..., dimensions={0} | all-to-all | bytes 786432 | tf_op jit(solution)/shard_map/all_to_all | solution.py:138
  24.2 1.1 %shard_map.76 = (f32[8,64,128]{2,1,0:T(8,128)S(1)}, bf16[64,128]{1,0:T(8,128)(2,1)S(1)}) custom-call(s32[1]{0:T(128)} %bitcast.3.upper_ref, bf16[8,192,128]{2,1,0:T(8,128)(2,1)S(1)} %all_to_all.10.steps_ref, f32[128,64]{1,0:T(8,128)S(1)} %constant_dynamic-slice_fusion.entry_ref), custom_call_target="tpu_custom_call" | custom-call | tf_op jit(solution)/shard_map/pallas_call | solution.py:127
  25.3 2.7 %collective-permute-start.3 = (bf16[64,128]{1,0:T(8,128)(2,1)S(1)}, bf16[64,128]{1,0:T(8,128)(2,1)S(1)}, u32[]{:S(2)}, u32[]{:S(2)}) collective-permute-start(bf16[64,128]{1,0:T(8,128)(2,1)S(1)} %get-tuple-element.51), channel_id=1, source_target_pairs={{0,9},{1,8},{2,11},{3,10},{4,13},{5,12},{6,15},{7,14},{16,25},{17,... | collective-permute-start | bytes 49160 | tf_op jit(solution)/shard_map/ppermute | solution.py:185
  28.0 0.7 %fusion.gain_ref = bf16[1024,128]{1,0:T(8,128)(2,1)S(1)} fusion(bf16[1024,1024]{1,0:T(8,128)(2,1)S(1)} %copy-done, bf16[1024,128]{1,0:T(8,128)(2,1)S(1)} %get-tuple-element.52), kind=kOutput, calls=%fused_computation.2 | convolution fusion | flops 268566528 | bytes 2621440 | tf_op jit(solution)/shard_map/dot_general | solution.py:27
  28.8 0.7 %collective-permute-done.3.entered_ref = bf16[64,128]{1,0:T(8,128)(2,1)S(1)} collective-permute-done((bf16[64,128]{1,0:T(8,128)(2,1)S(1)}, bf16[64,128]{1,0:T(8,128)(2,1)S(1)}, u32[]{:S(2)}, u32[]{:S(2)}) %collective-permute-start.3) | collective-permute-done | bytes 16416 | tf_op jit(solution)/shard_map/ppermute | solution.py:185
  29.4 0.2 shard_map.78
  29.6 7.6 %all_to_all.11 = bf16[8,64,128]{2,1,0:T(8,128)(2,1)S(1)} all-to-all(bf16[8,64,128]{2,1,0:T(8,128)(2,1)S(1)} %shard_map.78), channel_id=1, replica_groups={{0,1,2,3,4,5,6,7},{9,8,11,10,13,12,15,14},{16,17,18,19,20,21,22,23},{25..., dimensions={0} | all-to-all | bytes 262144 | tf_op jit(solution)/shard_map/all_to_all | solution.py:138
  37.2 1.2 %shard_map.79 = bf16[1024,512]{1,0:T(8,128)(2,1)} custom-call(bf16[1024,128]{1,0:T(8,128)(2,1)S(1)} %fusion.gain_ref, bf16[512,128]{1,0:T(8,128)(2,1)S(1)} %bitcast.17, bf16[1024,512]{1,0:T(8,128)(2,1)S(1)} %convolution_convert_fusion.applied_ref), custom_call_target="tpu_custom_call" | custom-call | tf_op jit(solution)/shard_map/pallas_call | solution.py:199
  (6 shorter events, 0.1 us)
Async XLA Ops:
  0.0 4.3 %copy-start = (bf16[1024,1024]{1,0:T(8,128)(2,1)S(1)}, bf16[1024,1024]{1,0:T(8,128)(2,1)}, u32[]{:S(2)}) copy-start(bf16[1024,1024]{1,0:T(8,128)(2,1)} %param.11) | copy-start | bytes 6291460
  0.0 6.8 %copy-start.2 = (bf16[1024,128]{1,0:T(8,128)(2,1)S(1)}, bf16[1024,128]{1,0:T(8,128)(2,1)}, u32[]{:S(2)}) copy-start(bf16[1024,128]{1,0:T(8,128)(2,1)} %param.9) | copy-start | bytes 786436
  0.0 6.8 %copy-start.3 = (bf16[1,1024,128]{2,1,0:T(8,128)(2,1)S(1)}, bf16[1,1024,128]{2,1,0:T(8,128)(2,1)}, u32[]{:S(2)}) copy-start(bf16[1,1024,128]{2,1,0:T(8,128)(2,1)} %param.8) | copy-start | bytes 786436
  0.0 9.6 %collective-permute-start.2 = (bf16[1024,128]{1,0:T(8,128)(2,1)}, bf16[1024,128]{1,0:T(8,128)(2,1)}, u32[]{:S(2)}, u32[]{:S(2)}) collective-permute-start(bf16[1024,128]{1,0:T(8,128)(2,1)} %bitcast.18), channel_id=1, source_target_pairs={{0,16},{16,0},{1,17},{17,1},{2,18},{18,2},{3,19},{19,3},{4,20},{20... | collective-permute-start | bytes 786440 | tf_op jit(solution)/shard_map/ppermute | solution.py:17
  3.0 7.6 %collective-permute-start.1 = (bf16[1024,128]{1,0:T(8,128)(2,1)}, bf16[1024,128]{1,0:T(8,128)(2,1)S(1)}, u32[]{:S(2)}, u32[]{:S(2)}) collective-permute-start(bf16[1024,128]{1,0:T(8,128)(2,1)} %param.10), channel_id=1, source_target_pairs={{1,0},{2,1},{3,2},{4,3},{5,4},{6,5},{7,6},{8,7},{9,8},{10,9},{11,1... | collective-permute-start | bytes 786440 | tf_op jit(solution)/shard_map/ppermute | solution.py:12
  7.1 4.4 %collective-permute-start = (bf16[128,128]{1,0:T(8,128)(2,1)S(1)}, bf16[128,128]{1,0:T(8,128)(2,1)S(1)}, u32[]{:S(2)}, u32[]{:S(2)}) collective-permute-start(bf16[128,128]{1,0:T(8,128)(2,1)S(1)} %fusion.1.refs_0_), channel_id=1, source_target_pairs={{0,16},{16,0},{1,17},{17,1},{2,18},{18,2},{3,19},{19,3},{4,20},{20... | collective-permute-start | bytes 98312 | tf_op jit(solution)/shard_map/ppermute | solution.py:17
  10.6 1.0 %copy-start.1 = (bf16[1,1024,128]{2,1,0:T(8,128)(2,1)S(1)}, bf16[1,1024,128]{2,1,0:T(8,128)(2,1)}, u32[]{:S(2)}) copy-start(bf16[1,1024,128]{2,1,0:T(8,128)(2,1)} %param.7) | copy-start | bytes 786436
  25.3 4.1 %collective-permute-start.3 = (bf16[64,128]{1,0:T(8,128)(2,1)S(1)}, bf16[64,128]{1,0:T(8,128)(2,1)S(1)}, u32[]{:S(2)}, u32[]{:S(2)}) collective-permute-start(bf16[64,128]{1,0:T(8,128)(2,1)S(1)} %get-tuple-element.51), channel_id=1, source_target_pairs={{0,9},{1,8},{2,11},{3,10},{4,13},{5,12},{6,15},{7,14},{16,25},{17,... | collective-permute-start | bytes 49160 | tf_op jit(solution)/shard_map/ppermute | solution.py:185

commit v29 on v28

--- a/solution.py
+++ b/solution.py
@@ -29,7 +29,7 @@
 
 SMEM = pl.BlockSpec(memory_space=pltpu.SMEM)
 VMEM = pl.BlockSpec(memory_space=pltpu.VMEM)
-PARTS = 4
+PARTS = 8
 
 
 def split(value):
@@ -42,7 +42,9 @@
     return both[: value.shape[0]] + both[value.shape[0] :]
 
 
-def make_shift(next_ref, applied_ref, shift_ref):
+def weigh(left_ref, others_ref, weights_ref, next_ref, applied_ref, high_ref, low_ref, shift_ref):
+    lefts = jnp.concatenate([left_ref[...], others_ref[...]], axis=1)
+    high_ref[...], low_ref[...] = split(wide(weights_ref[...], lefts))
     shift_ref[...] = project(next_ref[...], applied_ref[...]).T.astype(jnp.bfloat16)
 
 
@@ -54,15 +56,16 @@
 
 def make_maps(layers, *refs):
     cores = jnp.concatenate([ref[...] for ref in refs[:layers]], axis=0)
-    left_ref, others_ref, weights_ref, shift_ref, range_ref, sent_ref = refs[layers:]
-    lefts = jnp.concatenate([left_ref[...], others_ref[...]], axis=1)
-    range_ref[...] = (-product(lefts, cores)).astype(jnp.bfloat16)
-    map_t = wide(wide(weights_ref[...], lefts), cores).T.astype(jnp.bfloat16)
-    rank = map_t.shape[0]
+    left_ref, others_ref, high_ref, low_ref, shift_ref, range_ref, sent_ref = refs[layers:]
+    both = product(jnp.concatenate([high_ref[...], low_ref[...]]), cores)
+    rank = both.shape[1]
+    map_t = (both[:rank] + both[rank:]).T.astype(jnp.bfloat16)
     share = sent_ref.shape[1] - rank
     for target in range(sent_ref.shape[0]):
         sent_ref[target, :rank] = map_t
         sent_ref[target, rank:] = shift_ref[target * share : (target + 1) * share]
+    lefts = jnp.concatenate([left_ref[...], others_ref[...]], axis=1)
+    range_ref[...] = (-product(lefts, cores)).astype(jnp.bfloat16)
 
 
 def chain(steps_ref, state, values_ref, swap):
@@ -159,16 +162,20 @@
 
     (others,) = local(lay, lefts[1:], ((order, (layers - 1) * rank), half))
     next_rows, others = lax.optimization_barrier((next_rows, others))
-    (shift_t,) = local(make_shift, (next_rows, applied), ((width, rank), half))
     weights = project(next_rows, inverse_diag)
+    high, low, shift_t = local(
+        weigh,
+        (lefts[0], others, weights, next_rows, applied),
+        ((rank, layers * rank), half),
+        ((rank, layers * rank), half),
+        ((width, rank), half),
+    )
     entry = lax.dynamic_slice_in_dim(incoming, lower * share, share, 1)
     place = upper.reshape(1)
-    others, shift_t, weights, entry, place = lax.optimization_barrier(
-        (others, shift_t, weights, entry, place)
-    )
+    high, entry, place = lax.optimization_barrier((high, entry, place))
     tile_range, sent = local(
         lambda *refs: make_maps(layers, *refs),
-        (*cores, lefts[0], others, weights, shift_t),
+        (*cores, lefts[0], others, high, low, shift_t),
         ((order, rank), half),
         ((lowers, rank + share, rank), half),
     )

time: 38.8 us -> 40.4 us (1.041)
  matrix products: 3.91 us -> 4.86 us
  Pallas kernels: 4.62 us -> 5.31 us
    dot_general x2, matrix products: 0.74 us -> 1.69 us  [project(): lax.dot_general(basis, vectors, (((0,), (0,)), ((), ())), preferred_eleme...]
    pallas_call x6, Pallas kernels: 3.39 us -> 4.08 us  [local(): pl.pallas_call(kernel, in_specs=specs, out_specs=[VMEM] * len(outputs), o...]
  transfers between devices with their start and end apart: 4 -> 4, of which waited for: 2 -> 2; matrix products, arithmetic and copies ran while one was open for 13% -> 14% of each run, Pallas kernels for 4% -> 6%
where the time goes in v29:
time: 40.4 us; the launch traced here: 40.1 us
  blocking collectives  19.7 us (49%)
  starting transfers between devices  7.16 us (18%)
  Pallas kernels  5.31 us (13%)
  matrix products  4.86 us (12%)
  waiting for transfers between devices  2 us (5%)
  local copies, waits for them, and re-layouts  0.93 us (2%)
    all_to_all x2, blocking collectives, exchanged(): lax.all_to_all(blocks, 'row', 0, 0, axis_index_groups=members, tiled=True)  19.7 us
    pallas_call x6, Pallas kernels, local(): pl.pallas_call(kernel, in_specs=specs, out_specs=[VMEM] * len(outputs), o...  4.08 us
    ppermute x2, starting transfers between devices, rotated(): lax.ppermute(value, axis, [(source, (source + steps) % count) for source...  3.29 us
    dot_general x2, matrix products, product(): return jnp.dot(a, b, preferred_element_type=jnp.float32)  3.17 us
    ppermute x1, starting transfers between devices, body(): entered = lax.ppermute(last, 'row', list(enumerate(across)))  2.59 us
    dot_general x2, matrix products, project(): lax.dot_general(basis, vectors, (((0,), (0,)), ((), ())), preferred_eleme...  1.69 us
    ppermute x2, waiting for transfers between devices, rotated(): lax.ppermute(value, axis, [(source, (source + steps) % count) for source...  1.34 us
    ppermute x1, starting transfers between devices, shifted(): lax.ppermute(value, axis, [(source, source + steps) for source in range(l...  1.28 us
  transfers between devices with their start and end apart: 4, of which 2 were waited for; matrix products, arithmetic and copies ran while one was open for 14% of the time, Pallas kernels for 6%

profile of v29, /device:TPU:0, one launch (start us, length us, event | category | flops | bytes accessed | tf_op | source)
XLA Modules:
  0.0 40.1 jit_solution(4376025463627945261)
XLA Ops:
  0.0 0.0 copy-start
  0.0 3.0 %collective-permute-start.2 = (bf16[1024,128]{1,0:T(8,128)(2,1)}, bf16[1024,128]{1,0:T(8,128)(2,1)}, u32[]{:S(2)}, u32[]{:S(2)}) collective-permute-start(bf16[1024,128]{1,0:T(8,128)(2,1)} %bitcast.17), channel_id=1, source_target_pairs={{0,16},{16,0},{1,17},{17,1},{2,18},{18,2},{3,19},{19,3},{4,20},{20... | collective-permute-start | bytes 786440 | tf_op jit(solution)/shard_map/ppermute | solution.py:17
  3.0 1.3 %collective-permute-start.1 = (bf16[1024,128]{1,0:T(8,128)(2,1)}, bf16[1024,128]{1,0:T(8,128)(2,1)}, u32[]{:S(2)}, u32[]{:S(2)}) collective-permute-start(bf16[1024,128]{1,0:T(8,128)(2,1)} %param.10), channel_id=1, source_target_pairs={{1,0},{2,1},{3,2},{4,3},{5,4},{6,5},{7,6},{8,7},{9,8},{10,9},{11,1... | collective-permute-start | bytes 786440 | tf_op jit(solution)/shard_map/ppermute | solution.py:12
  4.3 0.0 copy-done
  4.3 2.5 %convolution_convert_fusion.applied_ref = bf16[1024,512]{1,0:T(8,128)(2,1)S(1)} fusion(bf16[1024,1024]{1,0:T(8,128)(2,1)S(1)} %copy-done, bf16[1024,512]{1,0:T(8,128)(2,1)} %param.12), kind=kOutput, calls=%fused_computation | convolution fusion | flops 1074266112 | bytes 4194304 | tf_op jit(solution)/shard_map/dot_general | solution.py:27
  6.8 0.0 copy-start.1
  6.8 0.3 fusion.1.refs_0_
  7.1 0.3 collective-permute-start
  7.4 0.9 %constant_dynamic-slice_fusion.entry_ref = f32[128,64]{1,0:T(8,128)S(1)} fusion(f32[128,512]{1,0:T(8,128)} %param.13, s32[]{:T(128)S(6)} %select_n.3), kind=kLoop, calls=%fused_computation.6 | loop fusion | bytes 65540 | tf_op jit(solution)/shard_map/dynamic_slice | solution.py:173
  8.3 1.3 %collective-permute-done.2.refs_0_ = bf16[1024,128]{1,0:T(8,128)(2,1)} collective-permute-done((bf16[1024,128]{1,0:T(8,128)(2,1)}, bf16[1024,128]{1,0:T(8,128)(2,1)}, u32[]{:S(2)}, u32[]{:S(2)}) %collective-permute-start.2) | collective-permute-done | bytes 262176 | tf_op jit(solution)/shard_map/ppermute | solution.py:17
  9.6 1.0 %shard_map.73.others_ref.refs_3_ = bf16[1024,128]{1,0:T(8,128)(2,1)S(1)} custom-call(bf16[1024,128]{1,0:T(8,128)(2,1)} %collective-permute-done.2.refs_0_), custom_call_target="tpu_custom_call" | custom-call | tf_op jit(solution)/shard_map/pallas_call | solution.py:130
  10.6 0.0 collective-permute-done.1.next_ref
  10.6 1.4 %fusion.3.weights_ref = f32[128,1024]{1,0:T(8,128)S(1)} fusion(bf16[1024,128]{1,0:T(8,128)(2,1)} %collective-permute-done.1.next_ref, bf16[1024,1024]{1,0:T(8,128)(2,1)S(1)} %copy-done), kind=kOutput, calls=%fused_computation.7 | convolution fusion | flops 268435456 | bytes 2883584 | tf_op jit(solution)/shard_map/dot_general | solution.py:21
  12.1 1.5 %shard_map.74 = (bf16[128,256]{1,0:T(8,128)(2,1)S(1)}, bf16[128,256]{1,0:T(8,128)(2,1)S(1)}, bf16[512,128]{1,0:T(8,128)(2,1)S(1)}) custom-call(bf16[1024,128]{1,0:T(8,128)(2,1)S(1)} %bitcast.18, bf16[1024,128]{1,0:T(8,128)(2,1)S(1)} %shard_map.73.others_ref.refs_3_, f32[128,1024]{1,0:T(8,128)S(1)} %fusion.3.weights_ref, ...), custom_call_target="tpu_custom_call" | custom-call | tf_op jit(solution)/shard_map/pallas_call | solution.py:130
  13.5 0.0 collective-permute-done.refs_1_
  13.5 0.3 shard_map.75
  13.9 12.1 %all_to_all.10.steps_ref = bf16[8,192,128]{2,1,0:T(8,128)(2,1)S(1)} all-to-all(bf16[8,192,128]{2,1,0:T(8,128)(2,1)S(1)} %get-tuple-element.45), channel_id=1, replica_groups={{0,1,2,3,4,5,6,7},{9,8,11,10,13,12,15,14},{16,17,18,19,20,21,22,23},{25..., dimensions={0} | all-to-all | bytes 786432 | tf_op jit(solution)/shard_map/all_to_all | solution.py:141
  26.0 1.1 %shard_map.76 = (f32[8,64,128]{2,1,0:T(8,128)S(1)}, bf16[64,128]{1,0:T(8,128)(2,1)S(1)}) custom-call(s32[1]{0:T(128)} %bitcast.3.upper_ref, bf16[8,192,128]{2,1,0:T(8,128)(2,1)S(1)} %all_to_all.10.steps_ref, f32[128,64]{1,0:T(8,128)S(1)} %constant_dynamic-slice_fusion.entry_ref), custom_call_target="tpu_custom_call" | custom-call | tf_op jit(solution)/shard_map/pallas_call | solution.py:130
  27.0 2.6 %collective-permute-start.3 = (bf16[64,128]{1,0:T(8,128)(2,1)S(1)}, bf16[64,128]{1,0:T(8,128)(2,1)S(1)}, u32[]{:S(2)}, u32[]{:S(2)}) collective-permute-start(bf16[64,128]{1,0:T(8,128)(2,1)S(1)} %get-tuple-element.53), channel_id=1, source_target_pairs={{0,9},{1,8},{2,11},{3,10},{4,13},{5,12},{6,15},{7,14},{16,25},{17,... | collective-permute-start | bytes 49160 | tf_op jit(solution)/shard_map/ppermute | solution.py:192
  29.6 0.7 %fusion.gain_ref = bf16[1024,128]{1,0:T(8,128)(2,1)S(1)} fusion(bf16[1024,1024]{1,0:T(8,128)(2,1)S(1)} %copy-done, bf16[1024,128]{1,0:T(8,128)(2,1)S(1)} %get-tuple-element.54), kind=kOutput, calls=%fused_computation.2 | convolution fusion | flops 268566528 | bytes 2621440 | tf_op jit(solution)/shard_map/dot_general | solution.py:27
  30.4 0.7 %collective-permute-done.3.entered_ref = bf16[64,128]{1,0:T(8,128)(2,1)S(1)} collective-permute-done((bf16[64,128]{1,0:T(8,128)(2,1)S(1)}, bf16[64,128]{1,0:T(8,128)(2,1)S(1)}, u32[]{:S(2)}, u32[]{:S(2)}) %collective-permute-start.3) | collective-permute-done | bytes 16416 | tf_op jit(solution)/shard_map/ppermute | solution.py:192
  31.1 0.2 shard_map.78
  31.3 7.6 %all_to_all.11 = bf16[8,64,128]{2,1,0:T(8,128)(2,1)S(1)} all-to-all(bf16[8,64,128]{2,1,0:T(8,128)(2,1)S(1)} %shard_map.78), channel_id=1, replica_groups={{0,1,2,3,4,5,6,7},{9,8,11,10,13,12,15,14},{16,17,18,19,20,21,22,23},{25..., dimensions={0} | all-to-all | bytes 262144 | tf_op jit(solution)/shard_map/all_to_all | solution.py:141
  38.8 1.2 %shard_map.79 = bf16[1024,512]{1,0:T(8,128)(2,1)} custom-call(bf16[1024,128]{1,0:T(8,128)(2,1)S(1)} %fusion.gain_ref, bf16[512,128]{1,0:T(8,128)(2,1)S(1)} %bitcast.20, bf16[1024,512]{1,0:T(8,128)(2,1)S(1)} %convolution_convert_fusion.applied_ref), custom_call_target="tpu_custom_call" | custom-call | tf_op jit(solution)/shard_map/pallas_call | solution.py:206
  (6 shorter events, 0.1 us)
Async XLA Ops:
  0.0 4.3 %copy-start = (bf16[1024,1024]{1,0:T(8,128)(2,1)S(1)}, bf16[1024,1024]{1,0:T(8,128)(2,1)}, u32[]{:S(2)}) copy-start(bf16[1024,1024]{1,0:T(8,128)(2,1)} %param.11) | copy-start | bytes 6291460
  0.0 6.8 %copy-start.2 = (bf16[1024,128]{1,0:T(8,128)(2,1)S(1)}, bf16[1024,128]{1,0:T(8,128)(2,1)}, u32[]{:S(2)}) copy-start(bf16[1024,128]{1,0:T(8,128)(2,1)} %param.9) | copy-start | bytes 786436
  0.0 6.8 %copy-start.3 = (bf16[1,1024,128]{2,1,0:T(8,128)(2,1)S(1)}, bf16[1,1024,128]{2,1,0:T(8,128)(2,1)}, u32[]{:S(2)}) copy-start(bf16[1,1024,128]{2,1,0:T(8,128)(2,1)} %param.8) | copy-start | bytes 786436
  0.0 9.6 %collective-permute-start.2 = (bf16[1024,128]{1,0:T(8,128)(2,1)}, bf16[1024,128]{1,0:T(8,128)(2,1)}, u32[]{:S(2)}, u32[]{:S(2)}) collective-permute-start(bf16[1024,128]{1,0:T(8,128)(2,1)} %bitcast.17), channel_id=1, source_target_pairs={{0,16},{16,0},{1,17},{17,1},{2,18},{18,2},{3,19},{19,3},{4,20},{20... | collective-permute-start | bytes 786440 | tf_op jit(solution)/shard_map/ppermute | solution.py:17
  3.0 7.6 %collective-permute-start.1 = (bf16[1024,128]{1,0:T(8,128)(2,1)}, bf16[1024,128]{1,0:T(8,128)(2,1)}, u32[]{:S(2)}, u32[]{:S(2)}) collective-permute-start(bf16[1024,128]{1,0:T(8,128)(2,1)} %param.10), channel_id=1, source_target_pairs={{1,0},{2,1},{3,2},{4,3},{5,4},{6,5},{7,6},{8,7},{9,8},{10,9},{11,1... | collective-permute-start | bytes 786440 | tf_op jit(solution)/shard_map/ppermute | solution.py:12
  6.8 5.2 %copy-start.1 = (bf16[1,1024,128]{2,1,0:T(8,128)(2,1)S(1)}, bf16[1,1024,128]{2,1,0:T(8,128)(2,1)}, u32[]{:S(2)}) copy-start(bf16[1,1024,128]{2,1,0:T(8,128)(2,1)} %param.7) | copy-start | bytes 786436
  7.1 6.4 %collective-permute-start = (bf16[128,128]{1,0:T(8,128)(2,1)S(1)}, bf16[128,128]{1,0:T(8,128)(2,1)S(1)}, u32[]{:S(2)}, u32[]{:S(2)}) collective-permute-start(bf16[128,128]{1,0:T(8,128)(2,1)S(1)} %fusion.1.refs_0_), channel_id=1, source_target_pairs={{0,16},{16,0},{1,17},{17,1},{2,18},{18,2},{3,19},{19,3},{4,20},{20... | collective-permute-start | bytes 98312 | tf_op jit(solution)/shard_map/ppermute | solution.py:17
  27.0 4.0 %collective-permute-start.3 = (bf16[64,128]{1,0:T(8,128)(2,1)S(1)}, bf16[64,128]{1,0:T(8,128)(2,1)S(1)}, u32[]{:S(2)}, u32[]{:S(2)}) collective-permute-start(bf16[64,128]{1,0:T(8,128)(2,1)S(1)} %get-tuple-element.53), channel_id=1, source_target_pairs={{0,9},{1,8},{2,11},{3,10},{4,13},{5,12},{6,15},{7,14},{16,25},{17,... | collective-permute-start | bytes 49160 | tf_op jit(solution)/shard_map/ppermute | solution.py:192

commit v30 on v28

--- a/solution.py
+++ b/solution.py
@@ -42,10 +42,6 @@
     return both[: value.shape[0]] + both[value.shape[0] :]
 
 
-def make_shift(next_ref, applied_ref, shift_ref):
-    shift_ref[...] = project(next_ref[...], applied_ref[...]).T.astype(jnp.bfloat16)
-
-
 def lay(*refs):
     rank = refs[0].shape[1]
     for layer, ref in enumerate(refs[:-1]):
@@ -54,15 +50,22 @@
 
 def make_maps(layers, *refs):
     cores = jnp.concatenate([ref[...] for ref in refs[:layers]], axis=0)
-    left_ref, others_ref, weights_ref, shift_ref, range_ref, sent_ref = refs[layers:]
+    left_ref, others_ref, weights_ref, next_ref, applied_ref, sent_ref = refs[layers:]
     lefts = jnp.concatenate([left_ref[...], others_ref[...]], axis=1)
-    range_ref[...] = (-product(lefts, cores)).astype(jnp.bfloat16)
+    shift_t = project(next_ref[...], applied_ref[...]).T.astype(jnp.bfloat16)
     map_t = wide(wide(weights_ref[...], lefts), cores).T.astype(jnp.bfloat16)
     rank = map_t.shape[0]
     share = sent_ref.shape[1] - rank
     for target in range(sent_ref.shape[0]):
         sent_ref[target, :rank] = map_t
-        sent_ref[target, rank:] = shift_ref[target * share : (target + 1) * share]
+        sent_ref[target, rank:] = shift_t[target * share : (target + 1) * share]
+
+
+def make_range(layers, *refs):
+    cores = jnp.concatenate([ref[...] for ref in refs[:layers]], axis=0)
+    left_ref, others_ref, range_ref = refs[layers:]
+    lefts = jnp.concatenate([left_ref[...], others_ref[...]], axis=1)
+    range_ref[...] = (-product(lefts, cores)).astype(jnp.bfloat16)
 
 
 def chain(steps_ref, state, values_ref, swap):
@@ -159,22 +162,18 @@
 
     (others,) = local(lay, lefts[1:], ((order, (layers - 1) * rank), half))
     next_rows, others = lax.optimization_barrier((next_rows, others))
-    (shift_t,) = local(make_shift, (next_rows, applied), ((width, rank), half))
     weights = project(next_rows, inverse_diag)
     entry = lax.dynamic_slice_in_dim(incoming, lower * share, share, 1)
     place = upper.reshape(1)
-    others, shift_t, weights, entry, place = lax.optimization_barrier(
-        (others, shift_t, weights, entry, place)
-    )
-    tile_range, sent = local(
+    others, weights, entry, place = lax.optimization_barrier((others, weights, entry, place))
+    (sent,) = local(
         lambda *refs: make_maps(layers, *refs),
-        (*cores, lefts[0], others, weights, shift_t),
-        ((order, rank), half),
+        (*cores, lefts[0], others, weights, next_rows, applied),
         ((lowers, rank + share, rank), half),
     )
-    sent, tile_range, entry, place = lax.optimization_barrier((sent, tile_range, entry, place))
+    sent, others, entry, place = lax.optimization_barrier((sent, others, entry, place))
     steps = exchanged(sent, near)
-    steps, tile_range, entry, place = lax.optimization_barrier((steps, tile_range, entry, place))
+    steps, others, entry, place = lax.optimization_barrier((steps, others, entry, place))
     values, last = local(
         first_half,
         (place, steps, entry),
@@ -183,7 +182,12 @@
         scalar=True,
     )
     entered = lax.ppermute(last, "row", list(enumerate(across)))
-    steps, tile_range, _ = lax.optimization_barrier((steps, tile_range, last))
+    steps, others, _ = lax.optimization_barrier((steps, others, last))
+    (tile_range,) = local(
+        lambda *refs: make_range(layers, *refs),
+        (*cores, lefts[0], others),
+        ((order, rank), half),
+    )
     gain = product(inverse_diag, tile_range).astype(half)
     values, maps = local(
         second_half,

time: 38.8 us -> 40.3 us (1.039)
  matrix products: 3.91 us -> 4.86 us
  Pallas kernels: 4.62 us -> 5.47 us
    dot_general x2, matrix products: 0.74 us -> 1.69 us  [project(): lax.dot_general(basis, vectors, (((0,), (0,)), ((), ())), preferred_eleme...]
    pallas_call x6, Pallas kernels: 3.39 us -> 4.24 us  [local(): pl.pallas_call(kernel, in_specs=specs, out_specs=[VMEM] * len(outputs), o...]
  transfers between devices with their start and end apart: 4 -> 4, of which waited for: 2 -> 2; matrix products, arithmetic and copies ran while one was open for 13% -> 14% of each run, Pallas kernels for 4% -> 3%
where the time goes in v30:
time: 40.3 us; the launch traced here: 39.9 us
  blocking collectives  19.7 us (49%)
  starting transfers between devices  7.16 us (18%)
  Pallas kernels  5.47 us (14%)
  matrix products  4.86 us (12%)
  waiting for transfers between devices  1.71 us (4%)
  local copies, waits for them, and re-layouts  0.93 us (2%)
    all_to_all x2, blocking collectives, exchanged(): lax.all_to_all(blocks, 'row', 0, 0, axis_index_groups=members, tiled=True)  19.7 us
    pallas_call x6, Pallas kernels, local(): pl.pallas_call(kernel, in_specs=specs, out_specs=[VMEM] * len(outputs), o...  4.24 us
    ppermute x2, starting transfers between devices, rotated(): lax.ppermute(value, axis, [(source, (source + steps) % count) for source...  3.29 us
    dot_general x2, matrix products, product(): return jnp.dot(a, b, preferred_element_type=jnp.float32)  3.18 us
    ppermute x1, starting transfers between devices, body(): entered = lax.ppermute(last, 'row', list(enumerate(across)))  2.59 us
    dot_general x2, matrix products, project(): lax.dot_general(basis, vectors, (((0,), (0,)), ((), ())), preferred_eleme...  1.69 us
    ppermute x2, waiting for transfers between devices, rotated(): lax.ppermute(value, axis, [(source, (source + steps) % count) for source...  1.34 us
    ppermute x1, starting transfers between devices, shifted(): lax.ppermute(value, axis, [(source, source + steps) for source in range(l...  1.28 us
  transfers between devices with their start and end apart: 4, of which 2 were waited for; matrix products, arithmetic and copies ran while one was open for 14% of the time, Pallas kernels for 3%

profile of v30, /device:TPU:0, one launch (start us, length us, event | category | flops | bytes accessed | tf_op | source)
XLA Modules:
  0.0 39.9 jit_solution(17442581351402714345)
XLA Ops:
  0.0 0.0 copy-start
  0.0 3.0 %collective-permute-start.2 = (bf16[1024,128]{1,0:T(8,128)(2,1)}, bf16[1024,128]{1,0:T(8,128)(2,1)}, u32[]{:S(2)}, u32[]{:S(2)}) collective-permute-start(bf16[1024,128]{1,0:T(8,128)(2,1)} %bitcast.17), channel_id=1, source_target_pairs={{0,16},{16,0},{1,17},{17,1},{2,18},{18,2},{3,19},{19,3},{4,20},{20... | collective-permute-start | bytes 786440 | tf_op jit(solution)/shard_map/ppermute | solution.py:17
  3.0 1.3 %collective-permute-start.1 = (bf16[1024,128]{1,0:T(8,128)(2,1)}, bf16[1024,128]{1,0:T(8,128)(2,1)}, u32[]{:S(2)}, u32[]{:S(2)}) collective-permute-start(bf16[1024,128]{1,0:T(8,128)(2,1)} %param.10), channel_id=1, source_target_pairs={{1,0},{2,1},{3,2},{4,3},{5,4},{6,5},{7,6},{8,7},{9,8},{10,9},{11,1... | collective-permute-start | bytes 786440 | tf_op jit(solution)/shard_map/ppermute | solution.py:12
  4.3 0.0 copy-done
  4.3 2.5 %convolution_convert_fusion.refs_6_.applied_ref = bf16[1024,512]{1,0:T(8,128)(2,1)S(1)} fusion(bf16[1024,1024]{1,0:T(8,128)(2,1)S(1)} %copy-done, bf16[1024,512]{1,0:T(8,128)(2,1)} %param.12), kind=kOutput, calls=%fused_computation | convolution fusion | flops 1074266112 | bytes 4194304 | tf_op jit(solution)/shard_map/dot_general | solution.py:27
  6.8 0.0 copy-start.1
  6.8 0.3 fusion.1.refs_0_
  7.1 0.3 collective-permute-start
  7.4 0.9 %constant_dynamic-slice_fusion.entry_ref = f32[128,64]{1,0:T(8,128)S(1)} fusion(f32[128,512]{1,0:T(8,128)} %param.13, s32[]{:T(128)S(6)} %select_n.3), kind=kLoop, calls=%fused_computation.6 | loop fusion | bytes 65540 | tf_op jit(solution)/shard_map/dynamic_slice | solution.py:166
  8.3 1.3 %collective-permute-done.2.refs_0_ = bf16[1024,128]{1,0:T(8,128)(2,1)} collective-permute-done((bf16[1024,128]{1,0:T(8,128)(2,1)}, bf16[1024,128]{1,0:T(8,128)(2,1)}, u32[]{:S(2)}, u32[]{:S(2)}) %collective-permute-start.2) | collective-permute-done | bytes 262176 | tf_op jit(solution)/shard_map/ppermute | solution.py:17
  9.6 1.0 %shard_map.73.refs_3_ = bf16[1024,128]{1,0:T(8,128)(2,1)S(1)} custom-call(bf16[1024,128]{1,0:T(8,128)(2,1)} %collective-permute-done.2.refs_0_), custom_call_target="tpu_custom_call" | custom-call | tf_op jit(solution)/shard_map/pallas_call | solution.py:130
  10.6 0.0 collective-permute-done.1.refs_5_
  10.6 1.4 %fusion.3.refs_4_ = f32[128,1024]{1,0:T(8,128)S(1)} fusion(bf16[1024,128]{1,0:T(8,128)(2,1)} %collective-permute-done.1.refs_5_, bf16[1024,1024]{1,0:T(8,128)(2,1)S(1)} %copy-done), kind=kOutput, calls=%fused_computation.7 | convolution fusion | flops 268435456 | bytes 2883584 | tf_op jit(solution)/shard_map/dot_general | solution.py:21
  12.0 0.0 collective-permute-done.refs_1_
  12.1 1.7 %shard_map.74 = bf16[8,192,128]{2,1,0:T(8,128)(2,1)S(1)} custom-call(bf16[128,128]{1,0:T(8,128)(2,1)S(1)} %fusion.1.refs_0_, bf16[128,128]{1,0:T(8,128)(2,1)S(1)} %collective-permute-done.refs_1_, bf16[1024,128]{1,0:T(8,128)(2,1)S(1)} %bitcast.18, bf16[1024,128]{1,0:T(8,128)(2,1)S(1)} %shard_map.73.refs_3_, f32[128,1024]{1,0:T(8,128)S(1)} %fusion.3.refs_4_, ...), custom_call_target="tpu_custom_call" | custom-call | tf_op jit(solution)/shard_map/pallas_call | solution.py:130
  13.7 12.1 %all_to_all.10.steps_ref = bf16[8,192,128]{2,1,0:T(8,128)(2,1)S(1)} all-to-all(bf16[8,192,128]{2,1,0:T(8,128)(2,1)S(1)} %shard_map.74), channel_id=1, replica_groups={{0,1,2,3,4,5,6,7},{9,8,11,10,13,12,15,14},{16,17,18,19,20,21,22,23},{25..., dimensions={0} | all-to-all | bytes 786432 | tf_op jit(solution)/shard_map/all_to_all | solution.py:141
  25.8 1.1 %shard_map.75 = (f32[8,64,128]{2,1,0:T(8,128)S(1)}, bf16[64,128]{1,0:T(8,128)(2,1)S(1)}) custom-call(s32[1]{0:T(128)} %bitcast.3.upper_ref, bf16[8,192,128]{2,1,0:T(8,128)(2,1)S(1)} %all_to_all.10.steps_ref, f32[128,64]{1,0:T(8,128)S(1)} %constant_dynamic-slice_fusion.entry_ref), custom_call_target="tpu_custom_call" | custom-call | tf_op jit(solution)/shard_map/pallas_call | solution.py:130
  26.9 2.6 %collective-permute-start.3 = (bf16[64,128]{1,0:T(8,128)(2,1)S(1)}, bf16[64,128]{1,0:T(8,128)(2,1)S(1)}, u32[]{:S(2)}, u32[]{:S(2)}) collective-permute-start(bf16[64,128]{1,0:T(8,128)(2,1)S(1)} %get-tuple-element.45), channel_id=1, source_target_pairs={{0,9},{1,8},{2,11},{3,10},{4,13},{5,12},{6,15},{7,14},{16,25},{17,... | collective-permute-start | bytes 49160 | tf_op jit(solution)/shard_map/ppermute | solution.py:184
  29.5 0.3 shard_map.76
  29.8 0.7 %fusion.gain_ref = bf16[1024,128]{1,0:T(8,128)(2,1)S(1)} fusion(bf16[1024,1024]{1,0:T(8,128)(2,1)S(1)} %copy-done, bf16[1024,128]{1,0:T(8,128)(2,1)S(1)} %shard_map.76), kind=kOutput, calls=%fused_computation.2 | convolution fusion | flops 268566528 | bytes 2621440 | tf_op jit(solution)/shard_map/dot_general | solution.py:27
  30.6 0.4 collective-permute-done.3.entered_ref
  30.9 0.2 shard_map.78
  31.1 7.6 %all_to_all.11 = bf16[8,64,128]{2,1,0:T(8,128)(2,1)S(1)} all-to-all(bf16[8,64,128]{2,1,0:T(8,128)(2,1)S(1)} %shard_map.78), channel_id=1, replica_groups={{0,1,2,3,4,5,6,7},{9,8,11,10,13,12,15,14},{16,17,18,19,20,21,22,23},{25..., dimensions={0} | all-to-all | bytes 262144 | tf_op jit(solution)/shard_map/all_to_all | solution.py:141
  38.7 1.2 %shard_map.79 = bf16[1024,512]{1,0:T(8,128)(2,1)} custom-call(bf16[1024,128]{1,0:T(8,128)(2,1)S(1)} %fusion.gain_ref, bf16[512,128]{1,0:T(8,128)(2,1)S(1)} %bitcast.20, bf16[1024,512]{1,0:T(8,128)(2,1)S(1)} %convolution_convert_fusion.refs_6_.applied_ref), custom_call_target="tpu_custom_call" | custom-call | tf_op jit(solution)/shard_map/pallas_call | solution.py:203
  (6 shorter events, 0.1 us)
Async XLA Ops:
  0.0 4.3 %copy-start = (bf16[1024,1024]{1,0:T(8,128)(2,1)S(1)}, bf16[1024,1024]{1,0:T(8,128)(2,1)}, u32[]{:S(2)}) copy-start(bf16[1024,1024]{1,0:T(8,128)(2,1)} %param.11) | copy-start | bytes 6291460
  0.0 6.8 %copy-start.2 = (bf16[1024,128]{1,0:T(8,128)(2,1)S(1)}, bf16[1024,128]{1,0:T(8,128)(2,1)}, u32[]{:S(2)}) copy-start(bf16[1024,128]{1,0:T(8,128)(2,1)} %param.9) | copy-start | bytes 786436
  0.0 6.8 %copy-start.3 = (bf16[1,1024,128]{2,1,0:T(8,128)(2,1)S(1)}, bf16[1,1024,128]{2,1,0:T(8,128)(2,1)}, u32[]{:S(2)}) copy-start(bf16[1,1024,128]{2,1,0:T(8,128)(2,1)} %param.8) | copy-start | bytes 786436
  0.0 9.6 %collective-permute-start.2 = (bf16[1024,128]{1,0:T(8,128)(2,1)}, bf16[1024,128]{1,0:T(8,128)(2,1)}, u32[]{:S(2)}, u32[]{:S(2)}) collective-permute-start(bf16[1024,128]{1,0:T(8,128)(2,1)} %bitcast.17), channel_id=1, source_target_pairs={{0,16},{16,0},{1,17},{17,1},{2,18},{18,2},{3,19},{19,3},{4,20},{20... | collective-permute-start | bytes 786440 | tf_op jit(solution)/shard_map/ppermute | solution.py:17
  3.0 7.6 %collective-permute-start.1 = (bf16[1024,128]{1,0:T(8,128)(2,1)}, bf16[1024,128]{1,0:T(8,128)(2,1)}, u32[]{:S(2)}, u32[]{:S(2)}) collective-permute-start(bf16[1024,128]{1,0:T(8,128)(2,1)} %param.10), channel_id=1, source_target_pairs={{1,0},{2,1},{3,2},{4,3},{5,4},{6,5},{7,6},{8,7},{9,8},{10,9},{11,1... | collective-permute-start | bytes 786440 | tf_op jit(solution)/shard_map/ppermute | solution.py:12
  6.8 5.2 %copy-start.1 = (bf16[1,1024,128]{2,1,0:T(8,128)(2,1)S(1)}, bf16[1,1024,128]{2,1,0:T(8,128)(2,1)}, u32[]{:S(2)}) copy-start(bf16[1,1024,128]{2,1,0:T(8,128)(2,1)} %param.7) | copy-start | bytes 786436
  7.1 4.9 %collective-permute-start = (bf16[128,128]{1,0:T(8,128)(2,1)S(1)}, bf16[128,128]{1,0:T(8,128)(2,1)S(1)}, u32[]{:S(2)}, u32[]{:S(2)}) collective-permute-start(bf16[128,128]{1,0:T(8,128)(2,1)S(1)} %fusion.1.refs_0_), channel_id=1, source_target_pairs={{0,16},{16,0},{1,17},{17,1},{2,18},{18,2},{3,19},{19,3},{4,20},{20... | collective-permute-start | bytes 98312 | tf_op jit(solution)/shard_map/ppermute | solution.py:17
  26.9 4.0 %collective-permute-start.3 = (bf16[64,128]{1,0:T(8,128)(2,1)S(1)}, bf16[64,128]{1,0:T(8,128)(2,1)S(1)}, u32[]{:S(2)}, u32[]{:S(2)}) collective-permute-start(bf16[64,128]{1,0:T(8,128)(2,1)S(1)} %get-tuple-element.45), channel_id=1, source_target_pairs={{0,9},{1,8},{2,11},{3,10},{4,13},{5,12},{6,15},{7,14},{16,25},{17,... | collective-permute-start | bytes 49160 | tf_op jit(solution)/shard_map/ppermute | solution.py:184

commit v31 on v30

--- a/solution.py
+++ b/solution.py
@@ -42,6 +42,10 @@
     return both[: value.shape[0]] + both[value.shape[0] :]
 
 
+def make_shift(next_ref, applied_ref, shift_ref):
+    shift_ref[...] = project(next_ref[...], applied_ref[...]).T.astype(jnp.bfloat16)
+
+
 def lay(*refs):
     rank = refs[0].shape[1]
     for layer, ref in enumerate(refs[:-1]):
@@ -50,15 +54,14 @@
 
 def make_maps(layers, *refs):
     cores = jnp.concatenate([ref[...] for ref in refs[:layers]], axis=0)
-    left_ref, others_ref, weights_ref, next_ref, applied_ref, sent_ref = refs[layers:]
+    left_ref, others_ref, weights_ref, shift_ref, sent_ref = refs[layers:]
     lefts = jnp.concatenate([left_ref[...], others_ref[...]], axis=1)
-    shift_t = project(next_ref[...], applied_ref[...]).T.astype(jnp.bfloat16)
     map_t = wide(wide(weights_ref[...], lefts), cores).T.astype(jnp.bfloat16)
     rank = map_t.shape[0]
     share = sent_ref.shape[1] - rank
     for target in range(sent_ref.shape[0]):
         sent_ref[target, :rank] = map_t
-        sent_ref[target, rank:] = shift_t[target * share : (target + 1) * share]
+        sent_ref[target, rank:] = shift_ref[target * share : (target + 1) * share]
 
 
 def make_range(layers, *refs):
@@ -162,13 +165,16 @@
 
     (others,) = local(lay, lefts[1:], ((order, (layers - 1) * rank), half))
     next_rows, others = lax.optimization_barrier((next_rows, others))
+    (shift_t,) = local(make_shift, (next_rows, applied), ((width, rank), half))
     weights = project(next_rows, inverse_diag)
     entry = lax.dynamic_slice_in_dim(incoming, lower * share, share, 1)
     place = upper.reshape(1)
-    others, weights, entry, place = lax.optimization_barrier((others, weights, entry, place))
+    others, shift_t, weights, entry, place = lax.optimization_barrier(
+        (others, shift_t, weights, entry, place)
+    )
     (sent,) = local(
         lambda *refs: make_maps(layers, *refs),
-        (*cores, lefts[0], others, weights, next_rows, applied),
+        (*cores, lefts[0], others, weights, shift_t),
         ((lowers, rank + share, rank), half),
     )
     sent, others, entry, place = lax.optimization_barrier((sent, others, entry, place))

time: 40.3 us -> 38.7 us (0.960)
  matrix products: 4.86 us -> 3.91 us
  Pallas kernels: 5.47 us -> 4.78 us
    dot_general x2, matrix products: 1.69 us -> 0.74 us  [project(): lax.dot_general(basis, vectors, (((0,), (0,)), ((), ())), preferred_eleme...]
    pallas_call x6 -> x7, Pallas kernels: 4.24 us -> 3.55 us  [local(): pl.pallas_call(kernel, in_specs=specs, out_specs=[VMEM] * len(outputs), o...]
  transfers between devices with their start and end apart: 4 -> 4, of which waited for: 2 -> 2; matrix products, arithmetic and copies ran while one was open for 14% -> 13% of each run, Pallas kernels for 3% -> 4%
where the time goes in v31:
time: 38.7 us; the launch traced here: 38.3 us
  blocking collectives  19.5 us (50%)
  starting transfers between devices  7.27 us (19%)
  Pallas kernels  4.78 us (12%)
  matrix products  3.91 us (10%)
  waiting for transfers between devices  1.72 us (4%)
  local copies, waits for them, and re-layouts  0.97 us (3%)
    all_to_all x2, blocking collectives, exchanged(): lax.all_to_all(blocks, 'row', 0, 0, axis_index_groups=members, tiled=True)  19.5 us
    pallas_call x7, Pallas kernels, local(): pl.pallas_call(kernel, in_specs=specs, out_specs=[VMEM] * len(outputs), o...  3.55 us
    ppermute x2, starting transfers between devices, rotated(): lax.ppermute(value, axis, [(source, (source + steps) % count) for source...  3.28 us
    dot_general x2, matrix products, product(): return jnp.dot(a, b, preferred_element_type=jnp.float32)  3.17 us
    ppermute x1, starting transfers between devices, body(): entered = lax.ppermute(last, 'row', list(enumerate(across)))  2.7 us
    ppermute x2, waiting for transfers between devices, rotated(): lax.ppermute(value, axis, [(source, (source + steps) % count) for source...  1.36 us
    ppermute x1, starting transfers between devices, shifted(): lax.ppermute(value, axis, [(source, source + steps) for source in range(l...  1.28 us
    pallas_call x1, Pallas kernels, body(): pl.pallas_call(solve, in_specs=[VMEM] * 3, out_specs=pl.BlockSpec(memory_...  1.23 us
  transfers between devices with their start and end apart: 4, of which 2 were waited for; matrix products, arithmetic and copies ran while one was open for 13% of the time, Pallas kernels for 4%

profile of v31, /device:TPU:0, one launch (start us, length us, event | category | flops | bytes accessed | tf_op | source)
XLA Modules:
  0.0 38.3 jit_solution(14849079427422601898)
XLA Ops:
  0.0 3.0 %collective-permute-start.2 = (bf16[1024,128]{1,0:T(8,128)(2,1)}, bf16[1024,128]{1,0:T(8,128)(2,1)}, u32[]{:S(2)}, u32[]{:S(2)}) collective-permute-start(bf16[1024,128]{1,0:T(8,128)(2,1)} %bitcast.17), channel_id=1, source_target_pairs={{0,16},{16,0},{1,17},{17,1},{2,18},{18,2},{3,19},{19,3},{4,20},{20... | collective-permute-start | bytes 786440 | tf_op jit(solution)/shard_map/ppermute | solution.py:17
  3.0 1.3 %collective-permute-start.1 = (bf16[1024,128]{1,0:T(8,128)(2,1)}, bf16[1024,128]{1,0:T(8,128)(2,1)S(1)}, u32[]{:S(2)}, u32[]{:S(2)}) collective-permute-start(bf16[1024,128]{1,0:T(8,128)(2,1)} %param.10), channel_id=1, source_target_pairs={{1,0},{2,1},{3,2},{4,3},{5,4},{6,5},{7,6},{8,7},{9,8},{10,9},{11,1... | collective-permute-start | bytes 786440 | tf_op jit(solution)/shard_map/ppermute | solution.py:12
  4.3 2.5 %convolution_convert_fusion.applied_ref = bf16[1024,512]{1,0:T(8,128)(2,1)S(1)} fusion(bf16[1024,1024]{1,0:T(8,128)(2,1)S(1)} %copy-done, bf16[1024,512]{1,0:T(8,128)(2,1)} %param.12), kind=kOutput, calls=%fused_computation | convolution fusion | flops 1074266112 | bytes 4194304 | tf_op jit(solution)/shard_map/dot_general | solution.py:27
  6.8 0.3 fusion.1.refs_0_
  7.1 0.3 collective-permute-start
  7.4 0.9 %constant_dynamic-slice_fusion.entry_ref = f32[128,64]{1,0:T(8,128)S(1)} fusion(f32[128,512]{1,0:T(8,128)} %param.13, s32[]{:T(128)S(6)} %select_n.3), kind=kLoop, calls=%fused_computation.6 | loop fusion | bytes 65540 | tf_op jit(solution)/shard_map/dynamic_slice | solution.py:170
  8.3 1.4 %collective-permute-done.2.refs_0_ = bf16[1024,128]{1,0:T(8,128)(2,1)} collective-permute-done((bf16[1024,128]{1,0:T(8,128)(2,1)}, bf16[1024,128]{1,0:T(8,128)(2,1)}, u32[]{:S(2)}, u32[]{:S(2)}) %collective-permute-start.2) | collective-permute-done | bytes 262176 | tf_op jit(solution)/shard_map/ppermute | solution.py:17
  9.6 1.0 %shard_map.73.refs_3_ = bf16[1024,128]{1,0:T(8,128)(2,1)S(1)} custom-call(bf16[1024,128]{1,0:T(8,128)(2,1)} %collective-permute-done.2.refs_0_), custom_call_target="tpu_custom_call" | custom-call | tf_op jit(solution)/shard_map/pallas_call | solution.py:133
  10.6 0.0 copy-start.1
  10.6 0.0 collective-permute-done.1.next_ref
  10.6 0.5 %fusion.3.refs_4_ = f32[128,1024]{1,0:T(8,128)S(1)} fusion(bf16[1024,128]{1,0:T(8,128)(2,1)S(1)} %collective-permute-done.1.next_ref, bf16[1024,1024]{1,0:T(8,128)(2,1)S(1)} %copy-done), kind=kOutput, calls=%fused_computation.7 | convolution fusion | flops 268435456 | bytes 2883584 | tf_op jit(solution)/shard_map/dot_general | solution.py:21
  11.1 0.4 %shard_map.74.refs_5_ = bf16[512,128]{1,0:T(8,128)(2,1)S(1)} custom-call(bf16[1024,128]{1,0:T(8,128)(2,1)S(1)} %collective-permute-done.1.next_ref, bf16[1024,512]{1,0:T(8,128)(2,1)S(1)} %convolution_convert_fusion.applied_ref), custom_call_target="tpu_custom_call" | custom-call | tf_op jit(solution)/shard_map/pallas_call | solution.py:133
  11.5 0.0 collective-permute-done.refs_1_
  11.5 0.0 copy-done.1
  11.6 0.6 %shard_map.75 = bf16[8,192,128]{2,1,0:T(8,128)(2,1)S(1)} custom-call(bf16[128,128]{1,0:T(8,128)(2,1)S(1)} %fusion.1.refs_0_, bf16[128,128]{1,0:T(8,128)(2,1)S(1)} %collective-permute-done.refs_1_, bf16[1024,128]{1,0:T(8,128)(2,1)S(1)} %bitcast.18, bf16[1024,128]{1,0:T(8,128)(2,1)S(1)} %shard_map.73.refs_3_, f32[128,1024]{1,0:T(8,128)S(1)} %fusion.3.refs_4_, ...), custom_call_target="tpu_custom_call" | custom-call | tf_op jit(solution)/shard_map/pallas_call | solution.py:133
  12.1 11.9 %all_to_all.10.steps_ref = bf16[8,192,128]{2,1,0:T(8,128)(2,1)S(1)} all-to-all(bf16[8,192,128]{2,1,0:T(8,128)(2,1)S(1)} %shard_map.75), channel_id=1, replica_groups={{0,1,2,3,4,5,6,7},{9,8,11,10,13,12,15,14},{16,17,18,19,20,21,22,23},{25..., dimensions={0} | all-to-all | bytes 786432 | tf_op jit(solution)/shard_map/all_to_all | solution.py:144
  24.1 1.1 %shard_map.76 = (f32[8,64,128]{2,1,0:T(8,128)S(1)}, bf16[64,128]{1,0:T(8,128)(2,1)S(1)}) custom-call(s32[1]{0:T(128)} %bitcast.3.upper_ref, bf16[8,192,128]{2,1,0:T(8,128)(2,1)S(1)} %all_to_all.10.steps_ref, f32[128,64]{1,0:T(8,128)S(1)} %constant_dynamic-slice_fusion.entry_ref), custom_call_target="tpu_custom_call" | custom-call | tf_op jit(solution)/shard_map/pallas_call | solution.py:133
  25.2 2.7 %collective-permute-start.3 = (bf16[64,128]{1,0:T(8,128)(2,1)S(1)}, bf16[64,128]{1,0:T(8,128)(2,1)S(1)}, u32[]{:S(2)}, u32[]{:S(2)}) collective-permute-start(bf16[64,128]{1,0:T(8,128)(2,1)S(1)} %get-tuple-element.47), channel_id=1, source_target_pairs={{0,9},{1,8},{2,11},{3,10},{4,13},{5,12},{6,15},{7,14},{16,25},{17,... | collective-permute-start | bytes 49160 | tf_op jit(solution)/shard_map/ppermute | solution.py:190
  27.9 0.3 shard_map.77
  28.2 0.7 %fusion.gain_ref = bf16[1024,128]{1,0:T(8,128)(2,1)S(1)} fusion(bf16[1024,1024]{1,0:T(8,128)(2,1)S(1)} %copy-done, bf16[1024,128]{1,0:T(8,128)(2,1)S(1)} %shard_map.77), kind=kOutput, calls=%fused_computation.2 | convolution fusion | flops 268566528 | bytes 2621440 | tf_op jit(solution)/shard_map/dot_general | solution.py:27
  28.9 0.4 collective-permute-done.3.entered_ref
  29.3 0.2 shard_map.79
  29.5 7.6 %all_to_all.11 = bf16[8,64,128]{2,1,0:T(8,128)(2,1)S(1)} all-to-all(bf16[8,64,128]{2,1,0:T(8,128)(2,1)S(1)} %shard_map.79), channel_id=1, replica_groups={{0,1,2,3,4,5,6,7},{9,8,11,10,13,12,15,14},{16,17,18,19,20,21,22,23},{25..., dimensions={0} | all-to-all | bytes 262144 | tf_op jit(solution)/shard_map/all_to_all | solution.py:144
  37.1 1.2 %shard_map.80 = bf16[1024,512]{1,0:T(8,128)(2,1)} custom-call(bf16[1024,128]{1,0:T(8,128)(2,1)S(1)} %fusion.gain_ref, bf16[512,128]{1,0:T(8,128)(2,1)S(1)} %bitcast.20, bf16[1024,512]{1,0:T(8,128)(2,1)S(1)} %convolution_convert_fusion.applied_ref), custom_call_target="tpu_custom_call" | custom-call | tf_op jit(solution)/shard_map/pallas_call | solution.py:209
  (7 shorter events, 0.1 us)
Async XLA Ops:
  0.0 4.3 %copy-start = (bf16[1024,1024]{1,0:T(8,128)(2,1)S(1)}, bf16[1024,1024]{1,0:T(8,128)(2,1)}, u32[]{:S(2)}) copy-start(bf16[1024,1024]{1,0:T(8,128)(2,1)} %param.11) | copy-start | bytes 6291460
  0.0 6.8 %copy-start.2 = (bf16[1024,128]{1,0:T(8,128)(2,1)S(1)}, bf16[1024,128]{1,0:T(8,128)(2,1)}, u32[]{:S(2)}) copy-start(bf16[1024,128]{1,0:T(8,128)(2,1)} %param.9) | copy-start | bytes 786436
  0.0 6.8 %copy-start.3 = (bf16[1,1024,128]{2,1,0:T(8,128)(2,1)S(1)}, bf16[1,1024,128]{2,1,0:T(8,128)(2,1)}, u32[]{:S(2)}) copy-start(bf16[1,1024,128]{2,1,0:T(8,128)(2,1)} %param.8) | copy-start | bytes 786436
  0.0 9.6 %collective-permute-start.2 = (bf16[1024,128]{1,0:T(8,128)(2,1)}, bf16[1024,128]{1,0:T(8,128)(2,1)}, u32[]{:S(2)}, u32[]{:S(2)}) collective-permute-start(bf16[1024,128]{1,0:T(8,128)(2,1)} %bitcast.17), channel_id=1, source_target_pairs={{0,16},{16,0},{1,17},{17,1},{2,18},{18,2},{3,19},{19,3},{4,20},{20... | collective-permute-start | bytes 786440 | tf_op jit(solution)/shard_map/ppermute | solution.py:17
  3.0 7.6 %collective-permute-start.1 = (bf16[1024,128]{1,0:T(8,128)(2,1)}, bf16[1024,128]{1,0:T(8,128)(2,1)S(1)}, u32[]{:S(2)}, u32[]{:S(2)}) collective-permute-start(bf16[1024,128]{1,0:T(8,128)(2,1)} %param.10), channel_id=1, source_target_pairs={{1,0},{2,1},{3,2},{4,3},{5,4},{6,5},{7,6},{8,7},{9,8},{10,9},{11,1... | collective-permute-start | bytes 786440 | tf_op jit(solution)/shard_map/ppermute | solution.py:12
  7.1 4.4 %collective-permute-start = (bf16[128,128]{1,0:T(8,128)(2,1)S(1)}, bf16[128,128]{1,0:T(8,128)(2,1)S(1)}, u32[]{:S(2)}, u32[]{:S(2)}) collective-permute-start(bf16[128,128]{1,0:T(8,128)(2,1)S(1)} %fusion.1.refs_0_), channel_id=1, source_target_pairs={{0,16},{16,0},{1,17},{17,1},{2,18},{18,2},{3,19},{19,3},{4,20},{20... | collective-permute-start | bytes 98312 | tf_op jit(solution)/shard_map/ppermute | solution.py:17
  10.6 1.0 %copy-start.1 = (bf16[1,1024,128]{2,1,0:T(8,128)(2,1)S(1)}, bf16[1,1024,128]{2,1,0:T(8,128)(2,1)}, u32[]{:S(2)}) copy-start(bf16[1,1024,128]{2,1,0:T(8,128)(2,1)} %param.7) | copy-start | bytes 786436
  25.2 4.1 %collective-permute-start.3 = (bf16[64,128]{1,0:T(8,128)(2,1)S(1)}, bf16[64,128]{1,0:T(8,128)(2,1)S(1)}, u32[]{:S(2)}, u32[]{:S(2)}) collective-permute-start(bf16[64,128]{1,0:T(8,128)(2,1)S(1)} %get-tuple-element.47), channel_id=1, source_target_pairs={{0,9},{1,8},{2,11},{3,10},{4,13},{5,12},{6,15},{7,14},{16,25},{17,... | collective-permute-start | bytes 49160 | tf_op jit(solution)/shard_map/ppermute | solution.py:190

commit v32 on v28

--- a/solution.py
+++ b/solution.py
@@ -42,10 +42,6 @@
     return both[: value.shape[0]] + both[value.shape[0] :]
 
 
-def make_shift(next_ref, applied_ref, shift_ref):
-    shift_ref[...] = project(next_ref[...], applied_ref[...]).T.astype(jnp.bfloat16)
-
-
 def lay(*refs):
     rank = refs[0].shape[1]
     for layer, ref in enumerate(refs[:-1]):
@@ -54,15 +50,16 @@
 
 def make_maps(layers, *refs):
     cores = jnp.concatenate([ref[...] for ref in refs[:layers]], axis=0)
-    left_ref, others_ref, weights_ref, shift_ref, range_ref, sent_ref = refs[layers:]
+    left_ref, others_ref, weights_ref, next_ref, applied_ref, range_ref, sent_ref = refs[layers:]
     lefts = jnp.concatenate([left_ref[...], others_ref[...]], axis=1)
+    shift_t = project(next_ref[...], applied_ref[...]).T.astype(jnp.bfloat16)
     range_ref[...] = (-product(lefts, cores)).astype(jnp.bfloat16)
     map_t = wide(wide(weights_ref[...], lefts), cores).T.astype(jnp.bfloat16)
     rank = map_t.shape[0]
     share = sent_ref.shape[1] - rank
     for target in range(sent_ref.shape[0]):
         sent_ref[target, :rank] = map_t
-        sent_ref[target, rank:] = shift_ref[target * share : (target + 1) * share]
+        sent_ref[target, rank:] = shift_t[target * share : (target + 1) * share]
 
 
 def chain(steps_ref, state, values_ref, swap):
@@ -159,16 +156,13 @@
 
     (others,) = local(lay, lefts[1:], ((order, (layers - 1) * rank), half))
     next_rows, others = lax.optimization_barrier((next_rows, others))
-    (shift_t,) = local(make_shift, (next_rows, applied), ((width, rank), half))
     weights = project(next_rows, inverse_diag)
     entry = lax.dynamic_slice_in_dim(incoming, lower * share, share, 1)
     place = upper.reshape(1)
-    others, shift_t, weights, entry, place = lax.optimization_barrier(
-        (others, shift_t, weights, entry, place)
-    )
+    weights, entry, place = lax.optimization_barrier((weights, entry, place))
     tile_range, sent = local(
         lambda *refs: make_maps(layers, *refs),
-        (*cores, lefts[0], others, weights, shift_t),
+        (*cores, lefts[0], others, weights, next_rows, applied),
         ((order, rank), half),
         ((lowers, rank + share, rank), half),
     )

time: 38.8 us -> 38.8 us (level)
    pallas_call x6 -> x5, Pallas kernels: 3.39 us -> 3.15 us  [local(): pl.pallas_call(kernel, in_specs=specs, out_specs=[VMEM] * len(outputs), o...]
  transfers between devices with their start and end apart: 4 -> 4, of which waited for: 2 -> 3; matrix products, arithmetic and copies ran while one was open for 13% -> 13% of each run, Pallas kernels for 4% -> 3%
where the time goes in v32:
time: 38.8 us; the launch traced here: 38.5 us
  blocking collectives  19.6 us (51%)
  starting transfers between devices  7.33 us (19%)
  Pallas kernels  4.38 us (11%)
  matrix products  3.92 us (10%)
  waiting for transfers between devices  2.13 us (5%)
  local copies, waits for them, and re-layouts  0.97 us (2%)
    all_to_all x2, blocking collectives, exchanged(): lax.all_to_all(blocks, 'row', 0, 0, axis_index_groups=members, tiled=True)  19.6 us
    ppermute x2, starting transfers between devices, rotated(): lax.ppermute(value, axis, [(source, (source + steps) % count) for source...  3.28 us
    dot_general x2, matrix products, product(): return jnp.dot(a, b, preferred_element_type=jnp.float32)  3.17 us
    pallas_call x5, Pallas kernels, local(): pl.pallas_call(kernel, in_specs=specs, out_specs=[VMEM] * len(outputs), o...  3.15 us
    ppermute x1, starting transfers between devices, body(): entered = lax.ppermute(last, 'row', list(enumerate(across)))  2.76 us
    ppermute x2, waiting for transfers between devices, rotated(): lax.ppermute(value, axis, [(source, (source + steps) % count) for source...  1.47 us
    ppermute x1, starting transfers between devices, shifted(): lax.ppermute(value, axis, [(source, source + steps) for source in range(l...  1.28 us
    pallas_call x1, Pallas kernels, body(): pl.pallas_call(solve, in_specs=[VMEM] * 3, out_specs=pl.BlockSpec(memory_...  1.23 us
  transfers between devices with their start and end apart: 4, of which 3 were waited for; matrix products, arithmetic and copies ran while one was open for 13% of the time, Pallas kernels for 3%

profile of v32, /device:TPU:0, one launch (start us, length us, event | category | flops | bytes accessed | tf_op | source)
XLA Modules:
  0.0 38.5 jit_solution(6102990223914298026)
XLA Ops:
  0.0 0.0 copy-start
  0.0 3.0 %collective-permute-start.2 = (bf16[1024,128]{1,0:T(8,128)(2,1)}, bf16[1024,128]{1,0:T(8,128)(2,1)}, u32[]{:S(2)}, u32[]{:S(2)}) collective-permute-start(bf16[1024,128]{1,0:T(8,128)(2,1)} %bitcast.18), channel_id=1, source_target_pairs={{0,16},{16,0},{1,17},{17,1},{2,18},{18,2},{3,19},{19,3},{4,20},{20... | collective-permute-start | bytes 786440 | tf_op jit(solution)/shard_map/ppermute | solution.py:17
  3.0 1.3 %collective-permute-start.1 = (bf16[1024,128]{1,0:T(8,128)(2,1)}, bf16[1024,128]{1,0:T(8,128)(2,1)S(1)}, u32[]{:S(2)}, u32[]{:S(2)}) collective-permute-start(bf16[1024,128]{1,0:T(8,128)(2,1)} %param.10), channel_id=1, source_target_pairs={{1,0},{2,1},{3,2},{4,3},{5,4},{6,5},{7,6},{8,7},{9,8},{10,9},{11,1... | collective-permute-start | bytes 786440 | tf_op jit(solution)/shard_map/ppermute | solution.py:12
  4.3 0.0 copy-done
  4.3 2.5 %convolution_convert_fusion.refs_6_.applied_ref = bf16[1024,512]{1,0:T(8,128)(2,1)S(1)} fusion(bf16[1024,1024]{1,0:T(8,128)(2,1)S(1)} %copy-done, bf16[1024,512]{1,0:T(8,128)(2,1)} %param.12), kind=kOutput, calls=%fused_computation | convolution fusion | flops 1074266112 | bytes 4194304 | tf_op jit(solution)/shard_map/dot_general | solution.py:27
  6.8 0.0 copy-done.2
  6.8 0.0 copy-done.3
  6.8 0.3 fusion.1.refs_0_
  7.1 0.3 collective-permute-start
  7.4 1.0 %constant_dynamic-slice_fusion.entry_ref = f32[128,64]{1,0:T(8,128)S(1)} fusion(f32[128,512]{1,0:T(8,128)} %param.13, s32[]{:T(128)S(6)} %select_n.3), kind=kLoop, calls=%fused_computation.6 | loop fusion | bytes 65540 | tf_op jit(solution)/shard_map/dynamic_slice | solution.py:160
  8.3 1.3 %collective-permute-done.2.refs_0_ = bf16[1024,128]{1,0:T(8,128)(2,1)} collective-permute-done((bf16[1024,128]{1,0:T(8,128)(2,1)}, bf16[1024,128]{1,0:T(8,128)(2,1)}, u32[]{:S(2)}, u32[]{:S(2)}) %collective-permute-start.2) | collective-permute-done | bytes 262176 | tf_op jit(solution)/shard_map/ppermute | solution.py:17
  9.6 1.0 %shard_map.73.refs_3_ = bf16[1024,128]{1,0:T(8,128)(2,1)S(1)} custom-call(bf16[1024,128]{1,0:T(8,128)(2,1)} %collective-permute-done.2.refs_0_), custom_call_target="tpu_custom_call" | custom-call | tf_op jit(solution)/shard_map/pallas_call | solution.py:124
  10.6 0.0 collective-permute-done.1.refs_5_
  10.6 0.5 %fusion.3.refs_4_ = f32[128,1024]{1,0:T(8,128)S(1)} fusion(bf16[1024,128]{1,0:T(8,128)(2,1)S(1)} %collective-permute-done.1.refs_5_, bf16[1024,1024]{1,0:T(8,128)(2,1)S(1)} %copy-done), kind=kOutput, calls=%fused_computation.7 | convolution fusion | flops 268435456 | bytes 2883584 | tf_op jit(solution)/shard_map/dot_general | solution.py:21
  11.1 0.2 collective-permute-done.refs_1_
  11.3 0.9 %shard_map.74 = (bf16[1024,128]{1,0:T(8,128)(2,1)S(1)}, bf16[8,192,128]{2,1,0:T(8,128)(2,1)S(1)}) custom-call(bf16[128,128]{1,0:T(8,128)(2,1)S(1)} %fusion.1.refs_0_, bf16[128,128]{1,0:T(8,128)(2,1)S(1)} %collective-permute-done.refs_1_, bf16[1024,128]{1,0:T(8,128)(2,1)S(1)} %bitcast.19, bf16[1024,128]{1,0:T(8,128)(2,1)S(1)} %shard_map.73.refs_3_, ...), custom_call_target="tpu_custom_call" | custom-call | tf_op jit(solution)/shard_map/pallas_call | solution.py:124
  12.1 12.1 %all_to_all.10.steps_ref = bf16[8,192,128]{2,1,0:T(8,128)(2,1)S(1)} all-to-all(bf16[8,192,128]{2,1,0:T(8,128)(2,1)S(1)} %get-tuple-element.39), channel_id=1, replica_groups={{0,1,2,3,4,5,6,7},{9,8,11,10,13,12,15,14},{16,17,18,19,20,21,22,23},{25..., dimensions={0} | all-to-all | bytes 786432 | tf_op jit(solution)/shard_map/all_to_all | solution.py:135
  24.2 1.1 %shard_map.75 = (f32[8,64,128]{2,1,0:T(8,128)S(1)}, bf16[64,128]{1,0:T(8,128)(2,1)S(1)}) custom-call(s32[1]{0:T(128)} %bitcast.3.upper_ref, bf16[8,192,128]{2,1,0:T(8,128)(2,1)S(1)} %all_to_all.10.steps_ref, f32[128,64]{1,0:T(8,128)S(1)} %constant_dynamic-slice_fusion.entry_ref), custom_call_target="tpu_custom_call" | custom-call | tf_op jit(solution)/shard_map/pallas_call | solution.py:124
  25.3 2.8 %collective-permute-start.3 = (bf16[64,128]{1,0:T(8,128)(2,1)S(1)}, bf16[64,128]{1,0:T(8,128)(2,1)S(1)}, u32[]{:S(2)}, u32[]{:S(2)}) collective-permute-start(bf16[64,128]{1,0:T(8,128)(2,1)S(1)} %get-tuple-element.47), channel_id=1, source_target_pairs={{0,9},{1,8},{2,11},{3,10},{4,13},{5,12},{6,15},{7,14},{16,25},{17,... | collective-permute-start | bytes 49160 | tf_op jit(solution)/shard_map/ppermute | solution.py:179
  28.1 0.7 %fusion.gain_ref = bf16[1024,128]{1,0:T(8,128)(2,1)S(1)} fusion(bf16[1024,1024]{1,0:T(8,128)(2,1)S(1)} %copy-done, bf16[1024,128]{1,0:T(8,128)(2,1)S(1)} %get-tuple-element.48), kind=kOutput, calls=%fused_computation.2 | convolution fusion | flops 268566528 | bytes 2621440 | tf_op jit(solution)/shard_map/dot_general | solution.py:27
  28.8 0.7 %collective-permute-done.3.entered_ref = bf16[64,128]{1,0:T(8,128)(2,1)S(1)} collective-permute-done((bf16[64,128]{1,0:T(8,128)(2,1)S(1)}, bf16[64,128]{1,0:T(8,128)(2,1)S(1)}, u32[]{:S(2)}, u32[]{:S(2)}) %collective-permute-start.3) | collective-permute-done | bytes 16416 | tf_op jit(solution)/shard_map/ppermute | solution.py:179
  29.5 0.2 shard_map.77
  29.7 7.6 %all_to_all.11 = bf16[8,64,128]{2,1,0:T(8,128)(2,1)S(1)} all-to-all(bf16[8,64,128]{2,1,0:T(8,128)(2,1)S(1)} %shard_map.77), channel_id=1, replica_groups={{0,1,2,3,4,5,6,7},{9,8,11,10,13,12,15,14},{16,17,18,19,20,21,22,23},{25..., dimensions={0} | all-to-all | bytes 262144 | tf_op jit(solution)/shard_map/all_to_all | solution.py:135
  37.3 1.2 %shard_map.78 = bf16[1024,512]{1,0:T(8,128)(2,1)} custom-call(bf16[1024,128]{1,0:T(8,128)(2,1)S(1)} %fusion.gain_ref, bf16[512,128]{1,0:T(8,128)(2,1)S(1)} %bitcast.17, bf16[1024,512]{1,0:T(8,128)(2,1)S(1)} %convolution_convert_fusion.refs_6_.applied_ref), custom_call_target="tpu_custom_call" | custom-call | tf_op jit(solution)/shard_map/pallas_call | solution.py:193
  (5 shorter events, 0.1 us)
Async XLA Ops:
  0.0 4.3 %copy-start = (bf16[1024,1024]{1,0:T(8,128)(2,1)S(1)}, bf16[1024,1024]{1,0:T(8,128)(2,1)}, u32[]{:S(2)}) copy-start(bf16[1024,1024]{1,0:T(8,128)(2,1)} %param.11) | copy-start | bytes 6291460
  0.0 6.8 %copy-start.2 = (bf16[1024,128]{1,0:T(8,128)(2,1)S(1)}, bf16[1024,128]{1,0:T(8,128)(2,1)}, u32[]{:S(2)}) copy-start(bf16[1024,128]{1,0:T(8,128)(2,1)} %param.9) | copy-start | bytes 786436
  0.0 6.8 %copy-start.3 = (bf16[1,1024,128]{2,1,0:T(8,128)(2,1)S(1)}, bf16[1,1024,128]{2,1,0:T(8,128)(2,1)}, u32[]{:S(2)}) copy-start(bf16[1,1024,128]{2,1,0:T(8,128)(2,1)} %param.8) | copy-start | bytes 786436
  0.0 9.6 %collective-permute-start.2 = (bf16[1024,128]{1,0:T(8,128)(2,1)}, bf16[1024,128]{1,0:T(8,128)(2,1)}, u32[]{:S(2)}, u32[]{:S(2)}) collective-permute-start(bf16[1024,128]{1,0:T(8,128)(2,1)} %bitcast.18), channel_id=1, source_target_pairs={{0,16},{16,0},{1,17},{17,1},{2,18},{18,2},{3,19},{19,3},{4,20},{20... | collective-permute-start | bytes 786440 | tf_op jit(solution)/shard_map/ppermute | solution.py:17
  3.0 7.6 %collective-permute-start.1 = (bf16[1024,128]{1,0:T(8,128)(2,1)}, bf16[1024,128]{1,0:T(8,128)(2,1)S(1)}, u32[]{:S(2)}, u32[]{:S(2)}) collective-permute-start(bf16[1024,128]{1,0:T(8,128)(2,1)} %param.10), channel_id=1, source_target_pairs={{1,0},{2,1},{3,2},{4,3},{5,4},{6,5},{7,6},{8,7},{9,8},{10,9},{11,1... | collective-permute-start | bytes 786440 | tf_op jit(solution)/shard_map/ppermute | solution.py:12
  7.1 4.2 %collective-permute-start = (bf16[128,128]{1,0:T(8,128)(2,1)S(1)}, bf16[128,128]{1,0:T(8,128)(2,1)S(1)}, u32[]{:S(2)}, u32[]{:S(2)}) collective-permute-start(bf16[128,128]{1,0:T(8,128)(2,1)S(1)} %fusion.1.refs_0_), channel_id=1, source_target_pairs={{0,16},{16,0},{1,17},{17,1},{2,18},{18,2},{3,19},{19,3},{4,20},{20... | collective-permute-start | bytes 98312 | tf_op jit(solution)/shard_map/ppermute | solution.py:17
  7.4 3.9 %copy-start.1 = (bf16[1,1024,128]{2,1,0:T(8,128)(2,1)S(1)}, bf16[1,1024,128]{2,1,0:T(8,128)(2,1)}, u32[]{:S(2)}) copy-start(bf16[1,1024,128]{2,1,0:T(8,128)(2,1)} %param.7) | copy-start | bytes 786436
  25.3 4.2 %collective-permute-start.3 = (bf16[64,128]{1,0:T(8,128)(2,1)S(1)}, bf16[64,128]{1,0:T(8,128)(2,1)S(1)}, u32[]{:S(2)}, u32[]{:S(2)}) collective-permute-start(bf16[64,128]{1,0:T(8,128)(2,1)S(1)} %get-tuple-element.47), channel_id=1, source_target_pairs={{0,9},{1,8},{2,11},{3,10},{4,13},{5,12},{6,15},{7,14},{16,25},{17,... | collective-permute-start | bytes 49160 | tf_op jit(solution)/shard_map/ppermute | solution.py:179

commit v33 on v31

--- a/solution.py
+++ b/solution.py
@@ -37,8 +37,9 @@
     return high, (value - high.astype(jnp.float32)).astype(jnp.bfloat16)
 
 
-def wide(value, matrix):
-    both = product(jnp.concatenate(split(value)), matrix)
+def wide(value, matrix, twice=False):
+    parts = jnp.concatenate(split(value))
+    both = product(jnp.concatenate([parts, parts], axis=1) if twice else parts, matrix)
     return both[: value.shape[0]] + both[value.shape[0] :]
 
 
@@ -83,7 +84,16 @@
 def first_half(upper_ref, steps_ref, entry_ref, values_ref, last_ref):
     @pl.when(upper_ref[0] == 0)
     def _():
-        last_ref[...] = chain(steps_ref, entry_ref[...].T, values_ref, 0).astype(jnp.bfloat16)
+        count, _, rank = steps_ref.shape
+        pairs = [product(steps_ref[k], steps_ref[k + 1, :rank]) for k in range(0, count, 2)]
+        state = entry_ref[...].T
+        for member, pair in zip(range(0, count, 2), pairs):
+            values_ref[member] = state
+            shift = steps_ref[member, rank:].astype(jnp.float32)
+            values_ref[member + 1] = wide(state, steps_ref[member, :rank]) + shift
+            moved = wide(state, jnp.concatenate(split(pair[:rank])), True)
+            state = moved + pair[rank:] + steps_ref[member + 1, rank:].astype(jnp.float32)
+        last_ref[...] = state.astype(jnp.bfloat16)
 
 
 def second_half(upper_ref, steps_ref, before_ref, values_ref, maps_ref):

time: 38.7 us -> 38.7 us (level)
  no operation moved by 1% of the time
where the time goes in v33:
time: 38.7 us; the launch traced here: 38.3 us
  blocking collectives  19.5 us (50%)
  starting transfers between devices  7.54 us (19%)
  Pallas kernels  4.49 us (12%)
  matrix products  3.91 us (10%)
  waiting for transfers between devices  1.72 us (4%)
  local copies, waits for them, and re-layouts  0.97 us (3%)
    all_to_all x2, blocking collectives, exchanged(): lax.all_to_all(blocks, 'row', 0, 0, axis_index_groups=members, tiled=True)  19.5 us
    ppermute x2, starting transfers between devices, rotated(): lax.ppermute(value, axis, [(source, (source + steps) % count) for source...  3.28 us
    pallas_call x7, Pallas kernels, local(): pl.pallas_call(kernel, in_specs=specs, out_specs=[VMEM] * len(outputs), o...  3.27 us
    dot_general x2, matrix products, product(): return jnp.dot(a, b, preferred_element_type=jnp.float32)  3.17 us
    ppermute x1, starting transfers between devices, body(): entered = lax.ppermute(last, 'row', list(enumerate(across)))  2.98 us
    ppermute x2, waiting for transfers between devices, rotated(): lax.ppermute(value, axis, [(source, (source + steps) % count) for source...  1.36 us
    ppermute x1, starting transfers between devices, shifted(): lax.ppermute(value, axis, [(source, source + steps) for source in range(l...  1.28 us
    pallas_call x1, Pallas kernels, body(): pl.pallas_call(solve, in_specs=[VMEM] * 3, out_specs=pl.BlockSpec(memory_...  1.23 us
  transfers between devices with their start and end apart: 4, of which 2 were waited for; matrix products, arithmetic and copies ran while one was open for 13% of the time, Pallas kernels for 4%

profile of v33, /device:TPU:0, one launch (start us, length us, event | category | flops | bytes accessed | tf_op | source)
XLA Modules:
  0.0 38.3 jit_solution(6102845564140794123)
XLA Ops:
  0.0 3.0 %collective-permute-start.2 = (bf16[1024,128]{1,0:T(8,128)(2,1)}, bf16[1024,128]{1,0:T(8,128)(2,1)}, u32[]{:S(2)}, u32[]{:S(2)}) collective-permute-start(bf16[1024,128]{1,0:T(8,128)(2,1)} %bitcast.17), channel_id=1, source_target_pairs={{0,16},{16,0},{1,17},{17,1},{2,18},{18,2},{3,19},{19,3},{4,20},{20... | collective-permute-start | bytes 786440 | tf_op jit(solution)/shard_map/ppermute | solution.py:17
  3.0 1.3 %collective-permute-start.1 = (bf16[1024,128]{1,0:T(8,128)(2,1)}, bf16[1024,128]{1,0:T(8,128)(2,1)S(1)}, u32[]{:S(2)}, u32[]{:S(2)}) collective-permute-start(bf16[1024,128]{1,0:T(8,128)(2,1)} %param.10), channel_id=1, source_target_pairs={{1,0},{2,1},{3,2},{4,3},{5,4},{6,5},{7,6},{8,7},{9,8},{10,9},{11,1... | collective-permute-start | bytes 786440 | tf_op jit(solution)/shard_map/ppermute | solution.py:12
  4.3 2.5 %convolution_convert_fusion.applied_ref = bf16[1024,512]{1,0:T(8,128)(2,1)S(1)} fusion(bf16[1024,1024]{1,0:T(8,128)(2,1)S(1)} %copy-done, bf16[1024,512]{1,0:T(8,128)(2,1)} %param.12), kind=kOutput, calls=%fused_computation | convolution fusion | flops 1074266112 | bytes 4194304 | tf_op jit(solution)/shard_map/dot_general | solution.py:27
  6.8 0.3 fusion.1.refs_0_
  7.1 0.3 collective-permute-start
  7.4 0.9 %constant_dynamic-slice_fusion.entry_ref = f32[128,64]{1,0:T(8,128)S(1)} fusion(f32[128,512]{1,0:T(8,128)} %param.13, s32[]{:T(128)S(6)} %select_n.3), kind=kLoop, calls=%fused_computation.6 | loop fusion | bytes 65540 | tf_op jit(solution)/shard_map/dynamic_slice | solution.py:180
  8.3 1.4 %collective-permute-done.2.refs_0_ = bf16[1024,128]{1,0:T(8,128)(2,1)} collective-permute-done((bf16[1024,128]{1,0:T(8,128)(2,1)}, bf16[1024,128]{1,0:T(8,128)(2,1)}, u32[]{:S(2)}, u32[]{:S(2)}) %collective-permute-start.2) | collective-permute-done | bytes 262176 | tf_op jit(solution)/shard_map/ppermute | solution.py:17
  9.6 1.0 %shard_map.73.refs_3_ = bf16[1024,128]{1,0:T(8,128)(2,1)S(1)} custom-call(bf16[1024,128]{1,0:T(8,128)(2,1)} %collective-permute-done.2.refs_0_), custom_call_target="tpu_custom_call" | custom-call | tf_op jit(solution)/shard_map/pallas_call | solution.py:143
  10.6 0.0 copy-start.1
  10.6 0.0 collective-permute-done.1.next_ref
  10.6 0.5 %fusion.3.refs_4_ = f32[128,1024]{1,0:T(8,128)S(1)} fusion(bf16[1024,128]{1,0:T(8,128)(2,1)S(1)} %collective-permute-done.1.next_ref, bf16[1024,1024]{1,0:T(8,128)(2,1)S(1)} %copy-done), kind=kOutput, calls=%fused_computation.7 | convolution fusion | flops 268435456 | bytes 2883584 | tf_op jit(solution)/shard_map/dot_general | solution.py:21
  11.1 0.4 %shard_map.74.refs_5_ = bf16[512,128]{1,0:T(8,128)(2,1)S(1)} custom-call(bf16[1024,128]{1,0:T(8,128)(2,1)S(1)} %collective-permute-done.1.next_ref, bf16[1024,512]{1,0:T(8,128)(2,1)S(1)} %convolution_convert_fusion.applied_ref), custom_call_target="tpu_custom_call" | custom-call | tf_op jit(solution)/shard_map/pallas_call | solution.py:143
  11.5 0.0 collective-permute-done.refs_1_
  11.5 0.0 copy-done.1
  11.6 0.6 %shard_map.75 = bf16[8,192,128]{2,1,0:T(8,128)(2,1)S(1)} custom-call(bf16[128,128]{1,0:T(8,128)(2,1)S(1)} %fusion.1.refs_0_, bf16[128,128]{1,0:T(8,128)(2,1)S(1)} %collective-permute-done.refs_1_, bf16[1024,128]{1,0:T(8,128)(2,1)S(1)} %bitcast.18, bf16[1024,128]{1,0:T(8,128)(2,1)S(1)} %shard_map.73.refs_3_, f32[128,1024]{1,0:T(8,128)S(1)} %fusion.3.refs_4_, ...), custom_call_target="tpu_custom_call" | custom-call | tf_op jit(solution)/shard_map/pallas_call | solution.py:143
  12.1 11.9 %all_to_all.10.steps_ref = bf16[8,192,128]{2,1,0:T(8,128)(2,1)S(1)} all-to-all(bf16[8,192,128]{2,1,0:T(8,128)(2,1)S(1)} %shard_map.75), channel_id=1, replica_groups={{0,1,2,3,4,5,6,7},{9,8,11,10,13,12,15,14},{16,17,18,19,20,21,22,23},{25..., dimensions={0} | all-to-all | bytes 786432 | tf_op jit(solution)/shard_map/all_to_all | solution.py:154
  24.1 0.8 %shard_map.76 = (f32[8,64,128]{2,1,0:T(8,128)S(1)}, bf16[64,128]{1,0:T(8,128)(2,1)S(1)}) custom-call(s32[1]{0:T(128)} %bitcast.3.upper_ref, bf16[8,192,128]{2,1,0:T(8,128)(2,1)S(1)} %all_to_all.10.steps_ref, f32[128,64]{1,0:T(8,128)S(1)} %constant_dynamic-slice_fusion.entry_ref), custom_call_target="tpu_custom_call" | custom-call | tf_op jit(solution)/shard_map/pallas_call | solution.py:143
  24.9 3.0 %collective-permute-start.3 = (bf16[64,128]{1,0:T(8,128)(2,1)S(1)}, bf16[64,128]{1,0:T(8,128)(2,1)S(1)}, u32[]{:S(2)}, u32[]{:S(2)}) collective-permute-start(bf16[64,128]{1,0:T(8,128)(2,1)S(1)} %get-tuple-element.47), channel_id=1, source_target_pairs={{0,9},{1,8},{2,11},{3,10},{4,13},{5,12},{6,15},{7,14},{16,25},{17,... | collective-permute-start | bytes 49160 | tf_op jit(solution)/shard_map/ppermute | solution.py:200
  27.9 0.3 shard_map.77
  28.2 0.7 %fusion.gain_ref = bf16[1024,128]{1,0:T(8,128)(2,1)S(1)} fusion(bf16[1024,1024]{1,0:T(8,128)(2,1)S(1)} %copy-done, bf16[1024,128]{1,0:T(8,128)(2,1)S(1)} %shard_map.77), kind=kOutput, calls=%fused_computation.2 | convolution fusion | flops 268566528 | bytes 2621440 | tf_op jit(solution)/shard_map/dot_general | solution.py:27
  28.9 0.4 collective-permute-done.3.entered_ref
  29.3 0.2 shard_map.79
  29.5 7.6 %all_to_all.11 = bf16[8,64,128]{2,1,0:T(8,128)(2,1)S(1)} all-to-all(bf16[8,64,128]{2,1,0:T(8,128)(2,1)S(1)} %shard_map.79), channel_id=1, replica_groups={{0,1,2,3,4,5,6,7},{9,8,11,10,13,12,15,14},{16,17,18,19,20,21,22,23},{25..., dimensions={0} | all-to-all | bytes 262144 | tf_op jit(solution)/shard_map/all_to_all | solution.py:154
  37.1 1.2 %shard_map.80 = bf16[1024,512]{1,0:T(8,128)(2,1)} custom-call(bf16[1024,128]{1,0:T(8,128)(2,1)S(1)} %fusion.gain_ref, bf16[512,128]{1,0:T(8,128)(2,1)S(1)} %bitcast.20, bf16[1024,512]{1,0:T(8,128)(2,1)S(1)} %convolution_convert_fusion.applied_ref), custom_call_target="tpu_custom_call" | custom-call | tf_op jit(solution)/shard_map/pallas_call | solution.py:219
  (7 shorter events, 0.1 us)
Async XLA Ops:
  0.0 4.3 %copy-start = (bf16[1024,1024]{1,0:T(8,128)(2,1)S(1)}, bf16[1024,1024]{1,0:T(8,128)(2,1)}, u32[]{:S(2)}) copy-start(bf16[1024,1024]{1,0:T(8,128)(2,1)} %param.11) | copy-start | bytes 6291460
  0.0 6.8 %copy-start.2 = (bf16[1024,128]{1,0:T(8,128)(2,1)S(1)}, bf16[1024,128]{1,0:T(8,128)(2,1)}, u32[]{:S(2)}) copy-start(bf16[1024,128]{1,0:T(8,128)(2,1)} %param.9) | copy-start | bytes 786436
  0.0 6.8 %copy-start.3 = (bf16[1,1024,128]{2,1,0:T(8,128)(2,1)S(1)}, bf16[1,1024,128]{2,1,0:T(8,128)(2,1)}, u32[]{:S(2)}) copy-start(bf16[1,1024,128]{2,1,0:T(8,128)(2,1)} %param.8) | copy-start | bytes 786436
  0.0 9.6 %collective-permute-start.2 = (bf16[1024,128]{1,0:T(8,128)(2,1)}, bf16[1024,128]{1,0:T(8,128)(2,1)}, u32[]{:S(2)}, u32[]{:S(2)}) collective-permute-start(bf16[1024,128]{1,0:T(8,128)(2,1)} %bitcast.17), channel_id=1, source_target_pairs={{0,16},{16,0},{1,17},{17,1},{2,18},{18,2},{3,19},{19,3},{4,20},{20... | collective-permute-start | bytes 786440 | tf_op jit(solution)/shard_map/ppermute | solution.py:17
  3.0 7.6 %collective-permute-start.1 = (bf16[1024,128]{1,0:T(8,128)(2,1)}, bf16[1024,128]{1,0:T(8,128)(2,1)S(1)}, u32[]{:S(2)}, u32[]{:S(2)}) collective-permute-start(bf16[1024,128]{1,0:T(8,128)(2,1)} %param.10), channel_id=1, source_target_pairs={{1,0},{2,1},{3,2},{4,3},{5,4},{6,5},{7,6},{8,7},{9,8},{10,9},{11,1... | collective-permute-start | bytes 786440 | tf_op jit(solution)/shard_map/ppermute | solution.py:12
  7.1 4.4 %collective-permute-start = (bf16[128,128]{1,0:T(8,128)(2,1)S(1)}, bf16[128,128]{1,0:T(8,128)(2,1)S(1)}, u32[]{:S(2)}, u32[]{:S(2)}) collective-permute-start(bf16[128,128]{1,0:T(8,128)(2,1)S(1)} %fusion.1.refs_0_), channel_id=1, source_target_pairs={{0,16},{16,0},{1,17},{17,1},{2,18},{18,2},{3,19},{19,3},{4,20},{20... | collective-permute-start | bytes 98312 | tf_op jit(solution)/shard_map/ppermute | solution.py:17
  10.6 1.0 %copy-start.1 = (bf16[1,1024,128]{2,1,0:T(8,128)(2,1)S(1)}, bf16[1,1024,128]{2,1,0:T(8,128)(2,1)}, u32[]{:S(2)}) copy-start(bf16[1,1024,128]{2,1,0:T(8,128)(2,1)} %param.7) | copy-start | bytes 786436
  24.9 4.4 %collective-permute-start.3 = (bf16[64,128]{1,0:T(8,128)(2,1)S(1)}, bf16[64,128]{1,0:T(8,128)(2,1)S(1)}, u32[]{:S(2)}, u32[]{:S(2)}) collective-permute-start(bf16[64,128]{1,0:T(8,128)(2,1)S(1)} %get-tuple-element.47), channel_id=1, source_target_pairs={{0,9},{1,8},{2,11},{3,10},{4,13},{5,12},{6,15},{7,14},{16,25},{17,... | collective-permute-start | bytes 49160 | tf_op jit(solution)/shard_map/ppermute | solution.py:200

commit v34 on v31

--- a/solution.py
+++ b/solution.py
@@ -29,7 +29,7 @@
 
 SMEM = pl.BlockSpec(memory_space=pltpu.SMEM)
 VMEM = pl.BlockSpec(memory_space=pltpu.VMEM)
-PARTS = 4
+PARTS = 2
 
 
 def split(value):

time: 38.7 us -> 38.7 us (level)
  no operation moved by 1% of the time
where the time goes in v34:
time: 38.7 us; the launch traced here: 38.4 us
  blocking collectives  19.5 us (50%)
  starting transfers between devices  7.27 us (19%)
  Pallas kernels  4.83 us (12%)
  matrix products  3.91 us (10%)
  waiting for transfers between devices  1.72 us (4%)
  local copies, waits for them, and re-layouts  0.97 us (3%)
    all_to_all x2, blocking collectives, exchanged(): lax.all_to_all(blocks, 'row', 0, 0, axis_index_groups=members, tiled=True)  19.5 us
    pallas_call x7, Pallas kernels, local(): pl.pallas_call(kernel, in_specs=specs, out_specs=[VMEM] * len(outputs), o...  3.55 us
    ppermute x2, starting transfers between devices, rotated(): lax.ppermute(value, axis, [(source, (source + steps) % count) for source...  3.28 us
    dot_general x2, matrix products, product(): return jnp.dot(a, b, preferred_element_type=jnp.float32)  3.17 us
    ppermute x1, starting transfers between devices, body(): entered = lax.ppermute(last, 'row', list(enumerate(across)))  2.7 us
    ppermute x2, waiting for transfers between devices, rotated(): lax.ppermute(value, axis, [(source, (source + steps) % count) for source...  1.36 us
    ppermute x1, starting transfers between devices, shifted(): lax.ppermute(value, axis, [(source, source + steps) for source in range(l...  1.28 us
    pallas_call x1, Pallas kernels, body(): pl.pallas_call(solve, in_specs=[VMEM] * 3, out_specs=pl.BlockSpec(memory_...  1.28 us
  transfers between devices with their start and end apart: 4, of which 2 were waited for; matrix products, arithmetic and copies ran while one was open for 13% of the time, Pallas kernels for 4%

profile of v34, /device:TPU:0, one launch (start us, length us, event | category | flops | bytes accessed | tf_op | source)
XLA Modules:
  0.0 38.4 jit_solution(16889328485656914173)
XLA Ops:
  0.0 3.0 %collective-permute-start.2 = (bf16[1024,128]{1,0:T(8,128)(2,1)}, bf16[1024,128]{1,0:T(8,128)(2,1)}, u32[]{:S(2)}, u32[]{:S(2)}) collective-permute-start(bf16[1024,128]{1,0:T(8,128)(2,1)} %bitcast.17), channel_id=1, source_target_pairs={{0,16},{16,0},{1,17},{17,1},{2,18},{18,2},{3,19},{19,3},{4,20},{20... | collective-permute-start | bytes 786440 | tf_op jit(solution)/shard_map/ppermute | solution.py:17
  3.0 1.3 %collective-permute-start.1 = (bf16[1024,128]{1,0:T(8,128)(2,1)}, bf16[1024,128]{1,0:T(8,128)(2,1)S(1)}, u32[]{:S(2)}, u32[]{:S(2)}) collective-permute-start(bf16[1024,128]{1,0:T(8,128)(2,1)} %param.10), channel_id=1, source_target_pairs={{1,0},{2,1},{3,2},{4,3},{5,4},{6,5},{7,6},{8,7},{9,8},{10,9},{11,1... | collective-permute-start | bytes 786440 | tf_op jit(solution)/shard_map/ppermute | solution.py:12
  4.3 2.5 %convolution_convert_fusion.applied_ref = bf16[1024,512]{1,0:T(8,128)(2,1)S(1)} fusion(bf16[1024,1024]{1,0:T(8,128)(2,1)S(1)} %copy-done, bf16[1024,512]{1,0:T(8,128)(2,1)} %param.12), kind=kOutput, calls=%fused_computation | convolution fusion | flops 1074266112 | bytes 4194304 | tf_op jit(solution)/shard_map/dot_general | solution.py:27
  6.8 0.3 fusion.1.refs_0_
  7.1 0.3 collective-permute-start
  7.4 0.9 %constant_dynamic-slice_fusion.entry_ref = f32[128,64]{1,0:T(8,128)S(1)} fusion(f32[128,512]{1,0:T(8,128)} %param.13, s32[]{:T(128)S(6)} %select_n.3), kind=kLoop, calls=%fused_computation.6 | loop fusion | bytes 65540 | tf_op jit(solution)/shard_map/dynamic_slice | solution.py:170
  8.3 1.4 %collective-permute-done.2.refs_0_ = bf16[1024,128]{1,0:T(8,128)(2,1)} collective-permute-done((bf16[1024,128]{1,0:T(8,128)(2,1)}, bf16[1024,128]{1,0:T(8,128)(2,1)}, u32[]{:S(2)}, u32[]{:S(2)}) %collective-permute-start.2) | collective-permute-done | bytes 262176 | tf_op jit(solution)/shard_map/ppermute | solution.py:17
  9.6 1.0 %shard_map.73.refs_3_ = bf16[1024,128]{1,0:T(8,128)(2,1)S(1)} custom-call(bf16[1024,128]{1,0:T(8,128)(2,1)} %collective-permute-done.2.refs_0_), custom_call_target="tpu_custom_call" | custom-call | tf_op jit(solution)/shard_map/pallas_call | solution.py:133
  10.6 0.0 copy-start.1
  10.6 0.0 collective-permute-done.1.next_ref
  10.6 0.5 %fusion.3.refs_4_ = f32[128,1024]{1,0:T(8,128)S(1)} fusion(bf16[1024,128]{1,0:T(8,128)(2,1)S(1)} %collective-permute-done.1.next_ref, bf16[1024,1024]{1,0:T(8,128)(2,1)S(1)} %copy-done), kind=kOutput, calls=%fused_computation.7 | convolution fusion | flops 268435456 | bytes 2883584 | tf_op jit(solution)/shard_map/dot_general | solution.py:21
  11.1 0.4 %shard_map.74.refs_5_ = bf16[512,128]{1,0:T(8,128)(2,1)S(1)} custom-call(bf16[1024,128]{1,0:T(8,128)(2,1)S(1)} %collective-permute-done.1.next_ref, bf16[1024,512]{1,0:T(8,128)(2,1)S(1)} %convolution_convert_fusion.applied_ref), custom_call_target="tpu_custom_call" | custom-call | tf_op jit(solution)/shard_map/pallas_call | solution.py:133
  11.5 0.0 collective-permute-done.refs_1_
  11.5 0.0 copy-done.1
  11.6 0.6 %shard_map.75 = bf16[8,192,128]{2,1,0:T(8,128)(2,1)S(1)} custom-call(bf16[128,128]{1,0:T(8,128)(2,1)S(1)} %fusion.1.refs_0_, bf16[128,128]{1,0:T(8,128)(2,1)S(1)} %collective-permute-done.refs_1_, bf16[1024,128]{1,0:T(8,128)(2,1)S(1)} %bitcast.18, bf16[1024,128]{1,0:T(8,128)(2,1)S(1)} %shard_map.73.refs_3_, f32[128,1024]{1,0:T(8,128)S(1)} %fusion.3.refs_4_, ...), custom_call_target="tpu_custom_call" | custom-call | tf_op jit(solution)/shard_map/pallas_call | solution.py:133
  12.1 11.9 %all_to_all.10.steps_ref = bf16[8,192,128]{2,1,0:T(8,128)(2,1)S(1)} all-to-all(bf16[8,192,128]{2,1,0:T(8,128)(2,1)S(1)} %shard_map.75), channel_id=1, replica_groups={{0,1,2,3,4,5,6,7},{9,8,11,10,13,12,15,14},{16,17,18,19,20,21,22,23},{25..., dimensions={0} | all-to-all | bytes 786432 | tf_op jit(solution)/shard_map/all_to_all | solution.py:144
  24.1 1.1 %shard_map.76 = (f32[8,64,128]{2,1,0:T(8,128)S(1)}, bf16[64,128]{1,0:T(8,128)(2,1)S(1)}) custom-call(s32[1]{0:T(128)} %bitcast.3.upper_ref, bf16[8,192,128]{2,1,0:T(8,128)(2,1)S(1)} %all_to_all.10.steps_ref, f32[128,64]{1,0:T(8,128)S(1)} %constant_dynamic-slice_fusion.entry_ref), custom_call_target="tpu_custom_call" | custom-call | tf_op jit(solution)/shard_map/pallas_call | solution.py:133
  25.2 2.7 %collective-permute-start.3 = (bf16[64,128]{1,0:T(8,128)(2,1)S(1)}, bf16[64,128]{1,0:T(8,128)(2,1)S(1)}, u32[]{:S(2)}, u32[]{:S(2)}) collective-permute-start(bf16[64,128]{1,0:T(8,128)(2,1)S(1)} %get-tuple-element.47), channel_id=1, source_target_pairs={{0,9},{1,8},{2,11},{3,10},{4,13},{5,12},{6,15},{7,14},{16,25},{17,... | collective-permute-start | bytes 49160 | tf_op jit(solution)/shard_map/ppermute | solution.py:190
  27.9 0.3 shard_map.77
  28.2 0.7 %fusion.gain_ref = bf16[1024,128]{1,0:T(8,128)(2,1)S(1)} fusion(bf16[1024,1024]{1,0:T(8,128)(2,1)S(1)} %copy-done, bf16[1024,128]{1,0:T(8,128)(2,1)S(1)} %shard_map.77), kind=kOutput, calls=%fused_computation.2 | convolution fusion | flops 268566528 | bytes 2621440 | tf_op jit(solution)/shard_map/dot_general | solution.py:27
  28.9 0.4 collective-permute-done.3.entered_ref
  29.3 0.2 shard_map.79
  29.5 7.6 %all_to_all.11 = bf16[8,64,128]{2,1,0:T(8,128)(2,1)S(1)} all-to-all(bf16[8,64,128]{2,1,0:T(8,128)(2,1)S(1)} %shard_map.79), channel_id=1, replica_groups={{0,1,2,3,4,5,6,7},{9,8,11,10,13,12,15,14},{16,17,18,19,20,21,22,23},{25..., dimensions={0} | all-to-all | bytes 262144 | tf_op jit(solution)/shard_map/all_to_all | solution.py:144
  37.1 1.3 %shard_map.80 = bf16[1024,512]{1,0:T(8,128)(2,1)} custom-call(bf16[1024,128]{1,0:T(8,128)(2,1)S(1)} %fusion.gain_ref, bf16[512,128]{1,0:T(8,128)(2,1)S(1)} %bitcast.20, bf16[1024,512]{1,0:T(8,128)(2,1)S(1)} %convolution_convert_fusion.applied_ref), custom_call_target="tpu_custom_call" | custom-call | tf_op jit(solution)/shard_map/pallas_call | solution.py:209
  (7 shorter events, 0.1 us)
Async XLA Ops:
  0.0 4.3 %copy-start = (bf16[1024,1024]{1,0:T(8,128)(2,1)S(1)}, bf16[1024,1024]{1,0:T(8,128)(2,1)}, u32[]{:S(2)}) copy-start(bf16[1024,1024]{1,0:T(8,128)(2,1)} %param.11) | copy-start | bytes 6291460
  0.0 6.8 %copy-start.2 = (bf16[1024,128]{1,0:T(8,128)(2,1)S(1)}, bf16[1024,128]{1,0:T(8,128)(2,1)}, u32[]{:S(2)}) copy-start(bf16[1024,128]{1,0:T(8,128)(2,1)} %param.9) | copy-start | bytes 786436
  0.0 6.8 %copy-start.3 = (bf16[1,1024,128]{2,1,0:T(8,128)(2,1)S(1)}, bf16[1,1024,128]{2,1,0:T(8,128)(2,1)}, u32[]{:S(2)}) copy-start(bf16[1,1024,128]{2,1,0:T(8,128)(2,1)} %param.8) | copy-start | bytes 786436
  0.0 9.6 %collective-permute-start.2 = (bf16[1024,128]{1,0:T(8,128)(2,1)}, bf16[1024,128]{1,0:T(8,128)(2,1)}, u32[]{:S(2)}, u32[]{:S(2)}) collective-permute-start(bf16[1024,128]{1,0:T(8,128)(2,1)} %bitcast.17), channel_id=1, source_target_pairs={{0,16},{16,0},{1,17},{17,1},{2,18},{18,2},{3,19},{19,3},{4,20},{20... | collective-permute-start | bytes 786440 | tf_op jit(solution)/shard_map/ppermute | solution.py:17
  3.0 7.6 %collective-permute-start.1 = (bf16[1024,128]{1,0:T(8,128)(2,1)}, bf16[1024,128]{1,0:T(8,128)(2,1)S(1)}, u32[]{:S(2)}, u32[]{:S(2)}) collective-permute-start(bf16[1024,128]{1,0:T(8,128)(2,1)} %param.10), channel_id=1, source_target_pairs={{1,0},{2,1},{3,2},{4,3},{5,4},{6,5},{7,6},{8,7},{9,8},{10,9},{11,1... | collective-permute-start | bytes 786440 | tf_op jit(solution)/shard_map/ppermute | solution.py:12
  7.1 4.4 %collective-permute-start = (bf16[128,128]{1,0:T(8,128)(2,1)S(1)}, bf16[128,128]{1,0:T(8,128)(2,1)S(1)}, u32[]{:S(2)}, u32[]{:S(2)}) collective-permute-start(bf16[128,128]{1,0:T(8,128)(2,1)S(1)} %fusion.1.refs_0_), channel_id=1, source_target_pairs={{0,16},{16,0},{1,17},{17,1},{2,18},{18,2},{3,19},{19,3},{4,20},{20... | collective-permute-start | bytes 98312 | tf_op jit(solution)/shard_map/ppermute | solution.py:17
  10.6 1.0 %copy-start.1 = (bf16[1,1024,128]{2,1,0:T(8,128)(2,1)S(1)}, bf16[1,1024,128]{2,1,0:T(8,128)(2,1)}, u32[]{:S(2)}) copy-start(bf16[1,1024,128]{2,1,0:T(8,128)(2,1)} %param.7) | copy-start | bytes 786436
  25.2 4.1 %collective-permute-start.3 = (bf16[64,128]{1,0:T(8,128)(2,1)S(1)}, bf16[64,128]{1,0:T(8,128)(2,1)S(1)}, u32[]{:S(2)}, u32[]{:S(2)}) collective-permute-start(bf16[64,128]{1,0:T(8,128)(2,1)S(1)} %get-tuple-element.47), channel_id=1, source_target_pairs={{0,9},{1,8},{2,11},{3,10},{4,13},{5,12},{6,15},{7,14},{16,25},{17,... | collective-permute-start | bytes 49160 | tf_op jit(solution)/shard_map/ppermute | solution.py:190
